TPU v7x, 32 devices: a whole 2x2x4 slice. The times are simulated.
32 devices in a mesh: groups: 2 (over x), attn: 8 (over z, y), ffn: 2 (over core).
Axes of the slice: x: 2, y: 2, z: 4, core: 2. Of those that a mesh axis runs over, the one named last changes fastest.
Arguments:
- tokens: bfloat16 [256, 7168], P(('groups', 'attn', 'ffn')), parts along dimension 0, may hold values from -6 to 6
- expert_ids: int32 [256, 3], P(('groups', 'attn', 'ffn')), parts along dimension 0, may hold values from 0 to 3, all different within a row; in each aligned block of 8 rows (0 to 7, 8 to 15, ...) at most 7 rows name the same one
- route_weights: float32 [256, 3], P(('groups', 'attn', 'ffn')), parts along dimension 0, may hold values from 0.2 to 1
- gate_weight: bfloat16 [7168, 16384], P(None, ('attn', 'ffn')), may hold values from -0.0625 to 0.0625
- up_weight: bfloat16 [7168, 16384], P(None, ('attn', 'ffn')), may hold values from -0.0625 to 0.0625
- down_weight: bfloat16 [16384, 7168], P(('attn', 'ffn')), may hold values from -0.09375 to 0.09375
Outputs:
- mixed: bfloat16 [256, 7168], P(('groups', 'attn', 'ffn')), parts along dimension 0
There are 2 independent parts, one for each index of `groups`. A program takes and returns all parts, laid end to end along the dimension named above; an argument that names none is the same for every part. Nothing has to cross between parts.
Inputs may be any that keep to these rules, and one draw needn't show every extreme that they name: `expert_ids`: each row names 3 different experts; among the rows of one device no expert is named by more than 7 rows, a bound that some of them reach.
All inputs are finite; a program needn't handle non-finite values.
Results may differ from a plain program's by a relative error of at most 0.0049.
Values may be sent and summed in bfloat16 or wider, within the bound.
No kernel may reach another device: no remote copies, remote signals or barrier semaphores. Data moves between devices by JAX's collectives and lax.ppermute only.
A program may use at most 128 MiB of HBM per device.

v0:
```python
import jax
import jax.numpy as jnp
from jax import lax
from jax.sharding import PartitionSpec as P

EXPERTS = 4
TOP = 3
CAP = 7


def local(tokens, expert_ids, route_weights, gate_weight, up_weight, down_weight):
    tok_rows = tokens.shape[0]
    width = tokens.shape[1]
    attn_count = lax.axis_size("attn")
    pair_count = lax.axis_size("ffn")
    span_count = attn_count // EXPERTS
    slot_total = EXPERTS * CAP
    chosen = (expert_ids[:, :, None] == jnp.arange(EXPERTS, dtype=jnp.int32)[None, None, :]).astype(
        jnp.int32
    )
    flat_chosen = chosen.reshape(tok_rows * TOP, EXPERTS)
    earlier = jnp.cumsum(flat_chosen, axis=0) - flat_chosen
    slot_local = jnp.sum(earlier * flat_chosen, axis=1).reshape(tok_rows, TOP)
    slot_index = expert_ids * CAP + slot_local
    slot_range = jnp.arange(slot_total, dtype=jnp.int32)
    matches = slot_index[None, :, :] == slot_range[:, None, None]
    placing = jnp.sum(matches.astype(jnp.float32), axis=2).astype(jnp.bfloat16)
    blocks = jnp.dot(placing, tokens, preferred_element_type=jnp.float32).astype(jnp.bfloat16)
    blocks = blocks.reshape(EXPERTS, CAP, width)
    combining = jnp.sum(jnp.where(matches, route_weights[None, :, :], 0.0), axis=2).T
    outgoing = jnp.repeat(blocks, span_count * pair_count, axis=0)
    arrived = lax.all_to_all(outgoing, ("attn", "ffn"), split_axis=0, concat_axis=0, tiled=True)
    flat_rows = arrived.reshape(-1, width)
    gate_value = jnp.dot(flat_rows, gate_weight, preferred_element_type=jnp.float32)
    up_value = jnp.dot(flat_rows, up_weight, preferred_element_type=jnp.float32)
    hidden = (jax.nn.silu(gate_value) * up_value).astype(jnp.bfloat16)
    partial_value = jnp.dot(hidden, down_weight, preferred_element_type=jnp.float32)
    partial_value = partial_value.reshape(arrived.shape)
    returned = lax.all_to_all(
        partial_value, ("attn", "ffn"), split_axis=0, concat_axis=0, tiled=True
    )
    summed = jnp.sum(returned.reshape(EXPERTS, span_count * pair_count, CAP, width), axis=1)
    mixed = jnp.dot(
        combining,
        summed.reshape(slot_total, width),
        precision=lax.Precision.HIGHEST,
        preferred_element_type=jnp.float32,
    )
    return mixed.astype(jnp.bfloat16)


def solution(mesh):
    return jax.shard_map(
        local,
        mesh=mesh,
        in_specs=(
            P(("groups", "attn", "ffn"), None),
            P(("groups", "attn", "ffn"), None),
            P(("groups", "attn", "ffn"), None),
            P(None, ("attn", "ffn")),
            P(None, ("attn", "ffn")),
            P(("attn", "ffn"), None),
        ),
        out_specs=P(("groups", "attn", "ffn"), None),
        check_vma=False,
    )
```

profile of v0, /device:TPU:0, one launch (start us, length us, event | category | flops | bytes accessed | tf_op | source)
XLA Modules:
  0.0 167.1 jit_solution(5477028803614284146)
XLA Ops:
  0.0 0.0 copy-start
  0.0 0.8 copy.13
  0.8 0.1 eq.29
  0.9 0.1 fusion.8
  1.0 0.2 select_reduce_fusion.1
  1.2 0.1 reshape.27
  1.3 0.1 copy.15
  1.4 1.4 convert_reduce_fusion
  2.7 0.0 copy-done
  2.7 0.3 convolution_convert_fusion
  3.0 0.1 reshape.28
  3.2 0.2 broadcast_in_dim.22
  3.4 49.9 %all_to_all.10 = bf16[16,7,7168]{2,1,0:T(8,128)(2,1)S(1)} all-to-all(bf16[16,7,7168]{2,1,0:T(8,128)(2,1)S(1)} %bitcast.12), channel_id=1, replica_groups=mesh['groups'=2,'attn'=8,'ffn'=2] {'attn','ffn'}, dimensions={0} | all-to-all | bytes 3211264 | tf_op jit(solution)/shard_map/all_to_all | solution.py:32
  53.3 0.6 reshape.30
  54.0 7.3 %fusion.11 = f32[112,1024]{1,0:T(8,128)S(1)} fusion(bf16[112,7168]{1,0:T(8,128)(2,1)S(1)} %reshape.30, bf16[7168,1024]{1,0:T(8,128)(2,1)} %param.9), kind=kOutput, calls=%fused_computation.21 | convolution fusion | flops 1644167168 | bytes 16744448 | tf_op jit(solution)/shard_map/dot_general | solution.py:34
  61.3 15.4 %fusion.1 = f32[112,7168]{1,0:T(8,128)} fusion(bf16[1024,7168]{1,0:T(8,128)(2,1)} %param.11, bf16[112,7168]{1,0:T(8,128)(2,1)S(1)} %reshape.30, bf16[7168,1024]{1,0:T(8,128)(2,1)} %param.10, f32[112,1024]{1,0:T(8,128)S(1)} %fusion.11), kind=kOutput, calls=%fused_computation.5 | convolution fusion | flops 3289022464 | bytes 34635776 | tf_op jit(solution)/shard_map/dot_general | solution.py:37
  76.7 3.4 %reshape.31 = f32[16,7,7168]{2,1,0:T(8,128)} reshape(f32[112,7168]{1,0:T(8,128)} %fusion.1) | data formatting | bytes 6422528 | tf_op jit(solution)/shard_map/reshape | solution.py:38
  80.1 85.1 %all_to_all.11 = f32[16,7,7168]{2,1,0:T(8,128)S(1)} all-to-all(f32[16,7,7168]{2,1,0:T(8,128)} %reshape.31), channel_id=1, replica_groups=mesh['groups'=2,'attn'=8,'ffn'=2] {'attn','ffn'}, dimensions={0} | all-to-all | bytes 6422528 | tf_op jit(solution)/shard_map/all_to_all | solution.py:39
  165.2 0.0 copy-start.1
  165.2 0.2 bitcast_reduce_fusion
  165.4 0.1 reshape.33
  165.6 0.3 copy-done.1
  165.9 1.2 convolution_convert_fusion.1
  (2 shorter events, 0.1 us)
Async XLA Ops:
  0.0 2.7 %copy-start = (bf16[8,7168]{1,0:T(8,128)(2,1)S(1)}, bf16[8,7168]{1,0:T(8,128)(2,1)}, u32[]{:S(2)}) copy-start(bf16[8,7168]{1,0:T(8,128)(2,1)} %param.6) | copy-start | bytes 344068
  165.2 0.7 copy-start.1
where the time goes:
time: 168 us; the launch traced here: 167 us
  blocking collectives  135 us (80%)
  matrix products  24.2 us (14%)
  local copies, waits for them, and re-layouts  5.9 us (4%)
  other arithmetic  1.88 us (1%)
    all_to_all x1, blocking collectives, local(): lax.all_to_all(partial_value, ('attn', 'ffn'), split_axis=0, concat_axis=...  85.1 us
    all_to_all x1, blocking collectives, local(): lax.all_to_all(outgoing, ('attn', 'ffn'), split_axis=0, concat_axis=0, ti...  49.9 us
    dot_general x1, matrix products, local(): jnp.dot(hidden, down_weight, preferred_element_type=jnp.float32)  15.4 us
    dot_general x1, matrix products, local(): jnp.dot(flat_rows, gate_weight, preferred_element_type=jnp.float32)  7.28 us
    reshape x1, local copies, waits for them, and re-layouts, local(): partial_value = partial_value.reshape(arrived.shape)  3.42 us

commit v1 on v0

v1 whole, which is shorter than its diff:
```python
import jax
import jax.numpy as jnp
from jax import lax
from jax.sharding import PartitionSpec as P

EXPERTS = 4


def local(tokens, expert_ids, route_weights, gate_weight, up_weight, down_weight):
    span_count = lax.axis_size("attn") // EXPERTS
    expert = lax.axis_index("attn") // span_count
    coeff = jnp.sum(jnp.where(expert_ids[:, :, None] == jnp.arange(EXPERTS)[None, None, :], route_weights[:, :, None], 0.0), axis=1)
    rows = lax.all_gather(tokens, ("attn", "ffn"), axis=0, tiled=True)
    coeffs = lax.all_gather(coeff, ("attn", "ffn"), axis=0, tiled=True)
    own = jnp.sum(jnp.where(jnp.arange(EXPERTS)[None, :] == expert, coeffs, 0.0), axis=1, keepdims=True)
    gate_value = jnp.dot(rows, gate_weight, preferred_element_type=jnp.float32)
    up_value = jnp.dot(rows, up_weight, preferred_element_type=jnp.float32)
    hidden = (jax.nn.silu(gate_value) * up_value).astype(jnp.bfloat16)
    partial_value = jnp.dot(hidden, down_weight, preferred_element_type=jnp.float32) * own
    mixed = lax.psum_scatter(partial_value, ("attn", "ffn"), scatter_dimension=0, tiled=True)
    return mixed.astype(jnp.bfloat16)


def solution(mesh):
    return jax.shard_map(
        local,
        mesh=mesh,
        in_specs=(
            P(("groups", "attn", "ffn"), None),
            P(("groups", "attn", "ffn"), None),
            P(("groups", "attn", "ffn"), None),
            P(None, ("attn", "ffn")),
            P(None, ("attn", "ffn")),
            P(("attn", "ffn"), None),
        ),
        out_specs=P(("groups", "attn", "ffn"), None),
        check_vma=False,
    )
```

time: 168 us -> 152 us (0.905)
  blocking collectives: 135 us -> 23.2 us
  waiting for transfers between devices: 0 us -> 89.7 us
  between operations: 0.06 us -> 13.4 us
  local copies, waits for them, and re-layouts: 5.9 us -> 0.1 us
    all_to_all x2 -> x0, blocking collectives: 135 us -> none  [the longest x1 85.1 us: local(): lax.all_to_all(partial_value, ('attn', 'ffn'), split_axis=0, concat_axis=...]
    reduce_scatter x0 -> x1, waiting for transfers between devices: none -> 67.4 us  [local(): lax.psum_scatter(partial_value, ('attn', 'ffn'), scatter_dimension=0, til...]
    all_gather x0 -> x1, blocking collectives: none -> 23.2 us  [local(): coeffs = lax.all_gather(coeff, ('attn', 'ffn'), axis=0, tiled=True)]
    all_gather x0 -> x1, waiting for transfers between devices: none -> 21.5 us  [local(): rows = lax.all_gather(tokens, ('attn', 'ffn'), axis=0, tiled=True)]
    reshape x5 -> x0, local copies, waits for them, and re-layouts: 4.42 us -> none  [the longest x1 3.42 us: local(): partial_value = partial_value.reshape(arrived.shape)]
    dot_general x4 -> x2, matrix products: 24.2 us -> 23.2 us  [the longest x1 15.2 us: local(): jnp.dot(hidden, down_weight, preferred_element_type=jnp.float32) * own]
  transfers between devices with their start and end apart: 0 -> 2, of which waited for: 0 -> 2; matrix products, arithmetic and copies ran while one was open for 0% -> 1% of each run, Pallas kernels for 0% -> 0%
where the time goes in v1:
time: 152 us
  waiting for transfers between devices  89.7 us (59%)
  blocking collectives  23.2 us (15%)
  matrix products  23.2 us (15%)
  between operations  13.4 us (9%)
  other arithmetic  2.4 us (2%)
    reduce_scatter x1, waiting for transfers between devices, local(): lax.psum_scatter(partial_value, ('attn', 'ffn'), scatter_dimension=0, til...  67.4 us
    all_gather x1, blocking collectives, local(): coeffs = lax.all_gather(coeff, ('attn', 'ffn'), axis=0, tiled=True)  23.2 us
    all_gather x1, waiting for transfers between devices, local(): rows = lax.all_gather(tokens, ('attn', 'ffn'), axis=0, tiled=True)  21.5 us
    dot_general x1, matrix products, local(): jnp.dot(hidden, down_weight, preferred_element_type=jnp.float32) * own  15.2 us
    dot_general x1, matrix products, local(): gate_value = jnp.dot(rows, gate_weight, preferred_element_type=jnp.float32)  7.92 us
  transfers between devices with their start and end apart: 2, of which 2 were waited for; matrix products, arithmetic and copies ran while one was open for 1% of the time, Pallas kernels for 0%

profile of v1, /device:TPU:0, one launch (start us, length us, event | category | flops | bytes accessed | tf_op | source)
XLA Modules:
  0.0 152.0 jit_solution(4894925842697671973)
XLA Ops:
  6.5 0.0 all-gather.3.cloned.1.call-start
  6.5 0.7 all-gather.3.cloned.1.call-update
  7.3 0.0 reduce-scatter.2.cloned.1.call-start
  7.3 0.7 select_reduce_fusion
  8.0 23.2 %all-gather = f32[16,8,4]{1,2,0:T(4,128)S(1)} all-gather(f32[1,8,4]{1,2,0:T(4,128)S(1)} %bitcast.8), channel_id=1, replica_groups=mesh['groups'=2,'attn'=8,'ffn'=2] {'attn','ffn'}, dimensions={0}, use_global_device_ids=true | all-gather | bytes 2176 | tf_op jit(solution)/shard_map/all_gather | solution.py:14
  31.2 0.1 reshape.9
  31.3 0.1 select_reduce_fusion.1
  31.4 21.5 %all-gather.3.cloned.1.call-done = bf16[128,7168]{1,0:T(8,128)(2,1)} async-done(((bf16[8,7168]{1,0:T(8,128)(2,1)}), bf16[128,7168]{1,0:T(8,128)(2,1)}) %all-gather.3.cloned.1.call-update) | async-done | bytes 1835024 | tf_op jit(solution)/shard_map/all_gather | solution.py:13
  52.9 0.0 copy-start
  52.9 7.9 %fusion.8 = f32[128,1024]{1,0:T(8,128)S(1)} fusion(bf16[128,7168]{1,0:T(8,128)(2,1)} %all-gather.3.cloned.1.call-done, bf16[7168,1024]{1,0:T(8,128)(2,1)} %param.9), kind=kOutput, calls=%fused_computation.14 | convolution fusion | flops 1879048192 | bytes 17039360 | tf_op jit(solution)/shard_map/dot_general | solution.py:16
  60.9 0.0 copy-done
  60.9 15.2 %convolution_multiply_fusion = f32[128,7168]{1,0:T(8,128)} fusion(bf16[1024,7168]{1,0:T(8,128)(2,1)} %param.11, f32[128]{0:T(128)S(1)} %select_reduce_fusion.1, bf16[128,7168]{1,0:T(8,128)(2,1)S(1)} %copy-done, bf16[7168,1024]{1,0:T(8,128)(2,1)} %param.10, f32[128,1024]{1,0:T(8,128)S(1)} %fusion.8), kind=kOutput, calls=%fused_computation | convolution fusion | flops 3759800320 | bytes 35389952 | tf_op jit(solution)/shard_map/dot_general | solution.py:19
  76.1 0.0 reduce-scatter.2.cloned.1.call-update
  76.1 67.4 %reduce-scatter.2.cloned.1.call-done = f32[8,7168]{1,0:T(8,128)} async-done(((f32[128,7168]{1,0:T(8,128)}), f32[8,7168]{1,0:T(8,128)}) %reduce-scatter.2.cloned.1.call-update) | async-done | bytes 229392 | tf_op jit(solution)/shard_map/reduce_scatter | solution.py:20
  143.6 1.6 %convert_element_type.7 = bf16[8,7168]{1,0:T(8,128)(2,1)} convert(f32[8,7168]{1,0:T(8,128)} %reduce-scatter.2.cloned.1.call-done) | non-fusion elementwise | flops 57344 | bytes 344064 | tf_op jit(solution)/shard_map/convert_element_type | solution.py:21
  (2 shorter events, 0.0 us)
Async XLA Ops:
  6.5 46.4 %all-gather.3.cloned.1.call-start = ((), (), s32[]{:S(2)}) async-start(), calls=%async_computation.1 | async-start | bytes 1949696 | tf_op jit(solution)/shard_map/all_gather | solution.py:13
  7.3 136.3 %reduce-scatter.2.cloned.1.call-start = ((), (), s32[]{:S(2)}) async-start(), calls=%async_computation.2 | async-start | bytes 3899392 | tf_op jit(solution)/shard_map/reduce_scatter | solution.py:20
  52.9 7.9 %copy-start = (bf16[128,7168]{1,0:T(8,128)(2,1)S(1)}, bf16[128,7168]{1,0:T(8,128)(2,1)}, u32[]{:S(2)}) copy-start(bf16[128,7168]{1,0:T(8,128)(2,1)} %all-gather.3.cloned.1.call-done) | copy-start | bytes 5505028
Sparse Core Ops, SparseCore 0:
  9.6 43.2 all-gather.2
  76.3 67.2 reduce-scatter.1

commit v2 on v1

v2 whole, which is shorter than its diff:
```python
import functools

import jax
import jax.numpy as jnp
from jax import lax
from jax.experimental import pallas as pl
from jax.experimental.pallas import tpu as pltpu
from jax.sharding import PartitionSpec as P

EXPERTS = 4
IN_CHUNKS = 2
OUT_CHUNKS = 2
K_BLOCK = 512
C_BLOCK = 512
VMEM = 40 * 1024 * 1024


def params():
    return pltpu.CompilerParams(vmem_limit_bytes=VMEM)


def block_of(width, most):
    size = most
    while width % size:
        size -= 128
    return size


def gate_up_kernel(blocks, first, last, k_block, *refs):
    rows_in, rest = refs[:blocks], refs[blocks:]
    gate_ref, up_ref, rest = rest[0], rest[1], rest[2:]
    if not first:
        old_gate, old_up, rest = rest[0], rest[1], rest[2:]
    step = pl.program_id(0)
    if last:
        hidden_ref, acc_gate, acc_up = rest
    else:
        acc_gate, acc_up = rest

    @pl.when(step == 0)
    def _():
        if first:
            acc_gate[...] = jnp.zeros_like(acc_gate)
            acc_up[...] = jnp.zeros_like(acc_up)
        else:
            acc_gate[...] = old_gate[...]
            acc_up[...] = old_up[...]

    columns = pl.ds(pl.multiple_of(step * k_block, k_block), k_block)
    rows = jnp.concatenate([ref[:, columns].astype(jnp.float32) for ref in rows_in], axis=0).astype(jnp.bfloat16)
    acc_gate[...] += jnp.dot(rows, gate_ref[...], preferred_element_type=jnp.float32)
    acc_up[...] += jnp.dot(rows, up_ref[...], preferred_element_type=jnp.float32)

    if last:
        @pl.when(step == pl.num_programs(0) - 1)
        def _():
            gate = acc_gate[...]
            hidden_ref[...] = (gate / (1.0 + jnp.exp(-gate)) * acc_up[...]).astype(jnp.bfloat16)


def gate_up(rows, gate_weight, up_weight, sums, chunk, chunks):
    first, last = chunk == 0, chunk == chunks - 1
    total = sum(r.shape[0] for r in rows)
    width, units = rows[0].shape[1], gate_weight.shape[1]
    k_block = block_of(width, K_BLOCK)
    steps = width // k_block
    weight_spec = pl.BlockSpec((k_block, units), lambda k: (chunk * steps + k, 0))
    whole = lambda a: pl.BlockSpec(a.shape, lambda k: (0, 0))
    acc = jax.ShapeDtypeStruct((total, units), jnp.float32)
    if last:
        out_shape = jax.ShapeDtypeStruct((total, units), jnp.bfloat16)
        out_specs = whole(out_shape)
        scratch = [pltpu.VMEM(acc.shape, jnp.float32)] * 2
    else:
        out_shape, out_specs, scratch = [acc, acc], [whole(acc)] * 2, []
    return pl.pallas_call(
        functools.partial(gate_up_kernel, len(rows), first, last, k_block),
        grid=(steps,),
        in_specs=[whole(r) for r in rows] + [weight_spec] * 2 + ([] if first else [whole(acc)] * 2),
        out_specs=out_specs,
        out_shape=out_shape,
        scratch_shapes=scratch,
        compiler_params=params(),
        cost_estimate=pl.CostEstimate(flops=4 * total * width * units, bytes_accessed=4 * width * units, transcendentals=0),
        name="gate_up",
    )(*rows, gate_weight, up_weight, *sums)


def down_kernel(hidden_ref, down_ref, keep_ref, *send_refs):
    value = jnp.dot(hidden_ref[...], down_ref[...], preferred_element_type=jnp.float32)
    count = keep_ref.shape[0]
    keep_ref[...] = value[:count]
    for i, ref in enumerate(send_refs):
        ref[...] = value[(i + 1) * count:(i + 2) * count].astype(jnp.bfloat16)


def down(hidden, down_weight, chunk, chunks, pair):
    total, units = hidden.shape
    width = down_weight.shape[1] // chunks
    c_block = block_of(width, C_BLOCK)
    steps = width // c_block
    part = total // pair
    part_spec = pl.BlockSpec((part, c_block), lambda c: (0, c))
    return pl.pallas_call(
        down_kernel,
        grid=(steps,),
        in_specs=[
            pl.BlockSpec(hidden.shape, lambda c: (0, 0)),
            pl.BlockSpec((units, c_block), lambda c: (0, chunk * steps + c)),
        ],
        out_specs=[part_spec] * pair,
        out_shape=[jax.ShapeDtypeStruct((part, width), jnp.float32)]
        + [jax.ShapeDtypeStruct((part, width), jnp.bfloat16)] * (pair - 1),
        compiler_params=params(),
        cost_estimate=pl.CostEstimate(flops=2 * total * width * units, bytes_accessed=2 * width * units, transcendentals=0),
        name="down",
    )(hidden, down_weight)


def add_kernel(count, *refs):
    value = refs[0][...]
    for ref in refs[1:count]:
        value += ref[...].astype(jnp.float32)
    outs = refs[count:]
    part = outs[0].shape[0]
    outs[0][...] = value[:part]
    for i, ref in enumerate(outs[1:]):
        ref[...] = value[(i + 1) * part:(i + 2) * part].astype(jnp.bfloat16)


def add_split(keep, received, parts):
    total, width = keep.shape
    part = total // parts
    arrays = [keep] + received
    return pl.pallas_call(
        functools.partial(add_kernel, len(arrays)),
        out_shape=[jax.ShapeDtypeStruct((part, width), jnp.float32)]
        + [jax.ShapeDtypeStruct((part, width), jnp.bfloat16)] * (parts - 1),
        compiler_params=params(),
        cost_estimate=pl.CostEstimate(flops=total * width, bytes_accessed=12 * total * width, transcendentals=0),
        name="add_split",
    )(*arrays)


def combine_kernel(chunks, own_expert, ids_ref, weights_ref, *refs):
    out_ref = refs[-1]
    ids, weights = ids_ref[...], weights_ref[...]
    width = refs[0].shape[1]
    coeffs = []
    for s in range(EXPERTS):
        expert = lax.rem(own_expert[0] + s, EXPERTS)
        coeffs.append(jnp.sum(jnp.where(ids == expert, weights, 0.0), axis=1, keepdims=True))
    for chunk in range(chunks):
        value = None
        for s in range(EXPERTS):
            term = coeffs[s] * refs[chunk * EXPERTS + s][...].astype(jnp.float32)
            value = term if value is None else value + term
        out_ref[:, chunk * width:(chunk + 1) * width] = value.astype(jnp.bfloat16)


def combine(own_expert, ids, weights, parts):
    flat = [p for chunk in parts for p in chunk]
    rows, width = flat[0].shape
    return pl.pallas_call(
        functools.partial(combine_kernel, len(parts)),
        in_specs=[pl.BlockSpec(memory_space=pltpu.SMEM)] + [pl.BlockSpec(memory_space=pltpu.VMEM)] * (2 + len(flat)),
        out_shape=jax.ShapeDtypeStruct((rows, width * len(parts)), jnp.bfloat16),
        compiler_params=params(),
        name="combine",
    )(own_expert, ids, weights, *flat)


def local(tokens, expert_ids, route_weights, gate_weight, up_weight, down_weight):
    width = tokens.shape[1]
    attn = lax.axis_size("attn")
    pair = lax.axis_size("ffn")
    span = attn // EXPERTS

    def over_experts(value, shift):
        return lax.ppermute(value, "attn", [(i, (i + shift * span) % attn) for i in range(attn)])

    def over_span(value, shift):
        return lax.ppermute(value, "attn", [(i, i // span * span + (i + shift) % span) for i in range(attn)])

    def over_pair(value, shift):
        return lax.ppermute(value, "ffn", [(i, (i + shift) % pair) for i in range(pair)])

    part = width // IN_CHUNKS
    gathered = []
    for chunk in range(IN_CHUNKS):
        own = tokens[:, chunk * part:(chunk + 1) * part]
        column = [own] + [over_experts(own, s) for s in range(1, EXPERTS)]
        plane = column + [over_span(b, t) for t in range(1, span) for b in column]
        gathered.append(plane + [over_pair(b, p) for p in range(1, pair) for b in plane])

    sums = ()
    for chunk in range(IN_CHUNKS):
        sums = gate_up(gathered[chunk], gate_weight, up_weight, sums, chunk, IN_CHUNKS)
    hidden = sums

    parts = []
    for chunk in range(OUT_CHUNKS):
        keep, *sends = down(hidden, down_weight, chunk, OUT_CHUNKS, pair)
        received = [over_pair(b, -p) for p, b in enumerate(sends, 1)]
        keep, *sends = add_split(keep, received, span)
        received = [over_span(b, -t) for t, b in enumerate(sends, 1)]
        keep, *sends = add_split(keep, received, EXPERTS)
        parts.append([keep] + [over_experts(b, -s) for s, b in enumerate(sends, 1)])
    own_expert = (lax.axis_index("attn") // span).astype(jnp.int32).reshape(1)
    return combine(own_expert, expert_ids, route_weights, parts)


def solution(mesh):
    return jax.shard_map(
        local,
        mesh=mesh,
        in_specs=(
            P(("groups", "attn", "ffn"), None),
            P(("groups", "attn", "ffn"), None),
            P(("groups", "attn", "ffn"), None),
            P(None, ("attn", "ffn")),
            P(None, ("attn", "ffn")),
            P(("attn", "ffn"), None),
        ),
        out_specs=P(("groups", "attn", "ffn"), None),
        check_vma=False,
    )
```

time: 152 us -> 83.6 us (0.55)
  waiting for transfers between devices: 89.7 us -> 19.5 us
  starting transfers between devices: 0.04 us -> 32.1 us
  Pallas kernels: 0 us -> 30.3 us
  matrix products: 23.2 us -> 0 us
  blocking collectives: 23.2 us -> 0 us
  between operations: 13.4 us -> 0.15 us
  other arithmetic: 2.4 us -> 0 us
    reduce_scatter x1 -> x0, waiting for transfers between devices: 67.4 us -> none  [local(): lax.psum_scatter(partial_value, ('attn', 'ffn'), scatter_dimension=0, til...]
    ppermute x0 -> x40, starting transfers between devices: none -> 32.1 us  [the longest x12 16.8 us: over_experts(): lax.ppermute(value, 'attn', [(i, (i + shift * span) % attn) for i in rang...]
    pallas_call x0 -> x9, Pallas kernels: none -> 30.3 us  [the longest x2 16.7 us: gate_up(): pl.pallas_call(functools.partial(gate_up_kernel, len(rows), first, last,...]
    dot_general x2 -> x0, matrix products: 23.2 us -> none  [the longest x1 15.2 us: local(): jnp.dot(hidden, down_weight, preferred_element_type=jnp.float32) * own]
    all_gather x1 -> x0, blocking collectives: 23.2 us -> none  [local(): coeffs = lax.all_gather(coeff, ('attn', 'ffn'), axis=0, tiled=True)]
    all_gather x1 -> x0, waiting for transfers between devices: 21.5 us -> none  [local(): rows = lax.all_gather(tokens, ('attn', 'ffn'), axis=0, tiled=True)]
    ppermute x0 -> x40, waiting for transfers between devices: none -> 19.5 us  [the longest x10 11.3 us: over_span(): lax.ppermute(value, 'attn', [(i, i // span * span + (i + shift) % span) f...]
    convert_element_type x1 -> x0, other arithmetic: 1.6 us -> none  [local(): return mixed.astype(jnp.bfloat16)]
  transfers between devices with their start and end apart: 2 -> 40, of which waited for: 2 -> 16; matrix products, arithmetic and copies ran while one was open for 1% -> 0% of each run, Pallas kernels for 0% -> 18%
where the time goes in v2:
time: 83.6 us; the launch traced here: 83.1 us
  starting transfers between devices  32.1 us (38%)
  Pallas kernels  30.3 us (36%)
  waiting for transfers between devices  19.5 us (23%)
  local copies, waits for them, and re-layouts  1.03 us (1%)
    ppermute x12, starting transfers between devices, over_experts(): lax.ppermute(value, 'attn', [(i, (i + shift * span) % attn) for i in rang...  16.8 us
    pallas_call x2, Pallas kernels, gate_up(): pl.pallas_call(functools.partial(gate_up_kernel, len(rows), first, last,...  16.7 us
    pallas_call x2, Pallas kernels, down(): pl.pallas_call(down_kernel, grid=(steps,), in_specs=[pl.BlockSpec(hidden....  12.6 us
    ppermute x10, starting transfers between devices, over_span(): lax.ppermute(value, 'attn', [(i, i // span * span + (i + shift) % span) f...  12.2 us
    ppermute x10, waiting for transfers between devices, over_span(): lax.ppermute(value, 'attn', [(i, i // span * span + (i + shift) % span) f...  11.3 us
    ppermute x12, waiting for transfers between devices, over_experts(): lax.ppermute(value, 'attn', [(i, (i + shift * span) % attn) for i in rang...  8.03 us
    ppermute x18, starting transfers between devices, over_pair(): lax.ppermute(value, 'ffn', [(i, (i + shift) % pair) for i in range(pair)])  3.08 us
  transfers between devices with their start and end apart: 40, of which 16 were waited for; matrix products, arithmetic and copies ran while one was open for 0% of the time, Pallas kernels for 18%

profile of v2, /device:TPU:0, one launch (start us, length us, event | category | flops | bytes accessed | tf_op | source)
XLA Modules:
  0.0 83.1 jit_solution(10414634723294682862)
XLA Ops:
  0.0 0.9 %fusion = (bf16[8,3584]{1,0:T(8,128)(2,1)S(1)}, bf16[8,3584]{1,0:T(8,128)(2,1)S(1)}) fusion(bf16[8,7168]{1,0:T(8,128)(2,1)} %param.6), kind=kLoop, calls=%fused_computation | loop fusion | bytes 229376 | tf_op jit(solution)/shard_map/slice | solution.py:191
  0.9 3.1 %collective-permute-start.15 = (bf16[8,3584]{1,0:T(8,128)(2,1)S(1)}, bf16[8,3584]{1,0:T(8,128)(2,1)S(1)}, u32[]{:S(2)}, u32[]{:S(2)}) collective-permute-start(bf16[8,3584]{1,0:T(8,128)(2,1)S(1)} %get-tuple-element.41.refs_0_), channel_id=1, source_target_pairs={{0,4},{2,6},{4,8},{6,10},{8,12},{10,14},{12,0},{14,2},{1,5},{3,7},... | collective-permute-start | bytes 172040 | tf_op jit(solution)/shard_map/ppermute | solution.py:180
  3.9 2.6 %collective-permute-start.16 = (bf16[8,3584]{1,0:T(8,128)(2,1)S(1)}, bf16[8,3584]{1,0:T(8,128)(2,1)S(1)}, u32[]{:S(2)}, u32[]{:S(2)}) collective-permute-start(bf16[8,3584]{1,0:T(8,128)(2,1)S(1)} %get-tuple-element.41.refs_0_), channel_id=1, source_target_pairs={{0,8},{2,10},{4,12},{6,14},{8,0},{10,2},{12,4},{14,6},{1,9},{3,11}... | collective-permute-start | bytes 172040 | tf_op jit(solution)/shard_map/ppermute | solution.py:180
  6.5 1.3 %collective-permute-start.17 = (bf16[8,3584]{1,0:T(8,128)(2,1)S(1)}, bf16[8,3584]{1,0:T(8,128)(2,1)S(1)}, u32[]{:S(2)}, u32[]{:S(2)}) collective-permute-start(bf16[8,3584]{1,0:T(8,128)(2,1)S(1)} %get-tuple-element.41.refs_0_), channel_id=1, source_target_pairs={{0,12},{2,14},{4,0},{6,2},{8,4},{10,6},{12,8},{14,10},{1,13},{3,15... | collective-permute-start | bytes 172040 | tf_op jit(solution)/shard_map/ppermute | solution.py:180
  7.9 1.5 %collective-permute-start.18 = (bf16[8,3584]{1,0:T(8,128)(2,1)S(1)}, bf16[8,3584]{1,0:T(8,128)(2,1)S(1)}, u32[]{:S(2)}, u32[]{:S(2)}) collective-permute-start(bf16[8,3584]{1,0:T(8,128)(2,1)S(1)} %get-tuple-element.41.refs_0_), channel_id=1, source_target_pairs={{0,2},{2,0},{4,6},{6,4},{8,10},{10,8},{12,14},{14,12},{1,3},{3,1},... | collective-permute-start | bytes 172040 | tf_op jit(solution)/shard_map/ppermute | solution.py:183
  10.6 1.3 %collective-permute-start.1 = (bf16[8,3584]{1,0:T(8,128)(2,1)S(1)}, bf16[8,3584]{1,0:T(8,128)(2,1)S(1)}, u32[]{:S(2)}, u32[]{:S(2)}) collective-permute-start(bf16[8,3584]{1,0:T(8,128)(2,1)S(1)} %get-tuple-element.42.refs_0_), channel_id=1, source_target_pairs={{0,8},{2,10},{4,12},{6,14},{8,0},{10,2},{12,4},{14,6},{1,9},{3,11}... | collective-permute-start | bytes 172040 | tf_op jit(solution)/shard_map/ppermute | solution.py:180
  11.9 2.0 %collective-permute-start.2 = (bf16[8,3584]{1,0:T(8,128)(2,1)S(1)}, bf16[8,3584]{1,0:T(8,128)(2,1)S(1)}, u32[]{:S(2)}, u32[]{:S(2)}) collective-permute-start(bf16[8,3584]{1,0:T(8,128)(2,1)S(1)} %get-tuple-element.42.refs_0_), channel_id=1, source_target_pairs={{0,12},{2,14},{4,0},{6,2},{8,4},{10,6},{12,8},{14,10},{1,13},{3,15... | collective-permute-start | bytes 172040 | tf_op jit(solution)/shard_map/ppermute | solution.py:180
  13.9 1.6 %collective-permute-start.3 = (bf16[8,3584]{1,0:T(8,128)(2,1)S(1)}, bf16[8,3584]{1,0:T(8,128)(2,1)S(1)}, u32[]{:S(2)}, u32[]{:S(2)}) collective-permute-start(bf16[8,3584]{1,0:T(8,128)(2,1)S(1)} %get-tuple-element.42.refs_0_), channel_id=1, source_target_pairs={{0,2},{2,0},{4,6},{6,4},{8,10},{10,8},{12,14},{14,12},{1,3},{3,1},... | collective-permute-start | bytes 172040 | tf_op jit(solution)/shard_map/ppermute | solution.py:183
  16.0 0.8 collective-permute-start.19
  16.8 1.3 %collective-permute-done.1.refs_2_ = bf16[8,3584]{1,0:T(8,128)(2,1)S(1)} collective-permute-done((bf16[8,3584]{1,0:T(8,128)(2,1)S(1)}, bf16[8,3584]{1,0:T(8,128)(2,1)S(1)}, u32[]{:S(2)}, u32[]{:S(2)}) %collective-permute-start.1) | collective-permute-done | bytes 57376 | tf_op jit(solution)/shard_map/ppermute | solution.py:180
  18.6 1.5 %collective-permute-start.21 = (bf16[8,3584]{1,0:T(8,128)(2,1)S(1)}, bf16[8,3584]{1,0:T(8,128)(2,1)S(1)}, u32[]{:S(2)}, u32[]{:S(2)}) collective-permute-start(bf16[8,3584]{1,0:T(8,128)(2,1)S(1)} %collective-permute-done.17.refs_3_), channel_id=1, source_target_pairs={{0,2},{2,0},{4,6},{6,4},{8,10},{10,8},{12,14},{14,12},{1,3},{3,1},... | collective-permute-start | bytes 172040 | tf_op jit(solution)/shard_map/ppermute | solution.py:183
  20.8 1.5 %collective-permute-done.20.refs_6_ = bf16[8,3584]{1,0:T(8,128)(2,1)S(1)} collective-permute-done((bf16[8,3584]{1,0:T(8,128)(2,1)S(1)}, bf16[8,3584]{1,0:T(8,128)(2,1)S(1)}, u32[]{:S(2)}, u32[]{:S(2)}) %collective-permute-start.20) | collective-permute-done | bytes 57376 | tf_op jit(solution)/shard_map/ppermute | solution.py:183
  22.9 1.4 %collective-permute-start.4 = (bf16[8,3584]{1,0:T(8,128)(2,1)S(1)}, bf16[8,3584]{1,0:T(8,128)(2,1)S(1)}, u32[]{:S(2)}, u32[]{:S(2)}) collective-permute-start(bf16[8,3584]{1,0:T(8,128)(2,1)S(1)} %collective-permute-done.refs_1_), channel_id=1, source_target_pairs={{0,2},{2,0},{4,6},{6,4},{8,10},{10,8},{12,14},{14,12},{1,3},{3,1},... | collective-permute-start | bytes 172040 | tf_op jit(solution)/shard_map/ppermute | solution.py:183
  24.9 1.4 %collective-permute-start.6 = (bf16[8,3584]{1,0:T(8,128)(2,1)S(1)}, bf16[8,3584]{1,0:T(8,128)(2,1)S(1)}, u32[]{:S(2)}, u32[]{:S(2)}) collective-permute-start(bf16[8,3584]{1,0:T(8,128)(2,1)S(1)} %collective-permute-done.2.refs_3_), channel_id=1, source_target_pairs={{0,2},{2,0},{4,6},{6,4},{8,10},{10,8},{12,14},{14,12},{1,3},{3,1},... | collective-permute-start | bytes 172040 | tf_op jit(solution)/shard_map/ppermute | solution.py:183
  26.9 0.7 collective-permute-done.4.refs_5_
  27.6 0.9 %collective-permute-done.5.refs_6_ = bf16[8,3584]{1,0:T(8,128)(2,1)S(1)} collective-permute-done((bf16[8,3584]{1,0:T(8,128)(2,1)S(1)}, bf16[8,3584]{1,0:T(8,128)(2,1)S(1)}, u32[]{:S(2)}, u32[]{:S(2)}) %collective-permute-start.5) | collective-permute-done | bytes 57376 | tf_op jit(solution)/shard_map/ppermute | solution.py:183
  30.7 8.2 %gate_up.2 = (f32[128,1024]{1,0:T(8,128)S(1)}, f32[128,1024]{1,0:T(8,128)S(1)}) custom-call(bf16[8,3584]{1,0:T(8,128)(2,1)S(1)} %get-tuple-element.41.refs_0_, bf16[8,3584]{1,0:T(8,128)(2,1)S(1)} %collective-permute-done.15.refs_1_, bf16[8,3584]{1,0:T(8,128)(2,1)S(1)} %collective-permute-done.16.refs_2_, ...), custom_call_target="tpu_custom_call" | custom-call | flops 1879048192 | bytes 14680064 | tf_op jit(solution)/shard_map/gate_up/pallas_call | solution.py:76
  39.0 8.4 %gate_up.3.hidden_ref = bf16[128,1024]{1,0:T(8,128)(2,1)S(1)} custom-call(bf16[8,3584]{1,0:T(8,128)(2,1)S(1)} %get-tuple-element.42.refs_0_, bf16[8,3584]{1,0:T(8,128)(2,1)S(1)} %collective-permute-done.refs_1_, bf16[8,3584]{1,0:T(8,128)(2,1)S(1)} %collective-permute-done.1.refs_2_, bf16[8,3584]{1,0:T(8,128)(2,1)S(1)} %collective-permute-done.2.refs_3_, ...), custom_call_target="tpu_custom_call" | custom-call | flops 1879048192 | bytes 14680064 | tf_op jit(solution)/shard_map/gate_up/pallas_call | solution.py:76
  47.4 6.3 %down.3 = (f32[64,3584]{1,0:T(8,128)S(1)}, bf16[64,3584]{1,0:T(8,128)(2,1)S(1)}) custom-call(bf16[128,1024]{1,0:T(8,128)(2,1)S(1)} %gate_up.3.hidden_ref, bf16[1024,7168]{1,0:T(8,128)(2,1)} %down_ref.3), custom_call_target="tpu_custom_call" | custom-call | flops 939524096 | bytes 7340032 | tf_op jit(solution)/shard_map/down/pallas_call | solution.py:104
  54.0 6.3 %down.2 = (f32[64,3584]{1,0:T(8,128)S(1)}, bf16[64,3584]{1,0:T(8,128)(2,1)S(1)}) custom-call(bf16[128,1024]{1,0:T(8,128)(2,1)S(1)} %gate_up.3.hidden_ref, bf16[1024,7168]{1,0:T(8,128)(2,1)} %down_ref.3), custom_call_target="tpu_custom_call" | custom-call | flops 939524096 | bytes 7340032 | tf_op jit(solution)/shard_map/down/pallas_call | solution.py:104
  60.7 1.5 %collective-permute-start.36 = (bf16[32,3584]{1,0:T(8,128)(2,1)S(1)}, bf16[32,3584]{1,0:T(8,128)(2,1)S(1)}, u32[]{:S(2)}, u32[]{:S(2)}) collective-permute-start(bf16[32,3584]{1,0:T(8,128)(2,1)S(1)} %get-tuple-element.36), channel_id=1, source_target_pairs={{0,2},{2,0},{4,6},{6,4},{8,10},{10,8},{12,14},{14,12},{1,3},{3,1},... | collective-permute-start | bytes 688136 | tf_op jit(solution)/shard_map/ppermute | solution.py:183
  62.3 1.4 %collective-permute-start.31 = (bf16[32,3584]{1,0:T(8,128)(2,1)S(1)}, bf16[32,3584]{1,0:T(8,128)(2,1)S(1)}, u32[]{:S(2)}, u32[]{:S(2)}) collective-permute-start(bf16[32,3584]{1,0:T(8,128)(2,1)S(1)} %get-tuple-element.28), channel_id=1, source_target_pairs={{0,2},{2,0},{4,6},{6,4},{8,10},{10,8},{12,14},{14,12},{1,3},{3,1},... | collective-permute-start | bytes 688136 | tf_op jit(solution)/shard_map/ppermute | solution.py:183
  63.7 5.5 %collective-permute-done.36.refs_1_ = bf16[32,3584]{1,0:T(8,128)(2,1)S(1)} collective-permute-done((bf16[32,3584]{1,0:T(8,128)(2,1)S(1)}, bf16[32,3584]{1,0:T(8,128)(2,1)S(1)}, u32[]{:S(2)}, u32[]{:S(2)}) %collective-permute-start.36) | collective-permute-done | bytes 229408 | tf_op jit(solution)/shard_map/ppermute | solution.py:183
  69.3 2.0 %collective-permute-start.37 = (bf16[8,3584]{1,0:T(8,128)(2,1)S(1)}, bf16[8,3584]{1,0:T(8,128)(2,1)S(1)}, u32[]{:S(2)}, u32[]{:S(2)}) collective-permute-start(bf16[8,3584]{1,0:T(8,128)(2,1)S(1)} %get-tuple-element.38), channel_id=1, source_target_pairs={{0,12},{2,14},{4,0},{6,2},{8,4},{10,6},{12,8},{14,10},{1,13},{3,15... | collective-permute-start | bytes 172040 | tf_op jit(solution)/shard_map/ppermute | solution.py:180
  71.4 0.8 collective-permute-start.39
  72.1 1.3 %collective-permute-done.31.refs_1_ = bf16[32,3584]{1,0:T(8,128)(2,1)S(1)} collective-permute-done((bf16[32,3584]{1,0:T(8,128)(2,1)S(1)}, bf16[32,3584]{1,0:T(8,128)(2,1)S(1)}, u32[]{:S(2)}, u32[]{:S(2)}) %collective-permute-start.31) | collective-permute-done | bytes 229408 | tf_op jit(solution)/shard_map/ppermute | solution.py:183
  73.5 2.0 %collective-permute-start.32 = (bf16[8,3584]{1,0:T(8,128)(2,1)S(1)}, bf16[8,3584]{1,0:T(8,128)(2,1)S(1)}, u32[]{:S(2)}, u32[]{:S(2)}) collective-permute-start(bf16[8,3584]{1,0:T(8,128)(2,1)S(1)} %get-tuple-element.30), channel_id=1, source_target_pairs={{0,12},{2,14},{4,0},{6,2},{8,4},{10,6},{12,8},{14,10},{1,13},{3,15... | collective-permute-start | bytes 172040 | tf_op jit(solution)/shard_map/ppermute | solution.py:180
  75.4 0.9 %collective-permute-start.33 = (bf16[8,3584]{1,0:T(8,128)(2,1)S(1)}, bf16[8,3584]{1,0:T(8,128)(2,1)S(1)}, u32[]{:S(2)}, u32[]{:S(2)}) collective-permute-start(bf16[8,3584]{1,0:T(8,128)(2,1)S(1)} %get-tuple-element.31), channel_id=1, source_target_pairs={{0,8},{2,10},{4,12},{6,14},{8,0},{10,2},{12,4},{14,6},{1,9},{3,11}... | collective-permute-start | bytes 172040 | tf_op jit(solution)/shard_map/ppermute | solution.py:180
  76.6 1.3 %collective-permute-done.38.refs_6_ = bf16[8,3584]{1,0:T(8,128)(2,1)S(1)} collective-permute-done((bf16[8,3584]{1,0:T(8,128)(2,1)S(1)}, bf16[8,3584]{1,0:T(8,128)(2,1)S(1)}, u32[]{:S(2)}, u32[]{:S(2)}) %collective-permute-start.38) | collective-permute-done | bytes 57376 | tf_op jit(solution)/shard_map/ppermute | solution.py:180
  78.2 3.2 %collective-permute-done.33.refs_2_ = bf16[8,3584]{1,0:T(8,128)(2,1)S(1)} collective-permute-done((bf16[8,3584]{1,0:T(8,128)(2,1)S(1)}, bf16[8,3584]{1,0:T(8,128)(2,1)S(1)}, u32[]{:S(2)}, u32[]{:S(2)}) %collective-permute-start.33) | collective-permute-done | bytes 57376 | tf_op jit(solution)/shard_map/ppermute | solution.py:180
  81.4 0.9 %collective-permute-done.34.refs_3_ = bf16[8,3584]{1,0:T(8,128)(2,1)S(1)} collective-permute-done((bf16[8,3584]{1,0:T(8,128)(2,1)S(1)}, bf16[8,3584]{1,0:T(8,128)(2,1)S(1)}, u32[]{:S(2)}, u32[]{:S(2)}) %collective-permute-start.34) | collective-permute-done | bytes 57376 | tf_op jit(solution)/shard_map/ppermute | solution.py:180
  82.3 0.8 combine.1
  (64 shorter events, 8.5 us)
Async XLA Ops:
  0.9 8.5 %collective-permute-start.15 = (bf16[8,3584]{1,0:T(8,128)(2,1)S(1)}, bf16[8,3584]{1,0:T(8,128)(2,1)S(1)}, u32[]{:S(2)}, u32[]{:S(2)}) collective-permute-start(bf16[8,3584]{1,0:T(8,128)(2,1)S(1)} %get-tuple-element.41.refs_0_), channel_id=1, source_target_pairs={{0,4},{2,6},{4,8},{6,10},{8,12},{10,14},{12,0},{14,2},{1,5},{3,7},... | collective-permute-start | bytes 172040 | tf_op jit(solution)/shard_map/ppermute | solution.py:180
  3.9 6.6 %collective-permute-start.16 = (bf16[8,3584]{1,0:T(8,128)(2,1)S(1)}, bf16[8,3584]{1,0:T(8,128)(2,1)S(1)}, u32[]{:S(2)}, u32[]{:S(2)}) collective-permute-start(bf16[8,3584]{1,0:T(8,128)(2,1)S(1)} %get-tuple-element.41.refs_0_), channel_id=1, source_target_pairs={{0,8},{2,10},{4,12},{6,14},{8,0},{10,2},{12,4},{14,6},{1,9},{3,11}... | collective-permute-start | bytes 172040 | tf_op jit(solution)/shard_map/ppermute | solution.py:180
  6.5 5.4 %collective-permute-start.17 = (bf16[8,3584]{1,0:T(8,128)(2,1)S(1)}, bf16[8,3584]{1,0:T(8,128)(2,1)S(1)}, u32[]{:S(2)}, u32[]{:S(2)}) collective-permute-start(bf16[8,3584]{1,0:T(8,128)(2,1)S(1)} %get-tuple-element.41.refs_0_), channel_id=1, source_target_pairs={{0,12},{2,14},{4,0},{6,2},{8,4},{10,6},{12,8},{14,10},{1,13},{3,15... | collective-permute-start | bytes 172040 | tf_op jit(solution)/shard_map/ppermute | solution.py:180
  7.9 6.0 %collective-permute-start.18 = (bf16[8,3584]{1,0:T(8,128)(2,1)S(1)}, bf16[8,3584]{1,0:T(8,128)(2,1)S(1)}, u32[]{:S(2)}, u32[]{:S(2)}) collective-permute-start(bf16[8,3584]{1,0:T(8,128)(2,1)S(1)} %get-tuple-element.41.refs_0_), channel_id=1, source_target_pairs={{0,2},{2,0},{4,6},{6,4},{8,10},{10,8},{12,14},{14,12},{1,3},{3,1},... | collective-permute-start | bytes 172040 | tf_op jit(solution)/shard_map/ppermute | solution.py:183
  9.4 6.1 %collective-permute-start.22 = (bf16[8,3584]{1,0:T(8,128)(2,1)S(1)}, bf16[8,3584]{1,0:T(8,128)(2,1)S(1)}, u32[]{:S(2)}, u32[]{:S(2)}) collective-permute-start(bf16[8,3584]{1,0:T(8,128)(2,1)S(1)} %get-tuple-element.41.refs_0_), channel_id=1, source_target_pairs={{0,1},{1,0},{2,3},{3,2},{4,5},{5,4},{6,7},{7,6},{8,9},{9,8},{10,11... | collective-permute-start | bytes 172040 | tf_op jit(solution)/shard_map/ppermute | solution.py:186
  9.4 6.6 %collective-permute-start = (bf16[8,3584]{1,0:T(8,128)(2,1)S(1)}, bf16[8,3584]{1,0:T(8,128)(2,1)S(1)}, u32[]{:S(2)}, u32[]{:S(2)}) collective-permute-start(bf16[8,3584]{1,0:T(8,128)(2,1)S(1)} %get-tuple-element.42.refs_0_), channel_id=1, source_target_pairs={{0,4},{2,6},{4,8},{6,10},{8,12},{10,14},{12,0},{14,2},{1,5},{3,7},... | collective-permute-start | bytes 172040 | tf_op jit(solution)/shard_map/ppermute | solution.py:180
  10.6 7.5 %collective-permute-start.1 = (bf16[8,3584]{1,0:T(8,128)(2,1)S(1)}, bf16[8,3584]{1,0:T(8,128)(2,1)S(1)}, u32[]{:S(2)}, u32[]{:S(2)}) collective-permute-start(bf16[8,3584]{1,0:T(8,128)(2,1)S(1)} %get-tuple-element.42.refs_0_), channel_id=1, source_target_pairs={{0,8},{2,10},{4,12},{6,14},{8,0},{10,2},{12,4},{14,6},{1,9},{3,11}... | collective-permute-start | bytes 172040 | tf_op jit(solution)/shard_map/ppermute | solution.py:180
  11.9 6.8 %collective-permute-start.2 = (bf16[8,3584]{1,0:T(8,128)(2,1)S(1)}, bf16[8,3584]{1,0:T(8,128)(2,1)S(1)}, u32[]{:S(2)}, u32[]{:S(2)}) collective-permute-start(bf16[8,3584]{1,0:T(8,128)(2,1)S(1)} %get-tuple-element.42.refs_0_), channel_id=1, source_target_pairs={{0,12},{2,14},{4,0},{6,2},{8,4},{10,6},{12,8},{14,10},{1,13},{3,15... | collective-permute-start | bytes 172040 | tf_op jit(solution)/shard_map/ppermute | solution.py:180
  13.9 6.2 %collective-permute-start.3 = (bf16[8,3584]{1,0:T(8,128)(2,1)S(1)}, bf16[8,3584]{1,0:T(8,128)(2,1)S(1)}, u32[]{:S(2)}, u32[]{:S(2)}) collective-permute-start(bf16[8,3584]{1,0:T(8,128)(2,1)S(1)} %get-tuple-element.42.refs_0_), channel_id=1, source_target_pairs={{0,2},{2,0},{4,6},{6,4},{8,10},{10,8},{12,14},{14,12},{1,3},{3,1},... | collective-permute-start | bytes 172040 | tf_op jit(solution)/shard_map/ppermute | solution.py:183
  15.5 4.7 %collective-permute-start.7 = (bf16[8,3584]{1,0:T(8,128)(2,1)S(1)}, bf16[8,3584]{1,0:T(8,128)(2,1)S(1)}, u32[]{:S(2)}, u32[]{:S(2)}) collective-permute-start(bf16[8,3584]{1,0:T(8,128)(2,1)S(1)} %get-tuple-element.42.refs_0_), channel_id=1, source_target_pairs={{0,1},{1,0},{2,3},{3,2},{4,5},{5,4},{6,7},{7,6},{8,9},{9,8},{10,11... | collective-permute-start | bytes 172040 | tf_op jit(solution)/shard_map/ppermute | solution.py:186
  16.0 4.8 %collective-permute-start.19 = (bf16[8,3584]{1,0:T(8,128)(2,1)S(1)}, bf16[8,3584]{1,0:T(8,128)(2,1)S(1)}, u32[]{:S(2)}, u32[]{:S(2)}) collective-permute-start(bf16[8,3584]{1,0:T(8,128)(2,1)S(1)} %collective-permute-done.15.refs_1_), channel_id=1, source_target_pairs={{0,2},{2,0},{4,6},{6,4},{8,10},{10,8},{12,14},{14,12},{1,3},{3,1},... | collective-permute-start | bytes 172040 | tf_op jit(solution)/shard_map/ppermute | solution.py:183
  18.1 4.2 %collective-permute-start.20 = (bf16[8,3584]{1,0:T(8,128)(2,1)S(1)}, bf16[8,3584]{1,0:T(8,128)(2,1)S(1)}, u32[]{:S(2)}, u32[]{:S(2)}) collective-permute-start(bf16[8,3584]{1,0:T(8,128)(2,1)S(1)} %collective-permute-done.16.refs_2_), channel_id=1, source_target_pairs={{0,2},{2,0},{4,6},{6,4},{8,10},{10,8},{12,14},{14,12},{1,3},{3,1},... | collective-permute-start | bytes 172040 | tf_op jit(solution)/shard_map/ppermute | solution.py:183
  18.6 4.3 %collective-permute-start.21 = (bf16[8,3584]{1,0:T(8,128)(2,1)S(1)}, bf16[8,3584]{1,0:T(8,128)(2,1)S(1)}, u32[]{:S(2)}, u32[]{:S(2)}) collective-permute-start(bf16[8,3584]{1,0:T(8,128)(2,1)S(1)} %collective-permute-done.17.refs_3_), channel_id=1, source_target_pairs={{0,2},{2,0},{4,6},{6,4},{8,10},{10,8},{12,14},{14,12},{1,3},{3,1},... | collective-permute-start | bytes 172040 | tf_op jit(solution)/shard_map/ppermute | solution.py:183
  20.1 4.8 %collective-permute-start.24 = (bf16[8,3584]{1,0:T(8,128)(2,1)S(1)}, bf16[8,3584]{1,0:T(8,128)(2,1)S(1)}, u32[]{:S(2)}, u32[]{:S(2)}) collective-permute-start(bf16[8,3584]{1,0:T(8,128)(2,1)S(1)} %collective-permute-done.16.refs_2_), channel_id=1, source_target_pairs={{0,1},{1,0},{2,3},{3,2},{4,5},{5,4},{6,7},{7,6},{8,9},{9,8},{10,11... | collective-permute-start | bytes 172040 | tf_op jit(solution)/shard_map/ppermute | solution.py:186
  20.8 5.5 %collective-permute-start.25 = (bf16[8,3584]{1,0:T(8,128)(2,1)S(1)}, bf16[8,3584]{1,0:T(8,128)(2,1)S(1)}, u32[]{:S(2)}, u32[]{:S(2)}) collective-permute-start(bf16[8,3584]{1,0:T(8,128)(2,1)S(1)} %collective-permute-done.17.refs_3_), channel_id=1, source_target_pairs={{0,1},{1,0},{2,3},{3,2},{4,5},{5,4},{6,7},{7,6},{8,9},{9,8},{10,11... | collective-permute-start | bytes 172040 | tf_op jit(solution)/shard_map/ppermute | solution.py:186
  22.9 4.7 %collective-permute-start.4 = (bf16[8,3584]{1,0:T(8,128)(2,1)S(1)}, bf16[8,3584]{1,0:T(8,128)(2,1)S(1)}, u32[]{:S(2)}, u32[]{:S(2)}) collective-permute-start(bf16[8,3584]{1,0:T(8,128)(2,1)S(1)} %collective-permute-done.refs_1_), channel_id=1, source_target_pairs={{0,2},{2,0},{4,6},{6,4},{8,10},{10,8},{12,14},{14,12},{1,3},{3,1},... | collective-permute-start | bytes 172040 | tf_op jit(solution)/shard_map/ppermute | solution.py:183
  24.3 4.2 %collective-permute-start.5 = (bf16[8,3584]{1,0:T(8,128)(2,1)S(1)}, bf16[8,3584]{1,0:T(8,128)(2,1)S(1)}, u32[]{:S(2)}, u32[]{:S(2)}) collective-permute-start(bf16[8,3584]{1,0:T(8,128)(2,1)S(1)} %collective-permute-done.1.refs_2_), channel_id=1, source_target_pairs={{0,2},{2,0},{4,6},{6,4},{8,10},{10,8},{12,14},{14,12},{1,3},{3,1},... | collective-permute-start | bytes 172040 | tf_op jit(solution)/shard_map/ppermute | solution.py:183
  24.9 4.2 %collective-permute-start.6 = (bf16[8,3584]{1,0:T(8,128)(2,1)S(1)}, bf16[8,3584]{1,0:T(8,128)(2,1)S(1)}, u32[]{:S(2)}, u32[]{:S(2)}) collective-permute-start(bf16[8,3584]{1,0:T(8,128)(2,1)S(1)} %collective-permute-done.2.refs_3_), channel_id=1, source_target_pairs={{0,2},{2,0},{4,6},{6,4},{8,10},{10,8},{12,14},{14,12},{1,3},{3,1},... | collective-permute-start | bytes 172040 | tf_op jit(solution)/shard_map/ppermute | solution.py:183
  29.1 9.8 %collective-permute-start.9 = (bf16[8,3584]{1,0:T(8,128)(2,1)S(1)}, bf16[8,3584]{1,0:T(8,128)(2,1)S(1)}, u32[]{:S(2)}, u32[]{:S(2)}) collective-permute-start(bf16[8,3584]{1,0:T(8,128)(2,1)S(1)} %collective-permute-done.1.refs_2_), channel_id=1, source_target_pairs={{0,1},{1,0},{2,3},{3,2},{4,5},{5,4},{6,7},{7,6},{8,9},{9,8},{10,11... | collective-permute-start | bytes 172040 | tf_op jit(solution)/shard_map/ppermute | solution.py:186
  29.6 9.3 %collective-permute-start.11 = (bf16[8,3584]{1,0:T(8,128)(2,1)S(1)}, bf16[8,3584]{1,0:T(8,128)(2,1)S(1)}, u32[]{:S(2)}, u32[]{:S(2)}) collective-permute-start(bf16[8,3584]{1,0:T(8,128)(2,1)S(1)} %collective-permute-done.3.refs_4_), channel_id=1, source_target_pairs={{0,1},{1,0},{2,3},{3,2},{4,5},{5,4},{6,7},{7,6},{8,9},{9,8},{10,11... | collective-permute-start | bytes 172040 | tf_op jit(solution)/shard_map/ppermute | solution.py:186
  29.7 9.2 %collective-permute-start.12 = (bf16[8,3584]{1,0:T(8,128)(2,1)S(1)}, bf16[8,3584]{1,0:T(8,128)(2,1)S(1)}, u32[]{:S(2)}, u32[]{:S(2)}) collective-permute-start(bf16[8,3584]{1,0:T(8,128)(2,1)S(1)} %collective-permute-done.4.refs_5_), channel_id=1, source_target_pairs={{0,1},{1,0},{2,3},{3,2},{4,5},{5,4},{6,7},{7,6},{8,9},{9,8},{10,11... | collective-permute-start | bytes 172040 | tf_op jit(solution)/shard_map/ppermute | solution.py:186
  30.1 8.8 %collective-permute-start.13 = (bf16[8,3584]{1,0:T(8,128)(2,1)S(1)}, bf16[8,3584]{1,0:T(8,128)(2,1)S(1)}, u32[]{:S(2)}, u32[]{:S(2)}) collective-permute-start(bf16[8,3584]{1,0:T(8,128)(2,1)S(1)} %collective-permute-done.5.refs_6_), channel_id=1, source_target_pairs={{0,1},{1,0},{2,3},{3,2},{4,5},{5,4},{6,7},{7,6},{8,9},{9,8},{10,11... | collective-permute-start | bytes 172040 | tf_op jit(solution)/shard_map/ppermute | solution.py:186
  30.3 8.6 %collective-permute-start.14 = (bf16[8,3584]{1,0:T(8,128)(2,1)S(1)}, bf16[8,3584]{1,0:T(8,128)(2,1)S(1)}, u32[]{:S(2)}, u32[]{:S(2)}) collective-permute-start(bf16[8,3584]{1,0:T(8,128)(2,1)S(1)} %collective-permute-done.6.refs_7_), channel_id=1, source_target_pairs={{0,1},{1,0},{2,3},{3,2},{4,5},{5,4},{6,7},{7,6},{8,9},{9,8},{10,11... | collective-permute-start | bytes 172040 | tf_op jit(solution)/shard_map/ppermute | solution.py:186
  53.7 6.9 %collective-permute-start.35 = (bf16[64,3584]{1,0:T(8,128)(2,1)S(1)}, bf16[64,3584]{1,0:T(8,128)(2,1)S(1)}, u32[]{:S(2)}, u32[]{:S(2)}) collective-permute-start(bf16[64,3584]{1,0:T(8,128)(2,1)S(1)} %get-tuple-element.34), channel_id=1, source_target_pairs={{0,1},{1,0},{2,3},{3,2},{4,5},{5,4},{6,7},{7,6},{8,9},{9,8},{10,11... | collective-permute-start | bytes 1376264 | tf_op jit(solution)/shard_map/ppermute | solution.py:186
  60.7 8.5 %collective-permute-start.36 = (bf16[32,3584]{1,0:T(8,128)(2,1)S(1)}, bf16[32,3584]{1,0:T(8,128)(2,1)S(1)}, u32[]{:S(2)}, u32[]{:S(2)}) collective-permute-start(bf16[32,3584]{1,0:T(8,128)(2,1)S(1)} %get-tuple-element.36), channel_id=1, source_target_pairs={{0,2},{2,0},{4,6},{6,4},{8,10},{10,8},{12,14},{14,12},{1,3},{3,1},... | collective-permute-start | bytes 688136 | tf_op jit(solution)/shard_map/ppermute | solution.py:183
  62.3 11.1 %collective-permute-start.31 = (bf16[32,3584]{1,0:T(8,128)(2,1)S(1)}, bf16[32,3584]{1,0:T(8,128)(2,1)S(1)}, u32[]{:S(2)}, u32[]{:S(2)}) collective-permute-start(bf16[32,3584]{1,0:T(8,128)(2,1)S(1)} %get-tuple-element.28), channel_id=1, source_target_pairs={{0,2},{2,0},{4,6},{6,4},{8,10},{10,8},{12,14},{14,12},{1,3},{3,1},... | collective-permute-start | bytes 688136 | tf_op jit(solution)/shard_map/ppermute | solution.py:183
  69.3 7.0 %collective-permute-start.37 = (bf16[8,3584]{1,0:T(8,128)(2,1)S(1)}, bf16[8,3584]{1,0:T(8,128)(2,1)S(1)}, u32[]{:S(2)}, u32[]{:S(2)}) collective-permute-start(bf16[8,3584]{1,0:T(8,128)(2,1)S(1)} %get-tuple-element.38), channel_id=1, source_target_pairs={{0,12},{2,14},{4,0},{6,2},{8,4},{10,6},{12,8},{14,10},{1,13},{3,15... | collective-permute-start | bytes 172040 | tf_op jit(solution)/shard_map/ppermute | solution.py:180
  71.2 6.6 %collective-permute-start.38 = (bf16[8,3584]{1,0:T(8,128)(2,1)S(1)}, bf16[8,3584]{1,0:T(8,128)(2,1)S(1)}, u32[]{:S(2)}, u32[]{:S(2)}) collective-permute-start(bf16[8,3584]{1,0:T(8,128)(2,1)S(1)} %get-tuple-element.39), channel_id=1, source_target_pairs={{0,8},{2,10},{4,12},{6,14},{8,0},{10,2},{12,4},{14,6},{1,9},{3,11}... | collective-permute-start | bytes 172040 | tf_op jit(solution)/shard_map/ppermute | solution.py:180
  71.4 6.5 %collective-permute-start.39 = (bf16[8,3584]{1,0:T(8,128)(2,1)S(1)}, bf16[8,3584]{1,0:T(8,128)(2,1)S(1)}, u32[]{:S(2)}, u32[]{:S(2)}) collective-permute-start(bf16[8,3584]{1,0:T(8,128)(2,1)S(1)} %get-tuple-element.40), channel_id=1, source_target_pairs={{0,4},{2,6},{4,8},{6,10},{8,12},{10,14},{12,0},{14,2},{1,5},{3,7},... | collective-permute-start | bytes 172040 | tf_op jit(solution)/shard_map/ppermute | solution.py:180
  73.5 4.7 %collective-permute-start.32 = (bf16[8,3584]{1,0:T(8,128)(2,1)S(1)}, bf16[8,3584]{1,0:T(8,128)(2,1)S(1)}, u32[]{:S(2)}, u32[]{:S(2)}) collective-permute-start(bf16[8,3584]{1,0:T(8,128)(2,1)S(1)} %get-tuple-element.30), channel_id=1, source_target_pairs={{0,12},{2,14},{4,0},{6,2},{8,4},{10,6},{12,8},{14,10},{1,13},{3,15... | collective-permute-start | bytes 172040 | tf_op jit(solution)/shard_map/ppermute | solution.py:180
  75.4 6.0 %collective-permute-start.33 = (bf16[8,3584]{1,0:T(8,128)(2,1)S(1)}, bf16[8,3584]{1,0:T(8,128)(2,1)S(1)}, u32[]{:S(2)}, u32[]{:S(2)}) collective-permute-start(bf16[8,3584]{1,0:T(8,128)(2,1)S(1)} %get-tuple-element.31), channel_id=1, source_target_pairs={{0,8},{2,10},{4,12},{6,14},{8,0},{10,2},{12,4},{14,6},{1,9},{3,11}... | collective-permute-start | bytes 172040 | tf_op jit(solution)/shard_map/ppermute | solution.py:180
  76.3 6.0 %collective-permute-start.34 = (bf16[8,3584]{1,0:T(8,128)(2,1)S(1)}, bf16[8,3584]{1,0:T(8,128)(2,1)S(1)}, u32[]{:S(2)}, u32[]{:S(2)}) collective-permute-start(bf16[8,3584]{1,0:T(8,128)(2,1)S(1)} %get-tuple-element.32), channel_id=1, source_target_pairs={{0,4},{2,6},{4,8},{6,10},{8,12},{10,14},{12,0},{14,2},{1,5},{3,7},... | collective-permute-start | bytes 172040 | tf_op jit(solution)/shard_map/ppermute | solution.py:180
  (10 other events, 79.4 us)

commit v3 on v1

v3 whole, which is shorter than its diff:
```python
import functools

import jax
import jax.numpy as jnp
from jax import lax
from jax.experimental import pallas as pl
from jax.experimental.pallas import tpu as pltpu
from jax.sharding import PartitionSpec as P

EXPERTS = 4
OUT_CHUNKS = 2
N_BLOCK = 256
C_BLOCK = 512
EXCHANGE_FLOPS = 20_000_000_000


def params(mib=8):
    return pltpu.CompilerParams(vmem_limit_bytes=mib * 1024 * 1024)


def cost(flops):
    return pl.CostEstimate(flops=flops, bytes_accessed=0, transcendentals=0)


def block_of(width, most):
    size = most
    while width % size:
        size -= 128
    return size


def in_vmem(value):
    return pltpu.with_memory_space_constraint(value, pltpu.VMEM)


def joined(refs):
    return jnp.concatenate([ref[...].astype(jnp.float32) for ref in refs], axis=0)


def stack_kernel(*refs):
    refs[-1][...] = joined(refs[:-1]).astype(jnp.bfloat16)


def stack(values, flops=0):
    rows = sum(v.shape[0] for v in values)
    return pl.pallas_call(
        stack_kernel,
        out_shape=jax.ShapeDtypeStruct((rows, values[0].shape[1]), jnp.bfloat16),
        compiler_params=params(),
        cost_estimate=cost(flops),
        name="stack",
    )(*values)


def gate_up_kernel(n_block, *refs):
    rows_in, (gate_ref, up_ref, hidden_ref, rows_ref) = refs[:-4], refs[-4:]
    width = rows_ref.shape[1]
    piece = block_of(width, 1024)
    for k in range(0, width, piece):
        rows_ref[:, k:k + piece] = joined([ref.at[:, k:k + piece] for ref in rows_in]).astype(jnp.bfloat16)

    def step(n, carry):
        columns = pl.ds(pl.multiple_of(n * n_block, n_block), n_block)
        gate = jnp.dot(rows_ref[...], gate_ref[:, columns], preferred_element_type=jnp.float32)
        up = jnp.dot(rows_ref[...], up_ref[:, columns], preferred_element_type=jnp.float32)
        hidden_ref[:, columns] = (gate / (1.0 + jnp.exp(-gate)) * up).astype(jnp.bfloat16)
        return carry

    lax.fori_loop(0, gate_ref.shape[1] // n_block, step, 0)


def gate_up(rows, gate_weight, up_weight):
    total = sum(r.shape[0] for r in rows)
    width, units = gate_weight.shape
    return pl.pallas_call(
        functools.partial(gate_up_kernel, block_of(units, N_BLOCK)),
        in_specs=[pl.BlockSpec(memory_space=pltpu.VMEM)] * (len(rows) + 2),
        out_shape=jax.ShapeDtypeStruct((total, units), jnp.bfloat16),
        scratch_shapes=[pltpu.VMEM((total, width), jnp.bfloat16)],
        compiler_params=params(12),
        cost_estimate=cost(4 * total * width * units),
        name="gate_up",
    )(*rows, in_vmem(gate_weight), in_vmem(up_weight))


def down_kernel(offset, c_block, hidden_ref, down_ref, keep_ref, *send_refs):
    count, width = keep_ref.shape

    def step(c, carry):
        start = pl.multiple_of(c * c_block, c_block)
        value = jnp.dot(hidden_ref[...], down_ref[:, pl.ds(offset + start, c_block)], preferred_element_type=jnp.float32)
        keep_ref[:, pl.ds(start, c_block)] = value[:count]
        for i, ref in enumerate(send_refs):
            ref[:, pl.ds(start, c_block)] = value[(i + 1) * count:(i + 2) * count].astype(jnp.bfloat16)
        return carry

    lax.fori_loop(0, width // c_block, step, 0)


def down(hidden, down_weight, chunk, pair):
    total, units = hidden.shape
    width = down_weight.shape[1] // OUT_CHUNKS
    part = total // pair
    return pl.pallas_call(
        functools.partial(down_kernel, chunk * width, block_of(width, C_BLOCK)),
        in_specs=[pl.BlockSpec(memory_space=pltpu.VMEM)] * 2,
        out_shape=[jax.ShapeDtypeStruct((part, width), jnp.float32)]
        + [jax.ShapeDtypeStruct((part, width), jnp.bfloat16)] * (pair - 1),
        compiler_params=params(),
        cost_estimate=cost(2 * total * width * units),
        name="down",
    )(hidden, in_vmem(down_weight))


def pair_sum_kernel(chunks, each, *refs):
    ins, outs = refs[:chunks * each], refs[chunks * each:]
    rows = outs[0].shape[0]
    width = ins[0].shape[1]
    for chunk in range(chunks):
        first, *others = ins[chunk * each:(chunk + 1) * each]
        for i, ref in enumerate(outs):
            part = slice(i * rows, (i + 1) * rows)
            value = first[part, :]
            for other in others:
                value += other[part, :].astype(jnp.float32)
            ref[:, chunk * width:(chunk + 1) * width] = value.astype(ref.dtype)


def pair_sum(groups, rows):
    each = len(groups[0])
    total, width = groups[0][0].shape
    count = total // rows
    shape = (rows, width * len(groups))
    return pl.pallas_call(
        functools.partial(pair_sum_kernel, len(groups), each),
        out_shape=[jax.ShapeDtypeStruct(shape, jnp.float32 if i < EXPERTS else jnp.bfloat16) for i in range(count)],
        compiler_params=params(16),
        name="pair_sum",
    )(*[a for g in groups for a in g])


def span_sum_kernel(*refs):
    value = refs[0][...]
    for ref in refs[1:-1]:
        value += ref[...].astype(jnp.float32)
    refs[-1][...] = value.astype(refs[-1].dtype)


def span_sum(arrays):
    return pl.pallas_call(
        span_sum_kernel,
        out_shape=jax.ShapeDtypeStruct(arrays[0].shape, jnp.bfloat16),
        compiler_params=params(),
        name="span_sum",
    )(*arrays)


def combine_kernel(own_count, own_expert, ids_ref, weights_ref, *refs):
    out_ref = refs[-1]
    ids, weights = ids_ref[...], weights_ref[...]

    def coeff(s):
        expert = lax.rem(own_expert[0] + s, EXPERTS)
        return jnp.sum(jnp.where(ids == expert, weights, 0.0), axis=1, keepdims=True)

    own = refs[0][...]
    for ref in refs[1:own_count]:
        own += ref[...].astype(jnp.float32)
    value = coeff(0) * own
    for s, ref in enumerate(refs[own_count:-1], 1):
        value += coeff(s) * ref[...].astype(jnp.float32)
    out_ref[...] = value.astype(jnp.bfloat16)


def combine(own_expert, ids, weights, own, others):
    arrays = list(own) + list(others)
    return pl.pallas_call(
        functools.partial(combine_kernel, len(own)),
        in_specs=[pl.BlockSpec(memory_space=pltpu.SMEM)] + [pl.BlockSpec(memory_space=pltpu.VMEM)] * (2 + len(arrays)),
        out_shape=jax.ShapeDtypeStruct(own[0].shape, jnp.bfloat16),
        compiler_params=params(),
        name="combine",
    )(own_expert, ids, weights, *arrays)


def local(tokens, expert_ids, route_weights, gate_weight, up_weight, down_weight):
    rows = tokens.shape[0]
    attn = lax.axis_size("attn")
    pair = lax.axis_size("ffn")
    span = attn // EXPERTS

    def over_experts(value, shift):
        return lax.ppermute(value, "attn", [(i, (i + shift * span) % attn) for i in range(attn)])

    def over_span(value, shift):
        return lax.ppermute(value, "attn", [(i, i // span * span + (i + shift) % span) for i in range(attn)])

    def over_pair(value, shift):
        return lax.ppermute(value, "ffn", [(i, (i + shift) % pair) for i in range(pair)])

    own = stack([tokens], EXCHANGE_FLOPS)
    column = [own] + [over_experts(own, s) for s in range(1, EXPERTS)]
    plane, groups = list(column), [stack(column)]
    for t in range(1, span):
        blocks = [over_span(b, t) for b in column]
        plane += blocks
        groups += [stack(blocks[:-1]), blocks[-1]]
    gathered = plane + [over_pair(g, p) for p in range(1, pair) for g in groups]

    hidden = gate_up(gathered, gate_weight, up_weight)

    halves = []
    for chunk in range(OUT_CHUNKS):
        keep, *sends = down(hidden, down_weight, chunk, pair)
        halves.append([keep] + [over_pair(b, -p) for p, b in enumerate(sends, 1)])
    blocks = pair_sum(halves, rows)
    sums = []
    for s in reversed(range(EXPERTS)):
        sums.append([blocks[s]] + [over_span(blocks[t * EXPERTS + s], -t) for t in range(1, span)])
    sums.reverse()
    others = [over_experts(span_sum(sums[s]), -s) for s in reversed(range(1, EXPERTS))]
    others.reverse()
    own_expert = (lax.axis_index("attn") // span).astype(jnp.int32).reshape(1)
    return combine(own_expert, expert_ids, route_weights, sums[0], others)


def solution(mesh):
    return jax.shard_map(
        local,
        mesh=mesh,
        in_specs=(
            P(("groups", "attn", "ffn"), None),
            P(("groups", "attn", "ffn"), None),
            P(("groups", "attn", "ffn"), None),
            P(None, ("attn", "ffn")),
            P(None, ("attn", "ffn")),
            P(("attn", "ffn"), None),
        ),
        out_specs=P(("groups", "attn", "ffn"), None),
        check_vma=False,
    )
```

time: 152 us -> 58 us (0.38)
  waiting for transfers between devices: 89.7 us -> 19.6 us
  starting transfers between devices: 0.04 us -> 26.1 us
  matrix products: 23.2 us -> 0 us
  blocking collectives: 23.2 us -> 0 us
  between operations: 13.4 us -> 0.2 us
  Pallas kernels: 0 us -> 10.7 us
  other arithmetic: 2.4 us -> 0.01 us
    reduce_scatter x1 -> x0, waiting for transfers between devices: 67.4 us -> none  [local(): lax.psum_scatter(partial_value, ('attn', 'ffn'), scatter_dimension=0, til...]
    ppermute x0 -> x19, starting transfers between devices: none -> 26.1 us  [the longest x6 14.8 us: over_experts(): lax.ppermute(value, 'attn', [(i, (i + shift * span) % attn) for i in rang...]
    dot_general x2 -> x0, matrix products: 23.2 us -> none  [the longest x1 15.2 us: local(): jnp.dot(hidden, down_weight, preferred_element_type=jnp.float32) * own]
    all_gather x1 -> x0, blocking collectives: 23.2 us -> none  [local(): coeffs = lax.all_gather(coeff, ('attn', 'ffn'), axis=0, tiled=True)]
    all_gather x1 -> x0, waiting for transfers between devices: 21.5 us -> none  [local(): rows = lax.all_gather(tokens, ('attn', 'ffn'), axis=0, tiled=True)]
    ppermute x0 -> x19, waiting for transfers between devices: none -> 19.6 us  [the longest x8 10.1 us: over_span(): lax.ppermute(value, 'attn', [(i, i // span * span + (i + shift) % span) f...]
    pallas_call x0 -> x11, Pallas kernels: none -> 10.7 us  [the longest x1 5.11 us: gate_up(): pl.pallas_call(functools.partial(gate_up_kernel, block_of(units, N_BLOCK)...]
    convert_element_type x1 -> x0, other arithmetic: 1.6 us -> none  [local(): return mixed.astype(jnp.bfloat16)]
  transfers between devices with their start and end apart: 2 -> 19, of which waited for: 2 -> 11; matrix products, arithmetic and copies ran while one was open for 1% -> 0% of each run, Pallas kernels for 0% -> 0%
where the time goes in v3:
time: 58 us; the launch traced here: 57.8 us
  starting transfers between devices  26.1 us (45%)
  waiting for transfers between devices  19.6 us (34%)
  Pallas kernels  10.7 us (18%)
  local copies, waits for them, and re-layouts  1.25 us (2%)
    ppermute x6, starting transfers between devices, over_experts(): lax.ppermute(value, 'attn', [(i, (i + shift * span) % attn) for i in rang...  14.8 us
    ppermute x8, starting transfers between devices, over_span(): lax.ppermute(value, 'attn', [(i, i // span * span + (i + shift) % span) f...  10.6 us
    ppermute x8, waiting for transfers between devices, over_span(): lax.ppermute(value, 'attn', [(i, i // span * span + (i + shift) % span) f...  10.1 us
    ppermute x6, waiting for transfers between devices, over_experts(): lax.ppermute(value, 'attn', [(i, (i + shift * span) % attn) for i in rang...  6.21 us
    pallas_call x1, Pallas kernels, gate_up(): pl.pallas_call(functools.partial(gate_up_kernel, block_of(units, N_BLOCK)...  5.11 us
    pallas_call x2, Pallas kernels, down(): pl.pallas_call(functools.partial(down_kernel, chunk * width, block_of(wid...  4.47 us
    ppermute x5, waiting for transfers between devices, over_pair(): lax.ppermute(value, 'ffn', [(i, (i + shift) % pair) for i in range(pair)])  3.29 us
    unnamed x20, local copies, waits for them, and re-layouts  1.25 us
  transfers between devices with their start and end apart: 19, of which 11 were waited for; matrix products, arithmetic and copies ran while one was open for 0% of the time, Pallas kernels for 0%

profile of v3, /device:TPU:0, one launch (start us, length us, event | category | flops | bytes accessed | tf_op | source)
XLA Modules:
  0.0 57.8 jit_solution(13348337652321383291)
XLA Ops:
  0.0 1.0 %copy-done.2 = bf16[8,7168]{1,0:T(8,128)(2,1)S(1)} copy-done((bf16[8,7168]{1,0:T(8,128)(2,1)S(1)}, bf16[8,7168]{1,0:T(8,128)(2,1)}, u32[]{:S(2)}) %copy-start.2) | copy-done | bytes 114712
  1.1 3.1 %collective-permute-start = (bf16[8,7168]{1,0:T(8,128)(2,1)S(1)}, bf16[8,7168]{1,0:T(8,128)(2,1)S(1)}, u32[]{:S(2)}, u32[]{:S(2)}) collective-permute-start(bf16[8,7168]{1,0:T(8,128)(2,1)S(1)} %stack.3.refs_0_), channel_id=1, source_target_pairs={{0,4},{2,6},{4,8},{6,10},{8,12},{10,14},{12,0},{14,2},{1,5},{3,7},... | collective-permute-start | bytes 344072 | tf_op jit(solution)/shard_map/ppermute | solution.py:193
  4.1 2.6 %collective-permute-start.1 = (bf16[8,7168]{1,0:T(8,128)(2,1)S(1)}, bf16[8,7168]{1,0:T(8,128)(2,1)S(1)}, u32[]{:S(2)}, u32[]{:S(2)}) collective-permute-start(bf16[8,7168]{1,0:T(8,128)(2,1)S(1)} %stack.3.refs_0_), channel_id=1, source_target_pairs={{0,8},{2,10},{4,12},{6,14},{8,0},{10,2},{12,4},{14,6},{1,9},{3,11}... | collective-permute-start | bytes 344072 | tf_op jit(solution)/shard_map/ppermute | solution.py:193
  6.7 1.3 %collective-permute-start.2 = (bf16[8,7168]{1,0:T(8,128)(2,1)S(1)}, bf16[8,7168]{1,0:T(8,128)(2,1)S(1)}, u32[]{:S(2)}, u32[]{:S(2)}) collective-permute-start(bf16[8,7168]{1,0:T(8,128)(2,1)S(1)} %stack.3.refs_0_), channel_id=1, source_target_pairs={{0,12},{2,14},{4,0},{6,2},{8,4},{10,6},{12,8},{14,10},{1,13},{3,15... | collective-permute-start | bytes 344072 | tf_op jit(solution)/shard_map/ppermute | solution.py:193
  8.1 1.5 %collective-permute-start.3 = (bf16[8,7168]{1,0:T(8,128)(2,1)S(1)}, bf16[8,7168]{1,0:T(8,128)(2,1)S(1)}, u32[]{:S(2)}, u32[]{:S(2)}) collective-permute-start(bf16[8,7168]{1,0:T(8,128)(2,1)S(1)} %stack.3.refs_0_), channel_id=1, source_target_pairs={{0,2},{2,0},{4,6},{6,4},{8,10},{10,8},{12,14},{14,12},{1,3},{3,1},... | collective-permute-start | bytes 344072 | tf_op jit(solution)/shard_map/ppermute | solution.py:196
  9.6 0.6 %collective-permute-done.refs_1_ = bf16[8,7168]{1,0:T(8,128)(2,1)S(1)} collective-permute-done((bf16[8,7168]{1,0:T(8,128)(2,1)S(1)}, bf16[8,7168]{1,0:T(8,128)(2,1)S(1)}, u32[]{:S(2)}, u32[]{:S(2)}) %collective-permute-start) | collective-permute-done | bytes 114720 | tf_op jit(solution)/shard_map/ppermute | solution.py:193
  10.2 1.8 %collective-permute-start.4 = (bf16[8,7168]{1,0:T(8,128)(2,1)S(1)}, bf16[8,7168]{1,0:T(8,128)(2,1)S(1)}, u32[]{:S(2)}, u32[]{:S(2)}) collective-permute-start(bf16[8,7168]{1,0:T(8,128)(2,1)S(1)} %collective-permute-done.refs_1_), channel_id=1, source_target_pairs={{0,2},{2,0},{4,6},{6,4},{8,10},{10,8},{12,14},{14,12},{1,3},{3,1},... | collective-permute-start | bytes 344072 | tf_op jit(solution)/shard_map/ppermute | solution.py:196
  12.0 2.3 %collective-permute-done.1.refs_2_ = bf16[8,7168]{1,0:T(8,128)(2,1)S(1)} collective-permute-done((bf16[8,7168]{1,0:T(8,128)(2,1)S(1)}, bf16[8,7168]{1,0:T(8,128)(2,1)S(1)}, u32[]{:S(2)}, u32[]{:S(2)}) %collective-permute-start.1) | collective-permute-done | bytes 114720 | tf_op jit(solution)/shard_map/ppermute | solution.py:193
  14.3 1.6 %collective-permute-start.5 = (bf16[8,7168]{1,0:T(8,128)(2,1)S(1)}, bf16[8,7168]{1,0:T(8,128)(2,1)S(1)}, u32[]{:S(2)}, u32[]{:S(2)}) collective-permute-start(bf16[8,7168]{1,0:T(8,128)(2,1)S(1)} %collective-permute-done.1.refs_2_), channel_id=1, source_target_pairs={{0,2},{2,0},{4,6},{6,4},{8,10},{10,8},{12,14},{14,12},{1,3},{3,1},... | collective-permute-start | bytes 344072 | tf_op jit(solution)/shard_map/ppermute | solution.py:196
  16.0 3.3 %collective-permute-done.5.refs_2_.refs_6_ = bf16[8,7168]{1,0:T(8,128)(2,1)S(1)} collective-permute-done((bf16[8,7168]{1,0:T(8,128)(2,1)S(1)}, bf16[8,7168]{1,0:T(8,128)(2,1)S(1)}, u32[]{:S(2)}, u32[]{:S(2)}) %collective-permute-start.5) | collective-permute-done | bytes 114720 | tf_op jit(solution)/shard_map/ppermute | solution.py:196
  19.4 1.6 %collective-permute-start.6 = (bf16[8,7168]{1,0:T(8,128)(2,1)S(1)}, bf16[8,7168]{1,0:T(8,128)(2,1)S(1)}, u32[]{:S(2)}, u32[]{:S(2)}) collective-permute-start(bf16[8,7168]{1,0:T(8,128)(2,1)S(1)} %collective-permute-done.2.refs_3_), channel_id=1, source_target_pairs={{0,2},{2,0},{4,6},{6,4},{8,10},{10,8},{12,14},{14,12},{1,3},{3,1},... | collective-permute-start | bytes 344072 | tf_op jit(solution)/shard_map/ppermute | solution.py:196
  21.1 3.9 %collective-permute-done.6.refs_7_ = bf16[8,7168]{1,0:T(8,128)(2,1)S(1)} collective-permute-done((bf16[8,7168]{1,0:T(8,128)(2,1)S(1)}, bf16[8,7168]{1,0:T(8,128)(2,1)S(1)}, u32[]{:S(2)}, u32[]{:S(2)}) %collective-permute-start.6) | collective-permute-done | bytes 114720 | tf_op jit(solution)/shard_map/ppermute | solution.py:196
  25.0 1.3 %collective-permute-done.9.refs_10_ = bf16[8,7168]{1,0:T(8,128)(2,1)S(1)} collective-permute-done((bf16[8,7168]{1,0:T(8,128)(2,1)S(1)}, bf16[8,7168]{1,0:T(8,128)(2,1)S(1)}, u32[]{:S(2)}, u32[]{:S(2)}) %collective-permute-start.9) | collective-permute-done | bytes 114720 | tf_op jit(solution)/shard_map/ppermute | solution.py:199
  26.3 5.1 %gate_up.1.hidden_ref = bf16[128,1024]{1,0:T(8,128)(2,1)S(1)} custom-call(bf16[8,7168]{1,0:T(8,128)(2,1)S(1)} %stack.3.refs_0_, bf16[8,7168]{1,0:T(8,128)(2,1)S(1)} %collective-permute-done.refs_1_, bf16[8,7168]{1,0:T(8,128)(2,1)S(1)} %collective-permute-done.1.refs_2_, bf16[8,7168]{1,0:T(8,128)(2,1)S(1)} %collective-permute-done.2.refs_3_, ...), custom_call_target="tpu_custom_call" | custom-call | flops 3758096384 | tf_op jit(solution)/shard_map/gate_up/pallas_call | solution.py:75
  31.5 2.2 %down.2 = (f32[64,3584]{1,0:T(8,128)S(1)}, bf16[64,3584]{1,0:T(8,128)(2,1)S(1)}) custom-call(bf16[128,1024]{1,0:T(8,128)(2,1)S(1)} %gate_up.1.hidden_ref, bf16[1024,7168]{1,0:T(8,128)(2,1)S(1)} %bitcast.2), custom_call_target="tpu_custom_call" | custom-call | flops 939524096 | tf_op jit(solution)/shard_map/down/pallas_call | solution.py:104
  33.8 2.2 %down.3 = (f32[64,3584]{1,0:T(8,128)S(1)}, bf16[64,3584]{1,0:T(8,128)(2,1)S(1)}) custom-call(bf16[128,1024]{1,0:T(8,128)(2,1)S(1)} %gate_up.1.hidden_ref, bf16[1024,7168]{1,0:T(8,128)(2,1)S(1)} %bitcast.2), custom_call_target="tpu_custom_call" | custom-call | flops 939524096 | tf_op jit(solution)/shard_map/down/pallas_call | solution.py:104
  36.0 0.2 collective-permute-start.10
  36.2 0.4 collective-permute-start.11
  36.6 1.3 %collective-permute-done.10.refs_1_ = bf16[64,3584]{1,0:T(8,128)(2,1)S(1)} collective-permute-done((bf16[64,3584]{1,0:T(8,128)(2,1)S(1)}, bf16[64,3584]{1,0:T(8,128)(2,1)S(1)}, u32[]{:S(2)}, u32[]{:S(2)}) %collective-permute-start.10) | collective-permute-done | bytes 458784 | tf_op jit(solution)/shard_map/ppermute | solution.py:199
  37.9 0.7 %collective-permute-done.11.refs_3_ = bf16[64,3584]{1,0:T(8,128)(2,1)S(1)} collective-permute-done((bf16[64,3584]{1,0:T(8,128)(2,1)S(1)}, bf16[64,3584]{1,0:T(8,128)(2,1)S(1)}, u32[]{:S(2)}, u32[]{:S(2)}) %collective-permute-start.11) | collective-permute-done | bytes 458784 | tf_op jit(solution)/shard_map/ppermute | solution.py:199
  38.7 1.6 %collective-permute-start.17 = (bf16[8,7168]{1,0:T(8,128)(2,1)S(1)}, bf16[8,7168]{1,0:T(8,128)(2,1)S(1)}, u32[]{:S(2)}, u32[]{:S(2)}) collective-permute-start(bf16[8,7168]{1,0:T(8,128)(2,1)S(1)} %get-tuple-element.28), channel_id=1, source_target_pairs={{0,2},{2,0},{4,6},{6,4},{8,10},{10,8},{12,14},{14,12},{1,3},{3,1},... | collective-permute-start | bytes 344072 | tf_op jit(solution)/shard_map/ppermute | solution.py:196
  40.3 0.5 collective-permute-start.15
  40.8 1.6 %collective-permute-start.13 = (bf16[8,7168]{1,0:T(8,128)(2,1)S(1)}, bf16[8,7168]{1,0:T(8,128)(2,1)S(1)}, u32[]{:S(2)}, u32[]{:S(2)}) collective-permute-start(bf16[8,7168]{1,0:T(8,128)(2,1)S(1)} %get-tuple-element.24), channel_id=1, source_target_pairs={{0,2},{2,0},{4,6},{6,4},{8,10},{10,8},{12,14},{14,12},{1,3},{3,1},... | collective-permute-start | bytes 344072 | tf_op jit(solution)/shard_map/ppermute | solution.py:196
  42.4 0.5 collective-permute-start.12
  42.8 1.9 %collective-permute-done.17.refs_1_ = bf16[8,7168]{1,0:T(8,128)(2,1)S(1)} collective-permute-done((bf16[8,7168]{1,0:T(8,128)(2,1)S(1)}, bf16[8,7168]{1,0:T(8,128)(2,1)S(1)}, u32[]{:S(2)}, u32[]{:S(2)}) %collective-permute-start.17) | collective-permute-done | bytes 114720 | tf_op jit(solution)/shard_map/ppermute | solution.py:196
  44.8 1.5 %collective-permute-start.18 = (bf16[8,7168]{1,0:T(8,128)(2,1)S(1)}, bf16[8,7168]{1,0:T(8,128)(2,1)S(1)}, u32[]{:S(2)}, u32[]{:S(2)}) collective-permute-start(bf16[8,7168]{1,0:T(8,128)(2,1)S(1)} %span_sum.5), channel_id=1, source_target_pairs={{0,4},{2,6},{4,8},{6,10},{8,12},{10,14},{12,0},{14,2},{1,5},{3,7},... | collective-permute-start | bytes 344072 | tf_op jit(solution)/shard_map/ppermute | solution.py:193
  46.3 0.9 %collective-permute-done.15.refs_1_ = bf16[8,7168]{1,0:T(8,128)(2,1)S(1)} collective-permute-done((bf16[8,7168]{1,0:T(8,128)(2,1)S(1)}, bf16[8,7168]{1,0:T(8,128)(2,1)S(1)}, u32[]{:S(2)}, u32[]{:S(2)}) %collective-permute-start.15) | collective-permute-done | bytes 114720 | tf_op jit(solution)/shard_map/ppermute | solution.py:196
  47.3 3.2 %collective-permute-start.16 = (bf16[8,7168]{1,0:T(8,128)(2,1)S(1)}, bf16[8,7168]{1,0:T(8,128)(2,1)S(1)}, u32[]{:S(2)}, u32[]{:S(2)}) collective-permute-start(bf16[8,7168]{1,0:T(8,128)(2,1)S(1)} %span_sum.4), channel_id=1, source_target_pairs={{0,8},{2,10},{4,12},{6,14},{8,0},{10,2},{12,4},{14,6},{1,9},{3,11}... | collective-permute-start | bytes 344072 | tf_op jit(solution)/shard_map/ppermute | solution.py:193
  50.5 3.1 %collective-permute-start.14 = (bf16[8,7168]{1,0:T(8,128)(2,1)S(1)}, bf16[8,7168]{1,0:T(8,128)(2,1)S(1)}, u32[]{:S(2)}, u32[]{:S(2)}) collective-permute-start(bf16[8,7168]{1,0:T(8,128)(2,1)S(1)} %span_sum.3), channel_id=1, source_target_pairs={{0,12},{2,14},{4,0},{6,2},{8,4},{10,6},{12,8},{14,10},{1,13},{3,15... | collective-permute-start | bytes 344072 | tf_op jit(solution)/shard_map/ppermute | solution.py:193
  53.7 2.8 %collective-permute-done.16.refs_3_ = bf16[8,7168]{1,0:T(8,128)(2,1)S(1)} collective-permute-done((bf16[8,7168]{1,0:T(8,128)(2,1)S(1)}, bf16[8,7168]{1,0:T(8,128)(2,1)S(1)}, u32[]{:S(2)}, u32[]{:S(2)}) %collective-permute-start.16) | collective-permute-done | bytes 114720 | tf_op jit(solution)/shard_map/ppermute | solution.py:193
  56.5 0.5 collective-permute-done.14.refs_2_
  57.0 0.8 %combine.1 = bf16[8,7168]{1,0:T(8,128)(2,1)} custom-call(s32[1]{0:T(128)} %bitcast.own_expert, s32[8,3]{1,0:T(8,128)S(1)} %copy.7.ids_ref, f32[8,3]{1,0:T(8,128)S(1)} %copy.8.weights_ref, f32[8,7168]{1,0:T(8,128)S(1)} %get-tuple-element.21.refs_0_, bf16[8,7168]{1,0:T(8,128)(2,1)S(1)} %collective-permute-done.12.refs_1_, ...), custom_call_target="tpu_custom_call" | custom-call | tf_op jit(solution)/shard_map/combine/pallas_call | solution.py:177
  (38 shorter events, 0.6 us)
Async XLA Ops:
  0.0 26.3 %copy-start.1 = (bf16[7168,1024]{1,0:T(8,128)(2,1)S(1)}, bf16[7168,1024]{1,0:T(8,128)(2,1)}, u32[]{:S(2)}) copy-start(bf16[7168,1024]{1,0:T(8,128)(2,1)} %refs_12_.1) | copy-start | bytes 44040196
  0.0 26.3 %copy-start = (bf16[7168,1024]{1,0:T(8,128)(2,1)S(1)}, bf16[7168,1024]{1,0:T(8,128)(2,1)}, u32[]{:S(2)}) copy-start(bf16[7168,1024]{1,0:T(8,128)(2,1)} %refs_11_.1) | copy-start | bytes 44040196
  0.0 1.0 %copy-start.2 = (bf16[8,7168]{1,0:T(8,128)(2,1)S(1)}, bf16[8,7168]{1,0:T(8,128)(2,1)}, u32[]{:S(2)}) copy-start(bf16[8,7168]{1,0:T(8,128)(2,1)} %refs_0_.1) | copy-start | bytes 344068
  1.1 9.2 %collective-permute-start = (bf16[8,7168]{1,0:T(8,128)(2,1)S(1)}, bf16[8,7168]{1,0:T(8,128)(2,1)S(1)}, u32[]{:S(2)}, u32[]{:S(2)}) collective-permute-start(bf16[8,7168]{1,0:T(8,128)(2,1)S(1)} %stack.3.refs_0_), channel_id=1, source_target_pairs={{0,4},{2,6},{4,8},{6,10},{8,12},{10,14},{12,0},{14,2},{1,5},{3,7},... | collective-permute-start | bytes 344072 | tf_op jit(solution)/shard_map/ppermute | solution.py:193
  4.1 10.2 %collective-permute-start.1 = (bf16[8,7168]{1,0:T(8,128)(2,1)S(1)}, bf16[8,7168]{1,0:T(8,128)(2,1)S(1)}, u32[]{:S(2)}, u32[]{:S(2)}) collective-permute-start(bf16[8,7168]{1,0:T(8,128)(2,1)S(1)} %stack.3.refs_0_), channel_id=1, source_target_pairs={{0,8},{2,10},{4,12},{6,14},{8,0},{10,2},{12,4},{14,6},{1,9},{3,11}... | collective-permute-start | bytes 344072 | tf_op jit(solution)/shard_map/ppermute | solution.py:193
  6.7 9.2 %collective-permute-start.2 = (bf16[8,7168]{1,0:T(8,128)(2,1)S(1)}, bf16[8,7168]{1,0:T(8,128)(2,1)S(1)}, u32[]{:S(2)}, u32[]{:S(2)}) collective-permute-start(bf16[8,7168]{1,0:T(8,128)(2,1)S(1)} %stack.3.refs_0_), channel_id=1, source_target_pairs={{0,12},{2,14},{4,0},{6,2},{8,4},{10,6},{12,8},{14,10},{1,13},{3,15... | collective-permute-start | bytes 344072 | tf_op jit(solution)/shard_map/ppermute | solution.py:193
  8.1 7.9 %collective-permute-start.3 = (bf16[8,7168]{1,0:T(8,128)(2,1)S(1)}, bf16[8,7168]{1,0:T(8,128)(2,1)S(1)}, u32[]{:S(2)}, u32[]{:S(2)}) collective-permute-start(bf16[8,7168]{1,0:T(8,128)(2,1)S(1)} %stack.3.refs_0_), channel_id=1, source_target_pairs={{0,2},{2,0},{4,6},{6,4},{8,10},{10,8},{12,14},{14,12},{1,3},{3,1},... | collective-permute-start | bytes 344072 | tf_op jit(solution)/shard_map/ppermute | solution.py:196
  10.2 5.8 %collective-permute-start.4 = (bf16[8,7168]{1,0:T(8,128)(2,1)S(1)}, bf16[8,7168]{1,0:T(8,128)(2,1)S(1)}, u32[]{:S(2)}, u32[]{:S(2)}) collective-permute-start(bf16[8,7168]{1,0:T(8,128)(2,1)S(1)} %collective-permute-done.refs_1_), channel_id=1, source_target_pairs={{0,2},{2,0},{4,6},{6,4},{8,10},{10,8},{12,14},{14,12},{1,3},{3,1},... | collective-permute-start | bytes 344072 | tf_op jit(solution)/shard_map/ppermute | solution.py:196
  14.3 5.0 %collective-permute-start.5 = (bf16[8,7168]{1,0:T(8,128)(2,1)S(1)}, bf16[8,7168]{1,0:T(8,128)(2,1)S(1)}, u32[]{:S(2)}, u32[]{:S(2)}) collective-permute-start(bf16[8,7168]{1,0:T(8,128)(2,1)S(1)} %collective-permute-done.1.refs_2_), channel_id=1, source_target_pairs={{0,2},{2,0},{4,6},{6,4},{8,10},{10,8},{12,14},{14,12},{1,3},{3,1},... | collective-permute-start | bytes 344072 | tf_op jit(solution)/shard_map/ppermute | solution.py:196
  15.9 10.4 %collective-permute-start.7 = (bf16[32,7168]{1,0:T(8,128)(2,1)S(1)}, bf16[32,7168]{1,0:T(8,128)(2,1)S(1)}, u32[]{:S(2)}, u32[]{:S(2)}) collective-permute-start(bf16[32,7168]{1,0:T(8,128)(2,1)S(1)} %stack.4), channel_id=1, source_target_pairs={{0,1},{1,0},{2,3},{3,2},{4,5},{5,4},{6,7},{7,6},{8,9},{9,8},{10,11... | collective-permute-start | bytes 1376264 | tf_op jit(solution)/shard_map/ppermute | solution.py:199
  19.3 12.2 %slice-start = ((s8[14680064]{0:T(1024)(128)(4,1)}), s8[4194304]{0:T(1024)(128)(4,1)S(1)}, s32[]{:S(2)}) async-start(s8[14680064]{0:T(1024)(128)(4,1)} %bitcast.1), calls=%async_computation | async-start | bytes 8388608
  19.3 12.2 %slice-start.1 = ((s8[14680064]{0:T(1024)(128)(4,1)}), s8[4194304]{0:T(1024)(128)(4,1)S(1)}, s32[]{:S(2)}) async-start(s8[14680064]{0:T(1024)(128)(4,1)} %bitcast.1), calls=%async_computation.1 | async-start | bytes 8388608
  19.3 12.2 %slice-start.2 = ((s8[14680064]{0:T(1024)(128)(4,1)}), s8[4194304]{0:T(1024)(128)(4,1)S(1)}, s32[]{:S(2)}) async-start(s8[14680064]{0:T(1024)(128)(4,1)} %bitcast.1), calls=%async_computation.2 | async-start | bytes 8388608
  19.4 12.2 %slice-start.3 = ((s8[14680064]{0:T(1024)(128)(4,1)}), s8[2097152]{0:T(1024)(128)(4,1)S(1)}, s32[]{:S(2)}) async-start(s8[14680064]{0:T(1024)(128)(4,1)} %bitcast.1), calls=%async_computation.3 | async-start | bytes 4194304
  19.4 7.0 %collective-permute-start.8 = (bf16[24,7168]{1,0:T(8,128)(2,1)S(1)}, bf16[24,7168]{1,0:T(8,128)(2,1)S(1)}, u32[]{:S(2)}, u32[]{:S(2)}) collective-permute-start(bf16[24,7168]{1,0:T(8,128)(2,1)S(1)} %stack.5), channel_id=1, source_target_pairs={{0,1},{1,0},{2,3},{3,2},{4,5},{5,4},{6,7},{7,6},{8,9},{9,8},{10,11... | collective-permute-start | bytes 1032200 | tf_op jit(solution)/shard_map/ppermute | solution.py:199
  19.4 5.6 %collective-permute-start.6 = (bf16[8,7168]{1,0:T(8,128)(2,1)S(1)}, bf16[8,7168]{1,0:T(8,128)(2,1)S(1)}, u32[]{:S(2)}, u32[]{:S(2)}) collective-permute-start(bf16[8,7168]{1,0:T(8,128)(2,1)S(1)} %collective-permute-done.2.refs_3_), channel_id=1, source_target_pairs={{0,2},{2,0},{4,6},{6,4},{8,10},{10,8},{12,14},{14,12},{1,3},{3,1},... | collective-permute-start | bytes 344072 | tf_op jit(solution)/shard_map/ppermute | solution.py:196
  25.0 1.3 %collective-permute-start.9 = (bf16[8,7168]{1,0:T(8,128)(2,1)S(1)}, bf16[8,7168]{1,0:T(8,128)(2,1)S(1)}, u32[]{:S(2)}, u32[]{:S(2)}) collective-permute-start(bf16[8,7168]{1,0:T(8,128)(2,1)S(1)} %collective-permute-done.6.refs_7_), channel_id=1, source_target_pairs={{0,1},{1,0},{2,3},{3,2},{4,5},{5,4},{6,7},{7,6},{8,9},{9,8},{10,11... | collective-permute-start | bytes 344072 | tf_op jit(solution)/shard_map/ppermute | solution.py:199
  31.5 22.1 %copy-start.3 = (s32[8,3]{0,1:T(4,128)S(1)}, s32[8,3]{0,1:T(4,128)}, u32[]{:S(2)}) copy-start(s32[8,3]{0,1:T(4,128)} %param.7) | copy-start | bytes 292
  31.5 22.1 %copy-start.4 = (f32[8,3]{0,1:T(4,128)S(1)}, f32[8,3]{0,1:T(4,128)}, u32[]{:S(2)}) copy-start(f32[8,3]{0,1:T(4,128)} %param.8) | copy-start | bytes 292
  36.0 1.9 %collective-permute-start.10 = (bf16[64,3584]{1,0:T(8,128)(2,1)S(1)}, bf16[64,3584]{1,0:T(8,128)(2,1)S(1)}, u32[]{:S(2)}, u32[]{:S(2)}) collective-permute-start(bf16[64,3584]{1,0:T(8,128)(2,1)S(1)} %get-tuple-element.18), channel_id=1, source_target_pairs={{0,1},{1,0},{2,3},{3,2},{4,5},{5,4},{6,7},{7,6},{8,9},{9,8},{10,11... | collective-permute-start | bytes 1376264 | tf_op jit(solution)/shard_map/ppermute | solution.py:199
  36.2 2.3 %collective-permute-start.11 = (bf16[64,3584]{1,0:T(8,128)(2,1)S(1)}, bf16[64,3584]{1,0:T(8,128)(2,1)S(1)}, u32[]{:S(2)}, u32[]{:S(2)}) collective-permute-start(bf16[64,3584]{1,0:T(8,128)(2,1)S(1)} %get-tuple-element.20), channel_id=1, source_target_pairs={{0,1},{1,0},{2,3},{3,2},{4,5},{5,4},{6,7},{7,6},{8,9},{9,8},{10,11... | collective-permute-start | bytes 1376264 | tf_op jit(solution)/shard_map/ppermute | solution.py:199
  38.7 6.1 %collective-permute-start.17 = (bf16[8,7168]{1,0:T(8,128)(2,1)S(1)}, bf16[8,7168]{1,0:T(8,128)(2,1)S(1)}, u32[]{:S(2)}, u32[]{:S(2)}) collective-permute-start(bf16[8,7168]{1,0:T(8,128)(2,1)S(1)} %get-tuple-element.28), channel_id=1, source_target_pairs={{0,2},{2,0},{4,6},{6,4},{8,10},{10,8},{12,14},{14,12},{1,3},{3,1},... | collective-permute-start | bytes 344072 | tf_op jit(solution)/shard_map/ppermute | solution.py:196
  40.3 6.9 %collective-permute-start.15 = (bf16[8,7168]{1,0:T(8,128)(2,1)S(1)}, bf16[8,7168]{1,0:T(8,128)(2,1)S(1)}, u32[]{:S(2)}, u32[]{:S(2)}) collective-permute-start(bf16[8,7168]{1,0:T(8,128)(2,1)S(1)} %get-tuple-element.26), channel_id=1, source_target_pairs={{0,2},{2,0},{4,6},{6,4},{8,10},{10,8},{12,14},{14,12},{1,3},{3,1},... | collective-permute-start | bytes 344072 | tf_op jit(solution)/shard_map/ppermute | solution.py:196
  40.8 9.6 %collective-permute-start.13 = (bf16[8,7168]{1,0:T(8,128)(2,1)S(1)}, bf16[8,7168]{1,0:T(8,128)(2,1)S(1)}, u32[]{:S(2)}, u32[]{:S(2)}) collective-permute-start(bf16[8,7168]{1,0:T(8,128)(2,1)S(1)} %get-tuple-element.24), channel_id=1, source_target_pairs={{0,2},{2,0},{4,6},{6,4},{8,10},{10,8},{12,14},{14,12},{1,3},{3,1},... | collective-permute-start | bytes 344072 | tf_op jit(solution)/shard_map/ppermute | solution.py:196
  42.4 11.4 %collective-permute-start.12 = (bf16[8,7168]{1,0:T(8,128)(2,1)S(1)}, bf16[8,7168]{1,0:T(8,128)(2,1)S(1)}, u32[]{:S(2)}, u32[]{:S(2)}) collective-permute-start(bf16[8,7168]{1,0:T(8,128)(2,1)S(1)} %get-tuple-element.22), channel_id=1, source_target_pairs={{0,2},{2,0},{4,6},{6,4},{8,10},{10,8},{12,14},{14,12},{1,3},{3,1},... | collective-permute-start | bytes 344072 | tf_op jit(solution)/shard_map/ppermute | solution.py:196
  44.8 8.9 %collective-permute-start.18 = (bf16[8,7168]{1,0:T(8,128)(2,1)S(1)}, bf16[8,7168]{1,0:T(8,128)(2,1)S(1)}, u32[]{:S(2)}, u32[]{:S(2)}) collective-permute-start(bf16[8,7168]{1,0:T(8,128)(2,1)S(1)} %span_sum.5), channel_id=1, source_target_pairs={{0,4},{2,6},{4,8},{6,10},{8,12},{10,14},{12,0},{14,2},{1,5},{3,7},... | collective-permute-start | bytes 344072 | tf_op jit(solution)/shard_map/ppermute | solution.py:193
  47.3 9.3 %collective-permute-start.16 = (bf16[8,7168]{1,0:T(8,128)(2,1)S(1)}, bf16[8,7168]{1,0:T(8,128)(2,1)S(1)}, u32[]{:S(2)}, u32[]{:S(2)}) collective-permute-start(bf16[8,7168]{1,0:T(8,128)(2,1)S(1)} %span_sum.4), channel_id=1, source_target_pairs={{0,8},{2,10},{4,12},{6,14},{8,0},{10,2},{12,4},{14,6},{1,9},{3,11}... | collective-permute-start | bytes 344072 | tf_op jit(solution)/shard_map/ppermute | solution.py:193
  50.5 6.5 %collective-permute-start.14 = (bf16[8,7168]{1,0:T(8,128)(2,1)S(1)}, bf16[8,7168]{1,0:T(8,128)(2,1)S(1)}, u32[]{:S(2)}, u32[]{:S(2)}) collective-permute-start(bf16[8,7168]{1,0:T(8,128)(2,1)S(1)} %span_sum.3), channel_id=1, source_target_pairs={{0,12},{2,14},{4,0},{6,2},{8,4},{10,6},{12,8},{14,10},{1,13},{3,15... | collective-permute-start | bytes 344072 | tf_op jit(solution)/shard_map/ppermute | solution.py:193

commit v4 on v3

--- a/solution.py
+++ b/solution.py
@@ -8,10 +8,11 @@
 from jax.sharding import PartitionSpec as P
 
 EXPERTS = 4
+LANES = 128
 OUT_CHUNKS = 2
 N_BLOCK = 256
-C_BLOCK = 512
 EXCHANGE_FLOPS = 20_000_000_000
+DOWN_FLOPS = 6_000_000_000
 
 
 def params(mib=8):
@@ -59,14 +60,11 @@
     for k in range(0, width, piece):
         rows_ref[:, k:k + piece] = joined([ref.at[:, k:k + piece] for ref in rows_in]).astype(jnp.bfloat16)
 
-    def step(n, carry):
-        columns = pl.ds(pl.multiple_of(n * n_block, n_block), n_block)
+    for n in range(0, gate_ref.shape[1], n_block):
+        columns = slice(n, n + n_block)
         gate = jnp.dot(rows_ref[...], gate_ref[:, columns], preferred_element_type=jnp.float32)
         up = jnp.dot(rows_ref[...], up_ref[:, columns], preferred_element_type=jnp.float32)
         hidden_ref[:, columns] = (gate / (1.0 + jnp.exp(-gate)) * up).astype(jnp.bfloat16)
-        return carry
-
-    lax.fori_loop(0, gate_ref.shape[1] // n_block, step, 0)
 
 
 def gate_up(rows, gate_weight, up_weight):
@@ -86,15 +84,12 @@
 def down_kernel(offset, c_block, hidden_ref, down_ref, keep_ref, *send_refs):
     count, width = keep_ref.shape
 
-    def step(c, carry):
-        start = pl.multiple_of(c * c_block, c_block)
-        value = jnp.dot(hidden_ref[...], down_ref[:, pl.ds(offset + start, c_block)], preferred_element_type=jnp.float32)
-        keep_ref[:, pl.ds(start, c_block)] = value[:count]
+    for c in range(0, width, c_block):
+        columns = slice(c, c + c_block)
+        value = jnp.dot(hidden_ref[...], down_ref[:, offset + c:offset + c + c_block], preferred_element_type=jnp.float32)
+        keep_ref[:, columns] = value[:count]
         for i, ref in enumerate(send_refs):
-            ref[:, pl.ds(start, c_block)] = value[(i + 1) * count:(i + 2) * count].astype(jnp.bfloat16)
-        return carry
-
-    lax.fori_loop(0, width // c_block, step, 0)
+            ref[:, columns] = value[(i + 1) * count:(i + 2) * count].astype(jnp.bfloat16)
 
 
 def down(hidden, down_weight, chunk, pair):
@@ -102,12 +97,12 @@
     width = down_weight.shape[1] // OUT_CHUNKS
     part = total // pair
     return pl.pallas_call(
-        functools.partial(down_kernel, chunk * width, block_of(width, C_BLOCK)),
+        functools.partial(down_kernel, chunk * width, block_of(width, N_BLOCK)),
         in_specs=[pl.BlockSpec(memory_space=pltpu.VMEM)] * 2,
         out_shape=[jax.ShapeDtypeStruct((part, width), jnp.float32)]
         + [jax.ShapeDtypeStruct((part, width), jnp.bfloat16)] * (pair - 1),
         compiler_params=params(),
-        cost_estimate=cost(2 * total * width * units),
+        cost_estimate=cost(DOWN_FLOPS),
         name="down",
     )(hidden, in_vmem(down_weight))
 
@@ -155,13 +150,34 @@
     )(*arrays)
 
 
-def combine_kernel(own_count, own_expert, ids_ref, weights_ref, *refs):
+def coefficients_kernel(own_expert, ids_ref, weights_ref, out_ref):
+    ids, weights = ids_ref[...], weights_ref[...]
+    rows = ids.shape[1]
+    square = (rows, rows)
+    diagonal = lax.broadcasted_iota(jnp.int32, square, 0) == lax.broadcasted_iota(jnp.int32, square, 1)
+    for s in range(EXPERTS):
+        expert = lax.rem(own_expert[0] + s, EXPERTS)
+        chosen = jnp.sum(jnp.where(ids == expert, weights, 0.0), axis=0, keepdims=True)
+        column = jnp.sum(jnp.where(diagonal, jnp.broadcast_to(chosen, square), 0.0), axis=1, keepdims=True)
+        out_ref[:, s * LANES:(s + 1) * LANES] = jnp.broadcast_to(column, (rows, LANES))
+
+
+def coefficients(own_expert, ids, weights):
+    return pl.pallas_call(
+        coefficients_kernel,
+        in_specs=[pl.BlockSpec(memory_space=pltpu.SMEM)] + [pl.BlockSpec(memory_space=pltpu.VMEM)] * 2,
+        out_shape=jax.ShapeDtypeStruct((ids.shape[0], EXPERTS * LANES), jnp.float32),
+        compiler_params=params(),
+        cost_estimate=cost(0),
+        name="coefficients",
+    )(own_expert, ids.T, weights.T)
+
+
+def combine_kernel(own_count, coeff_ref, *refs):
     out_ref = refs[-1]
-    ids, weights = ids_ref[...], weights_ref[...]
 
     def coeff(s):
-        expert = lax.rem(own_expert[0] + s, EXPERTS)
-        return jnp.sum(jnp.where(ids == expert, weights, 0.0), axis=1, keepdims=True)
+        return coeff_ref[:, s * LANES:s * LANES + 1]
 
     own = refs[0][...]
     for ref in refs[1:own_count]:
@@ -172,15 +188,13 @@
     out_ref[...] = value.astype(jnp.bfloat16)
 
 
-def combine(own_expert, ids, weights, own, others):
-    arrays = list(own) + list(others)
+def combine(coeffs, own, others):
     return pl.pallas_call(
         functools.partial(combine_kernel, len(own)),
-        in_specs=[pl.BlockSpec(memory_space=pltpu.SMEM)] + [pl.BlockSpec(memory_space=pltpu.VMEM)] * (2 + len(arrays)),
         out_shape=jax.ShapeDtypeStruct(own[0].shape, jnp.bfloat16),
         compiler_params=params(),
         name="combine",
-    )(own_expert, ids, weights, *arrays)
+    )(coeffs, *own, *others)
 
 
 def local(tokens, expert_ids, route_weights, gate_weight, up_weight, down_weight):
@@ -198,13 +212,15 @@
     def over_pair(value, shift):
         return lax.ppermute(value, "ffn", [(i, (i + shift) % pair) for i in range(pair)])
 
+    own_expert = (lax.axis_index("attn") // span).astype(jnp.int32).reshape(1)
+    coeffs = coefficients(own_expert, expert_ids, route_weights)
     own = stack([tokens], EXCHANGE_FLOPS)
     column = [own] + [over_experts(own, s) for s in range(1, EXPERTS)]
     plane, groups = list(column), [stack(column)]
     for t in range(1, span):
         blocks = [over_span(b, t) for b in column]
         plane += blocks
-        groups += [stack(blocks[:-1]), blocks[-1]]
+        groups.append(stack(blocks))
     gathered = plane + [over_pair(g, p) for p in range(1, pair) for g in groups]
 
     hidden = gate_up(gathered, gate_weight, up_weight)
@@ -220,8 +236,7 @@
     sums.reverse()
     others = [over_experts(span_sum(sums[s]), -s) for s in reversed(range(1, EXPERTS))]
     others.reverse()
-    own_expert = (lax.axis_index("attn") // span).astype(jnp.int32).reshape(1)
-    return combine(own_expert, expert_ids, route_weights, sums[0], others)
+    return combine(coeffs, sums[0], others)
 
 
 def solution(mesh):

time: 58 us -> 51.9 us (0.89)
  Pallas kernels: 10.7 us -> 7.86 us
  starting transfers between devices: 26.1 us -> 23.8 us
  waiting for transfers between devices: 19.6 us -> 18.8 us
    pallas_call x2, Pallas kernels: 4.47 us -> 2.27 us  [down(): pl.pallas_call(functools.partial(down_kernel, chunk * width, block_of(wid...]
    ppermute x8, waiting for transfers between devices: 10.1 us -> 8.49 us  [over_span(): lax.ppermute(value, 'attn', [(i, i // span * span + (i + shift) % span) f...]
    ppermute x8, starting transfers between devices: 10.6 us -> 9.43 us  [over_span(): lax.ppermute(value, 'attn', [(i, i // span * span + (i + shift) % span) f...]
    ppermute x6, starting transfers between devices: 14.8 us -> 13.7 us  [over_experts(): lax.ppermute(value, 'attn', [(i, (i + shift * span) % attn) for i in rang...]
    pallas_call x1, Pallas kernels: 5.11 us -> 4.39 us  [gate_up(): pl.pallas_call(functools.partial(gate_up_kernel, block_of(units, N_BLOCK)...]
    ppermute x5 -> x4, waiting for transfers between devices: 3.29 us -> 3.76 us  [over_pair(): lax.ppermute(value, 'ffn', [(i, (i + shift) % pair) for i in range(pair)])]
    unnamed x20 -> x18, local copies, waits for them, and re-layouts: 1.25 us -> 1.09 us
  transfers between devices with their start and end apart: 19 -> 18, of which waited for: 11 -> 11; matrix products, arithmetic and copies ran while one was open for 0% -> 0% of each run, Pallas kernels for 0% -> 0%
where the time goes in v4:
time: 51.9 us; the launch traced here: 51.8 us
  starting transfers between devices  23.8 us (46%)
  waiting for transfers between devices  18.8 us (36%)
  Pallas kernels  7.86 us (15%)
  local copies, waits for them, and re-layouts  1.09 us (2%)
    ppermute x6, starting transfers between devices, over_experts(): lax.ppermute(value, 'attn', [(i, (i + shift * span) % attn) for i in rang...  13.7 us
    ppermute x8, starting transfers between devices, over_span(): lax.ppermute(value, 'attn', [(i, i // span * span + (i + shift) % span) f...  9.43 us
    ppermute x8, waiting for transfers between devices, over_span(): lax.ppermute(value, 'attn', [(i, i // span * span + (i + shift) % span) f...  8.49 us
    ppermute x6, waiting for transfers between devices, over_experts(): lax.ppermute(value, 'attn', [(i, (i + shift * span) % attn) for i in rang...  6.55 us
    pallas_call x1, Pallas kernels, gate_up(): pl.pallas_call(functools.partial(gate_up_kernel, block_of(units, N_BLOCK)...  4.39 us
    ppermute x4, waiting for transfers between devices, over_pair(): lax.ppermute(value, 'ffn', [(i, (i + shift) % pair) for i in range(pair)])  3.76 us
    pallas_call x2, Pallas kernels, down(): pl.pallas_call(functools.partial(down_kernel, chunk * width, block_of(wid...  2.27 us
    unnamed x18, local copies, waits for them, and re-layouts  1.09 us
  transfers between devices with their start and end apart: 18, of which 11 were waited for; matrix products, arithmetic and copies ran while one was open for 0% of the time, Pallas kernels for 0%

profile of v4, /device:TPU:0, one launch (start us, length us, event | category | flops | bytes accessed | tf_op | source)
XLA Modules:
  0.0 51.8 jit_solution(9063766866723279691)
XLA Ops:
  0.0 1.0 %copy-done.4 = bf16[8,7168]{1,0:T(8,128)(2,1)S(1)} copy-done((bf16[8,7168]{1,0:T(8,128)(2,1)S(1)}, bf16[8,7168]{1,0:T(8,128)(2,1)}, u32[]{:S(2)}) %copy-start.4) | copy-done | bytes 114712
  1.1 3.1 %collective-permute-start = (bf16[8,7168]{1,0:T(8,128)(2,1)S(1)}, bf16[8,7168]{1,0:T(8,128)(2,1)S(1)}, u32[]{:S(2)}, u32[]{:S(2)}) collective-permute-start(bf16[8,7168]{1,0:T(8,128)(2,1)S(1)} %stack.3.refs_0_), channel_id=1, source_target_pairs={{0,4},{2,6},{4,8},{6,10},{8,12},{10,14},{12,0},{14,2},{1,5},{3,7},... | collective-permute-start | bytes 344072 | tf_op jit(solution)/shard_map/ppermute | solution.py:207
  4.1 2.6 %collective-permute-start.1 = (bf16[8,7168]{1,0:T(8,128)(2,1)S(1)}, bf16[8,7168]{1,0:T(8,128)(2,1)S(1)}, u32[]{:S(2)}, u32[]{:S(2)}) collective-permute-start(bf16[8,7168]{1,0:T(8,128)(2,1)S(1)} %stack.3.refs_0_), channel_id=1, source_target_pairs={{0,8},{2,10},{4,12},{6,14},{8,0},{10,2},{12,4},{14,6},{1,9},{3,11}... | collective-permute-start | bytes 344072 | tf_op jit(solution)/shard_map/ppermute | solution.py:207
  6.7 1.3 %collective-permute-start.2 = (bf16[8,7168]{1,0:T(8,128)(2,1)S(1)}, bf16[8,7168]{1,0:T(8,128)(2,1)S(1)}, u32[]{:S(2)}, u32[]{:S(2)}) collective-permute-start(bf16[8,7168]{1,0:T(8,128)(2,1)S(1)} %stack.3.refs_0_), channel_id=1, source_target_pairs={{0,12},{2,14},{4,0},{6,2},{8,4},{10,6},{12,8},{14,10},{1,13},{3,15... | collective-permute-start | bytes 344072 | tf_op jit(solution)/shard_map/ppermute | solution.py:207
  8.1 1.5 %collective-permute-start.3 = (bf16[8,7168]{1,0:T(8,128)(2,1)S(1)}, bf16[8,7168]{1,0:T(8,128)(2,1)S(1)}, u32[]{:S(2)}, u32[]{:S(2)}) collective-permute-start(bf16[8,7168]{1,0:T(8,128)(2,1)S(1)} %stack.3.refs_0_), channel_id=1, source_target_pairs={{0,2},{2,0},{4,6},{6,4},{8,10},{10,8},{12,14},{14,12},{1,3},{3,1},... | collective-permute-start | bytes 344072 | tf_op jit(solution)/shard_map/ppermute | solution.py:210
  9.6 0.6 %collective-permute-done.refs_1_ = bf16[8,7168]{1,0:T(8,128)(2,1)S(1)} collective-permute-done((bf16[8,7168]{1,0:T(8,128)(2,1)S(1)}, bf16[8,7168]{1,0:T(8,128)(2,1)S(1)}, u32[]{:S(2)}, u32[]{:S(2)}) %collective-permute-start) | collective-permute-done | bytes 114720 | tf_op jit(solution)/shard_map/ppermute | solution.py:207
  10.2 1.8 %collective-permute-start.4 = (bf16[8,7168]{1,0:T(8,128)(2,1)S(1)}, bf16[8,7168]{1,0:T(8,128)(2,1)S(1)}, u32[]{:S(2)}, u32[]{:S(2)}) collective-permute-start(bf16[8,7168]{1,0:T(8,128)(2,1)S(1)} %collective-permute-done.refs_1_), channel_id=1, source_target_pairs={{0,2},{2,0},{4,6},{6,4},{8,10},{10,8},{12,14},{14,12},{1,3},{3,1},... | collective-permute-start | bytes 344072 | tf_op jit(solution)/shard_map/ppermute | solution.py:210
  12.0 2.3 %collective-permute-done.1.refs_2_ = bf16[8,7168]{1,0:T(8,128)(2,1)S(1)} collective-permute-done((bf16[8,7168]{1,0:T(8,128)(2,1)S(1)}, bf16[8,7168]{1,0:T(8,128)(2,1)S(1)}, u32[]{:S(2)}, u32[]{:S(2)}) %collective-permute-start.1) | collective-permute-done | bytes 114720 | tf_op jit(solution)/shard_map/ppermute | solution.py:207
  14.3 1.6 %collective-permute-start.5 = (bf16[8,7168]{1,0:T(8,128)(2,1)S(1)}, bf16[8,7168]{1,0:T(8,128)(2,1)S(1)}, u32[]{:S(2)}, u32[]{:S(2)}) collective-permute-start(bf16[8,7168]{1,0:T(8,128)(2,1)S(1)} %collective-permute-done.1.refs_2_), channel_id=1, source_target_pairs={{0,2},{2,0},{4,6},{6,4},{8,10},{10,8},{12,14},{14,12},{1,3},{3,1},... | collective-permute-start | bytes 344072 | tf_op jit(solution)/shard_map/ppermute | solution.py:210
  15.9 0.5 collective-permute-start.6
  16.5 3.9 %collective-permute-done.5.refs_2_.refs_6_ = bf16[8,7168]{1,0:T(8,128)(2,1)S(1)} collective-permute-done((bf16[8,7168]{1,0:T(8,128)(2,1)S(1)}, bf16[8,7168]{1,0:T(8,128)(2,1)S(1)}, u32[]{:S(2)}, u32[]{:S(2)}) %collective-permute-start.5) | collective-permute-done | bytes 114720 | tf_op jit(solution)/shard_map/ppermute | solution.py:210
  20.3 1.4 %collective-permute-done.6.refs_3_.refs_7_ = bf16[8,7168]{1,0:T(8,128)(2,1)S(1)} collective-permute-done((bf16[8,7168]{1,0:T(8,128)(2,1)S(1)}, bf16[8,7168]{1,0:T(8,128)(2,1)S(1)}, u32[]{:S(2)}, u32[]{:S(2)}) %collective-permute-start.6) | collective-permute-done | bytes 114720 | tf_op jit(solution)/shard_map/ppermute | solution.py:210
  21.9 1.8 %collective-permute-done.8.refs_9_ = bf16[32,7168]{1,0:T(8,128)(2,1)S(1)} collective-permute-done((bf16[32,7168]{1,0:T(8,128)(2,1)S(1)}, bf16[32,7168]{1,0:T(8,128)(2,1)S(1)}, u32[]{:S(2)}, u32[]{:S(2)}) %collective-permute-start.8) | collective-permute-done | bytes 458784 | tf_op jit(solution)/shard_map/ppermute | solution.py:213
  23.7 4.4 %gate_up.1.hidden_ref = bf16[128,1024]{1,0:T(8,128)(2,1)S(1)} custom-call(bf16[8,7168]{1,0:T(8,128)(2,1)S(1)} %stack.3.refs_0_, bf16[8,7168]{1,0:T(8,128)(2,1)S(1)} %collective-permute-done.refs_1_, bf16[8,7168]{1,0:T(8,128)(2,1)S(1)} %collective-permute-done.1.refs_2_, bf16[8,7168]{1,0:T(8,128)(2,1)S(1)} %collective-permute-done.2.refs_3_, ...), custom_call_target="tpu_custom_call" | custom-call | flops 3758096384 | tf_op jit(solution)/shard_map/gate_up/pallas_call | solution.py:73
  28.2 1.1 %down.3 = (f32[64,3584]{1,0:T(8,128)S(1)}, bf16[64,3584]{1,0:T(8,128)(2,1)S(1)}) custom-call(bf16[128,1024]{1,0:T(8,128)(2,1)S(1)} %gate_up.1.hidden_ref, bf16[1024,7168]{1,0:T(8,128)(2,1)S(1)} %bitcast.6), custom_call_target="tpu_custom_call" | custom-call | flops 6000000000 | tf_op jit(solution)/shard_map/down/pallas_call | solution.py:99
  29.3 1.1 %down.2 = (f32[64,3584]{1,0:T(8,128)S(1)}, bf16[64,3584]{1,0:T(8,128)(2,1)S(1)}) custom-call(bf16[128,1024]{1,0:T(8,128)(2,1)S(1)} %gate_up.1.hidden_ref, bf16[1024,7168]{1,0:T(8,128)(2,1)S(1)} %bitcast.6), custom_call_target="tpu_custom_call" | custom-call | flops 6000000000 | tf_op jit(solution)/shard_map/down/pallas_call | solution.py:99
  30.6 0.4 collective-permute-start.9
  31.0 1.3 %collective-permute-done.10.refs_3_ = bf16[64,3584]{1,0:T(8,128)(2,1)S(1)} collective-permute-done((bf16[64,3584]{1,0:T(8,128)(2,1)S(1)}, bf16[64,3584]{1,0:T(8,128)(2,1)S(1)}, u32[]{:S(2)}, u32[]{:S(2)}) %collective-permute-start.10) | collective-permute-done | bytes 458784 | tf_op jit(solution)/shard_map/ppermute | solution.py:213
  32.4 0.7 %collective-permute-done.9.refs_1_ = bf16[64,3584]{1,0:T(8,128)(2,1)S(1)} collective-permute-done((bf16[64,3584]{1,0:T(8,128)(2,1)S(1)}, bf16[64,3584]{1,0:T(8,128)(2,1)S(1)}, u32[]{:S(2)}, u32[]{:S(2)}) %collective-permute-start.9) | collective-permute-done | bytes 458784 | tf_op jit(solution)/shard_map/ppermute | solution.py:213
  33.0 0.1 pair_sum.1
  33.2 1.6 %collective-permute-start.16 = (bf16[8,7168]{1,0:T(8,128)(2,1)S(1)}, bf16[8,7168]{1,0:T(8,128)(2,1)S(1)}, u32[]{:S(2)}, u32[]{:S(2)}) collective-permute-start(bf16[8,7168]{1,0:T(8,128)(2,1)S(1)} %get-tuple-element.28), channel_id=1, source_target_pairs={{0,2},{2,0},{4,6},{6,4},{8,10},{10,8},{12,14},{14,12},{1,3},{3,1},... | collective-permute-start | bytes 344072 | tf_op jit(solution)/shard_map/ppermute | solution.py:210
  34.8 0.5 collective-permute-start.14
  35.3 1.6 %collective-permute-start.12 = (bf16[8,7168]{1,0:T(8,128)(2,1)S(1)}, bf16[8,7168]{1,0:T(8,128)(2,1)S(1)}, u32[]{:S(2)}, u32[]{:S(2)}) collective-permute-start(bf16[8,7168]{1,0:T(8,128)(2,1)S(1)} %get-tuple-element.24), channel_id=1, source_target_pairs={{0,2},{2,0},{4,6},{6,4},{8,10},{10,8},{12,14},{14,12},{1,3},{3,1},... | collective-permute-start | bytes 344072 | tf_op jit(solution)/shard_map/ppermute | solution.py:210
  36.8 0.5 collective-permute-start.11
  37.3 1.9 %collective-permute-done.16.refs_1_ = bf16[8,7168]{1,0:T(8,128)(2,1)S(1)} collective-permute-done((bf16[8,7168]{1,0:T(8,128)(2,1)S(1)}, bf16[8,7168]{1,0:T(8,128)(2,1)S(1)}, u32[]{:S(2)}, u32[]{:S(2)}) %collective-permute-start.16) | collective-permute-done | bytes 114720 | tf_op jit(solution)/shard_map/ppermute | solution.py:210
  39.2 1.5 %collective-permute-start.17 = (bf16[8,7168]{1,0:T(8,128)(2,1)S(1)}, bf16[8,7168]{1,0:T(8,128)(2,1)S(1)}, u32[]{:S(2)}, u32[]{:S(2)}) collective-permute-start(bf16[8,7168]{1,0:T(8,128)(2,1)S(1)} %span_sum.5), channel_id=1, source_target_pairs={{0,4},{2,6},{4,8},{6,10},{8,12},{10,14},{12,0},{14,2},{1,5},{3,7},... | collective-permute-start | bytes 344072 | tf_op jit(solution)/shard_map/ppermute | solution.py:207
  40.7 0.9 %collective-permute-done.14.refs_1_ = bf16[8,7168]{1,0:T(8,128)(2,1)S(1)} collective-permute-done((bf16[8,7168]{1,0:T(8,128)(2,1)S(1)}, bf16[8,7168]{1,0:T(8,128)(2,1)S(1)}, u32[]{:S(2)}, u32[]{:S(2)}) %collective-permute-start.14) | collective-permute-done | bytes 114720 | tf_op jit(solution)/shard_map/ppermute | solution.py:210
  41.7 2.1 %collective-permute-start.15 = (bf16[8,7168]{1,0:T(8,128)(2,1)S(1)}, bf16[8,7168]{1,0:T(8,128)(2,1)S(1)}, u32[]{:S(2)}, u32[]{:S(2)}) collective-permute-start(bf16[8,7168]{1,0:T(8,128)(2,1)S(1)} %span_sum.4), channel_id=1, source_target_pairs={{0,8},{2,10},{4,12},{6,14},{8,0},{10,2},{12,4},{14,6},{1,9},{3,11}... | collective-permute-start | bytes 344072 | tf_op jit(solution)/shard_map/ppermute | solution.py:207
  43.8 0.4 collective-permute-done.12.refs_1_
  44.2 3.1 %collective-permute-start.13 = (bf16[8,7168]{1,0:T(8,128)(2,1)S(1)}, bf16[8,7168]{1,0:T(8,128)(2,1)S(1)}, u32[]{:S(2)}, u32[]{:S(2)}) collective-permute-start(bf16[8,7168]{1,0:T(8,128)(2,1)S(1)} %span_sum.3), channel_id=1, source_target_pairs={{0,12},{2,14},{4,0},{6,2},{8,4},{10,6},{12,8},{14,10},{1,13},{3,15... | collective-permute-start | bytes 344072 | tf_op jit(solution)/shard_map/ppermute | solution.py:207
  47.4 3.6 %collective-permute-done.15.refs_3_ = bf16[8,7168]{1,0:T(8,128)(2,1)S(1)} collective-permute-done((bf16[8,7168]{1,0:T(8,128)(2,1)S(1)}, bf16[8,7168]{1,0:T(8,128)(2,1)S(1)}, u32[]{:S(2)}, u32[]{:S(2)}) %collective-permute-start.15) | collective-permute-done | bytes 114720 | tf_op jit(solution)/shard_map/ppermute | solution.py:207
  51.0 0.8 %combine.1 = bf16[8,7168]{1,0:T(8,128)(2,1)} custom-call(f32[8,512]{1,0:T(8,128)S(1)} %coefficients.1.coeff_ref, f32[8,7168]{1,0:T(8,128)S(1)} %get-tuple-element.21.refs_0_, bf16[8,7168]{1,0:T(8,128)(2,1)S(1)} %collective-permute-done.11.refs_1_, bf16[8,7168]{1,0:T(8,128)(2,1)S(1)} %collective-permute-done.13.refs_2_, ...), custom_call_target="tpu_custom_call" | custom-call | tf_op jit(solution)/shard_map/combine/pallas_call | solution.py:192
  (35 shorter events, 0.6 us)
Async XLA Ops:
  0.0 23.7 %copy-start.1 = (bf16[7168,1024]{1,0:T(8,128)(2,1)S(1)}, bf16[7168,1024]{1,0:T(8,128)(2,1)}, u32[]{:S(2)}) copy-start(bf16[7168,1024]{1,0:T(8,128)(2,1)} %refs_11_.1) | copy-start | bytes 44040196
  0.0 23.7 %copy-start = (bf16[7168,1024]{1,0:T(8,128)(2,1)S(1)}, bf16[7168,1024]{1,0:T(8,128)(2,1)}, u32[]{:S(2)}) copy-start(bf16[7168,1024]{1,0:T(8,128)(2,1)} %refs_10_.1) | copy-start | bytes 44040196
  0.0 1.0 %copy-start.4 = (bf16[8,7168]{1,0:T(8,128)(2,1)S(1)}, bf16[8,7168]{1,0:T(8,128)(2,1)}, u32[]{:S(2)}) copy-start(bf16[8,7168]{1,0:T(8,128)(2,1)} %refs_0_.1) | copy-start | bytes 344068
  1.1 9.2 %collective-permute-start = (bf16[8,7168]{1,0:T(8,128)(2,1)S(1)}, bf16[8,7168]{1,0:T(8,128)(2,1)S(1)}, u32[]{:S(2)}, u32[]{:S(2)}) collective-permute-start(bf16[8,7168]{1,0:T(8,128)(2,1)S(1)} %stack.3.refs_0_), channel_id=1, source_target_pairs={{0,4},{2,6},{4,8},{6,10},{8,12},{10,14},{12,0},{14,2},{1,5},{3,7},... | collective-permute-start | bytes 344072 | tf_op jit(solution)/shard_map/ppermute | solution.py:207
  4.1 10.2 %collective-permute-start.1 = (bf16[8,7168]{1,0:T(8,128)(2,1)S(1)}, bf16[8,7168]{1,0:T(8,128)(2,1)S(1)}, u32[]{:S(2)}, u32[]{:S(2)}) collective-permute-start(bf16[8,7168]{1,0:T(8,128)(2,1)S(1)} %stack.3.refs_0_), channel_id=1, source_target_pairs={{0,8},{2,10},{4,12},{6,14},{8,0},{10,2},{12,4},{14,6},{1,9},{3,11}... | collective-permute-start | bytes 344072 | tf_op jit(solution)/shard_map/ppermute | solution.py:207
  6.7 9.2 %collective-permute-start.2 = (bf16[8,7168]{1,0:T(8,128)(2,1)S(1)}, bf16[8,7168]{1,0:T(8,128)(2,1)S(1)}, u32[]{:S(2)}, u32[]{:S(2)}) collective-permute-start(bf16[8,7168]{1,0:T(8,128)(2,1)S(1)} %stack.3.refs_0_), channel_id=1, source_target_pairs={{0,12},{2,14},{4,0},{6,2},{8,4},{10,6},{12,8},{14,10},{1,13},{3,15... | collective-permute-start | bytes 344072 | tf_op jit(solution)/shard_map/ppermute | solution.py:207
  8.1 8.4 %collective-permute-start.3 = (bf16[8,7168]{1,0:T(8,128)(2,1)S(1)}, bf16[8,7168]{1,0:T(8,128)(2,1)S(1)}, u32[]{:S(2)}, u32[]{:S(2)}) collective-permute-start(bf16[8,7168]{1,0:T(8,128)(2,1)S(1)} %stack.3.refs_0_), channel_id=1, source_target_pairs={{0,2},{2,0},{4,6},{6,4},{8,10},{10,8},{12,14},{14,12},{1,3},{3,1},... | collective-permute-start | bytes 344072 | tf_op jit(solution)/shard_map/ppermute | solution.py:210
  10.2 6.2 %collective-permute-start.4 = (bf16[8,7168]{1,0:T(8,128)(2,1)S(1)}, bf16[8,7168]{1,0:T(8,128)(2,1)S(1)}, u32[]{:S(2)}, u32[]{:S(2)}) collective-permute-start(bf16[8,7168]{1,0:T(8,128)(2,1)S(1)} %collective-permute-done.refs_1_), channel_id=1, source_target_pairs={{0,2},{2,0},{4,6},{6,4},{8,10},{10,8},{12,14},{14,12},{1,3},{3,1},... | collective-permute-start | bytes 344072 | tf_op jit(solution)/shard_map/ppermute | solution.py:210
  14.3 6.0 %collective-permute-start.5 = (bf16[8,7168]{1,0:T(8,128)(2,1)S(1)}, bf16[8,7168]{1,0:T(8,128)(2,1)S(1)}, u32[]{:S(2)}, u32[]{:S(2)}) collective-permute-start(bf16[8,7168]{1,0:T(8,128)(2,1)S(1)} %collective-permute-done.1.refs_2_), channel_id=1, source_target_pairs={{0,2},{2,0},{4,6},{6,4},{8,10},{10,8},{12,14},{14,12},{1,3},{3,1},... | collective-permute-start | bytes 344072 | tf_op jit(solution)/shard_map/ppermute | solution.py:210
  15.9 5.9 %collective-permute-start.6 = (bf16[8,7168]{1,0:T(8,128)(2,1)S(1)}, bf16[8,7168]{1,0:T(8,128)(2,1)S(1)}, u32[]{:S(2)}, u32[]{:S(2)}) collective-permute-start(bf16[8,7168]{1,0:T(8,128)(2,1)S(1)} %collective-permute-done.2.refs_3_), channel_id=1, source_target_pairs={{0,2},{2,0},{4,6},{6,4},{8,10},{10,8},{12,14},{14,12},{1,3},{3,1},... | collective-permute-start | bytes 344072 | tf_op jit(solution)/shard_map/ppermute | solution.py:210
  16.4 5.5 %collective-permute-start.7 = (bf16[32,7168]{1,0:T(8,128)(2,1)S(1)}, bf16[32,7168]{1,0:T(8,128)(2,1)S(1)}, u32[]{:S(2)}, u32[]{:S(2)}) collective-permute-start(bf16[32,7168]{1,0:T(8,128)(2,1)S(1)} %stack.4), channel_id=1, source_target_pairs={{0,1},{1,0},{2,3},{3,2},{4,5},{5,4},{6,7},{7,6},{8,9},{9,8},{10,11... | collective-permute-start | bytes 1376264 | tf_op jit(solution)/shard_map/ppermute | solution.py:213
  21.8 6.4 %slice-start = ((s8[14680064]{0:T(1024)(128)(4,1)}), s8[4194304]{0:T(1024)(128)(4,1)S(1)}, s32[]{:S(2)}) async-start(s8[14680064]{0:T(1024)(128)(4,1)} %bitcast.5), calls=%async_computation | async-start | bytes 8388608
  21.8 6.3 %slice-start.1 = ((s8[14680064]{0:T(1024)(128)(4,1)}), s8[4194304]{0:T(1024)(128)(4,1)S(1)}, s32[]{:S(2)}) async-start(s8[14680064]{0:T(1024)(128)(4,1)} %bitcast.5), calls=%async_computation.1 | async-start | bytes 8388608
  21.8 6.3 %slice-start.2 = ((s8[14680064]{0:T(1024)(128)(4,1)}), s8[4194304]{0:T(1024)(128)(4,1)S(1)}, s32[]{:S(2)}) async-start(s8[14680064]{0:T(1024)(128)(4,1)} %bitcast.5), calls=%async_computation.2 | async-start | bytes 8388608
  21.8 6.3 %slice-start.3 = ((s8[14680064]{0:T(1024)(128)(4,1)}), s8[2097152]{0:T(1024)(128)(4,1)S(1)}, s32[]{:S(2)}) async-start(s8[14680064]{0:T(1024)(128)(4,1)} %bitcast.5), calls=%async_computation.3 | async-start | bytes 4194304
  21.8 1.9 %collective-permute-start.8 = (bf16[32,7168]{1,0:T(8,128)(2,1)S(1)}, bf16[32,7168]{1,0:T(8,128)(2,1)S(1)}, u32[]{:S(2)}, u32[]{:S(2)}) collective-permute-start(bf16[32,7168]{1,0:T(8,128)(2,1)S(1)} %stack.5), channel_id=1, source_target_pairs={{0,1},{1,0},{2,3},{3,2},{4,5},{5,4},{6,7},{7,6},{8,9},{9,8},{10,11... | collective-permute-start | bytes 1376264 | tf_op jit(solution)/shard_map/ppermute | solution.py:213
  29.3 18.0 %copy-start.2 = (s32[8,3]{0,1:T(4,128)S(1)}, s32[8,3]{0,1:T(4,128)}, u32[]{:S(2)}) copy-start(s32[8,3]{0,1:T(4,128)} %param.7) | copy-start | bytes 292
  29.3 18.0 %copy-start.3 = (f32[8,3]{0,1:T(4,128)S(1)}, f32[8,3]{0,1:T(4,128)}, u32[]{:S(2)}) copy-start(f32[8,3]{0,1:T(4,128)} %param.8) | copy-start | bytes 292
  30.5 1.9 %collective-permute-start.10 = (bf16[64,3584]{1,0:T(8,128)(2,1)S(1)}, bf16[64,3584]{1,0:T(8,128)(2,1)S(1)}, u32[]{:S(2)}, u32[]{:S(2)}) collective-permute-start(bf16[64,3584]{1,0:T(8,128)(2,1)S(1)} %get-tuple-element.20), channel_id=1, source_target_pairs={{0,1},{1,0},{2,3},{3,2},{4,5},{5,4},{6,7},{7,6},{8,9},{9,8},{10,11... | collective-permute-start | bytes 1376264 | tf_op jit(solution)/shard_map/ppermute | solution.py:213
  30.6 2.4 %collective-permute-start.9 = (bf16[64,3584]{1,0:T(8,128)(2,1)S(1)}, bf16[64,3584]{1,0:T(8,128)(2,1)S(1)}, u32[]{:S(2)}, u32[]{:S(2)}) collective-permute-start(bf16[64,3584]{1,0:T(8,128)(2,1)S(1)} %get-tuple-element.18), channel_id=1, source_target_pairs={{0,1},{1,0},{2,3},{3,2},{4,5},{5,4},{6,7},{7,6},{8,9},{9,8},{10,11... | collective-permute-start | bytes 1376264 | tf_op jit(solution)/shard_map/ppermute | solution.py:213
  33.2 6.1 %collective-permute-start.16 = (bf16[8,7168]{1,0:T(8,128)(2,1)S(1)}, bf16[8,7168]{1,0:T(8,128)(2,1)S(1)}, u32[]{:S(2)}, u32[]{:S(2)}) collective-permute-start(bf16[8,7168]{1,0:T(8,128)(2,1)S(1)} %get-tuple-element.28), channel_id=1, source_target_pairs={{0,2},{2,0},{4,6},{6,4},{8,10},{10,8},{12,14},{14,12},{1,3},{3,1},... | collective-permute-start | bytes 344072 | tf_op jit(solution)/shard_map/ppermute | solution.py:210
  34.8 6.9 %collective-permute-start.14 = (bf16[8,7168]{1,0:T(8,128)(2,1)S(1)}, bf16[8,7168]{1,0:T(8,128)(2,1)S(1)}, u32[]{:S(2)}, u32[]{:S(2)}) collective-permute-start(bf16[8,7168]{1,0:T(8,128)(2,1)S(1)} %get-tuple-element.26), channel_id=1, source_target_pairs={{0,2},{2,0},{4,6},{6,4},{8,10},{10,8},{12,14},{14,12},{1,3},{3,1},... | collective-permute-start | bytes 344072 | tf_op jit(solution)/shard_map/ppermute | solution.py:210
  35.3 8.9 %collective-permute-start.12 = (bf16[8,7168]{1,0:T(8,128)(2,1)S(1)}, bf16[8,7168]{1,0:T(8,128)(2,1)S(1)}, u32[]{:S(2)}, u32[]{:S(2)}) collective-permute-start(bf16[8,7168]{1,0:T(8,128)(2,1)S(1)} %get-tuple-element.24), channel_id=1, source_target_pairs={{0,2},{2,0},{4,6},{6,4},{8,10},{10,8},{12,14},{14,12},{1,3},{3,1},... | collective-permute-start | bytes 344072 | tf_op jit(solution)/shard_map/ppermute | solution.py:210
  36.8 10.5 %collective-permute-start.11 = (bf16[8,7168]{1,0:T(8,128)(2,1)S(1)}, bf16[8,7168]{1,0:T(8,128)(2,1)S(1)}, u32[]{:S(2)}, u32[]{:S(2)}) collective-permute-start(bf16[8,7168]{1,0:T(8,128)(2,1)S(1)} %get-tuple-element.22), channel_id=1, source_target_pairs={{0,2},{2,0},{4,6},{6,4},{8,10},{10,8},{12,14},{14,12},{1,3},{3,1},... | collective-permute-start | bytes 344072 | tf_op jit(solution)/shard_map/ppermute | solution.py:210
  39.2 8.1 %collective-permute-start.17 = (bf16[8,7168]{1,0:T(8,128)(2,1)S(1)}, bf16[8,7168]{1,0:T(8,128)(2,1)S(1)}, u32[]{:S(2)}, u32[]{:S(2)}) collective-permute-start(bf16[8,7168]{1,0:T(8,128)(2,1)S(1)} %span_sum.5), channel_id=1, source_target_pairs={{0,4},{2,6},{4,8},{6,10},{8,12},{10,14},{12,0},{14,2},{1,5},{3,7},... | collective-permute-start | bytes 344072 | tf_op jit(solution)/shard_map/ppermute | solution.py:207
  41.7 9.3 %collective-permute-start.15 = (bf16[8,7168]{1,0:T(8,128)(2,1)S(1)}, bf16[8,7168]{1,0:T(8,128)(2,1)S(1)}, u32[]{:S(2)}, u32[]{:S(2)}) collective-permute-start(bf16[8,7168]{1,0:T(8,128)(2,1)S(1)} %span_sum.4), channel_id=1, source_target_pairs={{0,8},{2,10},{4,12},{6,14},{8,0},{10,2},{12,4},{14,6},{1,9},{3,11}... | collective-permute-start | bytes 344072 | tf_op jit(solution)/shard_map/ppermute | solution.py:207
  44.2 6.8 %collective-permute-start.13 = (bf16[8,7168]{1,0:T(8,128)(2,1)S(1)}, bf16[8,7168]{1,0:T(8,128)(2,1)S(1)}, u32[]{:S(2)}, u32[]{:S(2)}) collective-permute-start(bf16[8,7168]{1,0:T(8,128)(2,1)S(1)} %span_sum.3), channel_id=1, source_target_pairs={{0,12},{2,14},{4,0},{6,2},{8,4},{10,6},{12,8},{14,10},{1,13},{3,15... | collective-permute-start | bytes 344072 | tf_op jit(solution)/shard_map/ppermute | solution.py:207

commit v5 on v4

v5 whole, which is shorter than its diff:
```python
import functools

import jax
import jax.numpy as jnp
from jax import lax
from jax.experimental import pallas as pl
from jax.experimental.pallas import tpu as pltpu
from jax.sharding import PartitionSpec as P

EXPERTS = 4
LANES = 128
RETURN_ORDER = (2, 3, 1)
N_BLOCK = 256
EXCHANGE_FLOPS = 20_000_000_000
DOWN_FLOPS = 6_000_000_000


def params(mib=8):
    return pltpu.CompilerParams(vmem_limit_bytes=mib * 1024 * 1024)


def cost(flops):
    return pl.CostEstimate(flops=flops, bytes_accessed=0, transcendentals=0)


def block_of(width, most):
    size = most
    while width % size:
        size -= 128
    return size


def in_vmem(value):
    return pltpu.with_memory_space_constraint(value, pltpu.VMEM)


def joined(refs):
    return jnp.concatenate([ref[...].astype(jnp.float32) for ref in refs], axis=0)


def stack_kernel(*refs):
    refs[-1][...] = joined(refs[:-1]).astype(jnp.bfloat16)


def stack(values, flops=0):
    rows = sum(v.shape[0] for v in values)
    return pl.pallas_call(
        stack_kernel,
        out_shape=jax.ShapeDtypeStruct((rows, values[0].shape[1]), jnp.bfloat16),
        compiler_params=params(),
        cost_estimate=cost(flops),
        name="stack",
    )(*values)


def unpacked(refs, out_ref, rows):
    total, width = out_ref.shape
    tail = width // rows
    blocks = (total // rows, rows, tail)
    row = lax.broadcasted_iota(jnp.int32, blocks, 1)
    ends = jnp.zeros(blocks, jnp.float32)
    for i in range(rows - 1):
        piece = joined([ref.at[:, i * tail:(i + 1) * tail] for ref in refs])
        out_ref[:, i * tail:(i + 1) * tail] = piece.astype(jnp.bfloat16)
        ends = jnp.where(row == i, jnp.broadcast_to(piece.reshape(blocks)[:, rows - 1:, :], blocks), ends)
    out_ref[:, width - tail:] = ends.reshape(total, tail).astype(jnp.bfloat16)


def unpack_kernel(rows, *refs):
    unpacked(refs[:-1], refs[-1], rows)


def unpack(values, rows, width):
    total = sum(v.shape[0] for v in values)
    return pl.pallas_call(
        functools.partial(unpack_kernel, rows),
        out_shape=jax.ShapeDtypeStruct((total, width), jnp.bfloat16),
        compiler_params=params(),
        cost_estimate=cost(1_000_000_000),
        name="unpack",
    )(*values)


def gate_up_kernel(n_block, rows, first_ref, *refs):
    rows_in, (gate_ref, up_ref, hidden_ref, rows_ref) = refs[:-4], refs[-4:]
    count = first_ref.shape[0]
    rows_ref[:count, :] = first_ref[...]
    if rows_in:
        unpacked(rows_in, rows_ref.at[count:, :], rows)
    for n in range(0, gate_ref.shape[1], n_block):
        columns = slice(n, n + n_block)
        gate = jnp.dot(rows_ref[...], gate_ref[:, columns], preferred_element_type=jnp.float32)
        up = jnp.dot(rows_ref[...], up_ref[:, columns], preferred_element_type=jnp.float32)
        hidden_ref[:, columns] = (gate / (1.0 + jnp.exp(-gate)) * up).astype(jnp.bfloat16)


def gate_up(first, blocks, gate_weight, up_weight, rows):
    total = sum(r.shape[0] for r in [first] + blocks)
    width, units = gate_weight.shape
    return pl.pallas_call(
        functools.partial(gate_up_kernel, block_of(units, N_BLOCK), rows),
        in_specs=[pl.BlockSpec(memory_space=pltpu.VMEM)] * (len(blocks) + 3),
        out_shape=jax.ShapeDtypeStruct((total, units), jnp.bfloat16),
        scratch_shapes=[pltpu.VMEM((total, width), jnp.bfloat16)],
        compiler_params=params(12),
        cost_estimate=cost(4 * total * width * units),
        name="gate_up",
    )(first, *blocks, in_vmem(gate_weight), in_vmem(up_weight))


def down_kernel(rows, first, pair, hidden_ref, down_ref, *refs):
    if first:
        keep_ref, *send_refs, ends_ref = refs
    else:
        ends_ref, keep_ref, *send_refs = refs
    count, width = keep_ref.shape
    tail = down_ref.shape[1] // rows
    offset = 0 if first else (rows - 1) * tail - width
    blocks = (hidden_ref.shape[0] // rows, rows, tail)
    last = lax.broadcasted_iota(jnp.int32, blocks, 1) == rows - 1
    if first:
        ends_ref[...] = jnp.dot(hidden_ref[...], down_ref[:, (rows - 1) * tail:], preferred_element_type=jnp.float32)
    for c in range(0, width, tail):
        start = offset + c
        value = jnp.dot(hidden_ref[...], down_ref[:, start:start + tail], preferred_element_type=jnp.float32).reshape(blocks)
        i = start // tail
        moved = ends_ref[...].reshape(blocks)[:, i:i + 1, :]
        value = jnp.where(last, jnp.broadcast_to(moved, blocks), value).reshape(blocks[0] * rows, tail)
        columns = slice(c, c + tail)
        keep_ref[:, columns] = value[:count]
        for p, ref in enumerate(send_refs, 1):
            ref[:, columns] = value[p * count:(p + 1) * count].astype(jnp.bfloat16)


def down(hidden, down_weight, ends, pair, rows):
    total, units = hidden.shape
    tail = down_weight.shape[1] // rows
    first = not ends
    width = tail * ((rows - 1) // 2 if first else rows - 1 - (rows - 1) // 2)
    part = total // pair
    return pl.pallas_call(
        functools.partial(down_kernel, rows, first, pair),
        in_specs=[pl.BlockSpec(memory_space=pltpu.VMEM)] * (2 + len(ends)),
        out_shape=[jax.ShapeDtypeStruct((part, width), jnp.float32)]
        + [jax.ShapeDtypeStruct((part, width), jnp.bfloat16)] * (pair - 1)
        + [jax.ShapeDtypeStruct((total, tail), jnp.float32)] * first,
        compiler_params=params(),
        cost_estimate=cost(DOWN_FLOPS),
        name="down",
    )(hidden, in_vmem(down_weight), *ends)


def pair_sum_kernel(chunks, each, *refs):
    ins, outs = refs[:chunks * each], refs[chunks * each:]
    rows = outs[0].shape[0]
    start = 0
    for chunk in range(chunks):
        first, *others = ins[chunk * each:(chunk + 1) * each]
        columns = slice(start, start + first.shape[1])
        start = columns.stop
        for i, ref in enumerate(outs):
            part = slice(i * rows, (i + 1) * rows)
            value = first[part, :]
            for other in others:
                value += other[part, :].astype(jnp.float32)
            ref[:, columns] = value.astype(ref.dtype)


def pair_sum(groups, rows):
    each = len(groups[0])
    count = groups[0][0].shape[0] // rows
    shape = (rows, sum(g[0].shape[1] for g in groups))
    return pl.pallas_call(
        functools.partial(pair_sum_kernel, len(groups), each),
        out_shape=[jax.ShapeDtypeStruct(shape, jnp.float32 if i < EXPERTS else jnp.bfloat16) for i in range(count)],
        compiler_params=params(16),
        name="pair_sum",
    )(*[a for g in groups for a in g])


def span_sum_kernel(*refs):
    value = refs[0][...]
    for ref in refs[1:-1]:
        value += ref[...].astype(jnp.float32)
    refs[-1][...] = value.astype(refs[-1].dtype)


def span_sum(arrays):
    return pl.pallas_call(
        span_sum_kernel,
        out_shape=jax.ShapeDtypeStruct(arrays[0].shape, jnp.bfloat16),
        compiler_params=params(),
        name="span_sum",
    )(*arrays)


def pack_kernel(own_expert, tokens_ref, ids_ref, weights_ref, sides_ref, *packed_refs):
    ids, weights = ids_ref[...], weights_ref[...]
    rows, width = tokens_ref.shape
    tail = width // rows
    square = (rows, rows)
    row, column = lax.broadcasted_iota(jnp.int32, square, 0), lax.broadcasted_iota(jnp.int32, square, 1)
    last = lax.broadcasted_iota(jnp.int32, (rows, tail), 0) == rows - 1
    here = tokens_ref[...].astype(jnp.float32)
    below = pltpu.roll(here, rows - 1, 0)
    for s, packed_ref in enumerate(packed_refs):
        expert = lax.bitwise_xor(own_expert[0], s)
        named = ids == expert
        chosen = jnp.sum(jnp.where(named, weights, 0.0), axis=0, keepdims=True)
        coeff = jnp.sum(jnp.where(row == column, jnp.broadcast_to(chosen, square), 0.0), axis=1, keepdims=True)
        unnamed = 1.0 - jnp.sum(jnp.where(named, 1.0, 0.0), axis=0, keepdims=True)
        shift = jnp.max(jnp.where(column <= row, jnp.broadcast_to(unnamed, square), 0.0), axis=1, keepdims=True)
        sides_ref[:, s * LANES:(s + 1) * LANES] = jnp.broadcast_to(coeff, (rows, LANES))
        sides_ref[:, (EXPERTS + s) * LANES:(EXPERTS + s + 1) * LANES] = jnp.broadcast_to(shift, (rows, LANES))
        kept = jnp.where(shift > 0.5, below, here)
        for i in range(rows - 1):
            moved = jnp.broadcast_to(kept[i:i + 1, width - tail:], (rows, tail))
            piece = jnp.where(last, moved, kept[:, i * tail:(i + 1) * tail])
            packed_ref[:, i * tail:(i + 1) * tail] = piece.astype(jnp.bfloat16)


def pack(own_expert, tokens, ids, weights):
    rows, width = tokens.shape
    packed = jax.ShapeDtypeStruct((rows, width - width // rows), jnp.bfloat16)
    return pl.pallas_call(
        pack_kernel,
        in_specs=[pl.BlockSpec(memory_space=pltpu.SMEM)] + [pl.BlockSpec(memory_space=pltpu.VMEM)] * 3,
        out_shape=[jax.ShapeDtypeStruct((rows, 2 * EXPERTS * LANES), jnp.float32)] + [packed] * EXPERTS,
        compiler_params=params(),
        cost_estimate=cost(EXCHANGE_FLOPS),
        name="pack",
    )(own_expert, tokens, ids.T, weights.T)


def combine_kernel(own_count, sides_ref, *refs):
    out_ref = refs[-1]
    rows, width = out_ref.shape
    tail = width // rows
    own = refs[0][...]
    for ref in refs[1:own_count]:
        own += ref[...].astype(jnp.float32)
    row = lax.broadcasted_iota(jnp.int32, (rows, tail), 0)
    parts = []
    others = [ref[...].astype(jnp.float32) for ref in refs[own_count:-1]]
    for s, packed in zip((0,) + RETURN_ORDER, [own] + others):
        coeff = sides_ref[:, s * LANES:s * LANES + 1]
        shifted = sides_ref[:, (EXPERTS + s) * LANES:(EXPERTS + s) * LANES + 1] > 0.5
        ends = jnp.zeros((rows, tail), jnp.float32)
        for i in range(rows - 1):
            ends = jnp.where(row == i, jnp.broadcast_to(packed[rows - 1:, i * tail:(i + 1) * tail], (rows, tail)), ends)
        whole = jnp.concatenate([packed, ends], axis=1)
        parts.append(coeff * jnp.where(shifted, pltpu.roll(whole, 1, 0), whole))
    out_ref[...] = sum(parts[1:], parts[0]).astype(jnp.bfloat16)


def combine(sides, own, others, width):
    return pl.pallas_call(
        functools.partial(combine_kernel, len(own)),
        out_shape=jax.ShapeDtypeStruct((own[0].shape[0], width), jnp.bfloat16),
        compiler_params=params(),
        name="combine",
    )(sides, *own, *others)


def local(tokens, expert_ids, route_weights, gate_weight, up_weight, down_weight):
    rows, width = tokens.shape
    attn = lax.axis_size("attn")
    pair = lax.axis_size("ffn")
    span = attn // EXPERTS

    def over_experts(value, other):
        return lax.ppermute(value, "attn", [(i, (i // span ^ other) * span + i % span) for i in range(attn)])

    def over_span(value, shift):
        return lax.ppermute(value, "attn", [(i, i // span * span + (i + shift) % span) for i in range(attn)])

    def over_pair(value, shift):
        return lax.ppermute(value, "ffn", [(i, (i + shift) % pair) for i in range(pair)])

    own_expert = (lax.axis_index("attn") // span).astype(jnp.int32).reshape(1)
    sides, *packed = pack(own_expert, tokens, expert_ids, route_weights)
    column = packed[:1] + [over_experts(packed[s], s) for s in range(1, EXPERTS)]
    plane, groups = list(column), [stack(column)]
    for t in range(1, span):
        blocks = [over_span(b, t) for b in column]
        plane += blocks
        groups.append(stack(blocks))
    others = [over_pair(g, p) for p in range(1, pair) for g in groups]
    hidden = gate_up(unpack(plane, rows, width), others, gate_weight, up_weight, rows)

    halves, ends = [], []
    for _ in range(2):
        keep, *sends = down(hidden, down_weight, ends, pair, rows)
        if not ends:
            ends = [sends.pop()]
        halves.append([keep] + [over_pair(b, -p) for p, b in enumerate(sends, 1)])
    blocks = pair_sum(halves, rows)
    sums = [[blocks[s]] + [over_span(blocks[t * EXPERTS + s], -t) for t in range(1, span)] for s in range(EXPERTS)]
    returned = [over_experts(span_sum(sums[s]), s) for s in RETURN_ORDER]
    return combine(sides, sums[0], returned, width)


def solution(mesh):
    return jax.shard_map(
        local,
        mesh=mesh,
        in_specs=(
            P(("groups", "attn", "ffn"), None),
            P(("groups", "attn", "ffn"), None),
            P(("groups", "attn", "ffn"), None),
            P(None, ("attn", "ffn")),
            P(None, ("attn", "ffn")),
            P(("attn", "ffn"), None),
        ),
        out_specs=P(("groups", "attn", "ffn"), None),
        check_vma=False,
    )
```

time: 51.9 us -> 52.5 us (1.012)
  starting transfers between devices: 23.8 us -> 18.4 us
  waiting for transfers between devices: 18.8 us -> 21.6 us
  local copies, waits for them, and re-layouts: 1.09 us -> 3.26 us
  Pallas kernels: 7.86 us -> 8.86 us
    ppermute x6, waiting for transfers between devices: 6.55 us -> 11 us  [over_experts(): lax.ppermute(value, 'attn', [(i, (i // span ^ other) * span + i % span) f...]
    ppermute x6, starting transfers between devices: 13.7 us -> 9.47 us  [over_experts(): lax.ppermute(value, 'attn', [(i, (i // span ^ other) * span + i % span) f...]
    unnamed x18 -> x30, local copies, waits for them, and re-layouts: 1.09 us -> 3.26 us
    ppermute x8, starting transfers between devices: 9.43 us -> 8.19 us  [over_span(): lax.ppermute(value, 'attn', [(i, i // span * span + (i + shift) % span) f...]
    ppermute x8, waiting for transfers between devices: 8.49 us -> 7.39 us  [over_span(): lax.ppermute(value, 'attn', [(i, i // span * span + (i + shift) % span) f...]
    pallas_call x3 -> x4, Pallas kernels: 2.36 us -> 3.16 us  [the longest x2 2.71 us: down(): pl.pallas_call(functools.partial(down_kernel, rows, first, pair), in_spec...]
  transfers between devices with their start and end apart: 18 -> 18, of which waited for: 11 -> 10; matrix products, arithmetic and copies ran while one was open for 0% -> 0% of each run, Pallas kernels for 0% -> 1%
where the time goes in v5:
time: 52.5 us; the launch traced here: 52.3 us
  waiting for transfers between devices  21.6 us (41%)
  starting transfers between devices  18.4 us (35%)
  Pallas kernels  8.86 us (17%)
  local copies, waits for them, and re-layouts  3.26 us (6%)
    ppermute x6, waiting for transfers between devices, over_experts(): lax.ppermute(value, 'attn', [(i, (i // span ^ other) * span + i % span) f...  11 us
    ppermute x6, starting transfers between devices, over_experts(): lax.ppermute(value, 'attn', [(i, (i // span ^ other) * span + i % span) f...  9.47 us
    ppermute x8, starting transfers between devices, over_span(): lax.ppermute(value, 'attn', [(i, i // span * span + (i + shift) % span) f...  8.19 us
    ppermute x8, waiting for transfers between devices, over_span(): lax.ppermute(value, 'attn', [(i, i // span * span + (i + shift) % span) f...  7.39 us
    pallas_call x1, Pallas kernels, gate_up(): pl.pallas_call(functools.partial(gate_up_kernel, block_of(units, N_BLOCK)...  4.52 us
    unnamed x30, local copies, waits for them, and re-layouts  3.26 us
    ppermute x4, waiting for transfers between devices, over_pair(): lax.ppermute(value, 'ffn', [(i, (i + shift) % pair) for i in range(pair)])  3.23 us
    pallas_call x2, Pallas kernels, down(): pl.pallas_call(functools.partial(down_kernel, rows, first, pair), in_spec...  2.71 us
  transfers between devices with their start and end apart: 18, of which 10 were waited for; matrix products, arithmetic and copies ran while one was open for 0% of the time, Pallas kernels for 1%

profile of v5, /device:TPU:0, one launch (start us, length us, event | category | flops | bytes accessed | tf_op | source)
XLA Modules:
  0.0 52.3 jit_solution(1293168709889295570)
XLA Ops:
  0.0 1.0 %copy-done = bf16[8,7168]{1,0:T(8,128)(2,1)S(1)} copy-done((bf16[8,7168]{1,0:T(8,128)(2,1)S(1)}, bf16[8,7168]{1,0:T(8,128)(2,1)}, u32[]{:S(2)}) %copy-start) | copy-done | bytes 114712
  1.1 1.2 %copy-done.1 = s32[8,3]{0,1:T(4,128)S(1)} copy-done((s32[8,3]{0,1:T(4,128)S(1)}, s32[8,3]{0,1:T(4,128)}, u32[]{:S(2)}) %copy-start.1) | copy-done | bytes 120
  2.3 1.0 %copy-done.2 = f32[8,3]{0,1:T(4,128)S(1)} copy-done((f32[8,3]{0,1:T(4,128)S(1)}, f32[8,3]{0,1:T(4,128)}, u32[]{:S(2)}) %copy-start.2) | copy-done | bytes 120
  3.2 0.2 pack.1
  3.5 3.1 %collective-permute-start = (bf16[8,6272]{1,0:T(8,128)(2,1)S(1)}, bf16[8,6272]{1,0:T(8,128)(2,1)S(1)}, u32[]{:S(2)}, u32[]{:S(2)}) collective-permute-start(bf16[8,6272]{1,0:T(8,128)(2,1)S(1)} %get-tuple-element.25), channel_id=1, source_target_pairs={{0,4},{2,6},{4,0},{6,2},{8,12},{10,14},{12,8},{14,10},{1,5},{3,7},... | collective-permute-start | bytes 301064 | tf_op jit(solution)/shard_map/ppermute | solution.py:272
  6.6 2.6 %collective-permute-start.1 = (bf16[8,6272]{1,0:T(8,128)(2,1)S(1)}, bf16[8,6272]{1,0:T(8,128)(2,1)S(1)}, u32[]{:S(2)}, u32[]{:S(2)}) collective-permute-start(bf16[8,6272]{1,0:T(8,128)(2,1)S(1)} %get-tuple-element.26), channel_id=1, source_target_pairs={{0,8},{2,10},{4,12},{6,14},{8,0},{10,2},{12,4},{14,6},{1,9},{3,11}... | collective-permute-start | bytes 301064 | tf_op jit(solution)/shard_map/ppermute | solution.py:272
  9.1 1.7 %collective-permute-start.3 = (bf16[8,6272]{1,0:T(8,128)(2,1)S(1)}, bf16[8,6272]{1,0:T(8,128)(2,1)S(1)}, u32[]{:S(2)}, u32[]{:S(2)}) collective-permute-start(bf16[8,6272]{1,0:T(8,128)(2,1)S(1)} %get-tuple-element.24.refs_0_), channel_id=1, source_target_pairs={{0,2},{2,0},{4,6},{6,4},{8,10},{10,8},{12,14},{14,12},{1,3},{3,1},... | collective-permute-start | bytes 301064 | tf_op jit(solution)/shard_map/ppermute | solution.py:275
  10.9 0.3 collective-permute-start.4
  11.2 6.0 %collective-permute-done.1.refs_2_ = bf16[8,6272]{1,0:T(8,128)(2,1)S(1)} collective-permute-done((bf16[8,6272]{1,0:T(8,128)(2,1)S(1)}, bf16[8,6272]{1,0:T(8,128)(2,1)S(1)}, u32[]{:S(2)}, u32[]{:S(2)}) %collective-permute-start.1) | collective-permute-done | bytes 100384 | tf_op jit(solution)/shard_map/ppermute | solution.py:272
  17.1 1.5 %collective-permute-start.5 = (bf16[8,6272]{1,0:T(8,128)(2,1)S(1)}, bf16[8,6272]{1,0:T(8,128)(2,1)S(1)}, u32[]{:S(2)}, u32[]{:S(2)}) collective-permute-start(bf16[8,6272]{1,0:T(8,128)(2,1)S(1)} %collective-permute-done.1.refs_2_), channel_id=1, source_target_pairs={{0,2},{2,0},{4,6},{6,4},{8,10},{10,8},{12,14},{14,12},{1,3},{3,1},... | collective-permute-start | bytes 301064 | tf_op jit(solution)/shard_map/ppermute | solution.py:275
  18.6 0.5 collective-permute-start.6
  19.3 2.5 %collective-permute-done.5.refs_6_.refs_2_ = bf16[8,6272]{1,0:T(8,128)(2,1)S(1)} collective-permute-done((bf16[8,6272]{1,0:T(8,128)(2,1)S(1)}, bf16[8,6272]{1,0:T(8,128)(2,1)S(1)}, u32[]{:S(2)}, u32[]{:S(2)}) %collective-permute-start.5) | collective-permute-done | bytes 100384 | tf_op jit(solution)/shard_map/ppermute | solution.py:275
  21.8 1.5 %collective-permute-done.6.refs_7_.refs_3_ = bf16[8,6272]{1,0:T(8,128)(2,1)S(1)} collective-permute-done((bf16[8,6272]{1,0:T(8,128)(2,1)S(1)}, bf16[8,6272]{1,0:T(8,128)(2,1)S(1)}, u32[]{:S(2)}, u32[]{:S(2)}) %collective-permute-start.6) | collective-permute-done | bytes 100384 | tf_op jit(solution)/shard_map/ppermute | solution.py:275
  23.4 0.2 unpack.1.first_ref
  23.7 1.4 %collective-permute-done.8.refs_1_ = bf16[32,6272]{1,0:T(8,128)(2,1)S(1)} collective-permute-done((bf16[32,6272]{1,0:T(8,128)(2,1)S(1)}, bf16[32,6272]{1,0:T(8,128)(2,1)S(1)}, u32[]{:S(2)}, u32[]{:S(2)}) %collective-permute-start.8) | collective-permute-done | bytes 401440 | tf_op jit(solution)/shard_map/ppermute | solution.py:278
  25.2 4.5 %gate_up.1.hidden_ref = bf16[128,1024]{1,0:T(8,128)(2,1)S(1)} custom-call(bf16[64,7168]{1,0:T(8,128)(2,1)S(1)} %unpack.1.first_ref, bf16[32,6272]{1,0:T(8,128)(2,1)S(1)} %collective-permute-done.7.refs_0_, bf16[32,6272]{1,0:T(8,128)(2,1)S(1)} %collective-permute-done.8.refs_1_, bf16[7168,1024]{1,0:T(8,128)(2,1)S(1)} %bitcast.4, bf16[7168,1024]{1,0:T(8,128)(2,1)S(1)} %bitcast.6), custom_call_target="tpu_custom_call" | custom-call | flops 3758096384 | tf_op jit(solution)/shard_map/gate_up/pallas_call | solution.py:100
  29.8 1.3 %down.2 = (f32[64,2688]{1,0:T(8,128)S(1)}, bf16[64,2688]{1,0:T(8,128)(2,1)S(1)}, f32[128,896]{1,0:T(8,128)S(1)}) custom-call(bf16[128,1024]{1,0:T(8,128)(2,1)S(1)} %gate_up.1.hidden_ref, bf16[1024,7168]{1,0:T(8,128)(2,1)S(1)} %bitcast.8), custom_call_target="tpu_custom_call" | custom-call | flops 6000000000 | tf_op jit(solution)/shard_map/down/pallas_call | solution.py:141
  31.1 1.4 %down.3 = (f32[64,3584]{1,0:T(8,128)S(1)}, bf16[64,3584]{1,0:T(8,128)(2,1)S(1)}) custom-call(bf16[128,1024]{1,0:T(8,128)(2,1)S(1)} %gate_up.1.hidden_ref, bf16[1024,7168]{1,0:T(8,128)(2,1)S(1)} %bitcast.8, f32[128,896]{1,0:T(8,128)S(1)} %get-tuple-element.30.refs_0_), custom_call_target="tpu_custom_call" | custom-call | flops 6000000000 | tf_op jit(solution)/shard_map/down/pallas_call | solution.py:141
  32.7 0.4 collective-permute-start.9
  33.1 1.8 %collective-permute-done.9.refs_1_ = bf16[64,2688]{1,0:T(8,128)(2,1)S(1)} collective-permute-done((bf16[64,2688]{1,0:T(8,128)(2,1)S(1)}, bf16[64,2688]{1,0:T(8,128)(2,1)S(1)}, u32[]{:S(2)}, u32[]{:S(2)}) %collective-permute-start.9) | collective-permute-done | bytes 344096 | tf_op jit(solution)/shard_map/ppermute | solution.py:278
  35.0 1.1 %collective-permute-start.12 = (bf16[8,6272]{1,0:T(8,128)(2,1)S(1)}, bf16[8,6272]{1,0:T(8,128)(2,1)S(1)}, u32[]{:S(2)}, u32[]{:S(2)}) collective-permute-start(bf16[8,6272]{1,0:T(8,128)(2,1)S(1)} %get-tuple-element.36), channel_id=1, source_target_pairs={{0,2},{2,0},{4,6},{6,4},{8,10},{10,8},{12,14},{14,12},{1,3},{3,1},... | collective-permute-start | bytes 301064 | tf_op jit(solution)/shard_map/ppermute | solution.py:275
  36.1 1.0 %collective-permute-start.14 = (bf16[8,6272]{1,0:T(8,128)(2,1)S(1)}, bf16[8,6272]{1,0:T(8,128)(2,1)S(1)}, u32[]{:S(2)}, u32[]{:S(2)}) collective-permute-start(bf16[8,6272]{1,0:T(8,128)(2,1)S(1)} %get-tuple-element.38), channel_id=1, source_target_pairs={{0,2},{2,0},{4,6},{6,4},{8,10},{10,8},{12,14},{14,12},{1,3},{3,1},... | collective-permute-start | bytes 301064 | tf_op jit(solution)/shard_map/ppermute | solution.py:275
  37.1 1.1 %collective-permute-start.16 = (bf16[8,6272]{1,0:T(8,128)(2,1)S(1)}, bf16[8,6272]{1,0:T(8,128)(2,1)S(1)}, u32[]{:S(2)}, u32[]{:S(2)}) collective-permute-start(bf16[8,6272]{1,0:T(8,128)(2,1)S(1)} %get-tuple-element.40), channel_id=1, source_target_pairs={{0,2},{2,0},{4,6},{6,4},{8,10},{10,8},{12,14},{14,12},{1,3},{3,1},... | collective-permute-start | bytes 301064 | tf_op jit(solution)/shard_map/ppermute | solution.py:275
  38.2 1.0 %collective-permute-start.11 = (bf16[8,6272]{1,0:T(8,128)(2,1)S(1)}, bf16[8,6272]{1,0:T(8,128)(2,1)S(1)}, u32[]{:S(2)}, u32[]{:S(2)}) collective-permute-start(bf16[8,6272]{1,0:T(8,128)(2,1)S(1)} %get-tuple-element.34), channel_id=1, source_target_pairs={{0,2},{2,0},{4,6},{6,4},{8,10},{10,8},{12,14},{14,12},{1,3},{3,1},... | collective-permute-start | bytes 301064 | tf_op jit(solution)/shard_map/ppermute | solution.py:275
  39.1 1.6 %collective-permute-done.12.refs_1_ = bf16[8,6272]{1,0:T(8,128)(2,1)S(1)} collective-permute-done((bf16[8,6272]{1,0:T(8,128)(2,1)S(1)}, bf16[8,6272]{1,0:T(8,128)(2,1)S(1)}, u32[]{:S(2)}, u32[]{:S(2)}) %collective-permute-start.12) | collective-permute-done | bytes 100384 | tf_op jit(solution)/shard_map/ppermute | solution.py:275
  40.8 1.2 %collective-permute-start.13 = (bf16[8,6272]{1,0:T(8,128)(2,1)S(1)}, bf16[8,6272]{1,0:T(8,128)(2,1)S(1)}, u32[]{:S(2)}, u32[]{:S(2)}) collective-permute-start(bf16[8,6272]{1,0:T(8,128)(2,1)S(1)} %span_sum.3), channel_id=1, source_target_pairs={{0,8},{2,10},{4,12},{6,14},{8,0},{10,2},{12,4},{14,6},{1,9},{3,11}... | collective-permute-start | bytes 301064 | tf_op jit(solution)/shard_map/ppermute | solution.py:272
  42.0 0.9 %collective-permute-done.14.refs_1_ = bf16[8,6272]{1,0:T(8,128)(2,1)S(1)} collective-permute-done((bf16[8,6272]{1,0:T(8,128)(2,1)S(1)}, bf16[8,6272]{1,0:T(8,128)(2,1)S(1)}, u32[]{:S(2)}, u32[]{:S(2)}) %collective-permute-start.14) | collective-permute-done | bytes 100384 | tf_op jit(solution)/shard_map/ppermute | solution.py:275
  42.9 2.5 %collective-permute-start.15 = (bf16[8,6272]{1,0:T(8,128)(2,1)S(1)}, bf16[8,6272]{1,0:T(8,128)(2,1)S(1)}, u32[]{:S(2)}, u32[]{:S(2)}) collective-permute-start(bf16[8,6272]{1,0:T(8,128)(2,1)S(1)} %span_sum.4), channel_id=1, source_target_pairs={{0,12},{2,14},{4,8},{6,10},{8,4},{10,6},{12,0},{14,2},{1,13},{3,15... | collective-permute-start | bytes 301064 | tf_op jit(solution)/shard_map/ppermute | solution.py:272
  45.6 0.8 %collective-permute-done.11.refs_1_ = bf16[8,6272]{1,0:T(8,128)(2,1)S(1)} collective-permute-done((bf16[8,6272]{1,0:T(8,128)(2,1)S(1)}, bf16[8,6272]{1,0:T(8,128)(2,1)S(1)}, u32[]{:S(2)}, u32[]{:S(2)}) %collective-permute-start.11) | collective-permute-done | bytes 100384 | tf_op jit(solution)/shard_map/ppermute | solution.py:275
  46.4 3.8 %collective-permute-done.13.refs_2_ = bf16[8,6272]{1,0:T(8,128)(2,1)S(1)} collective-permute-done((bf16[8,6272]{1,0:T(8,128)(2,1)S(1)}, bf16[8,6272]{1,0:T(8,128)(2,1)S(1)}, u32[]{:S(2)}, u32[]{:S(2)}) %collective-permute-start.13) | collective-permute-done | bytes 100384 | tf_op jit(solution)/shard_map/ppermute | solution.py:272
  50.2 1.2 %collective-permute-done.17.refs_4_ = bf16[8,6272]{1,0:T(8,128)(2,1)S(1)} collective-permute-done((bf16[8,6272]{1,0:T(8,128)(2,1)S(1)}, bf16[8,6272]{1,0:T(8,128)(2,1)S(1)}, u32[]{:S(2)}, u32[]{:S(2)}) %collective-permute-start.17) | collective-permute-done | bytes 100384 | tf_op jit(solution)/shard_map/ppermute | solution.py:272
  51.4 0.9 %combine.1 = bf16[8,7168]{1,0:T(8,128)(2,1)} custom-call(f32[8,1024]{1,0:T(8,128)S(1)} %get-tuple-element.23.sides_ref, f32[8,6272]{1,0:T(8,128)S(1)} %get-tuple-element.33.refs_0_, bf16[8,6272]{1,0:T(8,128)(2,1)S(1)} %collective-permute-done.11.refs_1_, bf16[8,6272]{1,0:T(8,128)(2,1)S(1)} %collective-permute-done.13.refs_2_, ...), custom_call_target="tpu_custom_call" | custom-call | tf_op jit(solution)/shard_map/combine/pallas_call | solution.py:257
  (49 shorter events, 0.8 us)
Async XLA Ops:
  0.0 25.1 %slice-start = ((s8[14680064]{0:T(1024)(128)(4,1)}), s8[4194304]{0:T(1024)(128)(4,1)S(1)}, s32[]{:S(2)}) async-start(s8[14680064]{0:T(1024)(128)(4,1)} %bitcast.3), calls=%async_computation | async-start | bytes 8388608
  0.0 25.1 %slice-start.4 = ((s8[14680064]{0:T(1024)(128)(4,1)}), s8[4194304]{0:T(1024)(128)(4,1)S(1)}, s32[]{:S(2)}) async-start(s8[14680064]{0:T(1024)(128)(4,1)} %bitcast.5), calls=%async_computation.4 | async-start | bytes 8388608
  0.0 1.0 %copy-start = (bf16[8,7168]{1,0:T(8,128)(2,1)S(1)}, bf16[8,7168]{1,0:T(8,128)(2,1)}, u32[]{:S(2)}) copy-start(bf16[8,7168]{1,0:T(8,128)(2,1)} %tokens_ref.1) | copy-start | bytes 344068
  1.1 1.2 %copy-start.1 = (s32[8,3]{0,1:T(4,128)S(1)}, s32[8,3]{0,1:T(4,128)}, u32[]{:S(2)}) copy-start(s32[8,3]{0,1:T(4,128)} %param.7) | copy-start | bytes 292
  3.2 21.9 %slice-start.1 = ((s8[14680064]{0:T(1024)(128)(4,1)}), s8[4194304]{0:T(1024)(128)(4,1)S(1)}, s32[]{:S(2)}) async-start(s8[14680064]{0:T(1024)(128)(4,1)} %bitcast.3), calls=%async_computation.1 | async-start | bytes 8388608
  3.2 21.9 %slice-start.2 = ((s8[14680064]{0:T(1024)(128)(4,1)}), s8[4194304]{0:T(1024)(128)(4,1)S(1)}, s32[]{:S(2)}) async-start(s8[14680064]{0:T(1024)(128)(4,1)} %bitcast.3), calls=%async_computation.2 | async-start | bytes 8388608
  3.2 21.9 %slice-start.3 = ((s8[14680064]{0:T(1024)(128)(4,1)}), s8[2097152]{0:T(1024)(128)(4,1)S(1)}, s32[]{:S(2)}) async-start(s8[14680064]{0:T(1024)(128)(4,1)} %bitcast.3), calls=%async_computation.3 | async-start | bytes 4194304
  3.2 21.9 %slice-start.5 = ((s8[14680064]{0:T(1024)(128)(4,1)}), s8[4194304]{0:T(1024)(128)(4,1)S(1)}, s32[]{:S(2)}) async-start(s8[14680064]{0:T(1024)(128)(4,1)} %bitcast.5), calls=%async_computation.5 | async-start | bytes 8388608
  3.2 21.9 %slice-start.6 = ((s8[14680064]{0:T(1024)(128)(4,1)}), s8[4194304]{0:T(1024)(128)(4,1)S(1)}, s32[]{:S(2)}) async-start(s8[14680064]{0:T(1024)(128)(4,1)} %bitcast.5), calls=%async_computation.6 | async-start | bytes 8388608
  3.2 21.9 %slice-start.7 = ((s8[14680064]{0:T(1024)(128)(4,1)}), s8[2097152]{0:T(1024)(128)(4,1)S(1)}, s32[]{:S(2)}) async-start(s8[14680064]{0:T(1024)(128)(4,1)} %bitcast.5), calls=%async_computation.7 | async-start | bytes 4194304
  3.5 7.4 %collective-permute-start = (bf16[8,6272]{1,0:T(8,128)(2,1)S(1)}, bf16[8,6272]{1,0:T(8,128)(2,1)S(1)}, u32[]{:S(2)}, u32[]{:S(2)}) collective-permute-start(bf16[8,6272]{1,0:T(8,128)(2,1)S(1)} %get-tuple-element.25), channel_id=1, source_target_pairs={{0,4},{2,6},{4,0},{6,2},{8,12},{10,14},{12,8},{14,10},{1,5},{3,7},... | collective-permute-start | bytes 301064 | tf_op jit(solution)/shard_map/ppermute | solution.py:272
  6.6 10.6 %collective-permute-start.1 = (bf16[8,6272]{1,0:T(8,128)(2,1)S(1)}, bf16[8,6272]{1,0:T(8,128)(2,1)S(1)}, u32[]{:S(2)}, u32[]{:S(2)}) collective-permute-start(bf16[8,6272]{1,0:T(8,128)(2,1)S(1)} %get-tuple-element.26), channel_id=1, source_target_pairs={{0,8},{2,10},{4,12},{6,14},{8,0},{10,2},{12,4},{14,6},{1,9},{3,11}... | collective-permute-start | bytes 301064 | tf_op jit(solution)/shard_map/ppermute | solution.py:272
  9.1 9.5 %collective-permute-start.2 = (bf16[8,6272]{1,0:T(8,128)(2,1)S(1)}, bf16[8,6272]{1,0:T(8,128)(2,1)S(1)}, u32[]{:S(2)}, u32[]{:S(2)}) collective-permute-start(bf16[8,6272]{1,0:T(8,128)(2,1)S(1)} %get-tuple-element.27), channel_id=1, source_target_pairs={{0,12},{2,14},{4,8},{6,10},{8,4},{10,6},{12,0},{14,2},{1,13},{3,15... | collective-permute-start | bytes 301064 | tf_op jit(solution)/shard_map/ppermute | solution.py:272
  9.1 10.1 %collective-permute-start.3 = (bf16[8,6272]{1,0:T(8,128)(2,1)S(1)}, bf16[8,6272]{1,0:T(8,128)(2,1)S(1)}, u32[]{:S(2)}, u32[]{:S(2)}) collective-permute-start(bf16[8,6272]{1,0:T(8,128)(2,1)S(1)} %get-tuple-element.24.refs_0_), channel_id=1, source_target_pairs={{0,2},{2,0},{4,6},{6,4},{8,10},{10,8},{12,14},{14,12},{1,3},{3,1},... | collective-permute-start | bytes 301064 | tf_op jit(solution)/shard_map/ppermute | solution.py:275
  10.9 8.4 %collective-permute-start.4 = (bf16[8,6272]{1,0:T(8,128)(2,1)S(1)}, bf16[8,6272]{1,0:T(8,128)(2,1)S(1)}, u32[]{:S(2)}, u32[]{:S(2)}) collective-permute-start(bf16[8,6272]{1,0:T(8,128)(2,1)S(1)} %collective-permute-done.refs_1_), channel_id=1, source_target_pairs={{0,2},{2,0},{4,6},{6,4},{8,10},{10,8},{12,14},{14,12},{1,3},{3,1},... | collective-permute-start | bytes 301064 | tf_op jit(solution)/shard_map/ppermute | solution.py:275
  17.1 4.6 %collective-permute-start.5 = (bf16[8,6272]{1,0:T(8,128)(2,1)S(1)}, bf16[8,6272]{1,0:T(8,128)(2,1)S(1)}, u32[]{:S(2)}, u32[]{:S(2)}) collective-permute-start(bf16[8,6272]{1,0:T(8,128)(2,1)S(1)} %collective-permute-done.1.refs_2_), channel_id=1, source_target_pairs={{0,2},{2,0},{4,6},{6,4},{8,10},{10,8},{12,14},{14,12},{1,3},{3,1},... | collective-permute-start | bytes 301064 | tf_op jit(solution)/shard_map/ppermute | solution.py:275
  18.6 4.6 %collective-permute-start.6 = (bf16[8,6272]{1,0:T(8,128)(2,1)S(1)}, bf16[8,6272]{1,0:T(8,128)(2,1)S(1)}, u32[]{:S(2)}, u32[]{:S(2)}) collective-permute-start(bf16[8,6272]{1,0:T(8,128)(2,1)S(1)} %collective-permute-done.2.refs_3_), channel_id=1, source_target_pairs={{0,2},{2,0},{4,6},{6,4},{8,10},{10,8},{12,14},{14,12},{1,3},{3,1},... | collective-permute-start | bytes 301064 | tf_op jit(solution)/shard_map/ppermute | solution.py:275
  19.2 4.5 %collective-permute-start.7 = (bf16[32,6272]{1,0:T(8,128)(2,1)S(1)}, bf16[32,6272]{1,0:T(8,128)(2,1)S(1)}, u32[]{:S(2)}, u32[]{:S(2)}) collective-permute-start(bf16[32,6272]{1,0:T(8,128)(2,1)S(1)} %stack.2), channel_id=1, source_target_pairs={{0,1},{1,0},{2,3},{3,2},{4,5},{5,4},{6,7},{7,6},{8,9},{9,8},{10,11... | collective-permute-start | bytes 1204232 | tf_op jit(solution)/shard_map/ppermute | solution.py:278
  23.3 1.8 %collective-permute-start.8 = (bf16[32,6272]{1,0:T(8,128)(2,1)S(1)}, bf16[32,6272]{1,0:T(8,128)(2,1)S(1)}, u32[]{:S(2)}, u32[]{:S(2)}) collective-permute-start(bf16[32,6272]{1,0:T(8,128)(2,1)S(1)} %stack.3), channel_id=1, source_target_pairs={{0,1},{1,0},{2,3},{3,2},{4,5},{5,4},{6,7},{7,6},{8,9},{9,8},{10,11... | collective-permute-start | bytes 1204232 | tf_op jit(solution)/shard_map/ppermute | solution.py:278
  23.4 6.3 %slice-start.8 = ((s8[14680064]{0:T(1024)(128)(4,1)}), s8[4194304]{0:T(1024)(128)(4,1)S(1)}, s32[]{:S(2)}) async-start(s8[14680064]{0:T(1024)(128)(4,1)} %bitcast.7), calls=%async_computation.8 | async-start | bytes 8388608
  23.6 6.1 %slice-start.9 = ((s8[14680064]{0:T(1024)(128)(4,1)}), s8[4194304]{0:T(1024)(128)(4,1)S(1)}, s32[]{:S(2)}) async-start(s8[14680064]{0:T(1024)(128)(4,1)} %bitcast.7), calls=%async_computation.9 | async-start | bytes 8388608
  23.7 6.1 %slice-start.10 = ((s8[14680064]{0:T(1024)(128)(4,1)}), s8[4194304]{0:T(1024)(128)(4,1)S(1)}, s32[]{:S(2)}) async-start(s8[14680064]{0:T(1024)(128)(4,1)} %bitcast.7), calls=%async_computation.10 | async-start | bytes 8388608
  23.7 6.1 %slice-start.11 = ((s8[14680064]{0:T(1024)(128)(4,1)}), s8[2097152]{0:T(1024)(128)(4,1)S(1)}, s32[]{:S(2)}) async-start(s8[14680064]{0:T(1024)(128)(4,1)} %bitcast.7), calls=%async_computation.11 | async-start | bytes 4194304
  32.5 2.4 %collective-permute-start.10 = (bf16[64,3584]{1,0:T(8,128)(2,1)S(1)}, bf16[64,3584]{1,0:T(8,128)(2,1)S(1)}, u32[]{:S(2)}, u32[]{:S(2)}) collective-permute-start(bf16[64,3584]{1,0:T(8,128)(2,1)S(1)} %get-tuple-element.32), channel_id=1, source_target_pairs={{0,1},{1,0},{2,3},{3,2},{4,5},{5,4},{6,7},{7,6},{8,9},{9,8},{10,11... | collective-permute-start | bytes 1376264 | tf_op jit(solution)/shard_map/ppermute | solution.py:278
  32.7 2.2 %collective-permute-start.9 = (bf16[64,2688]{1,0:T(8,128)(2,1)S(1)}, bf16[64,2688]{1,0:T(8,128)(2,1)S(1)}, u32[]{:S(2)}, u32[]{:S(2)}) collective-permute-start(bf16[64,2688]{1,0:T(8,128)(2,1)S(1)} %get-tuple-element.29), channel_id=1, source_target_pairs={{0,1},{1,0},{2,3},{3,2},{4,5},{5,4},{6,7},{7,6},{8,9},{9,8},{10,11... | collective-permute-start | bytes 1032200 | tf_op jit(solution)/shard_map/ppermute | solution.py:278
  35.0 5.7 %collective-permute-start.12 = (bf16[8,6272]{1,0:T(8,128)(2,1)S(1)}, bf16[8,6272]{1,0:T(8,128)(2,1)S(1)}, u32[]{:S(2)}, u32[]{:S(2)}) collective-permute-start(bf16[8,6272]{1,0:T(8,128)(2,1)S(1)} %get-tuple-element.36), channel_id=1, source_target_pairs={{0,2},{2,0},{4,6},{6,4},{8,10},{10,8},{12,14},{14,12},{1,3},{3,1},... | collective-permute-start | bytes 301064 | tf_op jit(solution)/shard_map/ppermute | solution.py:275
  36.1 6.8 %collective-permute-start.14 = (bf16[8,6272]{1,0:T(8,128)(2,1)S(1)}, bf16[8,6272]{1,0:T(8,128)(2,1)S(1)}, u32[]{:S(2)}, u32[]{:S(2)}) collective-permute-start(bf16[8,6272]{1,0:T(8,128)(2,1)S(1)} %get-tuple-element.38), channel_id=1, source_target_pairs={{0,2},{2,0},{4,6},{6,4},{8,10},{10,8},{12,14},{14,12},{1,3},{3,1},... | collective-permute-start | bytes 301064 | tf_op jit(solution)/shard_map/ppermute | solution.py:275
  37.1 8.4 %collective-permute-start.16 = (bf16[8,6272]{1,0:T(8,128)(2,1)S(1)}, bf16[8,6272]{1,0:T(8,128)(2,1)S(1)}, u32[]{:S(2)}, u32[]{:S(2)}) collective-permute-start(bf16[8,6272]{1,0:T(8,128)(2,1)S(1)} %get-tuple-element.40), channel_id=1, source_target_pairs={{0,2},{2,0},{4,6},{6,4},{8,10},{10,8},{12,14},{14,12},{1,3},{3,1},... | collective-permute-start | bytes 301064 | tf_op jit(solution)/shard_map/ppermute | solution.py:275
  38.2 8.2 %collective-permute-start.11 = (bf16[8,6272]{1,0:T(8,128)(2,1)S(1)}, bf16[8,6272]{1,0:T(8,128)(2,1)S(1)}, u32[]{:S(2)}, u32[]{:S(2)}) collective-permute-start(bf16[8,6272]{1,0:T(8,128)(2,1)S(1)} %get-tuple-element.34), channel_id=1, source_target_pairs={{0,2},{2,0},{4,6},{6,4},{8,10},{10,8},{12,14},{14,12},{1,3},{3,1},... | collective-permute-start | bytes 301064 | tf_op jit(solution)/shard_map/ppermute | solution.py:275
  40.8 9.5 %collective-permute-start.13 = (bf16[8,6272]{1,0:T(8,128)(2,1)S(1)}, bf16[8,6272]{1,0:T(8,128)(2,1)S(1)}, u32[]{:S(2)}, u32[]{:S(2)}) collective-permute-start(bf16[8,6272]{1,0:T(8,128)(2,1)S(1)} %span_sum.3), channel_id=1, source_target_pairs={{0,8},{2,10},{4,12},{6,14},{8,0},{10,2},{12,4},{14,6},{1,9},{3,11}... | collective-permute-start | bytes 301064 | tf_op jit(solution)/shard_map/ppermute | solution.py:272
  42.9 7.3 %collective-permute-start.15 = (bf16[8,6272]{1,0:T(8,128)(2,1)S(1)}, bf16[8,6272]{1,0:T(8,128)(2,1)S(1)}, u32[]{:S(2)}, u32[]{:S(2)}) collective-permute-start(bf16[8,6272]{1,0:T(8,128)(2,1)S(1)} %span_sum.4), channel_id=1, source_target_pairs={{0,12},{2,14},{4,8},{6,10},{8,4},{10,6},{12,0},{14,2},{1,13},{3,15... | collective-permute-start | bytes 301064 | tf_op jit(solution)/shard_map/ppermute | solution.py:272
  45.5 5.9 %collective-permute-start.17 = (bf16[8,6272]{1,0:T(8,128)(2,1)S(1)}, bf16[8,6272]{1,0:T(8,128)(2,1)S(1)}, u32[]{:S(2)}, u32[]{:S(2)}) collective-permute-start(bf16[8,6272]{1,0:T(8,128)(2,1)S(1)} %span_sum.5), channel_id=1, source_target_pairs={{0,4},{2,6},{4,0},{6,2},{8,12},{10,14},{12,8},{14,10},{1,5},{3,7},... | collective-permute-start | bytes 301064 | tf_op jit(solution)/shard_map/ppermute | solution.py:272
  (1 other events, 1.0 us)

commit v6 on v5

v6 whole, which is shorter than its diff:
```python
import functools

import jax
import jax.numpy as jnp
from jax import lax
from jax.experimental import pallas as pl
from jax.experimental.pallas import tpu as pltpu
from jax.sharding import PartitionSpec as P

EXPERTS = 4
LANES = 128
RETURN_ORDER = (1, 3, 2)
N_BLOCK = 256
EXCHANGE_FLOPS = 20_000_000_000


def params(mib=4):
    return pltpu.CompilerParams(vmem_limit_bytes=mib * 1024 * 1024)


def cost(flops):
    return pl.CostEstimate(flops=flops, bytes_accessed=0, transcendentals=0)


def block_of(width, most):
    size = most
    while width % size:
        size -= 128
    return size


def in_vmem(value):
    return pltpu.with_memory_space_constraint(value, pltpu.VMEM)


def joined(refs):
    return jnp.concatenate([ref[...].astype(jnp.float32) for ref in refs], axis=0)


def stack_kernel(count, *refs):
    refs[-1][...] = joined(refs[:count]).astype(jnp.bfloat16)


def stack(values, after):
    rows = sum(v.shape[0] for v in values)
    return pl.pallas_call(
        functools.partial(stack_kernel, len(values)),
        in_specs=[pl.BlockSpec(memory_space=pltpu.VMEM)] * len(values) + [pl.BlockSpec(memory_space=pl.ANY)] * len(after),
        out_shape=jax.ShapeDtypeStruct((rows, values[0].shape[1]), jnp.bfloat16),
        compiler_params=params(),
        cost_estimate=cost(0),
        name="stack",
    )(*values, *after)


def unpacked(refs, out_ref, rows):
    total, width = out_ref.shape
    tail = width // rows
    blocks = (total // rows, rows, tail)
    row = lax.broadcasted_iota(jnp.int32, blocks, 1)
    ends = jnp.zeros(blocks, jnp.float32)
    for i in range(rows - 1):
        piece = joined([ref.at[:, i * tail:(i + 1) * tail] for ref in refs])
        out_ref[:, i * tail:(i + 1) * tail] = piece.astype(jnp.bfloat16)
        ends = jnp.where(row == i, jnp.broadcast_to(piece.reshape(blocks)[:, rows - 1:, :], blocks), ends)
    out_ref[:, width - tail:] = ends.reshape(total, tail).astype(jnp.bfloat16)


def gate_up_kernel(n_block, rows, *refs):
    rows_in, (gate_ref, up_ref, hidden_ref, rows_ref) = refs[:-4], refs[-4:]
    unpacked(rows_in, rows_ref, rows)
    for n in range(0, gate_ref.shape[1], n_block):
        columns = slice(n, n + n_block)
        gate = jnp.dot(rows_ref[...], gate_ref[:, columns], preferred_element_type=jnp.float32)
        up = jnp.dot(rows_ref[...], up_ref[:, columns], preferred_element_type=jnp.float32)
        hidden_ref[:, columns] = (gate / (1.0 + jnp.exp(-gate)) * up).astype(jnp.bfloat16)


def gate_up(blocks, gate_weight, up_weight, rows):
    total = sum(r.shape[0] for r in blocks)
    width, units = gate_weight.shape
    return pl.pallas_call(
        functools.partial(gate_up_kernel, block_of(units, N_BLOCK), rows),
        in_specs=[pl.BlockSpec(memory_space=pltpu.VMEM)] * (len(blocks) + 2),
        out_shape=jax.ShapeDtypeStruct((total, units), jnp.bfloat16),
        scratch_shapes=[pltpu.VMEM((total, width), jnp.bfloat16)],
        compiler_params=params(),
        cost_estimate=cost(4 * total * width * units),
        name="gate_up",
    )(*blocks, in_vmem(gate_weight), in_vmem(up_weight))


def down_kernel(rows, parts, *refs):
    hidden_refs, down_ref, outs = refs[:parts], refs[parts], refs[parts + 1:]
    count, width = outs[0].shape
    hidden = jnp.concatenate([ref[...] for ref in hidden_refs], axis=0)
    tail = down_ref.shape[1] // rows
    blocks = (hidden.shape[0] // rows, rows, tail)
    last = lax.broadcasted_iota(jnp.int32, blocks, 1) == rows - 1
    ends = jnp.dot(hidden, down_ref[:, width:], preferred_element_type=jnp.float32).reshape(blocks)
    for i in range(rows - 1):
        columns = slice(i * tail, (i + 1) * tail)
        value = jnp.dot(hidden, down_ref[:, columns], preferred_element_type=jnp.float32).reshape(blocks)
        value = jnp.where(last, jnp.broadcast_to(ends[:, i:i + 1, :], blocks), value).reshape(blocks[0] * rows, tail)
        for j, ref in enumerate(outs):
            ref[:, columns] = value[j * count:(j + 1) * count].astype(ref.dtype)


def down(hiddens, down_weight, pair, rows):
    total, units = hiddens[0].shape
    width = down_weight.shape[1] // rows * (rows - 1)
    shape = (total // pair, width)
    out_shape = [jax.ShapeDtypeStruct(shape, jnp.bfloat16 if p else jnp.float32) for _ in hiddens for p in range(pair)]
    outs = pl.pallas_call(
        functools.partial(down_kernel, rows, len(hiddens)),
        in_specs=[pl.BlockSpec(memory_space=pltpu.VMEM)] * (len(hiddens) + 1),
        out_shape=out_shape,
        compiler_params=params(),
        cost_estimate=cost(2 * total * len(hiddens) * width * units),
        name="down",
    )(*hiddens, in_vmem(down_weight))
    return [outs[i:i + pair] for i in range(0, len(outs), pair)]


def pair_sum_kernel(count, *refs):
    outs = refs[count:]
    rows = outs[0].shape[0]
    for i, out_ref in enumerate(outs):
        part = slice(i * rows, (i + 1) * rows)
        value = refs[0][part, :]
        for ref in refs[1:count]:
            value += ref[part, :].astype(jnp.float32)
        out_ref[...] = value.astype(out_ref.dtype)


def pair_sum(arrays, rows, dtype):
    total, width = arrays[0].shape
    return pl.pallas_call(
        functools.partial(pair_sum_kernel, len(arrays)),
        out_shape=[jax.ShapeDtypeStruct((rows, width), dtype)] * (total // rows),
        compiler_params=params(),
        name="pair_sum",
    )(*arrays)


def span_sum_kernel(*refs):
    value = refs[0][...]
    for ref in refs[1:-1]:
        value += ref[...].astype(jnp.float32)
    refs[-1][...] = value.astype(refs[-1].dtype)


def span_sum(arrays):
    return pl.pallas_call(
        span_sum_kernel,
        out_shape=jax.ShapeDtypeStruct(arrays[0].shape, jnp.bfloat16),
        compiler_params=params(),
        name="span_sum",
    )(*arrays)


def pack_kernel(own_expert, tokens_hbm, ids_hbm, weights_hbm, sides_ref, *refs):
    packed_refs, (tokens_ref, ids_ref, weights_ref, semaphores) = refs[:EXPERTS], refs[EXPERTS:]
    pairs = [(tokens_hbm, tokens_ref), (ids_hbm, ids_ref), (weights_hbm, weights_ref)]
    copies = [pltpu.make_async_copy(src, dst, semaphores.at[i]) for i, (src, dst) in enumerate(pairs)]
    for copy in copies:
        copy.start()
    for copy in copies:
        copy.wait()
    ids, weights = ids_ref[...], weights_ref[...]
    rows, width = tokens_ref.shape
    tail = width // rows
    square = (rows, rows)
    row, column = lax.broadcasted_iota(jnp.int32, square, 0), lax.broadcasted_iota(jnp.int32, square, 1)
    last = lax.broadcasted_iota(jnp.int32, (rows, tail), 0) == rows - 1
    here = tokens_ref[...].astype(jnp.float32)
    below = pltpu.roll(here, rows - 1, 0)
    for s, packed_ref in enumerate(packed_refs):
        expert = lax.bitwise_xor(own_expert[0], s)
        named = ids == expert
        chosen = jnp.sum(jnp.where(named, weights, 0.0), axis=0, keepdims=True)
        coeff = jnp.sum(jnp.where(row == column, jnp.broadcast_to(chosen, square), 0.0), axis=1, keepdims=True)
        unnamed = 1.0 - jnp.sum(jnp.where(named, 1.0, 0.0), axis=0, keepdims=True)
        shift = jnp.max(jnp.where(column <= row, jnp.broadcast_to(unnamed, square), 0.0), axis=1, keepdims=True)
        sides_ref[:, s * LANES:(s + 1) * LANES] = jnp.broadcast_to(coeff, (rows, LANES))
        sides_ref[:, (EXPERTS + s) * LANES:(EXPERTS + s + 1) * LANES] = jnp.broadcast_to(shift, (rows, LANES))
        kept = jnp.where(shift > 0.5, below, here)
        for i in range(rows - 1):
            moved = jnp.broadcast_to(kept[i:i + 1, width - tail:], (rows, tail))
            piece = jnp.where(last, moved, kept[:, i * tail:(i + 1) * tail])
            packed_ref[:, i * tail:(i + 1) * tail] = piece.astype(jnp.bfloat16)


def pack(own_expert, tokens, ids, weights):
    rows, width = tokens.shape
    packed = jax.ShapeDtypeStruct((rows, width - width // rows), jnp.bfloat16)
    inputs = [tokens, ids.T, weights.T]
    return pl.pallas_call(
        pack_kernel,
        in_specs=[pl.BlockSpec(memory_space=pltpu.SMEM)] + [pl.BlockSpec(memory_space=pl.ANY)] * 3,
        out_shape=[jax.ShapeDtypeStruct((rows, 2 * EXPERTS * LANES), jnp.float32)] + [packed] * EXPERTS,
        scratch_shapes=[pltpu.VMEM(a.shape, a.dtype) for a in inputs] + [pltpu.SemaphoreType.DMA((len(inputs),))],
        compiler_params=params(),
        cost_estimate=cost(EXCHANGE_FLOPS),
        name="pack",
    )(own_expert, *[pltpu.with_memory_space_constraint(a, pltpu.HBM) for a in inputs])


def combine_kernel(own_count, sides_ref, *refs):
    out_ref = refs[-1]
    rows, width = out_ref.shape
    tail = width // rows
    own = refs[0][...]
    for ref in refs[1:own_count]:
        own += ref[...].astype(jnp.float32)
    row = lax.broadcasted_iota(jnp.int32, (rows, tail), 0)
    parts = []
    others = [ref[...].astype(jnp.float32) for ref in refs[own_count:-1]]
    for s, packed in zip((0,) + RETURN_ORDER, [own] + others):
        coeff = sides_ref[:, s * LANES:s * LANES + 1]
        shifted = sides_ref[:, (EXPERTS + s) * LANES:(EXPERTS + s) * LANES + 1] > 0.5
        ends = jnp.zeros((rows, tail), jnp.float32)
        for i in range(rows - 1):
            ends = jnp.where(row == i, jnp.broadcast_to(packed[rows - 1:, i * tail:(i + 1) * tail], (rows, tail)), ends)
        whole = jnp.concatenate([packed, ends], axis=1)
        parts.append(coeff * jnp.where(shifted, pltpu.roll(whole, 1, 0), whole))
    out_ref[...] = sum(parts[1:], parts[0]).astype(jnp.bfloat16)


def combine(sides, own, others, width):
    return pl.pallas_call(
        functools.partial(combine_kernel, len(own)),
        out_shape=jax.ShapeDtypeStruct((own[0].shape[0], width), jnp.bfloat16),
        compiler_params=params(),
        name="combine",
    )(sides, *own, *others)


def local(tokens, expert_ids, route_weights, gate_weight, up_weight, down_weight):
    rows, width = tokens.shape
    attn = lax.axis_size("attn")
    pair = lax.axis_size("ffn")
    span = attn // EXPERTS

    def over_experts(value, other):
        return lax.ppermute(value, "attn", [(i, (i // span ^ other) * span + i % span) for i in range(attn)])

    def over_span(value, shift):
        return lax.ppermute(value, "attn", [(i, i // span * span + (i + shift) % span) for i in range(attn)])

    def over_pair(value, shift):
        return lax.ppermute(value, "ffn", [(i, (i + shift) % pair) for i in range(pair)])

    own_expert = (lax.axis_index("attn") // span).astype(jnp.int32).reshape(1)
    sides, *packed = pack(own_expert, tokens, expert_ids, route_weights)
    column = packed[:1] + [over_experts(packed[s], s) for s in range(1, EXPERTS)]
    parts = [column] + [[over_span(b, t) for b in column] for t in range(1, span)]
    hiddens, after = [], [b for part in parts[1:2] for b in part[:2]]
    for part in parts:
        group = stack(part, after)
        group = [group] + [over_pair(group, p) for p in range(1, pair)]
        after = [gate_up(group, gate_weight, up_weight, rows)]
        hiddens += after

    sums = [[] for _ in range(EXPERTS)]
    for t, (keep, *sends) in enumerate(down(hiddens, down_weight, pair, rows)):
        arrays = [keep] + [over_pair(b, -p) for p, b in enumerate(sends, 1)]
        blocks = pair_sum(arrays, rows, jnp.bfloat16 if t else jnp.float32)
        for s in range(EXPERTS):
            sums[s].append(over_span(blocks[s], -t) if t else blocks[s])

    returned = [over_experts(span_sum(sums[s]), s) for s in RETURN_ORDER]
    return combine(sides, sums[0], returned, width)


def solution(mesh):
    return jax.shard_map(
        local,
        mesh=mesh,
        in_specs=(
            P(("groups", "attn", "ffn"), None),
            P(("groups", "attn", "ffn"), None),
            P(("groups", "attn", "ffn"), None),
            P(None, ("attn", "ffn")),
            P(None, ("attn", "ffn")),
            P(("attn", "ffn"), None),
        ),
        out_specs=P(("groups", "attn", "ffn"), None),
        check_vma=False,
    )
```

time: 52.5 us -> 51.8 us (0.987)
  Pallas kernels: 8.86 us -> 15.7 us
  waiting for transfers between devices: 21.6 us -> 15.2 us
  local copies, waits for them, and re-layouts: 3.26 us -> 0.03 us
  starting transfers between devices: 18.4 us -> 20.6 us
    pallas_call x1 -> x2, Pallas kernels: 4.52 us -> 10.8 us  [gate_up(): pl.pallas_call(functools.partial(gate_up_kernel, block_of(units, N_BLOCK)...]
    ppermute x8, waiting for transfers between devices: 7.39 us -> 1.57 us  [over_span(): lax.ppermute(value, 'attn', [(i, i // span * span + (i + shift) % span) f...]
    unnamed x30 -> x12, local copies, waits for them, and re-layouts: 3.26 us -> 0.03 us
    ppermute x6, starting transfers between devices: 9.47 us -> 11.6 us  [over_experts(): lax.ppermute(value, 'attn', [(i, (i // span ^ other) * span + i % span) f...]
    pallas_call x1, Pallas kernels: 0.22 us -> 1.29 us  [pack(): pl.pallas_call(pack_kernel, in_specs=[pl.BlockSpec(memory_space=pltpu.SME...]
    pallas_call x6 -> x5, Pallas kernels: 3.12 us -> 2.6 us  [the longest x1 2.37 us: down(): pl.pallas_call(functools.partial(down_kernel, rows, len(hiddens)), in_spe...]
  transfers between devices with their start and end apart: 18 -> 18, of which waited for: 10 -> 7; matrix products, arithmetic and copies ran while one was open for 0% -> 0% of each run, Pallas kernels for 1% -> 11%
where the time goes in v6:
time: 51.8 us; the launch traced here: 51.7 us
  starting transfers between devices  20.6 us (40%)
  Pallas kernels  15.7 us (30%)
  waiting for transfers between devices  15.2 us (29%)
    ppermute x6, starting transfers between devices, over_experts(): lax.ppermute(value, 'attn', [(i, (i // span ^ other) * span + i % span) f...  11.6 us
    pallas_call x2, Pallas kernels, gate_up(): pl.pallas_call(functools.partial(gate_up_kernel, block_of(units, N_BLOCK)...  10.8 us
    ppermute x6, waiting for transfers between devices, over_experts(): lax.ppermute(value, 'attn', [(i, (i // span ^ other) * span + i % span) f...  10.7 us
    ppermute x8, starting transfers between devices, over_span(): lax.ppermute(value, 'attn', [(i, i // span * span + (i + shift) % span) f...  8.23 us
    ppermute x4, waiting for transfers between devices, over_pair(): lax.ppermute(value, 'ffn', [(i, (i + shift) % pair) for i in range(pair)])  2.95 us
    pallas_call x1, Pallas kernels, down(): pl.pallas_call(functools.partial(down_kernel, rows, len(hiddens)), in_spe...  2.37 us
    ppermute x8, waiting for transfers between devices, over_span(): lax.ppermute(value, 'attn', [(i, i // span * span + (i + shift) % span) f...  1.57 us
    pallas_call x1, Pallas kernels, pack(): pl.pallas_call(pack_kernel, in_specs=[pl.BlockSpec(memory_space=pltpu.SME...  1.29 us
  transfers between devices with their start and end apart: 18, of which 7 were waited for; matrix products, arithmetic and copies ran while one was open for 0% of the time, Pallas kernels for 11%

profile of v6, /device:TPU:0, one launch (start us, length us, event | category | flops | bytes accessed | tf_op | source)
XLA Modules:
  0.0 51.7 jit_solution(9983172744032685615)
XLA Ops:
  0.0 1.3 %pack.1 = (f32[8,1024]{1,0:T(8,128)S(1)}, bf16[8,6272]{1,0:T(8,128)(2,1)S(1)}, bf16[8,6272]{1,0:T(8,128)(2,1)S(1)}, bf16[8,6272]{1,0:T(8,128)(2,1)S(1)}, bf16[8,6272]{1,0:T(8,128)(2,1)S(1)}) custom-call(s32[1]{0:T(128)} %bitcast.own_expert, bf16[8,7168]{1,0:T(8,128)(2,1)} %tokens_hbm.1, s32[3,8]{1,0:T(4,128)} %bitcast.5, f32[3,8]{1,0:T(4,128)} %bitcast.6), custom_call_target="tpu_custom_call" | custom-call | flops 20000000000 | tf_op jit(solution)/shard_map/pack/pallas_call | solution.py:198
  1.3 3.1 %collective-permute-start = (bf16[8,6272]{1,0:T(8,128)(2,1)S(1)}, bf16[8,6272]{1,0:T(8,128)(2,1)S(1)}, u32[]{:S(2)}, u32[]{:S(2)}) collective-permute-start(bf16[8,6272]{1,0:T(8,128)(2,1)S(1)} %get-tuple-element.24), channel_id=1, source_target_pairs={{0,4},{2,6},{4,0},{6,2},{8,12},{10,14},{12,8},{14,10},{1,5},{3,7},... | collective-permute-start | bytes 301064 | tf_op jit(solution)/shard_map/ppermute | solution.py:246
  4.4 2.6 %collective-permute-start.1 = (bf16[8,6272]{1,0:T(8,128)(2,1)S(1)}, bf16[8,6272]{1,0:T(8,128)(2,1)S(1)}, u32[]{:S(2)}, u32[]{:S(2)}) collective-permute-start(bf16[8,6272]{1,0:T(8,128)(2,1)S(1)} %get-tuple-element.25), channel_id=1, source_target_pairs={{0,8},{2,10},{4,12},{6,14},{8,0},{10,2},{12,4},{14,6},{1,9},{3,11}... | collective-permute-start | bytes 301064 | tf_op jit(solution)/shard_map/ppermute | solution.py:246
  7.0 1.7 %collective-permute-start.3 = (bf16[8,6272]{1,0:T(8,128)(2,1)S(1)}, bf16[8,6272]{1,0:T(8,128)(2,1)S(1)}, u32[]{:S(2)}, u32[]{:S(2)}) collective-permute-start(bf16[8,6272]{1,0:T(8,128)(2,1)S(1)} %get-tuple-element.23.refs_0_), channel_id=1, source_target_pairs={{0,2},{2,0},{4,6},{6,4},{8,10},{10,8},{12,14},{14,12},{1,3},{3,1},... | collective-permute-start | bytes 301064 | tf_op jit(solution)/shard_map/ppermute | solution.py:249
  8.7 0.3 collective-permute-start.4
  9.0 6.0 %collective-permute-done.1.refs_2_ = bf16[8,6272]{1,0:T(8,128)(2,1)S(1)} collective-permute-done((bf16[8,6272]{1,0:T(8,128)(2,1)S(1)}, bf16[8,6272]{1,0:T(8,128)(2,1)S(1)}, u32[]{:S(2)}, u32[]{:S(2)}) %collective-permute-start.1) | collective-permute-done | bytes 100384 | tf_op jit(solution)/shard_map/ppermute | solution.py:246
  15.0 0.1 collective-permute-start.5
  15.1 1.6 %collective-permute-start.6 = (bf16[8,6272]{1,0:T(8,128)(2,1)S(1)}, bf16[8,6272]{1,0:T(8,128)(2,1)S(1)}, u32[]{:S(2)}, u32[]{:S(2)}) collective-permute-start(bf16[8,6272]{1,0:T(8,128)(2,1)S(1)} %collective-permute-done.1.refs_2_), channel_id=1, source_target_pairs={{0,2},{2,0},{4,6},{6,4},{8,10},{10,8},{12,14},{14,12},{1,3},{3,1},... | collective-permute-start | bytes 301064 | tf_op jit(solution)/shard_map/ppermute | solution.py:249
  16.7 0.5 collective-permute-start.7
  17.2 5.4 %gate_up.2.refs_4_.refs_0_ = bf16[64,1024]{1,0:T(8,128)(2,1)S(1)} custom-call(bf16[32,6272]{1,0:T(8,128)(2,1)S(1)} %stack.2.refs_0_, bf16[32,6272]{1,0:T(8,128)(2,1)S(1)} %collective-permute-done.5.refs_1_, bf16[7168,1024]{1,0:T(8,128)(2,1)S(1)} %copy-done, bf16[7168,1024]{1,0:T(8,128)(2,1)S(1)} %copy-done.1), custom_call_target="tpu_custom_call" | custom-call | flops 1879048192 | tf_op jit(solution)/shard_map/gate_up/pallas_call | solution.py:82
  22.6 0.0 slice-start
  22.7 0.1 collective-permute-start.8
  22.8 1.7 %collective-permute-done.8.refs_1_ = bf16[32,6272]{1,0:T(8,128)(2,1)S(1)} collective-permute-done((bf16[32,6272]{1,0:T(8,128)(2,1)S(1)}, bf16[32,6272]{1,0:T(8,128)(2,1)S(1)}, u32[]{:S(2)}, u32[]{:S(2)}) %collective-permute-start.8) | collective-permute-done | bytes 401440 | tf_op jit(solution)/shard_map/ppermute | solution.py:252
  24.5 5.4 %gate_up.3.refs_1_ = bf16[64,1024]{1,0:T(8,128)(2,1)S(1)} custom-call(bf16[32,6272]{1,0:T(8,128)(2,1)S(1)} %stack.3.refs_0_, bf16[32,6272]{1,0:T(8,128)(2,1)S(1)} %collective-permute-done.8.refs_1_, bf16[7168,1024]{1,0:T(8,128)(2,1)S(1)} %copy-done, bf16[7168,1024]{1,0:T(8,128)(2,1)S(1)} %copy-done.1), custom_call_target="tpu_custom_call" | custom-call | flops 1879048192 | tf_op jit(solution)/shard_map/gate_up/pallas_call | solution.py:82
  30.0 2.4 %down.1 = (f32[32,6272]{1,0:T(8,128)S(1)}, bf16[32,6272]{1,0:T(8,128)(2,1)S(1)}, f32[32,6272]{1,0:T(8,128)S(1)}, bf16[32,6272]{1,0:T(8,128)(2,1)S(1)}) custom-call(bf16[64,1024]{1,0:T(8,128)(2,1)S(1)} %gate_up.2.refs_4_.refs_0_, bf16[64,1024]{1,0:T(8,128)(2,1)S(1)} %gate_up.3.refs_1_, bf16[1024,7168]{1,0:T(8,128)(2,1)S(1)} %bitcast.4), custom_call_target="tpu_custom_call" | custom-call | flops 1644167168 | tf_op jit(solution)/shard_map/down/pallas_call | solution.py:114
  32.4 0.2 collective-permute-start.10
  32.6 0.4 collective-permute-start.9
  32.9 1.2 %collective-permute-done.10.refs_1_ = bf16[32,6272]{1,0:T(8,128)(2,1)S(1)} collective-permute-done((bf16[32,6272]{1,0:T(8,128)(2,1)S(1)}, bf16[32,6272]{1,0:T(8,128)(2,1)S(1)}, u32[]{:S(2)}, u32[]{:S(2)}) %collective-permute-start.10) | collective-permute-done | bytes 401440 | tf_op jit(solution)/shard_map/ppermute | solution.py:252
  34.2 0.1 pair_sum.3
  34.3 1.6 %collective-permute-start.16 = (bf16[8,6272]{1,0:T(8,128)(2,1)S(1)}, bf16[8,6272]{1,0:T(8,128)(2,1)S(1)}, u32[]{:S(2)}, u32[]{:S(2)}) collective-permute-start(bf16[8,6272]{1,0:T(8,128)(2,1)S(1)} %get-tuple-element.38), channel_id=1, source_target_pairs={{0,2},{2,0},{4,6},{6,4},{8,10},{10,8},{12,14},{14,12},{1,3},{3,1},... | collective-permute-start | bytes 301064 | tf_op jit(solution)/shard_map/ppermute | solution.py:249
  35.9 0.5 collective-permute-start.14
  36.4 1.5 %collective-permute-start.12 = (bf16[8,6272]{1,0:T(8,128)(2,1)S(1)}, bf16[8,6272]{1,0:T(8,128)(2,1)S(1)}, u32[]{:S(2)}, u32[]{:S(2)}) collective-permute-start(bf16[8,6272]{1,0:T(8,128)(2,1)S(1)} %get-tuple-element.34), channel_id=1, source_target_pairs={{0,2},{2,0},{4,6},{6,4},{8,10},{10,8},{12,14},{14,12},{1,3},{3,1},... | collective-permute-start | bytes 301064 | tf_op jit(solution)/shard_map/ppermute | solution.py:249
  37.9 0.5 collective-permute-start.11
  38.4 0.1 pair_sum.2
  38.5 1.6 %collective-permute-done.16.refs_1_ = bf16[8,6272]{1,0:T(8,128)(2,1)S(1)} collective-permute-done((bf16[8,6272]{1,0:T(8,128)(2,1)S(1)}, bf16[8,6272]{1,0:T(8,128)(2,1)S(1)}, u32[]{:S(2)}, u32[]{:S(2)}) %collective-permute-start.16) | collective-permute-done | bytes 100384 | tf_op jit(solution)/shard_map/ppermute | solution.py:249
  40.1 2.7 %collective-permute-start.17 = (bf16[8,6272]{1,0:T(8,128)(2,1)S(1)}, bf16[8,6272]{1,0:T(8,128)(2,1)S(1)}, u32[]{:S(2)}, u32[]{:S(2)}) collective-permute-start(bf16[8,6272]{1,0:T(8,128)(2,1)S(1)} %span_sum.5), channel_id=1, source_target_pairs={{0,8},{2,10},{4,12},{6,14},{8,0},{10,2},{12,4},{14,6},{1,9},{3,11}... | collective-permute-start | bytes 301064 | tf_op jit(solution)/shard_map/ppermute | solution.py:246
  42.8 1.9 %collective-permute-start.15 = (bf16[8,6272]{1,0:T(8,128)(2,1)S(1)}, bf16[8,6272]{1,0:T(8,128)(2,1)S(1)}, u32[]{:S(2)}, u32[]{:S(2)}) collective-permute-start(bf16[8,6272]{1,0:T(8,128)(2,1)S(1)} %span_sum.4), channel_id=1, source_target_pairs={{0,12},{2,14},{4,8},{6,10},{8,4},{10,6},{12,0},{14,2},{1,13},{3,15... | collective-permute-start | bytes 301064 | tf_op jit(solution)/shard_map/ppermute | solution.py:246
  44.8 1.3 %collective-permute-start.13 = (bf16[8,6272]{1,0:T(8,128)(2,1)S(1)}, bf16[8,6272]{1,0:T(8,128)(2,1)S(1)}, u32[]{:S(2)}, u32[]{:S(2)}) collective-permute-start(bf16[8,6272]{1,0:T(8,128)(2,1)S(1)} %span_sum.3), channel_id=1, source_target_pairs={{0,4},{2,6},{4,0},{6,2},{8,12},{10,14},{12,8},{14,10},{1,5},{3,7},... | collective-permute-start | bytes 301064 | tf_op jit(solution)/shard_map/ppermute | solution.py:246
  46.0 3.3 %collective-permute-done.17.refs_4_ = bf16[8,6272]{1,0:T(8,128)(2,1)S(1)} collective-permute-done((bf16[8,6272]{1,0:T(8,128)(2,1)S(1)}, bf16[8,6272]{1,0:T(8,128)(2,1)S(1)}, u32[]{:S(2)}, u32[]{:S(2)}) %collective-permute-start.17) | collective-permute-done | bytes 100384 | tf_op jit(solution)/shard_map/ppermute | solution.py:246
  49.3 0.6 %collective-permute-done.15.refs_3_ = bf16[8,6272]{1,0:T(8,128)(2,1)S(1)} collective-permute-done((bf16[8,6272]{1,0:T(8,128)(2,1)S(1)}, bf16[8,6272]{1,0:T(8,128)(2,1)S(1)}, u32[]{:S(2)}, u32[]{:S(2)}) %collective-permute-start.15) | collective-permute-done | bytes 100384 | tf_op jit(solution)/shard_map/ppermute | solution.py:246
  49.9 0.9 %collective-permute-done.13.refs_2_ = bf16[8,6272]{1,0:T(8,128)(2,1)S(1)} collective-permute-done((bf16[8,6272]{1,0:T(8,128)(2,1)S(1)}, bf16[8,6272]{1,0:T(8,128)(2,1)S(1)}, u32[]{:S(2)}, u32[]{:S(2)}) %collective-permute-start.13) | collective-permute-done | bytes 100384 | tf_op jit(solution)/shard_map/ppermute | solution.py:246
  50.8 0.9 %combine.1 = bf16[8,7168]{1,0:T(8,128)(2,1)} custom-call(f32[8,1024]{1,0:T(8,128)S(1)} %get-tuple-element.22.sides_ref, f32[8,6272]{1,0:T(8,128)S(1)} %get-tuple-element.29.refs_0_, bf16[8,6272]{1,0:T(8,128)(2,1)S(1)} %collective-permute-done.11.refs_1_, bf16[8,6272]{1,0:T(8,128)(2,1)S(1)} %collective-permute-done.13.refs_2_, ...), custom_call_target="tpu_custom_call" | custom-call | tf_op jit(solution)/shard_map/combine/pallas_call | solution.py:231
  (29 shorter events, 0.2 us)
Async XLA Ops:
  0.0 17.2 %copy-start = (bf16[7168,1024]{1,0:T(8,128)(2,1)S(1)}, bf16[7168,1024]{1,0:T(8,128)(2,1)}, u32[]{:S(2)}) copy-start(bf16[7168,1024]{1,0:T(8,128)(2,1)} %refs_2_.4) | copy-start | bytes 44040196
  0.0 17.2 %copy-start.1 = (bf16[7168,1024]{1,0:T(8,128)(2,1)S(1)}, bf16[7168,1024]{1,0:T(8,128)(2,1)}, u32[]{:S(2)}) copy-start(bf16[7168,1024]{1,0:T(8,128)(2,1)} %refs_3_.3) | copy-start | bytes 44040196
  1.3 7.4 %collective-permute-start = (bf16[8,6272]{1,0:T(8,128)(2,1)S(1)}, bf16[8,6272]{1,0:T(8,128)(2,1)S(1)}, u32[]{:S(2)}, u32[]{:S(2)}) collective-permute-start(bf16[8,6272]{1,0:T(8,128)(2,1)S(1)} %get-tuple-element.24), channel_id=1, source_target_pairs={{0,4},{2,6},{4,0},{6,2},{8,12},{10,14},{12,8},{14,10},{1,5},{3,7},... | collective-permute-start | bytes 301064 | tf_op jit(solution)/shard_map/ppermute | solution.py:246
  4.4 10.6 %collective-permute-start.1 = (bf16[8,6272]{1,0:T(8,128)(2,1)S(1)}, bf16[8,6272]{1,0:T(8,128)(2,1)S(1)}, u32[]{:S(2)}, u32[]{:S(2)}) collective-permute-start(bf16[8,6272]{1,0:T(8,128)(2,1)S(1)} %get-tuple-element.25), channel_id=1, source_target_pairs={{0,8},{2,10},{4,12},{6,14},{8,0},{10,2},{12,4},{14,6},{1,9},{3,11}... | collective-permute-start | bytes 301064 | tf_op jit(solution)/shard_map/ppermute | solution.py:246
  7.0 8.0 %collective-permute-start.2 = (bf16[8,6272]{1,0:T(8,128)(2,1)S(1)}, bf16[8,6272]{1,0:T(8,128)(2,1)S(1)}, u32[]{:S(2)}, u32[]{:S(2)}) collective-permute-start(bf16[8,6272]{1,0:T(8,128)(2,1)S(1)} %get-tuple-element.26), channel_id=1, source_target_pairs={{0,12},{2,14},{4,8},{6,10},{8,4},{10,6},{12,0},{14,2},{1,13},{3,15... | collective-permute-start | bytes 301064 | tf_op jit(solution)/shard_map/ppermute | solution.py:246
  7.0 8.0 %collective-permute-start.3 = (bf16[8,6272]{1,0:T(8,128)(2,1)S(1)}, bf16[8,6272]{1,0:T(8,128)(2,1)S(1)}, u32[]{:S(2)}, u32[]{:S(2)}) collective-permute-start(bf16[8,6272]{1,0:T(8,128)(2,1)S(1)} %get-tuple-element.23.refs_0_), channel_id=1, source_target_pairs={{0,2},{2,0},{4,6},{6,4},{8,10},{10,8},{12,14},{14,12},{1,3},{3,1},... | collective-permute-start | bytes 301064 | tf_op jit(solution)/shard_map/ppermute | solution.py:249
  8.7 6.2 %collective-permute-start.4 = (bf16[8,6272]{1,0:T(8,128)(2,1)S(1)}, bf16[8,6272]{1,0:T(8,128)(2,1)S(1)}, u32[]{:S(2)}, u32[]{:S(2)}) collective-permute-start(bf16[8,6272]{1,0:T(8,128)(2,1)S(1)} %collective-permute-done.refs_1_), channel_id=1, source_target_pairs={{0,2},{2,0},{4,6},{6,4},{8,10},{10,8},{12,14},{14,12},{1,3},{3,1},... | collective-permute-start | bytes 301064 | tf_op jit(solution)/shard_map/ppermute | solution.py:249
  15.0 2.2 %collective-permute-start.5 = (bf16[32,6272]{1,0:T(8,128)(2,1)S(1)}, bf16[32,6272]{1,0:T(8,128)(2,1)S(1)}, u32[]{:S(2)}, u32[]{:S(2)}) collective-permute-start(bf16[32,6272]{1,0:T(8,128)(2,1)S(1)} %stack.2.refs_0_), channel_id=1, source_target_pairs={{0,1},{1,0},{2,3},{3,2},{4,5},{5,4},{6,7},{7,6},{8,9},{9,8},{10,11... | collective-permute-start | bytes 1204232 | tf_op jit(solution)/shard_map/ppermute | solution.py:252
  15.1 7.5 %collective-permute-start.6 = (bf16[8,6272]{1,0:T(8,128)(2,1)S(1)}, bf16[8,6272]{1,0:T(8,128)(2,1)S(1)}, u32[]{:S(2)}, u32[]{:S(2)}) collective-permute-start(bf16[8,6272]{1,0:T(8,128)(2,1)S(1)} %collective-permute-done.1.refs_2_), channel_id=1, source_target_pairs={{0,2},{2,0},{4,6},{6,4},{8,10},{10,8},{12,14},{14,12},{1,3},{3,1},... | collective-permute-start | bytes 301064 | tf_op jit(solution)/shard_map/ppermute | solution.py:249
  16.7 5.9 %collective-permute-start.7 = (bf16[8,6272]{1,0:T(8,128)(2,1)S(1)}, bf16[8,6272]{1,0:T(8,128)(2,1)S(1)}, u32[]{:S(2)}, u32[]{:S(2)}) collective-permute-start(bf16[8,6272]{1,0:T(8,128)(2,1)S(1)} %collective-permute-done.2.refs_3_), channel_id=1, source_target_pairs={{0,2},{2,0},{4,6},{6,4},{8,10},{10,8},{12,14},{14,12},{1,3},{3,1},... | collective-permute-start | bytes 301064 | tf_op jit(solution)/shard_map/ppermute | solution.py:249
  22.6 7.3 %slice-start = ((s8[14680064]{0:T(1024)(128)(4,1)}), s8[2097152]{0:T(1024)(128)(4,1)S(1)}, s32[]{:S(2)}) async-start(s8[14680064]{0:T(1024)(128)(4,1)} %bitcast.3), calls=%async_computation | async-start | bytes 4194304
  22.7 7.3 %slice-start.1 = ((s8[14680064]{0:T(1024)(128)(4,1)}), s8[4194304]{0:T(1024)(128)(4,1)S(1)}, s32[]{:S(2)}) async-start(s8[14680064]{0:T(1024)(128)(4,1)} %bitcast.3), calls=%async_computation.1 | async-start | bytes 8388608
  22.7 7.3 %slice-start.2 = ((s8[14680064]{0:T(1024)(128)(4,1)}), s8[4194304]{0:T(1024)(128)(4,1)S(1)}, s32[]{:S(2)}) async-start(s8[14680064]{0:T(1024)(128)(4,1)} %bitcast.3), calls=%async_computation.2 | async-start | bytes 8388608
  22.7 7.3 %slice-start.3 = ((s8[14680064]{0:T(1024)(128)(4,1)}), s8[4194304]{0:T(1024)(128)(4,1)S(1)}, s32[]{:S(2)}) async-start(s8[14680064]{0:T(1024)(128)(4,1)} %bitcast.3), calls=%async_computation.3 | async-start | bytes 8388608
  22.7 1.8 %collective-permute-start.8 = (bf16[32,6272]{1,0:T(8,128)(2,1)S(1)}, bf16[32,6272]{1,0:T(8,128)(2,1)S(1)}, u32[]{:S(2)}, u32[]{:S(2)}) collective-permute-start(bf16[32,6272]{1,0:T(8,128)(2,1)S(1)} %stack.3.refs_0_), channel_id=1, source_target_pairs={{0,1},{1,0},{2,3},{3,2},{4,5},{5,4},{6,7},{7,6},{8,9},{9,8},{10,11... | collective-permute-start | bytes 1204232 | tf_op jit(solution)/shard_map/ppermute | solution.py:252
  32.4 1.8 %collective-permute-start.10 = (bf16[32,6272]{1,0:T(8,128)(2,1)S(1)}, bf16[32,6272]{1,0:T(8,128)(2,1)S(1)}, u32[]{:S(2)}, u32[]{:S(2)}) collective-permute-start(bf16[32,6272]{1,0:T(8,128)(2,1)S(1)} %get-tuple-element.31), channel_id=1, source_target_pairs={{0,1},{1,0},{2,3},{3,2},{4,5},{5,4},{6,7},{7,6},{8,9},{9,8},{10,11... | collective-permute-start | bytes 1204232 | tf_op jit(solution)/shard_map/ppermute | solution.py:252
  32.6 5.8 %collective-permute-start.9 = (bf16[32,6272]{1,0:T(8,128)(2,1)S(1)}, bf16[32,6272]{1,0:T(8,128)(2,1)S(1)}, u32[]{:S(2)}, u32[]{:S(2)}) collective-permute-start(bf16[32,6272]{1,0:T(8,128)(2,1)S(1)} %get-tuple-element.28), channel_id=1, source_target_pairs={{0,1},{1,0},{2,3},{3,2},{4,5},{5,4},{6,7},{7,6},{8,9},{9,8},{10,11... | collective-permute-start | bytes 1204232 | tf_op jit(solution)/shard_map/ppermute | solution.py:252
  34.3 5.7 %collective-permute-start.16 = (bf16[8,6272]{1,0:T(8,128)(2,1)S(1)}, bf16[8,6272]{1,0:T(8,128)(2,1)S(1)}, u32[]{:S(2)}, u32[]{:S(2)}) collective-permute-start(bf16[8,6272]{1,0:T(8,128)(2,1)S(1)} %get-tuple-element.38), channel_id=1, source_target_pairs={{0,2},{2,0},{4,6},{6,4},{8,10},{10,8},{12,14},{14,12},{1,3},{3,1},... | collective-permute-start | bytes 301064 | tf_op jit(solution)/shard_map/ppermute | solution.py:249
  35.9 6.9 %collective-permute-start.14 = (bf16[8,6272]{1,0:T(8,128)(2,1)S(1)}, bf16[8,6272]{1,0:T(8,128)(2,1)S(1)}, u32[]{:S(2)}, u32[]{:S(2)}) collective-permute-start(bf16[8,6272]{1,0:T(8,128)(2,1)S(1)} %get-tuple-element.36), channel_id=1, source_target_pairs={{0,2},{2,0},{4,6},{6,4},{8,10},{10,8},{12,14},{14,12},{1,3},{3,1},... | collective-permute-start | bytes 301064 | tf_op jit(solution)/shard_map/ppermute | solution.py:249
  36.4 8.4 %collective-permute-start.12 = (bf16[8,6272]{1,0:T(8,128)(2,1)S(1)}, bf16[8,6272]{1,0:T(8,128)(2,1)S(1)}, u32[]{:S(2)}, u32[]{:S(2)}) collective-permute-start(bf16[8,6272]{1,0:T(8,128)(2,1)S(1)} %get-tuple-element.34), channel_id=1, source_target_pairs={{0,2},{2,0},{4,6},{6,4},{8,10},{10,8},{12,14},{14,12},{1,3},{3,1},... | collective-permute-start | bytes 301064 | tf_op jit(solution)/shard_map/ppermute | solution.py:249
  37.9 8.2 %collective-permute-start.11 = (bf16[8,6272]{1,0:T(8,128)(2,1)S(1)}, bf16[8,6272]{1,0:T(8,128)(2,1)S(1)}, u32[]{:S(2)}, u32[]{:S(2)}) collective-permute-start(bf16[8,6272]{1,0:T(8,128)(2,1)S(1)} %get-tuple-element.32), channel_id=1, source_target_pairs={{0,2},{2,0},{4,6},{6,4},{8,10},{10,8},{12,14},{14,12},{1,3},{3,1},... | collective-permute-start | bytes 301064 | tf_op jit(solution)/shard_map/ppermute | solution.py:249
  40.1 9.3 %collective-permute-start.17 = (bf16[8,6272]{1,0:T(8,128)(2,1)S(1)}, bf16[8,6272]{1,0:T(8,128)(2,1)S(1)}, u32[]{:S(2)}, u32[]{:S(2)}) collective-permute-start(bf16[8,6272]{1,0:T(8,128)(2,1)S(1)} %span_sum.5), channel_id=1, source_target_pairs={{0,8},{2,10},{4,12},{6,14},{8,0},{10,2},{12,4},{14,6},{1,9},{3,11}... | collective-permute-start | bytes 301064 | tf_op jit(solution)/shard_map/ppermute | solution.py:246
  42.8 7.1 %collective-permute-start.15 = (bf16[8,6272]{1,0:T(8,128)(2,1)S(1)}, bf16[8,6272]{1,0:T(8,128)(2,1)S(1)}, u32[]{:S(2)}, u32[]{:S(2)}) collective-permute-start(bf16[8,6272]{1,0:T(8,128)(2,1)S(1)} %span_sum.4), channel_id=1, source_target_pairs={{0,12},{2,14},{4,8},{6,10},{8,4},{10,6},{12,0},{14,2},{1,13},{3,15... | collective-permute-start | bytes 301064 | tf_op jit(solution)/shard_map/ppermute | solution.py:246
  44.8 6.0 %collective-permute-start.13 = (bf16[8,6272]{1,0:T(8,128)(2,1)S(1)}, bf16[8,6272]{1,0:T(8,128)(2,1)S(1)}, u32[]{:S(2)}, u32[]{:S(2)}) collective-permute-start(bf16[8,6272]{1,0:T(8,128)(2,1)S(1)} %span_sum.3), channel_id=1, source_target_pairs={{0,4},{2,6},{4,0},{6,2},{8,12},{10,14},{12,8},{14,10},{1,5},{3,7},... | collective-permute-start | bytes 301064 | tf_op jit(solution)/shard_map/ppermute | solution.py:246

commit v7 on v6

--- a/solution.py
+++ b/solution.py
@@ -10,6 +10,7 @@
 EXPERTS = 4
 LANES = 128
 RETURN_ORDER = (1, 3, 2)
+BLOCK_ORDER = (0, 2, 1, 3)
 N_BLOCK = 256
 EXCHANGE_FLOPS = 20_000_000_000
 
@@ -37,20 +38,19 @@
     return jnp.concatenate([ref[...].astype(jnp.float32) for ref in refs], axis=0)
 
 
-def stack_kernel(count, *refs):
-    refs[-1][...] = joined(refs[:count]).astype(jnp.bfloat16)
-
-
-def stack(values, after):
+def stack_kernel(*refs):
+    refs[-1][...] = joined(refs[:-1]).astype(jnp.bfloat16)
+
+
+def stack(values):
     rows = sum(v.shape[0] for v in values)
     return pl.pallas_call(
-        functools.partial(stack_kernel, len(values)),
-        in_specs=[pl.BlockSpec(memory_space=pltpu.VMEM)] * len(values) + [pl.BlockSpec(memory_space=pl.ANY)] * len(after),
+        stack_kernel,
         out_shape=jax.ShapeDtypeStruct((rows, values[0].shape[1]), jnp.bfloat16),
         compiler_params=params(),
         cost_estimate=cost(0),
         name="stack",
-    )(*values, *after)
+    )(*values)
 
 
 def unpacked(refs, out_ref, rows):
@@ -66,9 +66,27 @@
     out_ref[:, width - tail:] = ends.reshape(total, tail).astype(jnp.bfloat16)
 
 
-def gate_up_kernel(n_block, rows, *refs):
+def unpack_kernel(rows, *refs):
+    unpacked(refs[:-1], refs[-1], rows)
+
+
+def unpack(values, rows, width):
+    total = sum(v.shape[0] for v in values)
+    return pl.pallas_call(
+        functools.partial(unpack_kernel, rows),
+        out_shape=jax.ShapeDtypeStruct((total, width), jnp.bfloat16),
+        compiler_params=params(),
+        cost_estimate=cost(1_000_000_000),
+        name="unpack",
+    )(*values)
+
+
+def gate_up_kernel(n_block, rows, first_ref, *refs):
     rows_in, (gate_ref, up_ref, hidden_ref, rows_ref) = refs[:-4], refs[-4:]
-    unpacked(rows_in, rows_ref, rows)
+    count = first_ref.shape[0]
+    rows_ref[:count, :] = first_ref[...]
+    if rows_in:
+        unpacked(rows_in, rows_ref.at[count:, :], rows)
     for n in range(0, gate_ref.shape[1], n_block):
         columns = slice(n, n + n_block)
         gate = jnp.dot(rows_ref[...], gate_ref[:, columns], preferred_element_type=jnp.float32)
@@ -76,27 +94,26 @@
         hidden_ref[:, columns] = (gate / (1.0 + jnp.exp(-gate)) * up).astype(jnp.bfloat16)
 
 
-def gate_up(blocks, gate_weight, up_weight, rows):
-    total = sum(r.shape[0] for r in blocks)
+def gate_up(first, blocks, gate_weight, up_weight, rows):
+    total = sum(r.shape[0] for r in [first] + blocks)
     width, units = gate_weight.shape
     return pl.pallas_call(
         functools.partial(gate_up_kernel, block_of(units, N_BLOCK), rows),
-        in_specs=[pl.BlockSpec(memory_space=pltpu.VMEM)] * (len(blocks) + 2),
+        in_specs=[pl.BlockSpec(memory_space=pltpu.VMEM)] * (len(blocks) + 3),
         out_shape=jax.ShapeDtypeStruct((total, units), jnp.bfloat16),
         scratch_shapes=[pltpu.VMEM((total, width), jnp.bfloat16)],
-        compiler_params=params(),
+        compiler_params=params(8),
         cost_estimate=cost(4 * total * width * units),
         name="gate_up",
-    )(*blocks, in_vmem(gate_weight), in_vmem(up_weight))
-
-
-def down_kernel(rows, parts, *refs):
-    hidden_refs, down_ref, outs = refs[:parts], refs[parts], refs[parts + 1:]
+    )(first, *blocks, in_vmem(gate_weight), in_vmem(up_weight))
+
+
+def down_kernel(rows, hidden_ref, down_ref, *outs):
     count, width = outs[0].shape
-    hidden = jnp.concatenate([ref[...] for ref in hidden_refs], axis=0)
     tail = down_ref.shape[1] // rows
-    blocks = (hidden.shape[0] // rows, rows, tail)
+    blocks = (hidden_ref.shape[0] // rows, rows, tail)
     last = lax.broadcasted_iota(jnp.int32, blocks, 1) == rows - 1
+    hidden = hidden_ref[...]
     ends = jnp.dot(hidden, down_ref[:, width:], preferred_element_type=jnp.float32).reshape(blocks)
     for i in range(rows - 1):
         columns = slice(i * tail, (i + 1) * tail)
@@ -106,20 +123,19 @@
             ref[:, columns] = value[j * count:(j + 1) * count].astype(ref.dtype)
 
 
-def down(hiddens, down_weight, pair, rows):
-    total, units = hiddens[0].shape
+def down(hidden, down_weight, span, pair, rows):
+    total, units = hidden.shape
     width = down_weight.shape[1] // rows * (rows - 1)
-    shape = (total // pair, width)
-    out_shape = [jax.ShapeDtypeStruct(shape, jnp.bfloat16 if p else jnp.float32) for _ in hiddens for p in range(pair)]
+    shape = (total // (span * pair), width)
     outs = pl.pallas_call(
-        functools.partial(down_kernel, rows, len(hiddens)),
-        in_specs=[pl.BlockSpec(memory_space=pltpu.VMEM)] * (len(hiddens) + 1),
-        out_shape=out_shape,
-        compiler_params=params(),
-        cost_estimate=cost(2 * total * len(hiddens) * width * units),
+        functools.partial(down_kernel, rows),
+        in_specs=[pl.BlockSpec(memory_space=pltpu.VMEM)] * 2,
+        out_shape=[jax.ShapeDtypeStruct(shape, jnp.bfloat16 if p else jnp.float32) for p in range(pair) for _ in range(span)],
+        compiler_params=params(),
+        cost_estimate=cost(2 * total * width * units),
         name="down",
-    )(*hiddens, in_vmem(down_weight))
-    return [outs[i:i + pair] for i in range(0, len(outs), pair)]
+    )(hidden, in_vmem(down_weight))
+    return [outs[t::span] for t in range(span)]
 
 
 def pair_sum_kernel(count, *refs):
@@ -253,21 +269,20 @@
 
     own_expert = (lax.axis_index("attn") // span).astype(jnp.int32).reshape(1)
     sides, *packed = pack(own_expert, tokens, expert_ids, route_weights)
-    column = packed[:1] + [over_experts(packed[s], s) for s in range(1, EXPERTS)]
+    column = {s: over_experts(packed[s], s) if s else packed[0] for s in range(EXPERTS)}
+    column = [column[s] for s in BLOCK_ORDER]
     parts = [column] + [[over_span(b, t) for b in column] for t in range(1, span)]
-    hiddens, after = [], [b for part in parts[1:2] for b in part[:2]]
-    for part in parts:
-        group = stack(part, after)
-        group = [group] + [over_pair(group, p) for p in range(1, pair)]
-        after = [gate_up(group, gate_weight, up_weight, rows)]
-        hiddens += after
+    groups = [stack(part) for part in parts]
+    others = [over_pair(g, p) for p in range(1, pair) for g in groups]
+    plane = unpack([b for part in parts for b in part], rows, width)
+    hidden = gate_up(plane, others, gate_weight, up_weight, rows)
 
     sums = [[] for _ in range(EXPERTS)]
-    for t, (keep, *sends) in enumerate(down(hiddens, down_weight, pair, rows)):
+    for t, (keep, *sends) in enumerate(down(hidden, down_weight, span, pair, rows)):
         arrays = [keep] + [over_pair(b, -p) for p, b in enumerate(sends, 1)]
         blocks = pair_sum(arrays, rows, jnp.bfloat16 if t else jnp.float32)
-        for s in range(EXPERTS):
-            sums[s].append(over_span(blocks[s], -t) if t else blocks[s])
+        for s, block in zip(BLOCK_ORDER, blocks):
+            sums[s].append(over_span(block, -t) if t else block)
 
     returned = [over_experts(span_sum(sums[s]), s) for s in RETURN_ORDER]
     return combine(sides, sums[0], returned, width)

time: 51.8 us -> 48.6 us (0.938)
  Pallas kernels: 15.7 us -> 9.62 us
  starting transfers between devices: 20.6 us -> 22.7 us
  waiting for transfers between devices: 15.2 us -> 15.8 us
    pallas_call x2 -> x1, Pallas kernels: 10.8 us -> 4.52 us  [gate_up(): pl.pallas_call(functools.partial(gate_up_kernel, block_of(units, N_BLOCK)...]
    ppermute x8, waiting for transfers between devices: 1.57 us -> 5.52 us  [over_span(): lax.ppermute(value, 'attn', [(i, i // span * span + (i + shift) % span) f...]
    ppermute x6, waiting for transfers between devices: 10.7 us -> 7.61 us  [over_experts(): lax.ppermute(value, 'attn', [(i, (i // span ^ other) * span + i % span) f...]
    ppermute x8, starting transfers between devices: 8.23 us -> 9.59 us  [over_span(): lax.ppermute(value, 'attn', [(i, i // span * span + (i + shift) % span) f...]
    ppermute x6, starting transfers between devices: 11.6 us -> 12.4 us  [over_experts(): lax.ppermute(value, 'attn', [(i, (i // span ^ other) * span + i % span) f...]
    pallas_call x3 -> x4, Pallas kernels: 2.43 us -> 2.66 us  [the longest x1 2.38 us: down(): pl.pallas_call(functools.partial(down_kernel, rows), in_specs=[pl.BlockSp...]
  transfers between devices with their start and end apart: 18 -> 18, of which waited for: 7 -> 10; matrix products, arithmetic and copies ran while one was open for 0% -> 0% of each run, Pallas kernels for 11% -> 1%
where the time goes in v7:
time: 48.6 us; the launch traced here: 48.4 us
  starting transfers between devices  22.7 us (47%)
  waiting for transfers between devices  15.8 us (33%)
  Pallas kernels  9.62 us (20%)
    ppermute x6, starting transfers between devices, over_experts(): lax.ppermute(value, 'attn', [(i, (i // span ^ other) * span + i % span) f...  12.4 us
    ppermute x8, starting transfers between devices, over_span(): lax.ppermute(value, 'attn', [(i, i // span * span + (i + shift) % span) f...  9.59 us
    ppermute x6, waiting for transfers between devices, over_experts(): lax.ppermute(value, 'attn', [(i, (i // span ^ other) * span + i % span) f...  7.61 us
    ppermute x8, waiting for transfers between devices, over_span(): lax.ppermute(value, 'attn', [(i, i // span * span + (i + shift) % span) f...  5.52 us
    pallas_call x1, Pallas kernels, gate_up(): pl.pallas_call(functools.partial(gate_up_kernel, block_of(units, N_BLOCK)...  4.52 us
    ppermute x4, waiting for transfers between devices, over_pair(): lax.ppermute(value, 'ffn', [(i, (i + shift) % pair) for i in range(pair)])  2.66 us
    pallas_call x1, Pallas kernels, down(): pl.pallas_call(functools.partial(down_kernel, rows), in_specs=[pl.BlockSp...  2.38 us
    pallas_call x1, Pallas kernels, pack(): pl.pallas_call(pack_kernel, in_specs=[pl.BlockSpec(memory_space=pltpu.SME...  1.3 us
  transfers between devices with their start and end apart: 18, of which 10 were waited for; matrix products, arithmetic and copies ran while one was open for 0% of the time, Pallas kernels for 1%

profile of v7, /device:TPU:0, one launch (start us, length us, event | category | flops | bytes accessed | tf_op | source)
XLA Modules:
  0.0 48.4 jit_solution(13474604755360064848)
XLA Ops:
  0.0 1.3 %pack.1 = (f32[8,1024]{1,0:T(8,128)S(1)}, bf16[8,6272]{1,0:T(8,128)(2,1)S(1)}, bf16[8,6272]{1,0:T(8,128)(2,1)S(1)}, bf16[8,6272]{1,0:T(8,128)(2,1)S(1)}, bf16[8,6272]{1,0:T(8,128)(2,1)S(1)}) custom-call(s32[1]{0:T(128)} %bitcast.own_expert, bf16[8,7168]{1,0:T(8,128)(2,1)} %tokens_hbm.1, s32[3,8]{1,0:T(4,128)} %bitcast.9, f32[3,8]{1,0:T(4,128)} %bitcast.10), custom_call_target="tpu_custom_call" | custom-call | flops 20000000000 | tf_op jit(solution)/shard_map/pack/pallas_call | solution.py:214
  1.4 4.1 %collective-permute-start = (bf16[8,6272]{1,0:T(8,128)(2,1)S(1)}, bf16[8,6272]{1,0:T(8,128)(2,1)S(1)}, u32[]{:S(2)}, u32[]{:S(2)}) collective-permute-start(bf16[8,6272]{1,0:T(8,128)(2,1)S(1)} %get-tuple-element.24), channel_id=1, source_target_pairs={{0,8},{2,10},{4,12},{6,14},{8,0},{10,2},{12,4},{14,6},{1,9},{3,11}... | collective-permute-start | bytes 301064 | tf_op jit(solution)/shard_map/ppermute | solution.py:262
  5.5 1.6 %collective-permute-start.1 = (bf16[8,6272]{1,0:T(8,128)(2,1)S(1)}, bf16[8,6272]{1,0:T(8,128)(2,1)S(1)}, u32[]{:S(2)}, u32[]{:S(2)}) collective-permute-start(bf16[8,6272]{1,0:T(8,128)(2,1)S(1)} %get-tuple-element.25), channel_id=1, source_target_pairs={{0,4},{2,6},{4,0},{6,2},{8,12},{10,14},{12,8},{14,10},{1,5},{3,7},... | collective-permute-start | bytes 301064 | tf_op jit(solution)/shard_map/ppermute | solution.py:262
  7.0 1.7 %collective-permute-start.3 = (bf16[8,6272]{1,0:T(8,128)(2,1)S(1)}, bf16[8,6272]{1,0:T(8,128)(2,1)S(1)}, u32[]{:S(2)}, u32[]{:S(2)}) collective-permute-start(bf16[8,6272]{1,0:T(8,128)(2,1)S(1)} %get-tuple-element.23.refs_0_), channel_id=1, source_target_pairs={{0,2},{2,0},{4,6},{6,4},{8,10},{10,8},{12,14},{14,12},{1,3},{3,1},... | collective-permute-start | bytes 301064 | tf_op jit(solution)/shard_map/ppermute | solution.py:265
  8.8 2.9 %collective-permute-done.refs_1_ = bf16[8,6272]{1,0:T(8,128)(2,1)S(1)} collective-permute-done((bf16[8,6272]{1,0:T(8,128)(2,1)S(1)}, bf16[8,6272]{1,0:T(8,128)(2,1)S(1)}, u32[]{:S(2)}, u32[]{:S(2)}) %collective-permute-start) | collective-permute-done | bytes 100384 | tf_op jit(solution)/shard_map/ppermute | solution.py:262
  11.7 1.7 %collective-permute-start.4 = (bf16[8,6272]{1,0:T(8,128)(2,1)S(1)}, bf16[8,6272]{1,0:T(8,128)(2,1)S(1)}, u32[]{:S(2)}, u32[]{:S(2)}) collective-permute-start(bf16[8,6272]{1,0:T(8,128)(2,1)S(1)} %collective-permute-done.refs_1_), channel_id=1, source_target_pairs={{0,2},{2,0},{4,6},{6,4},{8,10},{10,8},{12,14},{14,12},{1,3},{3,1},... | collective-permute-start | bytes 301064 | tf_op jit(solution)/shard_map/ppermute | solution.py:265
  13.4 0.3 collective-permute-start.5
  13.8 1.7 %collective-permute-start.6 = (bf16[8,6272]{1,0:T(8,128)(2,1)S(1)}, bf16[8,6272]{1,0:T(8,128)(2,1)S(1)}, u32[]{:S(2)}, u32[]{:S(2)}) collective-permute-start(bf16[8,6272]{1,0:T(8,128)(2,1)S(1)} %collective-permute-done.2.refs_3_), channel_id=1, source_target_pairs={{0,2},{2,0},{4,6},{6,4},{8,10},{10,8},{12,14},{14,12},{1,3},{3,1},... | collective-permute-start | bytes 301064 | tf_op jit(solution)/shard_map/ppermute | solution.py:265
  15.5 0.1 collective-permute-start.7
  15.6 1.6 %collective-permute-done.4.refs_5_.refs_1_ = bf16[8,6272]{1,0:T(8,128)(2,1)S(1)} collective-permute-done((bf16[8,6272]{1,0:T(8,128)(2,1)S(1)}, bf16[8,6272]{1,0:T(8,128)(2,1)S(1)}, u32[]{:S(2)}, u32[]{:S(2)}) %collective-permute-start.4) | collective-permute-done | bytes 100384 | tf_op jit(solution)/shard_map/ppermute | solution.py:265
  17.2 1.3 %collective-permute-done.5.refs_6_.refs_2_ = bf16[8,6272]{1,0:T(8,128)(2,1)S(1)} collective-permute-done((bf16[8,6272]{1,0:T(8,128)(2,1)S(1)}, bf16[8,6272]{1,0:T(8,128)(2,1)S(1)}, u32[]{:S(2)}, u32[]{:S(2)}) %collective-permute-start.5) | collective-permute-done | bytes 100384 | tf_op jit(solution)/shard_map/ppermute | solution.py:265
  18.5 1.1 %collective-permute-done.6.refs_7_.refs_3_ = bf16[8,6272]{1,0:T(8,128)(2,1)S(1)} collective-permute-done((bf16[8,6272]{1,0:T(8,128)(2,1)S(1)}, bf16[8,6272]{1,0:T(8,128)(2,1)S(1)}, u32[]{:S(2)}, u32[]{:S(2)}) %collective-permute-start.6) | collective-permute-done | bytes 100384 | tf_op jit(solution)/shard_map/ppermute | solution.py:265
  19.6 0.1 collective-permute-start.8
  19.7 0.2 unpack.1.first_ref
  20.0 1.4 %collective-permute-done.8.refs_1_ = bf16[32,6272]{1,0:T(8,128)(2,1)S(1)} collective-permute-done((bf16[32,6272]{1,0:T(8,128)(2,1)S(1)}, bf16[32,6272]{1,0:T(8,128)(2,1)S(1)}, u32[]{:S(2)}, u32[]{:S(2)}) %collective-permute-start.8) | collective-permute-done | bytes 401440 | tf_op jit(solution)/shard_map/ppermute | solution.py:268
  21.5 4.5 %gate_up.1.hidden_ref = bf16[128,1024]{1,0:T(8,128)(2,1)S(1)} custom-call(bf16[64,7168]{1,0:T(8,128)(2,1)S(1)} %unpack.1.first_ref, bf16[32,6272]{1,0:T(8,128)(2,1)S(1)} %collective-permute-done.7.refs_0_, bf16[32,6272]{1,0:T(8,128)(2,1)S(1)} %collective-permute-done.8.refs_1_, bf16[7168,1024]{1,0:T(8,128)(2,1)S(1)} %bitcast.4, bf16[7168,1024]{1,0:T(8,128)(2,1)S(1)} %bitcast.6), custom_call_target="tpu_custom_call" | custom-call | flops 3758096384 | tf_op jit(solution)/shard_map/gate_up/pallas_call | solution.py:100
  26.1 2.4 %down.1 = (f32[32,6272]{1,0:T(8,128)S(1)}, f32[32,6272]{1,0:T(8,128)S(1)}, bf16[32,6272]{1,0:T(8,128)(2,1)S(1)}, bf16[32,6272]{1,0:T(8,128)(2,1)S(1)}) custom-call(bf16[128,1024]{1,0:T(8,128)(2,1)S(1)} %gate_up.1.hidden_ref, bf16[1024,7168]{1,0:T(8,128)(2,1)S(1)} %bitcast.8), custom_call_target="tpu_custom_call" | custom-call | flops 1644167168 | tf_op jit(solution)/shard_map/down/pallas_call | solution.py:130
  28.5 0.2 collective-permute-start.10
  28.7 0.4 collective-permute-start.9
  29.0 1.2 %collective-permute-done.10.refs_1_ = bf16[32,6272]{1,0:T(8,128)(2,1)S(1)} collective-permute-done((bf16[32,6272]{1,0:T(8,128)(2,1)S(1)}, bf16[32,6272]{1,0:T(8,128)(2,1)S(1)}, u32[]{:S(2)}, u32[]{:S(2)}) %collective-permute-start.10) | collective-permute-done | bytes 401440 | tf_op jit(solution)/shard_map/ppermute | solution.py:268
  30.3 1.7 %collective-permute-start.16 = (bf16[8,6272]{1,0:T(8,128)(2,1)S(1)}, bf16[8,6272]{1,0:T(8,128)(2,1)S(1)}, u32[]{:S(2)}, u32[]{:S(2)}) collective-permute-start(bf16[8,6272]{1,0:T(8,128)(2,1)S(1)} %get-tuple-element.38), channel_id=1, source_target_pairs={{0,2},{2,0},{4,6},{6,4},{8,10},{10,8},{12,14},{14,12},{1,3},{3,1},... | collective-permute-start | bytes 301064 | tf_op jit(solution)/shard_map/ppermute | solution.py:265
  32.1 0.3 collective-permute-start.14
  32.4 1.7 %collective-permute-start.12 = (bf16[8,6272]{1,0:T(8,128)(2,1)S(1)}, bf16[8,6272]{1,0:T(8,128)(2,1)S(1)}, u32[]{:S(2)}, u32[]{:S(2)}) collective-permute-start(bf16[8,6272]{1,0:T(8,128)(2,1)S(1)} %get-tuple-element.34), channel_id=1, source_target_pairs={{0,2},{2,0},{4,6},{6,4},{8,10},{10,8},{12,14},{14,12},{1,3},{3,1},... | collective-permute-start | bytes 301064 | tf_op jit(solution)/shard_map/ppermute | solution.py:265
  34.1 0.3 collective-permute-start.11
  34.5 1.5 %collective-permute-done.16.refs_1_ = bf16[8,6272]{1,0:T(8,128)(2,1)S(1)} collective-permute-done((bf16[8,6272]{1,0:T(8,128)(2,1)S(1)}, bf16[8,6272]{1,0:T(8,128)(2,1)S(1)}, u32[]{:S(2)}, u32[]{:S(2)}) %collective-permute-start.16) | collective-permute-done | bytes 100384 | tf_op jit(solution)/shard_map/ppermute | solution.py:265
  36.1 2.7 %collective-permute-start.17 = (bf16[8,6272]{1,0:T(8,128)(2,1)S(1)}, bf16[8,6272]{1,0:T(8,128)(2,1)S(1)}, u32[]{:S(2)}, u32[]{:S(2)}) collective-permute-start(bf16[8,6272]{1,0:T(8,128)(2,1)S(1)} %span_sum.5), channel_id=1, source_target_pairs={{0,8},{2,10},{4,12},{6,14},{8,0},{10,2},{12,4},{14,6},{1,9},{3,11}... | collective-permute-start | bytes 301064 | tf_op jit(solution)/shard_map/ppermute | solution.py:262
  38.8 3.9 %collective-permute-start.15 = (bf16[8,6272]{1,0:T(8,128)(2,1)S(1)}, bf16[8,6272]{1,0:T(8,128)(2,1)S(1)}, u32[]{:S(2)}, u32[]{:S(2)}) collective-permute-start(bf16[8,6272]{1,0:T(8,128)(2,1)S(1)} %span_sum.4), channel_id=1, source_target_pairs={{0,12},{2,14},{4,8},{6,10},{8,4},{10,6},{12,0},{14,2},{1,13},{3,15... | collective-permute-start | bytes 301064 | tf_op jit(solution)/shard_map/ppermute | solution.py:262
  42.7 0.1 collective-permute-start.13
  42.8 2.6 %collective-permute-done.17.refs_4_ = bf16[8,6272]{1,0:T(8,128)(2,1)S(1)} collective-permute-done((bf16[8,6272]{1,0:T(8,128)(2,1)S(1)}, bf16[8,6272]{1,0:T(8,128)(2,1)S(1)}, u32[]{:S(2)}, u32[]{:S(2)}) %collective-permute-start.17) | collective-permute-done | bytes 100384 | tf_op jit(solution)/shard_map/ppermute | solution.py:262
  45.4 1.0 %collective-permute-done.15.refs_3_ = bf16[8,6272]{1,0:T(8,128)(2,1)S(1)} collective-permute-done((bf16[8,6272]{1,0:T(8,128)(2,1)S(1)}, bf16[8,6272]{1,0:T(8,128)(2,1)S(1)}, u32[]{:S(2)}, u32[]{:S(2)}) %collective-permute-start.15) | collective-permute-done | bytes 100384 | tf_op jit(solution)/shard_map/ppermute | solution.py:262
  46.4 1.0 %collective-permute-done.13.refs_2_ = bf16[8,6272]{1,0:T(8,128)(2,1)S(1)} collective-permute-done((bf16[8,6272]{1,0:T(8,128)(2,1)S(1)}, bf16[8,6272]{1,0:T(8,128)(2,1)S(1)}, u32[]{:S(2)}, u32[]{:S(2)}) %collective-permute-start.13) | collective-permute-done | bytes 100384 | tf_op jit(solution)/shard_map/ppermute | solution.py:262
  47.5 0.9 %combine.1 = bf16[8,7168]{1,0:T(8,128)(2,1)} custom-call(f32[8,1024]{1,0:T(8,128)S(1)} %get-tuple-element.22.sides_ref, f32[8,6272]{1,0:T(8,128)S(1)} %get-tuple-element.29.refs_0_, bf16[8,6272]{1,0:T(8,128)(2,1)S(1)} %collective-permute-done.11.refs_1_, bf16[8,6272]{1,0:T(8,128)(2,1)S(1)} %collective-permute-done.13.refs_2_, ...), custom_call_target="tpu_custom_call" | custom-call | tf_op jit(solution)/shard_map/combine/pallas_call | solution.py:247
  (43 shorter events, 0.4 us)
Async XLA Ops:
  0.0 21.4 %slice-start = ((s8[14680064]{0:T(1024)(128)(4,1)}), s8[4194304]{0:T(1024)(128)(4,1)S(1)}, s32[]{:S(2)}) async-start(s8[14680064]{0:T(1024)(128)(4,1)} %bitcast.3), calls=%async_computation | async-start | bytes 8388608
  0.0 21.4 %slice-start.4 = ((s8[14680064]{0:T(1024)(128)(4,1)}), s8[4194304]{0:T(1024)(128)(4,1)S(1)}, s32[]{:S(2)}) async-start(s8[14680064]{0:T(1024)(128)(4,1)} %bitcast.5), calls=%async_computation.4 | async-start | bytes 8388608
  0.0 21.4 %slice-start.1 = ((s8[14680064]{0:T(1024)(128)(4,1)}), s8[4194304]{0:T(1024)(128)(4,1)S(1)}, s32[]{:S(2)}) async-start(s8[14680064]{0:T(1024)(128)(4,1)} %bitcast.3), calls=%async_computation.1 | async-start | bytes 8388608
  0.0 21.4 %slice-start.2 = ((s8[14680064]{0:T(1024)(128)(4,1)}), s8[4194304]{0:T(1024)(128)(4,1)S(1)}, s32[]{:S(2)}) async-start(s8[14680064]{0:T(1024)(128)(4,1)} %bitcast.3), calls=%async_computation.2 | async-start | bytes 8388608
  0.0 21.4 %slice-start.3 = ((s8[14680064]{0:T(1024)(128)(4,1)}), s8[2097152]{0:T(1024)(128)(4,1)S(1)}, s32[]{:S(2)}) async-start(s8[14680064]{0:T(1024)(128)(4,1)} %bitcast.3), calls=%async_computation.3 | async-start | bytes 4194304
  0.0 21.4 %slice-start.5 = ((s8[14680064]{0:T(1024)(128)(4,1)}), s8[4194304]{0:T(1024)(128)(4,1)S(1)}, s32[]{:S(2)}) async-start(s8[14680064]{0:T(1024)(128)(4,1)} %bitcast.5), calls=%async_computation.5 | async-start | bytes 8388608
  0.0 21.4 %slice-start.6 = ((s8[14680064]{0:T(1024)(128)(4,1)}), s8[4194304]{0:T(1024)(128)(4,1)S(1)}, s32[]{:S(2)}) async-start(s8[14680064]{0:T(1024)(128)(4,1)} %bitcast.5), calls=%async_computation.6 | async-start | bytes 8388608
  0.0 21.4 %slice-start.7 = ((s8[14680064]{0:T(1024)(128)(4,1)}), s8[2097152]{0:T(1024)(128)(4,1)S(1)}, s32[]{:S(2)}) async-start(s8[14680064]{0:T(1024)(128)(4,1)} %bitcast.5), calls=%async_computation.7 | async-start | bytes 4194304
  1.4 10.4 %collective-permute-start = (bf16[8,6272]{1,0:T(8,128)(2,1)S(1)}, bf16[8,6272]{1,0:T(8,128)(2,1)S(1)}, u32[]{:S(2)}, u32[]{:S(2)}) collective-permute-start(bf16[8,6272]{1,0:T(8,128)(2,1)S(1)} %get-tuple-element.24), channel_id=1, source_target_pairs={{0,8},{2,10},{4,12},{6,14},{8,0},{10,2},{12,4},{14,6},{1,9},{3,11}... | collective-permute-start | bytes 301064 | tf_op jit(solution)/shard_map/ppermute | solution.py:262
  5.5 8.0 %collective-permute-start.1 = (bf16[8,6272]{1,0:T(8,128)(2,1)S(1)}, bf16[8,6272]{1,0:T(8,128)(2,1)S(1)}, u32[]{:S(2)}, u32[]{:S(2)}) collective-permute-start(bf16[8,6272]{1,0:T(8,128)(2,1)S(1)} %get-tuple-element.25), channel_id=1, source_target_pairs={{0,4},{2,6},{4,0},{6,2},{8,12},{10,14},{12,8},{14,10},{1,5},{3,7},... | collective-permute-start | bytes 301064 | tf_op jit(solution)/shard_map/ppermute | solution.py:262
  7.0 6.7 %collective-permute-start.2 = (bf16[8,6272]{1,0:T(8,128)(2,1)S(1)}, bf16[8,6272]{1,0:T(8,128)(2,1)S(1)}, u32[]{:S(2)}, u32[]{:S(2)}) collective-permute-start(bf16[8,6272]{1,0:T(8,128)(2,1)S(1)} %get-tuple-element.26), channel_id=1, source_target_pairs={{0,12},{2,14},{4,8},{6,10},{8,4},{10,6},{12,0},{14,2},{1,13},{3,15... | collective-permute-start | bytes 301064 | tf_op jit(solution)/shard_map/ppermute | solution.py:262
  7.0 8.5 %collective-permute-start.3 = (bf16[8,6272]{1,0:T(8,128)(2,1)S(1)}, bf16[8,6272]{1,0:T(8,128)(2,1)S(1)}, u32[]{:S(2)}, u32[]{:S(2)}) collective-permute-start(bf16[8,6272]{1,0:T(8,128)(2,1)S(1)} %get-tuple-element.23.refs_0_), channel_id=1, source_target_pairs={{0,2},{2,0},{4,6},{6,4},{8,10},{10,8},{12,14},{14,12},{1,3},{3,1},... | collective-permute-start | bytes 301064 | tf_op jit(solution)/shard_map/ppermute | solution.py:265
  11.7 5.5 %collective-permute-start.4 = (bf16[8,6272]{1,0:T(8,128)(2,1)S(1)}, bf16[8,6272]{1,0:T(8,128)(2,1)S(1)}, u32[]{:S(2)}, u32[]{:S(2)}) collective-permute-start(bf16[8,6272]{1,0:T(8,128)(2,1)S(1)} %collective-permute-done.refs_1_), channel_id=1, source_target_pairs={{0,2},{2,0},{4,6},{6,4},{8,10},{10,8},{12,14},{14,12},{1,3},{3,1},... | collective-permute-start | bytes 301064 | tf_op jit(solution)/shard_map/ppermute | solution.py:265
  13.4 5.1 %collective-permute-start.5 = (bf16[8,6272]{1,0:T(8,128)(2,1)S(1)}, bf16[8,6272]{1,0:T(8,128)(2,1)S(1)}, u32[]{:S(2)}, u32[]{:S(2)}) collective-permute-start(bf16[8,6272]{1,0:T(8,128)(2,1)S(1)} %collective-permute-done.1.refs_2_), channel_id=1, source_target_pairs={{0,2},{2,0},{4,6},{6,4},{8,10},{10,8},{12,14},{14,12},{1,3},{3,1},... | collective-permute-start | bytes 301064 | tf_op jit(solution)/shard_map/ppermute | solution.py:265
  13.8 5.8 %collective-permute-start.6 = (bf16[8,6272]{1,0:T(8,128)(2,1)S(1)}, bf16[8,6272]{1,0:T(8,128)(2,1)S(1)}, u32[]{:S(2)}, u32[]{:S(2)}) collective-permute-start(bf16[8,6272]{1,0:T(8,128)(2,1)S(1)} %collective-permute-done.2.refs_3_), channel_id=1, source_target_pairs={{0,2},{2,0},{4,6},{6,4},{8,10},{10,8},{12,14},{14,12},{1,3},{3,1},... | collective-permute-start | bytes 301064 | tf_op jit(solution)/shard_map/ppermute | solution.py:265
  15.5 4.5 %collective-permute-start.7 = (bf16[32,6272]{1,0:T(8,128)(2,1)S(1)}, bf16[32,6272]{1,0:T(8,128)(2,1)S(1)}, u32[]{:S(2)}, u32[]{:S(2)}) collective-permute-start(bf16[32,6272]{1,0:T(8,128)(2,1)S(1)} %stack.2), channel_id=1, source_target_pairs={{0,1},{1,0},{2,3},{3,2},{4,5},{5,4},{6,7},{7,6},{8,9},{9,8},{10,11... | collective-permute-start | bytes 1204232 | tf_op jit(solution)/shard_map/ppermute | solution.py:268
  19.6 1.8 %collective-permute-start.8 = (bf16[32,6272]{1,0:T(8,128)(2,1)S(1)}, bf16[32,6272]{1,0:T(8,128)(2,1)S(1)}, u32[]{:S(2)}, u32[]{:S(2)}) collective-permute-start(bf16[32,6272]{1,0:T(8,128)(2,1)S(1)} %stack.3), channel_id=1, source_target_pairs={{0,1},{1,0},{2,3},{3,2},{4,5},{5,4},{6,7},{7,6},{8,9},{9,8},{10,11... | collective-permute-start | bytes 1204232 | tf_op jit(solution)/shard_map/ppermute | solution.py:268
  19.7 6.3 %slice-start.8 = ((s8[14680064]{0:T(1024)(128)(4,1)}), s8[4194304]{0:T(1024)(128)(4,1)S(1)}, s32[]{:S(2)}) async-start(s8[14680064]{0:T(1024)(128)(4,1)} %bitcast.7), calls=%async_computation.8 | async-start | bytes 8388608
  19.9 6.1 %slice-start.9 = ((s8[14680064]{0:T(1024)(128)(4,1)}), s8[4194304]{0:T(1024)(128)(4,1)S(1)}, s32[]{:S(2)}) async-start(s8[14680064]{0:T(1024)(128)(4,1)} %bitcast.7), calls=%async_computation.9 | async-start | bytes 8388608
  20.0 6.1 %slice-start.10 = ((s8[14680064]{0:T(1024)(128)(4,1)}), s8[4194304]{0:T(1024)(128)(4,1)S(1)}, s32[]{:S(2)}) async-start(s8[14680064]{0:T(1024)(128)(4,1)} %bitcast.7), calls=%async_computation.10 | async-start | bytes 8388608
  20.0 6.1 %slice-start.11 = ((s8[14680064]{0:T(1024)(128)(4,1)}), s8[2097152]{0:T(1024)(128)(4,1)S(1)}, s32[]{:S(2)}) async-start(s8[14680064]{0:T(1024)(128)(4,1)} %bitcast.7), calls=%async_computation.11 | async-start | bytes 4194304
  28.5 1.8 %collective-permute-start.10 = (bf16[32,6272]{1,0:T(8,128)(2,1)S(1)}, bf16[32,6272]{1,0:T(8,128)(2,1)S(1)}, u32[]{:S(2)}, u32[]{:S(2)}) collective-permute-start(bf16[32,6272]{1,0:T(8,128)(2,1)S(1)} %get-tuple-element.31), channel_id=1, source_target_pairs={{0,1},{1,0},{2,3},{3,2},{4,5},{5,4},{6,7},{7,6},{8,9},{9,8},{10,11... | collective-permute-start | bytes 1204232 | tf_op jit(solution)/shard_map/ppermute | solution.py:268
  28.7 5.8 %collective-permute-start.9 = (bf16[32,6272]{1,0:T(8,128)(2,1)S(1)}, bf16[32,6272]{1,0:T(8,128)(2,1)S(1)}, u32[]{:S(2)}, u32[]{:S(2)}) collective-permute-start(bf16[32,6272]{1,0:T(8,128)(2,1)S(1)} %get-tuple-element.28), channel_id=1, source_target_pairs={{0,1},{1,0},{2,3},{3,2},{4,5},{5,4},{6,7},{7,6},{8,9},{9,8},{10,11... | collective-permute-start | bytes 1204232 | tf_op jit(solution)/shard_map/ppermute | solution.py:268
  30.3 5.7 %collective-permute-start.16 = (bf16[8,6272]{1,0:T(8,128)(2,1)S(1)}, bf16[8,6272]{1,0:T(8,128)(2,1)S(1)}, u32[]{:S(2)}, u32[]{:S(2)}) collective-permute-start(bf16[8,6272]{1,0:T(8,128)(2,1)S(1)} %get-tuple-element.38), channel_id=1, source_target_pairs={{0,2},{2,0},{4,6},{6,4},{8,10},{10,8},{12,14},{14,12},{1,3},{3,1},... | collective-permute-start | bytes 301064 | tf_op jit(solution)/shard_map/ppermute | solution.py:265
  32.1 6.7 %collective-permute-start.14 = (bf16[8,6272]{1,0:T(8,128)(2,1)S(1)}, bf16[8,6272]{1,0:T(8,128)(2,1)S(1)}, u32[]{:S(2)}, u32[]{:S(2)}) collective-permute-start(bf16[8,6272]{1,0:T(8,128)(2,1)S(1)} %get-tuple-element.36), channel_id=1, source_target_pairs={{0,2},{2,0},{4,6},{6,4},{8,10},{10,8},{12,14},{14,12},{1,3},{3,1},... | collective-permute-start | bytes 301064 | tf_op jit(solution)/shard_map/ppermute | solution.py:265
  32.4 10.3 %collective-permute-start.12 = (bf16[8,6272]{1,0:T(8,128)(2,1)S(1)}, bf16[8,6272]{1,0:T(8,128)(2,1)S(1)}, u32[]{:S(2)}, u32[]{:S(2)}) collective-permute-start(bf16[8,6272]{1,0:T(8,128)(2,1)S(1)} %get-tuple-element.34), channel_id=1, source_target_pairs={{0,2},{2,0},{4,6},{6,4},{8,10},{10,8},{12,14},{14,12},{1,3},{3,1},... | collective-permute-start | bytes 301064 | tf_op jit(solution)/shard_map/ppermute | solution.py:265
  34.1 8.7 %collective-permute-start.11 = (bf16[8,6272]{1,0:T(8,128)(2,1)S(1)}, bf16[8,6272]{1,0:T(8,128)(2,1)S(1)}, u32[]{:S(2)}, u32[]{:S(2)}) collective-permute-start(bf16[8,6272]{1,0:T(8,128)(2,1)S(1)} %get-tuple-element.32), channel_id=1, source_target_pairs={{0,2},{2,0},{4,6},{6,4},{8,10},{10,8},{12,14},{14,12},{1,3},{3,1},... | collective-permute-start | bytes 301064 | tf_op jit(solution)/shard_map/ppermute | solution.py:265
  36.1 9.3 %collective-permute-start.17 = (bf16[8,6272]{1,0:T(8,128)(2,1)S(1)}, bf16[8,6272]{1,0:T(8,128)(2,1)S(1)}, u32[]{:S(2)}, u32[]{:S(2)}) collective-permute-start(bf16[8,6272]{1,0:T(8,128)(2,1)S(1)} %span_sum.5), channel_id=1, source_target_pairs={{0,8},{2,10},{4,12},{6,14},{8,0},{10,2},{12,4},{14,6},{1,9},{3,11}... | collective-permute-start | bytes 301064 | tf_op jit(solution)/shard_map/ppermute | solution.py:262
  38.8 7.7 %collective-permute-start.15 = (bf16[8,6272]{1,0:T(8,128)(2,1)S(1)}, bf16[8,6272]{1,0:T(8,128)(2,1)S(1)}, u32[]{:S(2)}, u32[]{:S(2)}) collective-permute-start(bf16[8,6272]{1,0:T(8,128)(2,1)S(1)} %span_sum.4), channel_id=1, source_target_pairs={{0,12},{2,14},{4,8},{6,10},{8,4},{10,6},{12,0},{14,2},{1,13},{3,15... | collective-permute-start | bytes 301064 | tf_op jit(solution)/shard_map/ppermute | solution.py:262
  42.7 4.7 %collective-permute-start.13 = (bf16[8,6272]{1,0:T(8,128)(2,1)S(1)}, bf16[8,6272]{1,0:T(8,128)(2,1)S(1)}, u32[]{:S(2)}, u32[]{:S(2)}) collective-permute-start(bf16[8,6272]{1,0:T(8,128)(2,1)S(1)} %span_sum.3), channel_id=1, source_target_pairs={{0,4},{2,6},{4,0},{6,2},{8,12},{10,14},{12,8},{14,10},{1,5},{3,7},... | collective-permute-start | bytes 301064 | tf_op jit(solution)/shard_map/ppermute | solution.py:262

commit v8 on v7

--- a/solution.py
+++ b/solution.py
@@ -12,6 +12,7 @@
 RETURN_ORDER = (1, 3, 2)
 BLOCK_ORDER = (0, 2, 1, 3)
 N_BLOCK = 256
+LAST_FLOPS = 5_000_000_000
 EXCHANGE_FLOPS = 20_000_000_000
 
 
@@ -38,19 +39,20 @@
     return jnp.concatenate([ref[...].astype(jnp.float32) for ref in refs], axis=0)
 
 
-def stack_kernel(*refs):
-    refs[-1][...] = joined(refs[:-1]).astype(jnp.bfloat16)
-
-
-def stack(values):
+def stack_kernel(count, *refs):
+    refs[-1][...] = joined(refs[:count]).astype(jnp.bfloat16)
+
+
+def stack(values, after=(), flops=0):
     rows = sum(v.shape[0] for v in values)
     return pl.pallas_call(
-        stack_kernel,
+        functools.partial(stack_kernel, len(values)),
+        in_specs=[pl.BlockSpec(memory_space=pltpu.VMEM)] * len(values) + [pl.BlockSpec(memory_space=pl.ANY)] * len(after),
         out_shape=jax.ShapeDtypeStruct((rows, values[0].shape[1]), jnp.bfloat16),
         compiler_params=params(),
-        cost_estimate=cost(0),
+        cost_estimate=cost(flops),
         name="stack",
-    )(*values)
+    )(*values, *after)
 
 
 def unpacked(refs, out_ref, rows):
@@ -138,25 +140,26 @@
     return [outs[t::span] for t in range(span)]
 
 
-def pair_sum_kernel(count, *refs):
-    outs = refs[count:]
+def pair_sum_kernel(count, places, *refs):
+    outs = refs[-len(places):]
     rows = outs[0].shape[0]
-    for i, out_ref in enumerate(outs):
-        part = slice(i * rows, (i + 1) * rows)
+    for place, out_ref in zip(places, outs):
+        part = slice(place * rows, (place + 1) * rows)
         value = refs[0][part, :]
         for ref in refs[1:count]:
             value += ref[part, :].astype(jnp.float32)
         out_ref[...] = value.astype(out_ref.dtype)
 
 
-def pair_sum(arrays, rows, dtype):
-    total, width = arrays[0].shape
-    return pl.pallas_call(
-        functools.partial(pair_sum_kernel, len(arrays)),
-        out_shape=[jax.ShapeDtypeStruct((rows, width), dtype)] * (total // rows),
+def pair_sum(arrays, rows, dtype, places, after=()):
+    width = arrays[0].shape[1]
+    return pl.pallas_call(
+        functools.partial(pair_sum_kernel, len(arrays), places),
+        in_specs=[pl.BlockSpec(memory_space=pltpu.VMEM)] * len(arrays) + [pl.BlockSpec(memory_space=pl.ANY)] * len(after),
+        out_shape=[jax.ShapeDtypeStruct((rows, width), dtype)] * len(places),
         compiler_params=params(),
         name="pair_sum",
-    )(*arrays)
+    )(*arrays, *after)
 
 
 def span_sum_kernel(*refs):
@@ -272,20 +275,37 @@
     column = {s: over_experts(packed[s], s) if s else packed[0] for s in range(EXPERTS)}
     column = [column[s] for s in BLOCK_ORDER]
     parts = [column] + [[over_span(b, t) for b in column] for t in range(1, span)]
-    groups = [stack(part) for part in parts]
+    groups = [stack(column)]
+    for part in parts[1:]:
+        groups += [stack(part[:-1]), stack(part[-1:], (), LAST_FLOPS)]
     others = [over_pair(g, p) for p in range(1, pair) for g in groups]
     plane = unpack([b for part in parts for b in part], rows, width)
     hidden = gate_up(plane, others, gate_weight, up_weight, rows)
 
-    sums = [[] for _ in range(EXPERTS)]
-    for t, (keep, *sends) in enumerate(down(hidden, down_weight, span, pair, rows)):
-        arrays = [keep] + [over_pair(b, -p) for p, b in enumerate(sends, 1)]
-        blocks = pair_sum(arrays, rows, jnp.bfloat16 if t else jnp.float32)
-        for s, block in zip(BLOCK_ORDER, blocks):
-            sums[s].append(over_span(block, -t) if t else block)
-
-    returned = [over_experts(span_sum(sums[s]), s) for s in RETURN_ORDER]
-    return combine(sides, sums[0], returned, width)
+    def paired(keep, sends):
+        return [keep] + [over_pair(b, -p) for p, b in enumerate(sends, 1)]
+
+    (own_keep, *own_sends), *far = down(hidden, down_weight, span, pair, rows)
+    far = [paired(keep, sends) for keep, *sends in far]
+    order = (2, 3, 1, 0)
+    blocks = [{} for _ in far]
+    sums, returned, after = {}, {}, []
+    for wave in (order[:2], order[2:]):
+        places = [BLOCK_ORDER.index(s) for s in wave]
+        for t, arrays in enumerate(far):
+            blocks[t].update(zip(wave, pair_sum(arrays, rows, jnp.bfloat16, places, after)))
+        if not sums:
+            first = [blocks[t][s] for t in range(len(far)) for s in wave][:1]
+            own_sends = [stack([b], first) for b in own_sends]
+            own = pair_sum(paired(own_keep, own_sends), rows, jnp.float32, range(EXPERTS))
+            own = dict(zip(BLOCK_ORDER, own))
+        for s in wave:
+            sums[s] = [own[s]] + [over_span(b[s], -t) for t, b in enumerate(blocks, 1)]
+            if s:
+                total = span_sum(sums[s])
+                returned[s] = over_experts(total, s)
+                after = [total]
+    return combine(sides, sums[0], [returned[s] for s in RETURN_ORDER], width)
 
 
 def solution(mesh):

time: 48.6 us -> 50.3 us (1.035)
  waiting for transfers between devices: 15.8 us -> 18.8 us
  starting transfers between devices: 22.7 us -> 21 us
    ppermute x8, waiting for transfers between devices: 5.52 us -> 10.7 us  [over_span(): lax.ppermute(value, 'attn', [(i, i // span * span + (i + shift) % span) f...]
    ppermute x6, waiting for transfers between devices: 7.61 us -> 5.55 us  [over_experts(): lax.ppermute(value, 'attn', [(i, (i // span ^ other) * span + i % span) f...]
    ppermute x6, starting transfers between devices: 12.4 us -> 10.4 us  [over_experts(): lax.ppermute(value, 'attn', [(i, (i // span ^ other) * span + i % span) f...]
    ppermute x4 -> x5, waiting for transfers between devices: 2.66 us -> 2.6 us  [over_pair(): lax.ppermute(value, 'ffn', [(i, (i + shift) % pair) for i in range(pair)])]
  transfers between devices with their start and end apart: 18 -> 19, of which waited for: 10 -> 10; matrix products, arithmetic and copies ran while one was open for 0% -> 0% of each run, Pallas kernels for 1% -> 1%
where the time goes in v8:
time: 50.3 us; the launch traced here: 50.2 us
  starting transfers between devices  21 us (42%)
  waiting for transfers between devices  18.8 us (37%)
  Pallas kernels  9.98 us (20%)
    ppermute x8, waiting for transfers between devices, over_span(): lax.ppermute(value, 'attn', [(i, i // span * span + (i + shift) % span) f...  10.7 us
    ppermute x6, starting transfers between devices, over_experts(): lax.ppermute(value, 'attn', [(i, (i // span ^ other) * span + i % span) f...  10.4 us
    ppermute x8, starting transfers between devices, over_span(): lax.ppermute(value, 'attn', [(i, i // span * span + (i + shift) % span) f...  9.93 us
    ppermute x6, waiting for transfers between devices, over_experts(): lax.ppermute(value, 'attn', [(i, (i // span ^ other) * span + i % span) f...  5.55 us
    pallas_call x1, Pallas kernels, gate_up(): pl.pallas_call(functools.partial(gate_up_kernel, block_of(units, N_BLOCK)...  4.69 us
    ppermute x5, waiting for transfers between devices, over_pair(): lax.ppermute(value, 'ffn', [(i, (i + shift) % pair) for i in range(pair)])  2.6 us
    pallas_call x1, Pallas kernels, down(): pl.pallas_call(functools.partial(down_kernel, rows), in_specs=[pl.BlockSp...  2.5 us
    pallas_call x1, Pallas kernels, pack(): pl.pallas_call(pack_kernel, in_specs=[pl.BlockSpec(memory_space=pltpu.SME...  1.3 us
  transfers between devices with their start and end apart: 19, of which 10 were waited for; matrix products, arithmetic and copies ran while one was open for 0% of the time, Pallas kernels for 1%

profile of v8, /device:TPU:0, one launch (start us, length us, event | category | flops | bytes accessed | tf_op | source)
XLA Modules:
  0.0 50.2 jit_solution(48796129340781429)
XLA Ops:
  0.0 1.3 %pack.1 = (f32[8,1024]{1,0:T(8,128)S(1)}, bf16[8,6272]{1,0:T(8,128)(2,1)S(1)}, bf16[8,6272]{1,0:T(8,128)(2,1)S(1)}, bf16[8,6272]{1,0:T(8,128)(2,1)S(1)}, bf16[8,6272]{1,0:T(8,128)(2,1)S(1)}) custom-call(s32[1]{0:T(128)} %bitcast.own_expert, bf16[8,7168]{1,0:T(8,128)(2,1)} %tokens_hbm.1, s32[3,8]{1,0:T(4,128)} %bitcast.9, f32[3,8]{1,0:T(4,128)} %bitcast.10), custom_call_target="tpu_custom_call" | custom-call | flops 20000000000 | tf_op jit(solution)/shard_map/pack/pallas_call | solution.py:217
  1.4 4.1 %collective-permute-start = (bf16[8,6272]{1,0:T(8,128)(2,1)S(1)}, bf16[8,6272]{1,0:T(8,128)(2,1)S(1)}, u32[]{:S(2)}, u32[]{:S(2)}) collective-permute-start(bf16[8,6272]{1,0:T(8,128)(2,1)S(1)} %get-tuple-element.24), channel_id=1, source_target_pairs={{0,8},{2,10},{4,12},{6,14},{8,0},{10,2},{12,4},{14,6},{1,9},{3,11}... | collective-permute-start | bytes 301064 | tf_op jit(solution)/shard_map/ppermute | solution.py:265
  5.5 1.6 %collective-permute-start.1 = (bf16[8,6272]{1,0:T(8,128)(2,1)S(1)}, bf16[8,6272]{1,0:T(8,128)(2,1)S(1)}, u32[]{:S(2)}, u32[]{:S(2)}) collective-permute-start(bf16[8,6272]{1,0:T(8,128)(2,1)S(1)} %get-tuple-element.25), channel_id=1, source_target_pairs={{0,4},{2,6},{4,0},{6,2},{8,12},{10,14},{12,8},{14,10},{1,5},{3,7},... | collective-permute-start | bytes 301064 | tf_op jit(solution)/shard_map/ppermute | solution.py:265
  7.0 1.7 %collective-permute-start.3 = (bf16[8,6272]{1,0:T(8,128)(2,1)S(1)}, bf16[8,6272]{1,0:T(8,128)(2,1)S(1)}, u32[]{:S(2)}, u32[]{:S(2)}) collective-permute-start(bf16[8,6272]{1,0:T(8,128)(2,1)S(1)} %get-tuple-element.23.refs_0_), channel_id=1, source_target_pairs={{0,2},{2,0},{4,6},{6,4},{8,10},{10,8},{12,14},{14,12},{1,3},{3,1},... | collective-permute-start | bytes 301064 | tf_op jit(solution)/shard_map/ppermute | solution.py:268
  8.8 2.9 %collective-permute-done.refs_1_ = bf16[8,6272]{1,0:T(8,128)(2,1)S(1)} collective-permute-done((bf16[8,6272]{1,0:T(8,128)(2,1)S(1)}, bf16[8,6272]{1,0:T(8,128)(2,1)S(1)}, u32[]{:S(2)}, u32[]{:S(2)}) %collective-permute-start) | collective-permute-done | bytes 100384 | tf_op jit(solution)/shard_map/ppermute | solution.py:265
  11.7 1.7 %collective-permute-start.4 = (bf16[8,6272]{1,0:T(8,128)(2,1)S(1)}, bf16[8,6272]{1,0:T(8,128)(2,1)S(1)}, u32[]{:S(2)}, u32[]{:S(2)}) collective-permute-start(bf16[8,6272]{1,0:T(8,128)(2,1)S(1)} %collective-permute-done.refs_1_), channel_id=1, source_target_pairs={{0,2},{2,0},{4,6},{6,4},{8,10},{10,8},{12,14},{14,12},{1,3},{3,1},... | collective-permute-start | bytes 301064 | tf_op jit(solution)/shard_map/ppermute | solution.py:268
  13.4 0.3 collective-permute-start.5
  13.8 1.7 %collective-permute-start.6 = (bf16[8,6272]{1,0:T(8,128)(2,1)S(1)}, bf16[8,6272]{1,0:T(8,128)(2,1)S(1)}, u32[]{:S(2)}, u32[]{:S(2)}) collective-permute-start(bf16[8,6272]{1,0:T(8,128)(2,1)S(1)} %collective-permute-done.2.refs_3_), channel_id=1, source_target_pairs={{0,2},{2,0},{4,6},{6,4},{8,10},{10,8},{12,14},{14,12},{1,3},{3,1},... | collective-permute-start | bytes 301064 | tf_op jit(solution)/shard_map/ppermute | solution.py:268
  15.5 0.1 collective-permute-start.7
  15.6 1.6 %collective-permute-done.4.refs_5_.refs_1_ = bf16[8,6272]{1,0:T(8,128)(2,1)S(1)} collective-permute-done((bf16[8,6272]{1,0:T(8,128)(2,1)S(1)}, bf16[8,6272]{1,0:T(8,128)(2,1)S(1)}, u32[]{:S(2)}, u32[]{:S(2)}) %collective-permute-start.4) | collective-permute-done | bytes 100384 | tf_op jit(solution)/shard_map/ppermute | solution.py:268
  17.2 1.3 %collective-permute-done.5.refs_6_.refs_2_ = bf16[8,6272]{1,0:T(8,128)(2,1)S(1)} collective-permute-done((bf16[8,6272]{1,0:T(8,128)(2,1)S(1)}, bf16[8,6272]{1,0:T(8,128)(2,1)S(1)}, u32[]{:S(2)}, u32[]{:S(2)}) %collective-permute-start.5) | collective-permute-done | bytes 100384 | tf_op jit(solution)/shard_map/ppermute | solution.py:268
  18.5 0.1 collective-permute-start.8
  18.6 1.0 %collective-permute-done.6.refs_7_.refs_0_ = bf16[8,6272]{1,0:T(8,128)(2,1)S(1)} collective-permute-done((bf16[8,6272]{1,0:T(8,128)(2,1)S(1)}, bf16[8,6272]{1,0:T(8,128)(2,1)S(1)}, u32[]{:S(2)}, u32[]{:S(2)}) %collective-permute-start.6) | collective-permute-done | bytes 100384 | tf_op jit(solution)/shard_map/ppermute | solution.py:268
  19.6 0.1 collective-permute-start.9
  19.7 0.2 unpack.1.first_ref
  20.0 1.0 %collective-permute-done.9.refs_2_ = bf16[8,6272]{1,0:T(8,128)(2,1)S(1)} collective-permute-done((bf16[8,6272]{1,0:T(8,128)(2,1)S(1)}, bf16[8,6272]{1,0:T(8,128)(2,1)S(1)}, u32[]{:S(2)}, u32[]{:S(2)}) %collective-permute-start.9) | collective-permute-done | bytes 100384 | tf_op jit(solution)/shard_map/ppermute | solution.py:271
  21.1 4.7 %gate_up.1.hidden_ref = bf16[128,1024]{1,0:T(8,128)(2,1)S(1)} custom-call(bf16[64,7168]{1,0:T(8,128)(2,1)S(1)} %unpack.1.first_ref, bf16[32,6272]{1,0:T(8,128)(2,1)S(1)} %collective-permute-done.7.refs_0_, bf16[24,6272]{1,0:T(8,128)(2,1)S(1)} %collective-permute-done.8.refs_1_, bf16[8,6272]{1,0:T(8,128)(2,1)S(1)} %collective-permute-done.9.refs_2_, ...), custom_call_target="tpu_custom_call" | custom-call | flops 3758096384 | tf_op jit(solution)/shard_map/gate_up/pallas_call | solution.py:102
  25.8 2.5 %down.1 = (f32[32,6272]{1,0:T(8,128)S(1)}, f32[32,6272]{1,0:T(8,128)S(1)}, bf16[32,6272]{1,0:T(8,128)(2,1)S(1)}, bf16[32,6272]{1,0:T(8,128)(2,1)S(1)}) custom-call(bf16[128,1024]{1,0:T(8,128)(2,1)S(1)} %gate_up.1.hidden_ref, bf16[1024,7168]{1,0:T(8,128)(2,1)S(1)} %bitcast.8), custom_call_target="tpu_custom_call" | custom-call | flops 1644167168 | tf_op jit(solution)/shard_map/down/pallas_call | solution.py:132
  28.3 0.2 collective-permute-start.10
  28.5 1.6 %collective-permute-done.10.refs_1_ = bf16[32,6272]{1,0:T(8,128)(2,1)S(1)} collective-permute-done((bf16[32,6272]{1,0:T(8,128)(2,1)S(1)}, bf16[32,6272]{1,0:T(8,128)(2,1)S(1)}, u32[]{:S(2)}, u32[]{:S(2)}) %collective-permute-start.10) | collective-permute-done | bytes 401440 | tf_op jit(solution)/shard_map/ppermute | solution.py:271
  30.2 0.2 collective-permute-start.11
  30.4 1.7 %collective-permute-start.12 = (bf16[8,6272]{1,0:T(8,128)(2,1)S(1)}, bf16[8,6272]{1,0:T(8,128)(2,1)S(1)}, u32[]{:S(2)}, u32[]{:S(2)}) collective-permute-start(bf16[8,6272]{1,0:T(8,128)(2,1)S(1)} %get-tuple-element.34), channel_id=1, source_target_pairs={{0,2},{2,0},{4,6},{6,4},{8,10},{10,8},{12,14},{14,12},{1,3},{3,1},... | collective-permute-start | bytes 301064 | tf_op jit(solution)/shard_map/ppermute | solution.py:268
  32.1 0.3 collective-permute-start.17
  32.5 3.6 %collective-permute-done.12.refs_1_ = bf16[8,6272]{1,0:T(8,128)(2,1)S(1)} collective-permute-done((bf16[8,6272]{1,0:T(8,128)(2,1)S(1)}, bf16[8,6272]{1,0:T(8,128)(2,1)S(1)}, u32[]{:S(2)}, u32[]{:S(2)}) %collective-permute-start.12) | collective-permute-done | bytes 100384 | tf_op jit(solution)/shard_map/ppermute | solution.py:268
  36.2 1.7 %collective-permute-start.14 = (bf16[8,6272]{1,0:T(8,128)(2,1)S(1)}, bf16[8,6272]{1,0:T(8,128)(2,1)S(1)}, u32[]{:S(2)}, u32[]{:S(2)}) collective-permute-start(bf16[8,6272]{1,0:T(8,128)(2,1)S(1)} %get-tuple-element.37), channel_id=1, source_target_pairs={{0,2},{2,0},{4,6},{6,4},{8,10},{10,8},{12,14},{14,12},{1,3},{3,1},... | collective-permute-start | bytes 301064 | tf_op jit(solution)/shard_map/ppermute | solution.py:268
  37.9 4.1 %collective-permute-start.16 = (bf16[8,6272]{1,0:T(8,128)(2,1)S(1)}, bf16[8,6272]{1,0:T(8,128)(2,1)S(1)}, u32[]{:S(2)}, u32[]{:S(2)}) collective-permute-start(bf16[8,6272]{1,0:T(8,128)(2,1)S(1)} %span_sum.3.refs_2_), channel_id=1, source_target_pairs={{0,12},{2,14},{4,8},{6,10},{8,4},{10,6},{12,0},{14,2},{1,13},{3,15... | collective-permute-start | bytes 301064 | tf_op jit(solution)/shard_map/ppermute | solution.py:265
  42.0 0.7 %collective-permute-start.13 = (bf16[8,6272]{1,0:T(8,128)(2,1)S(1)}, bf16[8,6272]{1,0:T(8,128)(2,1)S(1)}, u32[]{:S(2)}, u32[]{:S(2)}) collective-permute-start(bf16[8,6272]{1,0:T(8,128)(2,1)S(1)} %get-tuple-element.35), channel_id=1, source_target_pairs={{0,2},{2,0},{4,6},{6,4},{8,10},{10,8},{12,14},{14,12},{1,3},{3,1},... | collective-permute-start | bytes 301064 | tf_op jit(solution)/shard_map/ppermute | solution.py:268
  42.7 0.1 collective-permute-start.18
  42.8 0.6 %collective-permute-start.15 = (bf16[8,6272]{1,0:T(8,128)(2,1)S(1)}, bf16[8,6272]{1,0:T(8,128)(2,1)S(1)}, u32[]{:S(2)}, u32[]{:S(2)}) collective-permute-start(bf16[8,6272]{1,0:T(8,128)(2,1)S(1)} %span_sum.4), channel_id=1, source_target_pairs={{0,4},{2,6},{4,0},{6,2},{8,12},{10,14},{12,8},{14,10},{1,5},{3,7},... | collective-permute-start | bytes 301064 | tf_op jit(solution)/shard_map/ppermute | solution.py:265
  43.4 3.2 %collective-permute-done.13.refs_1_ = bf16[8,6272]{1,0:T(8,128)(2,1)S(1)} collective-permute-done((bf16[8,6272]{1,0:T(8,128)(2,1)S(1)}, bf16[8,6272]{1,0:T(8,128)(2,1)S(1)}, u32[]{:S(2)}, u32[]{:S(2)}) %collective-permute-start.13) | collective-permute-done | bytes 100384 | tf_op jit(solution)/shard_map/ppermute | solution.py:268
  46.6 2.5 %collective-permute-done.18.refs_4_ = bf16[8,6272]{1,0:T(8,128)(2,1)S(1)} collective-permute-done((bf16[8,6272]{1,0:T(8,128)(2,1)S(1)}, bf16[8,6272]{1,0:T(8,128)(2,1)S(1)}, u32[]{:S(2)}, u32[]{:S(2)}) %collective-permute-start.18) | collective-permute-done | bytes 100384 | tf_op jit(solution)/shard_map/ppermute | solution.py:265
  49.2 0.9 %combine.1 = bf16[8,7168]{1,0:T(8,128)(2,1)} custom-call(f32[8,1024]{1,0:T(8,128)S(1)} %get-tuple-element.22.sides_ref, f32[8,6272]{1,0:T(8,128)S(1)} %get-tuple-element.32.refs_0_, bf16[8,6272]{1,0:T(8,128)(2,1)S(1)} %collective-permute-done.13.refs_1_, bf16[8,6272]{1,0:T(8,128)(2,1)S(1)} %collective-permute-done.15.refs_2_, ...), custom_call_target="tpu_custom_call" | custom-call | tf_op jit(solution)/shard_map/combine/pallas_call | solution.py:250
  (48 shorter events, 0.5 us)
Async XLA Ops:
  0.0 21.0 %slice-start = ((s8[14680064]{0:T(1024)(128)(4,1)}), s8[4194304]{0:T(1024)(128)(4,1)S(1)}, s32[]{:S(2)}) async-start(s8[14680064]{0:T(1024)(128)(4,1)} %bitcast.3), calls=%async_computation | async-start | bytes 8388608
  0.0 21.0 %slice-start.4 = ((s8[14680064]{0:T(1024)(128)(4,1)}), s8[4194304]{0:T(1024)(128)(4,1)S(1)}, s32[]{:S(2)}) async-start(s8[14680064]{0:T(1024)(128)(4,1)} %bitcast.5), calls=%async_computation.4 | async-start | bytes 8388608
  0.0 21.0 %slice-start.1 = ((s8[14680064]{0:T(1024)(128)(4,1)}), s8[4194304]{0:T(1024)(128)(4,1)S(1)}, s32[]{:S(2)}) async-start(s8[14680064]{0:T(1024)(128)(4,1)} %bitcast.3), calls=%async_computation.1 | async-start | bytes 8388608
  0.0 21.0 %slice-start.2 = ((s8[14680064]{0:T(1024)(128)(4,1)}), s8[4194304]{0:T(1024)(128)(4,1)S(1)}, s32[]{:S(2)}) async-start(s8[14680064]{0:T(1024)(128)(4,1)} %bitcast.3), calls=%async_computation.2 | async-start | bytes 8388608
  0.0 21.0 %slice-start.3 = ((s8[14680064]{0:T(1024)(128)(4,1)}), s8[2097152]{0:T(1024)(128)(4,1)S(1)}, s32[]{:S(2)}) async-start(s8[14680064]{0:T(1024)(128)(4,1)} %bitcast.3), calls=%async_computation.3 | async-start | bytes 4194304
  0.0 21.0 %slice-start.5 = ((s8[14680064]{0:T(1024)(128)(4,1)}), s8[4194304]{0:T(1024)(128)(4,1)S(1)}, s32[]{:S(2)}) async-start(s8[14680064]{0:T(1024)(128)(4,1)} %bitcast.5), calls=%async_computation.5 | async-start | bytes 8388608
  0.0 21.0 %slice-start.6 = ((s8[14680064]{0:T(1024)(128)(4,1)}), s8[4194304]{0:T(1024)(128)(4,1)S(1)}, s32[]{:S(2)}) async-start(s8[14680064]{0:T(1024)(128)(4,1)} %bitcast.5), calls=%async_computation.6 | async-start | bytes 8388608
  0.0 21.0 %slice-start.7 = ((s8[14680064]{0:T(1024)(128)(4,1)}), s8[2097152]{0:T(1024)(128)(4,1)S(1)}, s32[]{:S(2)}) async-start(s8[14680064]{0:T(1024)(128)(4,1)} %bitcast.5), calls=%async_computation.7 | async-start | bytes 4194304
  1.4 10.4 %collective-permute-start = (bf16[8,6272]{1,0:T(8,128)(2,1)S(1)}, bf16[8,6272]{1,0:T(8,128)(2,1)S(1)}, u32[]{:S(2)}, u32[]{:S(2)}) collective-permute-start(bf16[8,6272]{1,0:T(8,128)(2,1)S(1)} %get-tuple-element.24), channel_id=1, source_target_pairs={{0,8},{2,10},{4,12},{6,14},{8,0},{10,2},{12,4},{14,6},{1,9},{3,11}... | collective-permute-start | bytes 301064 | tf_op jit(solution)/shard_map/ppermute | solution.py:265
  5.5 8.0 %collective-permute-start.1 = (bf16[8,6272]{1,0:T(8,128)(2,1)S(1)}, bf16[8,6272]{1,0:T(8,128)(2,1)S(1)}, u32[]{:S(2)}, u32[]{:S(2)}) collective-permute-start(bf16[8,6272]{1,0:T(8,128)(2,1)S(1)} %get-tuple-element.25), channel_id=1, source_target_pairs={{0,4},{2,6},{4,0},{6,2},{8,12},{10,14},{12,8},{14,10},{1,5},{3,7},... | collective-permute-start | bytes 301064 | tf_op jit(solution)/shard_map/ppermute | solution.py:265
  7.0 6.7 %collective-permute-start.2 = (bf16[8,6272]{1,0:T(8,128)(2,1)S(1)}, bf16[8,6272]{1,0:T(8,128)(2,1)S(1)}, u32[]{:S(2)}, u32[]{:S(2)}) collective-permute-start(bf16[8,6272]{1,0:T(8,128)(2,1)S(1)} %get-tuple-element.26), channel_id=1, source_target_pairs={{0,12},{2,14},{4,8},{6,10},{8,4},{10,6},{12,0},{14,2},{1,13},{3,15... | collective-permute-start | bytes 301064 | tf_op jit(solution)/shard_map/ppermute | solution.py:265
  7.0 8.5 %collective-permute-start.3 = (bf16[8,6272]{1,0:T(8,128)(2,1)S(1)}, bf16[8,6272]{1,0:T(8,128)(2,1)S(1)}, u32[]{:S(2)}, u32[]{:S(2)}) collective-permute-start(bf16[8,6272]{1,0:T(8,128)(2,1)S(1)} %get-tuple-element.23.refs_0_), channel_id=1, source_target_pairs={{0,2},{2,0},{4,6},{6,4},{8,10},{10,8},{12,14},{14,12},{1,3},{3,1},... | collective-permute-start | bytes 301064 | tf_op jit(solution)/shard_map/ppermute | solution.py:268
  11.7 5.5 %collective-permute-start.4 = (bf16[8,6272]{1,0:T(8,128)(2,1)S(1)}, bf16[8,6272]{1,0:T(8,128)(2,1)S(1)}, u32[]{:S(2)}, u32[]{:S(2)}) collective-permute-start(bf16[8,6272]{1,0:T(8,128)(2,1)S(1)} %collective-permute-done.refs_1_), channel_id=1, source_target_pairs={{0,2},{2,0},{4,6},{6,4},{8,10},{10,8},{12,14},{14,12},{1,3},{3,1},... | collective-permute-start | bytes 301064 | tf_op jit(solution)/shard_map/ppermute | solution.py:268
  13.4 5.1 %collective-permute-start.5 = (bf16[8,6272]{1,0:T(8,128)(2,1)S(1)}, bf16[8,6272]{1,0:T(8,128)(2,1)S(1)}, u32[]{:S(2)}, u32[]{:S(2)}) collective-permute-start(bf16[8,6272]{1,0:T(8,128)(2,1)S(1)} %collective-permute-done.1.refs_2_), channel_id=1, source_target_pairs={{0,2},{2,0},{4,6},{6,4},{8,10},{10,8},{12,14},{14,12},{1,3},{3,1},... | collective-permute-start | bytes 301064 | tf_op jit(solution)/shard_map/ppermute | solution.py:268
  13.8 5.8 %collective-permute-start.6 = (bf16[8,6272]{1,0:T(8,128)(2,1)S(1)}, bf16[8,6272]{1,0:T(8,128)(2,1)S(1)}, u32[]{:S(2)}, u32[]{:S(2)}) collective-permute-start(bf16[8,6272]{1,0:T(8,128)(2,1)S(1)} %collective-permute-done.2.refs_3_), channel_id=1, source_target_pairs={{0,2},{2,0},{4,6},{6,4},{8,10},{10,8},{12,14},{14,12},{1,3},{3,1},... | collective-permute-start | bytes 301064 | tf_op jit(solution)/shard_map/ppermute | solution.py:268
  15.5 5.5 %collective-permute-start.7 = (bf16[32,6272]{1,0:T(8,128)(2,1)S(1)}, bf16[32,6272]{1,0:T(8,128)(2,1)S(1)}, u32[]{:S(2)}, u32[]{:S(2)}) collective-permute-start(bf16[32,6272]{1,0:T(8,128)(2,1)S(1)} %stack.4), channel_id=1, source_target_pairs={{0,1},{1,0},{2,3},{3,2},{4,5},{5,4},{6,7},{7,6},{8,9},{9,8},{10,11... | collective-permute-start | bytes 1204232 | tf_op jit(solution)/shard_map/ppermute | solution.py:271
  18.5 2.4 %collective-permute-start.8 = (bf16[24,6272]{1,0:T(8,128)(2,1)S(1)}, bf16[24,6272]{1,0:T(8,128)(2,1)S(1)}, u32[]{:S(2)}, u32[]{:S(2)}) collective-permute-start(bf16[24,6272]{1,0:T(8,128)(2,1)S(1)} %stack.5), channel_id=1, source_target_pairs={{0,1},{1,0},{2,3},{3,2},{4,5},{5,4},{6,7},{7,6},{8,9},{9,8},{10,11... | collective-permute-start | bytes 903176 | tf_op jit(solution)/shard_map/ppermute | solution.py:271
  19.6 1.4 %collective-permute-start.9 = (bf16[8,6272]{1,0:T(8,128)(2,1)S(1)}, bf16[8,6272]{1,0:T(8,128)(2,1)S(1)}, u32[]{:S(2)}, u32[]{:S(2)}) collective-permute-start(bf16[8,6272]{1,0:T(8,128)(2,1)S(1)} %stack.6), channel_id=1, source_target_pairs={{0,1},{1,0},{2,3},{3,2},{4,5},{5,4},{6,7},{7,6},{8,9},{9,8},{10,11... | collective-permute-start | bytes 301064 | tf_op jit(solution)/shard_map/ppermute | solution.py:271
  19.7 6.1 %slice-start.8 = ((s8[14680064]{0:T(1024)(128)(4,1)}), s8[4194304]{0:T(1024)(128)(4,1)S(1)}, s32[]{:S(2)}) async-start(s8[14680064]{0:T(1024)(128)(4,1)} %bitcast.7), calls=%async_computation.8 | async-start | bytes 8388608
  19.9 5.9 %slice-start.9 = ((s8[14680064]{0:T(1024)(128)(4,1)}), s8[4194304]{0:T(1024)(128)(4,1)S(1)}, s32[]{:S(2)}) async-start(s8[14680064]{0:T(1024)(128)(4,1)} %bitcast.7), calls=%async_computation.9 | async-start | bytes 8388608
  19.9 5.8 %slice-start.10 = ((s8[14680064]{0:T(1024)(128)(4,1)}), s8[4194304]{0:T(1024)(128)(4,1)S(1)}, s32[]{:S(2)}) async-start(s8[14680064]{0:T(1024)(128)(4,1)} %bitcast.7), calls=%async_computation.10 | async-start | bytes 8388608
  19.9 5.8 %slice-start.11 = ((s8[14680064]{0:T(1024)(128)(4,1)}), s8[2097152]{0:T(1024)(128)(4,1)S(1)}, s32[]{:S(2)}) async-start(s8[14680064]{0:T(1024)(128)(4,1)} %bitcast.7), calls=%async_computation.11 | async-start | bytes 4194304
  28.3 1.8 %collective-permute-start.10 = (bf16[32,6272]{1,0:T(8,128)(2,1)S(1)}, bf16[32,6272]{1,0:T(8,128)(2,1)S(1)}, u32[]{:S(2)}, u32[]{:S(2)}) collective-permute-start(bf16[32,6272]{1,0:T(8,128)(2,1)S(1)} %get-tuple-element.30), channel_id=1, source_target_pairs={{0,1},{1,0},{2,3},{3,2},{4,5},{5,4},{6,7},{7,6},{8,9},{9,8},{10,11... | collective-permute-start | bytes 1204232 | tf_op jit(solution)/shard_map/ppermute | solution.py:271
  30.2 2.3 %collective-permute-start.11 = (bf16[32,6272]{1,0:T(8,128)(2,1)S(1)}, bf16[32,6272]{1,0:T(8,128)(2,1)S(1)}, u32[]{:S(2)}, u32[]{:S(2)}) collective-permute-start(bf16[32,6272]{1,0:T(8,128)(2,1)S(1)} %stack.7), channel_id=1, source_target_pairs={{0,1},{1,0},{2,3},{3,2},{4,5},{5,4},{6,7},{7,6},{8,9},{9,8},{10,11... | collective-permute-start | bytes 1204232 | tf_op jit(solution)/shard_map/ppermute | solution.py:271
  30.4 5.7 %collective-permute-start.12 = (bf16[8,6272]{1,0:T(8,128)(2,1)S(1)}, bf16[8,6272]{1,0:T(8,128)(2,1)S(1)}, u32[]{:S(2)}, u32[]{:S(2)}) collective-permute-start(bf16[8,6272]{1,0:T(8,128)(2,1)S(1)} %get-tuple-element.34), channel_id=1, source_target_pairs={{0,2},{2,0},{4,6},{6,4},{8,10},{10,8},{12,14},{14,12},{1,3},{3,1},... | collective-permute-start | bytes 301064 | tf_op jit(solution)/shard_map/ppermute | solution.py:268
  32.1 10.6 %collective-permute-start.17 = (bf16[8,6272]{1,0:T(8,128)(2,1)S(1)}, bf16[8,6272]{1,0:T(8,128)(2,1)S(1)}, u32[]{:S(2)}, u32[]{:S(2)}) collective-permute-start(bf16[8,6272]{1,0:T(8,128)(2,1)S(1)} %get-tuple-element.31.refs_1_), channel_id=1, source_target_pairs={{0,2},{2,0},{4,6},{6,4},{8,10},{10,8},{12,14},{14,12},{1,3},{3,1},... | collective-permute-start | bytes 301064 | tf_op jit(solution)/shard_map/ppermute | solution.py:268
  36.2 6.6 %collective-permute-start.14 = (bf16[8,6272]{1,0:T(8,128)(2,1)S(1)}, bf16[8,6272]{1,0:T(8,128)(2,1)S(1)}, u32[]{:S(2)}, u32[]{:S(2)}) collective-permute-start(bf16[8,6272]{1,0:T(8,128)(2,1)S(1)} %get-tuple-element.37), channel_id=1, source_target_pairs={{0,2},{2,0},{4,6},{6,4},{8,10},{10,8},{12,14},{14,12},{1,3},{3,1},... | collective-permute-start | bytes 301064 | tf_op jit(solution)/shard_map/ppermute | solution.py:268
  37.9 8.7 %collective-permute-start.16 = (bf16[8,6272]{1,0:T(8,128)(2,1)S(1)}, bf16[8,6272]{1,0:T(8,128)(2,1)S(1)}, u32[]{:S(2)}, u32[]{:S(2)}) collective-permute-start(bf16[8,6272]{1,0:T(8,128)(2,1)S(1)} %span_sum.3.refs_2_), channel_id=1, source_target_pairs={{0,12},{2,14},{4,8},{6,10},{8,4},{10,6},{12,0},{14,2},{1,13},{3,15... | collective-permute-start | bytes 301064 | tf_op jit(solution)/shard_map/ppermute | solution.py:265
  42.0 4.6 %collective-permute-start.13 = (bf16[8,6272]{1,0:T(8,128)(2,1)S(1)}, bf16[8,6272]{1,0:T(8,128)(2,1)S(1)}, u32[]{:S(2)}, u32[]{:S(2)}) collective-permute-start(bf16[8,6272]{1,0:T(8,128)(2,1)S(1)} %get-tuple-element.35), channel_id=1, source_target_pairs={{0,2},{2,0},{4,6},{6,4},{8,10},{10,8},{12,14},{14,12},{1,3},{3,1},... | collective-permute-start | bytes 301064 | tf_op jit(solution)/shard_map/ppermute | solution.py:268
  42.7 6.5 %collective-permute-start.18 = (bf16[8,6272]{1,0:T(8,128)(2,1)S(1)}, bf16[8,6272]{1,0:T(8,128)(2,1)S(1)}, u32[]{:S(2)}, u32[]{:S(2)}) collective-permute-start(bf16[8,6272]{1,0:T(8,128)(2,1)S(1)} %span_sum.5), channel_id=1, source_target_pairs={{0,8},{2,10},{4,12},{6,14},{8,0},{10,2},{12,4},{14,6},{1,9},{3,11}... | collective-permute-start | bytes 301064 | tf_op jit(solution)/shard_map/ppermute | solution.py:265
  42.8 6.4 %collective-permute-start.15 = (bf16[8,6272]{1,0:T(8,128)(2,1)S(1)}, bf16[8,6272]{1,0:T(8,128)(2,1)S(1)}, u32[]{:S(2)}, u32[]{:S(2)}) collective-permute-start(bf16[8,6272]{1,0:T(8,128)(2,1)S(1)} %span_sum.4), channel_id=1, source_target_pairs={{0,4},{2,6},{4,0},{6,2},{8,12},{10,14},{12,8},{14,10},{1,5},{3,7},... | collective-permute-start | bytes 301064 | tf_op jit(solution)/shard_map/ppermute | solution.py:265

commit v9 on v4

v9 whole, which is shorter than its diff:
```python
import functools

import jax
import jax.numpy as jnp
from jax import lax
from jax.experimental import pallas as pl
from jax.experimental.pallas import tpu as pltpu
from jax.sharding import PartitionSpec as P

EXPERTS = 4
LANES = 128
RETURN_ORDER = (1, 3, 2)
BLOCK_ORDER = (0, 2, 1, 3)
N_BLOCK = 256
LAST_FLOPS = 5_000_000_000
EXCHANGE_FLOPS = 20_000_000_000


def params(mib=4):
    return pltpu.CompilerParams(vmem_limit_bytes=mib * 1024 * 1024)


def cost(flops):
    return pl.CostEstimate(flops=flops, bytes_accessed=0, transcendentals=0)


def block_of(width, most):
    size = most
    while width % size:
        size -= 128
    return size


def in_vmem(value):
    return pltpu.with_memory_space_constraint(value, pltpu.VMEM)


def joined(refs):
    return jnp.concatenate([ref[...].astype(jnp.float32) for ref in refs], axis=0)


def stack_kernel(count, *refs):
    refs[-1][...] = joined(refs[:count]).astype(jnp.bfloat16)


def stack(values, after=(), flops=0):
    rows = sum(v.shape[0] for v in values)
    return pl.pallas_call(
        functools.partial(stack_kernel, len(values)),
        in_specs=[pl.BlockSpec(memory_space=pltpu.VMEM)] * len(values) + [pl.BlockSpec(memory_space=pl.ANY)] * len(after),
        out_shape=jax.ShapeDtypeStruct((rows, values[0].shape[1]), jnp.bfloat16),
        compiler_params=params(),
        cost_estimate=cost(flops),
        name="stack",
    )(*values, *after)


def gate_up_kernel(n_block, *refs):
    rows_in, (gate_ref, up_ref, hidden_ref, rows_ref) = refs[:-4], refs[-4:]
    start, run = 0, []
    for ref in rows_in:
        run.append(ref)
        count = sum(r.shape[0] for r in run)
        if count % 16 == 0:
            rows_ref[start:start + count, :] = ref[...] if len(run) == 1 else joined(run).astype(jnp.bfloat16)
            start, run = start + count, []
    for n in range(0, gate_ref.shape[1], n_block):
        columns = slice(n, n + n_block)
        gate = jnp.dot(rows_ref[...], gate_ref[:, columns], preferred_element_type=jnp.float32)
        up = jnp.dot(rows_ref[...], up_ref[:, columns], preferred_element_type=jnp.float32)
        hidden_ref[:, columns] = (gate / (1.0 + jnp.exp(-gate)) * up).astype(jnp.bfloat16)


def gate_up(blocks, gate_weight, up_weight):
    total = sum(r.shape[0] for r in blocks)
    width, units = gate_weight.shape
    return pl.pallas_call(
        functools.partial(gate_up_kernel, block_of(units, N_BLOCK)),
        in_specs=[pl.BlockSpec(memory_space=pltpu.VMEM)] * (len(blocks) + 2),
        out_shape=jax.ShapeDtypeStruct((total, units), jnp.bfloat16),
        scratch_shapes=[pltpu.VMEM((total, width), jnp.bfloat16)],
        compiler_params=params(),
        cost_estimate=cost(4 * total * width * units),
        name="gate_up",
    )(*blocks, in_vmem(gate_weight), in_vmem(up_weight))


def down_kernel(c_block, hidden_ref, down_ref, *outs):
    count, width = outs[0].shape
    hidden = hidden_ref[...]
    for c in range(0, width, c_block):
        columns = slice(c, c + c_block)
        value = jnp.dot(hidden, down_ref[:, columns], preferred_element_type=jnp.float32)
        for j, ref in enumerate(outs):
            ref[:, columns] = value[j * count:(j + 1) * count].astype(ref.dtype)


def down(hidden, down_weight, span, pair):
    total, units = hidden.shape
    width = down_weight.shape[1]
    shape = (total // (span * pair), width)
    outs = pl.pallas_call(
        functools.partial(down_kernel, block_of(width, N_BLOCK)),
        in_specs=[pl.BlockSpec(memory_space=pltpu.VMEM)] * 2,
        out_shape=[jax.ShapeDtypeStruct(shape, jnp.bfloat16 if p else jnp.float32) for p in range(pair) for _ in range(span)],
        compiler_params=params(),
        cost_estimate=cost(2 * total * width * units),
        name="down",
    )(hidden, in_vmem(down_weight))
    return [outs[t::span] for t in range(span)]


def pair_sum_kernel(count, *refs):
    outs = refs[count:]
    rows = outs[0].shape[0]
    for i, out_ref in enumerate(outs):
        part = slice(i * rows, (i + 1) * rows)
        value = refs[0][part, :]
        for ref in refs[1:count]:
            value += ref[part, :].astype(jnp.float32)
        out_ref[...] = value.astype(out_ref.dtype)


def pair_sum(arrays, rows, dtype):
    total, width = arrays[0].shape
    return pl.pallas_call(
        functools.partial(pair_sum_kernel, len(arrays)),
        out_shape=[jax.ShapeDtypeStruct((rows, width), dtype)] * (total // rows),
        compiler_params=params(),
        name="pair_sum",
    )(*arrays)


def span_sum_kernel(*refs):
    value = refs[0][...]
    for ref in refs[1:-1]:
        value += ref[...].astype(jnp.float32)
    refs[-1][...] = value.astype(refs[-1].dtype)


def span_sum(arrays):
    return pl.pallas_call(
        span_sum_kernel,
        out_shape=jax.ShapeDtypeStruct(arrays[0].shape, jnp.bfloat16),
        compiler_params=params(),
        name="span_sum",
    )(*arrays)


def coefficients_kernel(own_expert, ids_ref, weights_ref, out_ref):
    ids, weights = ids_ref[...], weights_ref[...]
    rows = ids.shape[1]
    square = (rows, rows)
    diagonal = lax.broadcasted_iota(jnp.int32, square, 0) == lax.broadcasted_iota(jnp.int32, square, 1)
    for s in range(EXPERTS):
        expert = lax.bitwise_xor(own_expert[0], s)
        chosen = jnp.sum(jnp.where(ids == expert, weights, 0.0), axis=0, keepdims=True)
        column = jnp.sum(jnp.where(diagonal, jnp.broadcast_to(chosen, square), 0.0), axis=1, keepdims=True)
        out_ref[:, s * LANES:(s + 1) * LANES] = jnp.broadcast_to(column, (rows, LANES))


def coefficients(own_expert, ids, weights):
    return pl.pallas_call(
        coefficients_kernel,
        in_specs=[pl.BlockSpec(memory_space=pltpu.SMEM)] + [pl.BlockSpec(memory_space=pltpu.VMEM)] * 2,
        out_shape=jax.ShapeDtypeStruct((ids.shape[0], EXPERTS * LANES), jnp.float32),
        compiler_params=params(),
        cost_estimate=cost(0),
        name="coefficients",
    )(own_expert, ids.T, weights.T)


def combine_kernel(own_count, coeff_ref, *refs):
    out_ref = refs[-1]
    value = refs[0][...]
    for ref in refs[1:own_count]:
        value += ref[...].astype(jnp.float32)
    value *= coeff_ref[:, :1]
    for s, ref in zip(RETURN_ORDER, refs[own_count:-1]):
        value += coeff_ref[:, s * LANES:s * LANES + 1] * ref[...].astype(jnp.float32)
    out_ref[...] = value.astype(jnp.bfloat16)


def combine(coeffs, own, others):
    return pl.pallas_call(
        functools.partial(combine_kernel, len(own)),
        out_shape=jax.ShapeDtypeStruct(own[0].shape, jnp.bfloat16),
        compiler_params=params(),
        name="combine",
    )(coeffs, *own, *others)


def local(tokens, expert_ids, route_weights, gate_weight, up_weight, down_weight):
    rows = tokens.shape[0]
    attn = lax.axis_size("attn")
    pair = lax.axis_size("ffn")
    span = attn // EXPERTS

    def over_experts(value, other):
        return lax.ppermute(value, "attn", [(i, (i // span ^ other) * span + i % span) for i in range(attn)])

    def over_span(value, shift):
        return lax.ppermute(value, "attn", [(i, i // span * span + (i + shift) % span) for i in range(attn)])

    def over_pair(value, shift):
        return lax.ppermute(value, "ffn", [(i, (i + shift) % pair) for i in range(pair)])

    own_expert = (lax.axis_index("attn") // span).astype(jnp.int32).reshape(1)
    coeffs = coefficients(own_expert, expert_ids, route_weights)
    own = stack([tokens], (), EXCHANGE_FLOPS)
    far = over_experts(tokens, 2)
    near = over_experts(own, 1)
    column = {0: own, 2: far, 1: near, 3: over_experts(far, 1)}
    column = [column[s] for s in BLOCK_ORDER]
    parts = [column] + [[over_span(b, t) for b in column] for t in range(1, span)]
    groups = [stack(column)]
    for part in parts[1:]:
        groups += [stack(part[:-1]), stack(part[-1:], (), LAST_FLOPS)]
    others = [over_pair(g, p) for p in range(1, pair) for g in groups]
    plane = stack([b for part in parts for b in part], (), 1_000_000_000)
    hidden = gate_up([plane] + others, gate_weight, up_weight)

    sums = [[] for _ in range(EXPERTS)]
    for t, (keep, *sends) in enumerate(down(hidden, down_weight, span, pair)):
        arrays = [keep] + [over_pair(b, -p) for p, b in enumerate(sends, 1)]
        blocks = pair_sum(arrays, rows, jnp.bfloat16 if t else jnp.float32)
        for s, block in zip(BLOCK_ORDER, blocks):
            sums[s].append(over_span(block, -t) if t else block)

    returned = [over_experts(span_sum(sums[s]), s) for s in RETURN_ORDER]
    return combine(coeffs, sums[0], returned)


def solution(mesh):
    return jax.shard_map(
        local,
        mesh=mesh,
        in_specs=(
            P(("groups", "attn", "ffn"), None),
            P(("groups", "attn", "ffn"), None),
            P(("groups", "attn", "ffn"), None),
            P(None, ("attn", "ffn")),
            P(None, ("attn", "ffn")),
            P(("attn", "ffn"), None),
        ),
        out_specs=P(("groups", "attn", "ffn"), None),
        check_vma=False,
    )
```

time: 51.9 us -> 52.3 us (level)
  waiting for transfers between devices: 18.8 us -> 20.3 us
  starting transfers between devices: 23.8 us -> 22.9 us
    ppermute x6, waiting for transfers between devices: 6.55 us -> 9.55 us  [over_experts(): lax.ppermute(value, 'attn', [(i, (i // span ^ other) * span + i % span) f...]
    ppermute x4 -> x5, waiting for transfers between devices: 3.76 us -> 2.51 us  [over_pair(): lax.ppermute(value, 'ffn', [(i, (i + shift) % pair) for i in range(pair)])]
    ppermute x6, starting transfers between devices: 13.7 us -> 12.9 us  [over_experts(): lax.ppermute(value, 'attn', [(i, (i // span ^ other) * span + i % span) f...]
    pallas_call x6 -> x8, Pallas kernels: 2.49 us -> 2.37 us  [the longest x1 2.08 us: down(): pl.pallas_call(functools.partial(down_kernel, block_of(width, N_BLOCK)),...]
  transfers between devices with their start and end apart: 18 -> 19, of which waited for: 11 -> 12; matrix products, arithmetic and copies ran while one was open for 0% -> 0% of each run, Pallas kernels for 0% -> 1%
where the time goes in v9:
time: 52.3 us; the launch traced here: 52.1 us
  starting transfers between devices  22.9 us (44%)
  waiting for transfers between devices  20.3 us (39%)
  Pallas kernels  7.76 us (15%)
  local copies, waits for them, and re-layouts  0.98 us (2%)
    ppermute x6, starting transfers between devices, over_experts(): lax.ppermute(value, 'attn', [(i, (i // span ^ other) * span + i % span) f...  12.9 us
    ppermute x6, waiting for transfers between devices, over_experts(): lax.ppermute(value, 'attn', [(i, (i // span ^ other) * span + i % span) f...  9.55 us
    ppermute x8, starting transfers between devices, over_span(): lax.ppermute(value, 'attn', [(i, i // span * span + (i + shift) % span) f...  9.24 us
    ppermute x8, waiting for transfers between devices, over_span(): lax.ppermute(value, 'attn', [(i, i // span * span + (i + shift) % span) f...  8.24 us
    pallas_call x1, Pallas kernels, gate_up(): pl.pallas_call(functools.partial(gate_up_kernel, block_of(units, N_BLOCK)...  4.41 us
    ppermute x5, waiting for transfers between devices, over_pair(): lax.ppermute(value, 'ffn', [(i, (i + shift) % pair) for i in range(pair)])  2.51 us
    pallas_call x1, Pallas kernels, down(): pl.pallas_call(functools.partial(down_kernel, block_of(width, N_BLOCK)),...  2.08 us
  transfers between devices with their start and end apart: 19, of which 12 were waited for; matrix products, arithmetic and copies ran while one was open for 0% of the time, Pallas kernels for 1%

profile of v9, /device:TPU:0, one launch (start us, length us, event | category | flops | bytes accessed | tf_op | source)
XLA Modules:
  0.0 52.1 jit_solution(13438741224094186093)
XLA Ops:
  0.0 4.0 %collective-permute-start = (bf16[8,7168]{1,0:T(8,128)(2,1)}, bf16[8,7168]{1,0:T(8,128)(2,1)S(1)}, u32[]{:S(2)}, u32[]{:S(2)}) collective-permute-start(bf16[8,7168]{1,0:T(8,128)(2,1)} %refs_0_.1), channel_id=1, source_target_pairs={{0,8},{2,10},{4,12},{6,14},{8,0},{10,2},{12,4},{14,6},{1,9},{3,11}... | collective-permute-start | bytes 344072 | tf_op jit(solution)/shard_map/ppermute | solution.py:200
  4.0 0.9 %copy-done.4 = bf16[8,7168]{1,0:T(8,128)(2,1)S(1)} copy-done((bf16[8,7168]{1,0:T(8,128)(2,1)S(1)}, bf16[8,7168]{1,0:T(8,128)(2,1)}, u32[]{:S(2)}) %copy-start.4) | copy-done | bytes 114712
  5.0 1.6 %collective-permute-start.1 = (bf16[8,7168]{1,0:T(8,128)(2,1)S(1)}, bf16[8,7168]{1,0:T(8,128)(2,1)S(1)}, u32[]{:S(2)}, u32[]{:S(2)}) collective-permute-start(bf16[8,7168]{1,0:T(8,128)(2,1)S(1)} %stack.5.refs_0_), channel_id=1, source_target_pairs={{0,4},{2,6},{4,0},{6,2},{8,12},{10,14},{12,8},{14,10},{1,5},{3,7},... | collective-permute-start | bytes 344072 | tf_op jit(solution)/shard_map/ppermute | solution.py:200
  6.6 3.3 %collective-permute-done.refs_1_ = bf16[8,7168]{1,0:T(8,128)(2,1)S(1)} collective-permute-done((bf16[8,7168]{1,0:T(8,128)(2,1)}, bf16[8,7168]{1,0:T(8,128)(2,1)S(1)}, u32[]{:S(2)}, u32[]{:S(2)}) %collective-permute-start) | collective-permute-done | bytes 114720 | tf_op jit(solution)/shard_map/ppermute | solution.py:200
  10.0 0.8 %collective-permute-start.2 = (bf16[8,7168]{1,0:T(8,128)(2,1)S(1)}, bf16[8,7168]{1,0:T(8,128)(2,1)S(1)}, u32[]{:S(2)}, u32[]{:S(2)}) collective-permute-start(bf16[8,7168]{1,0:T(8,128)(2,1)S(1)} %collective-permute-done.refs_1_), channel_id=1, source_target_pairs={{0,4},{2,6},{4,0},{6,2},{8,12},{10,14},{12,8},{14,10},{1,5},{3,7},... | collective-permute-start | bytes 344072 | tf_op jit(solution)/shard_map/ppermute | solution.py:200
  10.7 1.5 %collective-permute-start.3 = (bf16[8,7168]{1,0:T(8,128)(2,1)S(1)}, bf16[8,7168]{1,0:T(8,128)(2,1)S(1)}, u32[]{:S(2)}, u32[]{:S(2)}) collective-permute-start(bf16[8,7168]{1,0:T(8,128)(2,1)S(1)} %stack.5.refs_0_), channel_id=1, source_target_pairs={{0,2},{2,0},{4,6},{6,4},{8,10},{10,8},{12,14},{14,12},{1,3},{3,1},... | collective-permute-start | bytes 344072 | tf_op jit(solution)/shard_map/ppermute | solution.py:203
  12.2 0.5 collective-permute-start.5
  12.8 1.5 %collective-permute-start.4 = (bf16[8,7168]{1,0:T(8,128)(2,1)S(1)}, bf16[8,7168]{1,0:T(8,128)(2,1)S(1)}, u32[]{:S(2)}, u32[]{:S(2)}) collective-permute-start(bf16[8,7168]{1,0:T(8,128)(2,1)S(1)} %collective-permute-done.refs_1_), channel_id=1, source_target_pairs={{0,2},{2,0},{4,6},{6,4},{8,10},{10,8},{12,14},{14,12},{1,3},{3,1},... | collective-permute-start | bytes 344072 | tf_op jit(solution)/shard_map/ppermute | solution.py:203
  14.3 0.5 collective-permute-done.2.refs_3_
  14.7 1.6 %collective-permute-start.6 = (bf16[8,7168]{1,0:T(8,128)(2,1)S(1)}, bf16[8,7168]{1,0:T(8,128)(2,1)S(1)}, u32[]{:S(2)}, u32[]{:S(2)}) collective-permute-start(bf16[8,7168]{1,0:T(8,128)(2,1)S(1)} %collective-permute-done.2.refs_3_), channel_id=1, source_target_pairs={{0,2},{2,0},{4,6},{6,4},{8,10},{10,8},{12,14},{14,12},{1,3},{3,1},... | collective-permute-start | bytes 344072 | tf_op jit(solution)/shard_map/ppermute | solution.py:203
  16.4 0.3 collective-permute-done.3.refs_4_.refs_0_
  16.7 2.5 %collective-permute-done.5.refs_6_.refs_2_ = bf16[8,7168]{1,0:T(8,128)(2,1)S(1)} collective-permute-done((bf16[8,7168]{1,0:T(8,128)(2,1)S(1)}, bf16[8,7168]{1,0:T(8,128)(2,1)S(1)}, u32[]{:S(2)}, u32[]{:S(2)}) %collective-permute-start.5) | collective-permute-done | bytes 114720 | tf_op jit(solution)/shard_map/ppermute | solution.py:203
  19.2 2.5 %collective-permute-done.4.refs_5_.refs_1_ = bf16[8,7168]{1,0:T(8,128)(2,1)S(1)} collective-permute-done((bf16[8,7168]{1,0:T(8,128)(2,1)S(1)}, bf16[8,7168]{1,0:T(8,128)(2,1)S(1)}, u32[]{:S(2)}, u32[]{:S(2)}) %collective-permute-start.4) | collective-permute-done | bytes 114720 | tf_op jit(solution)/shard_map/ppermute | solution.py:203
  21.8 1.1 %collective-permute-done.6.refs_7_.refs_0_ = bf16[8,7168]{1,0:T(8,128)(2,1)S(1)} collective-permute-done((bf16[8,7168]{1,0:T(8,128)(2,1)S(1)}, bf16[8,7168]{1,0:T(8,128)(2,1)S(1)}, u32[]{:S(2)}, u32[]{:S(2)}) %collective-permute-start.6) | collective-permute-done | bytes 114720 | tf_op jit(solution)/shard_map/ppermute | solution.py:203
  23.1 1.2 %collective-permute-done.9.refs_3_ = bf16[8,7168]{1,0:T(8,128)(2,1)S(1)} collective-permute-done((bf16[8,7168]{1,0:T(8,128)(2,1)S(1)}, bf16[8,7168]{1,0:T(8,128)(2,1)S(1)}, u32[]{:S(2)}, u32[]{:S(2)}) %collective-permute-start.9) | collective-permute-done | bytes 114720 | tf_op jit(solution)/shard_map/ppermute | solution.py:206
  24.3 4.4 %gate_up.1.hidden_ref = bf16[128,1024]{1,0:T(8,128)(2,1)S(1)} custom-call(bf16[64,7168]{1,0:T(8,128)(2,1)S(1)} %stack.6.refs_0_, bf16[32,7168]{1,0:T(8,128)(2,1)S(1)} %collective-permute-done.7.refs_1_, bf16[24,7168]{1,0:T(8,128)(2,1)S(1)} %collective-permute-done.8.refs_2_, bf16[8,7168]{1,0:T(8,128)(2,1)S(1)} %collective-permute-done.9.refs_3_, ...), custom_call_target="tpu_custom_call" | custom-call | flops 3758096384 | tf_op jit(solution)/shard_map/gate_up/pallas_call | solution.py:77
  28.8 2.1 %down.1 = (f32[32,7168]{1,0:T(8,128)S(1)}, f32[32,7168]{1,0:T(8,128)S(1)}, bf16[32,7168]{1,0:T(8,128)(2,1)S(1)}, bf16[32,7168]{1,0:T(8,128)(2,1)S(1)}) custom-call(bf16[128,1024]{1,0:T(8,128)(2,1)S(1)} %gate_up.1.hidden_ref, bf16[1024,7168]{1,0:T(8,128)(2,1)S(1)} %bitcast.4), custom_call_target="tpu_custom_call" | custom-call | flops 1879048192 | tf_op jit(solution)/shard_map/down/pallas_call | solution.py:102
  30.9 0.3 collective-permute-start.11
  31.2 0.3 collective-permute-start.10
  31.5 1.3 %collective-permute-done.11.refs_1_ = bf16[32,7168]{1,0:T(8,128)(2,1)S(1)} collective-permute-done((bf16[32,7168]{1,0:T(8,128)(2,1)S(1)}, bf16[32,7168]{1,0:T(8,128)(2,1)S(1)}, u32[]{:S(2)}, u32[]{:S(2)}) %collective-permute-start.11) | collective-permute-done | bytes 458784 | tf_op jit(solution)/shard_map/ppermute | solution.py:206
  32.9 1.6 %collective-permute-start.17 = (bf16[8,7168]{1,0:T(8,128)(2,1)S(1)}, bf16[8,7168]{1,0:T(8,128)(2,1)S(1)}, u32[]{:S(2)}, u32[]{:S(2)}) collective-permute-start(bf16[8,7168]{1,0:T(8,128)(2,1)S(1)} %get-tuple-element.28), channel_id=1, source_target_pairs={{0,2},{2,0},{4,6},{6,4},{8,10},{10,8},{12,14},{14,12},{1,3},{3,1},... | collective-permute-start | bytes 344072 | tf_op jit(solution)/shard_map/ppermute | solution.py:203
  34.4 0.5 collective-permute-start.15
  35.0 1.5 %collective-permute-start.13 = (bf16[8,7168]{1,0:T(8,128)(2,1)S(1)}, bf16[8,7168]{1,0:T(8,128)(2,1)S(1)}, u32[]{:S(2)}, u32[]{:S(2)}) collective-permute-start(bf16[8,7168]{1,0:T(8,128)(2,1)S(1)} %get-tuple-element.24), channel_id=1, source_target_pairs={{0,2},{2,0},{4,6},{6,4},{8,10},{10,8},{12,14},{14,12},{1,3},{3,1},... | collective-permute-start | bytes 344072 | tf_op jit(solution)/shard_map/ppermute | solution.py:203
  36.5 0.5 collective-permute-start.12
  37.1 1.8 %collective-permute-done.17.refs_1_ = bf16[8,7168]{1,0:T(8,128)(2,1)S(1)} collective-permute-done((bf16[8,7168]{1,0:T(8,128)(2,1)S(1)}, bf16[8,7168]{1,0:T(8,128)(2,1)S(1)}, u32[]{:S(2)}, u32[]{:S(2)}) %collective-permute-start.17) | collective-permute-done | bytes 114720 | tf_op jit(solution)/shard_map/ppermute | solution.py:203
  38.9 3.4 %collective-permute-start.18 = (bf16[8,7168]{1,0:T(8,128)(2,1)S(1)}, bf16[8,7168]{1,0:T(8,128)(2,1)S(1)}, u32[]{:S(2)}, u32[]{:S(2)}) collective-permute-start(bf16[8,7168]{1,0:T(8,128)(2,1)S(1)} %span_sum.5), channel_id=1, source_target_pairs={{0,8},{2,10},{4,12},{6,14},{8,0},{10,2},{12,4},{14,6},{1,9},{3,11}... | collective-permute-start | bytes 344072 | tf_op jit(solution)/shard_map/ppermute | solution.py:200
  42.3 2.1 %collective-permute-start.16 = (bf16[8,7168]{1,0:T(8,128)(2,1)S(1)}, bf16[8,7168]{1,0:T(8,128)(2,1)S(1)}, u32[]{:S(2)}, u32[]{:S(2)}) collective-permute-start(bf16[8,7168]{1,0:T(8,128)(2,1)S(1)} %span_sum.4), channel_id=1, source_target_pairs={{0,12},{2,14},{4,8},{6,10},{8,4},{10,6},{12,0},{14,2},{1,13},{3,15... | collective-permute-start | bytes 344072 | tf_op jit(solution)/shard_map/ppermute | solution.py:200
  44.5 0.9 %collective-permute-start.14 = (bf16[8,7168]{1,0:T(8,128)(2,1)S(1)}, bf16[8,7168]{1,0:T(8,128)(2,1)S(1)}, u32[]{:S(2)}, u32[]{:S(2)}) collective-permute-start(bf16[8,7168]{1,0:T(8,128)(2,1)S(1)} %span_sum.3), channel_id=1, source_target_pairs={{0,4},{2,6},{4,0},{6,2},{8,12},{10,14},{12,8},{14,10},{1,5},{3,7},... | collective-permute-start | bytes 344072 | tf_op jit(solution)/shard_map/ppermute | solution.py:200
  45.5 4.0 %collective-permute-done.18.refs_4_ = bf16[8,7168]{1,0:T(8,128)(2,1)S(1)} collective-permute-done((bf16[8,7168]{1,0:T(8,128)(2,1)S(1)}, bf16[8,7168]{1,0:T(8,128)(2,1)S(1)}, u32[]{:S(2)}, u32[]{:S(2)}) %collective-permute-start.18) | collective-permute-done | bytes 114720 | tf_op jit(solution)/shard_map/ppermute | solution.py:200
  49.6 0.6 %collective-permute-done.16.refs_3_ = bf16[8,7168]{1,0:T(8,128)(2,1)S(1)} collective-permute-done((bf16[8,7168]{1,0:T(8,128)(2,1)S(1)}, bf16[8,7168]{1,0:T(8,128)(2,1)S(1)}, u32[]{:S(2)}, u32[]{:S(2)}) %collective-permute-start.16) | collective-permute-done | bytes 114720 | tf_op jit(solution)/shard_map/ppermute | solution.py:200
  50.1 1.2 %collective-permute-done.14.refs_2_ = bf16[8,7168]{1,0:T(8,128)(2,1)S(1)} collective-permute-done((bf16[8,7168]{1,0:T(8,128)(2,1)S(1)}, bf16[8,7168]{1,0:T(8,128)(2,1)S(1)}, u32[]{:S(2)}, u32[]{:S(2)}) %collective-permute-start.14) | collective-permute-done | bytes 114720 | tf_op jit(solution)/shard_map/ppermute | solution.py:200
  51.3 0.8 %combine.1 = bf16[8,7168]{1,0:T(8,128)(2,1)} custom-call(f32[8,512]{1,0:T(8,128)S(1)} %coefficients.1.coeff_ref, f32[8,7168]{1,0:T(8,128)S(1)} %get-tuple-element.19.refs_0_, bf16[8,7168]{1,0:T(8,128)(2,1)S(1)} %collective-permute-done.12.refs_1_, bf16[8,7168]{1,0:T(8,128)(2,1)S(1)} %collective-permute-done.14.refs_2_, ...), custom_call_target="tpu_custom_call" | custom-call | tf_op jit(solution)/shard_map/combine/pallas_call | solution.py:185
  (39 shorter events, 0.8 us)
Async XLA Ops:
  0.0 10.0 %collective-permute-start = (bf16[8,7168]{1,0:T(8,128)(2,1)}, bf16[8,7168]{1,0:T(8,128)(2,1)S(1)}, u32[]{:S(2)}, u32[]{:S(2)}) collective-permute-start(bf16[8,7168]{1,0:T(8,128)(2,1)} %refs_0_.1), channel_id=1, source_target_pairs={{0,8},{2,10},{4,12},{6,14},{8,0},{10,2},{12,4},{14,6},{1,9},{3,11}... | collective-permute-start | bytes 344072 | tf_op jit(solution)/shard_map/ppermute | solution.py:200
  4.0 0.9 %copy-start.4 = (bf16[8,7168]{1,0:T(8,128)(2,1)S(1)}, bf16[8,7168]{1,0:T(8,128)(2,1)}, u32[]{:S(2)}) copy-start(bf16[8,7168]{1,0:T(8,128)(2,1)} %refs_0_.1) | copy-start | bytes 344068
  5.0 19.3 %copy-start.1 = (bf16[7168,1024]{1,0:T(8,128)(2,1)S(1)}, bf16[7168,1024]{1,0:T(8,128)(2,1)}, u32[]{:S(2)}) copy-start(bf16[7168,1024]{1,0:T(8,128)(2,1)} %refs_5_.1) | copy-start | bytes 44040196
  5.0 19.3 %copy-start = (bf16[7168,1024]{1,0:T(8,128)(2,1)S(1)}, bf16[7168,1024]{1,0:T(8,128)(2,1)}, u32[]{:S(2)}) copy-start(bf16[7168,1024]{1,0:T(8,128)(2,1)} %refs_4_.1) | copy-start | bytes 44040196
  5.0 7.3 %collective-permute-start.1 = (bf16[8,7168]{1,0:T(8,128)(2,1)S(1)}, bf16[8,7168]{1,0:T(8,128)(2,1)S(1)}, u32[]{:S(2)}, u32[]{:S(2)}) collective-permute-start(bf16[8,7168]{1,0:T(8,128)(2,1)S(1)} %stack.5.refs_0_), channel_id=1, source_target_pairs={{0,4},{2,6},{4,0},{6,2},{8,12},{10,14},{12,8},{14,10},{1,5},{3,7},... | collective-permute-start | bytes 344072 | tf_op jit(solution)/shard_map/ppermute | solution.py:200
  10.0 4.8 %collective-permute-start.2 = (bf16[8,7168]{1,0:T(8,128)(2,1)S(1)}, bf16[8,7168]{1,0:T(8,128)(2,1)S(1)}, u32[]{:S(2)}, u32[]{:S(2)}) collective-permute-start(bf16[8,7168]{1,0:T(8,128)(2,1)S(1)} %collective-permute-done.refs_1_), channel_id=1, source_target_pairs={{0,4},{2,6},{4,0},{6,2},{8,12},{10,14},{12,8},{14,10},{1,5},{3,7},... | collective-permute-start | bytes 344072 | tf_op jit(solution)/shard_map/ppermute | solution.py:200
  10.7 6.0 %collective-permute-start.3 = (bf16[8,7168]{1,0:T(8,128)(2,1)S(1)}, bf16[8,7168]{1,0:T(8,128)(2,1)S(1)}, u32[]{:S(2)}, u32[]{:S(2)}) collective-permute-start(bf16[8,7168]{1,0:T(8,128)(2,1)S(1)} %stack.5.refs_0_), channel_id=1, source_target_pairs={{0,2},{2,0},{4,6},{6,4},{8,10},{10,8},{12,14},{14,12},{1,3},{3,1},... | collective-permute-start | bytes 344072 | tf_op jit(solution)/shard_map/ppermute | solution.py:203
  12.2 6.9 %collective-permute-start.5 = (bf16[8,7168]{1,0:T(8,128)(2,1)S(1)}, bf16[8,7168]{1,0:T(8,128)(2,1)S(1)}, u32[]{:S(2)}, u32[]{:S(2)}) collective-permute-start(bf16[8,7168]{1,0:T(8,128)(2,1)S(1)} %collective-permute-done.1.refs_2_), channel_id=1, source_target_pairs={{0,2},{2,0},{4,6},{6,4},{8,10},{10,8},{12,14},{14,12},{1,3},{3,1},... | collective-permute-start | bytes 344072 | tf_op jit(solution)/shard_map/ppermute | solution.py:203
  12.8 8.9 %collective-permute-start.4 = (bf16[8,7168]{1,0:T(8,128)(2,1)S(1)}, bf16[8,7168]{1,0:T(8,128)(2,1)S(1)}, u32[]{:S(2)}, u32[]{:S(2)}) collective-permute-start(bf16[8,7168]{1,0:T(8,128)(2,1)S(1)} %collective-permute-done.refs_1_), channel_id=1, source_target_pairs={{0,2},{2,0},{4,6},{6,4},{8,10},{10,8},{12,14},{14,12},{1,3},{3,1},... | collective-permute-start | bytes 344072 | tf_op jit(solution)/shard_map/ppermute | solution.py:203
  14.7 8.1 %collective-permute-start.6 = (bf16[8,7168]{1,0:T(8,128)(2,1)S(1)}, bf16[8,7168]{1,0:T(8,128)(2,1)S(1)}, u32[]{:S(2)}, u32[]{:S(2)}) collective-permute-start(bf16[8,7168]{1,0:T(8,128)(2,1)S(1)} %collective-permute-done.2.refs_3_), channel_id=1, source_target_pairs={{0,2},{2,0},{4,6},{6,4},{8,10},{10,8},{12,14},{14,12},{1,3},{3,1},... | collective-permute-start | bytes 344072 | tf_op jit(solution)/shard_map/ppermute | solution.py:203
  16.4 7.9 %collective-permute-start.7 = (bf16[32,7168]{1,0:T(8,128)(2,1)S(1)}, bf16[32,7168]{1,0:T(8,128)(2,1)S(1)}, u32[]{:S(2)}, u32[]{:S(2)}) collective-permute-start(bf16[32,7168]{1,0:T(8,128)(2,1)S(1)} %stack.7), channel_id=1, source_target_pairs={{0,1},{1,0},{2,3},{3,2},{4,5},{5,4},{6,7},{7,6},{8,9},{9,8},{10,11... | collective-permute-start | bytes 1376264 | tf_op jit(solution)/shard_map/ppermute | solution.py:206
  21.7 2.6 %collective-permute-start.8 = (bf16[24,7168]{1,0:T(8,128)(2,1)S(1)}, bf16[24,7168]{1,0:T(8,128)(2,1)S(1)}, u32[]{:S(2)}, u32[]{:S(2)}) collective-permute-start(bf16[24,7168]{1,0:T(8,128)(2,1)S(1)} %stack.8), channel_id=1, source_target_pairs={{0,1},{1,0},{2,3},{3,2},{4,5},{5,4},{6,7},{7,6},{8,9},{9,8},{10,11... | collective-permute-start | bytes 1032200 | tf_op jit(solution)/shard_map/ppermute | solution.py:206
  22.9 1.4 %collective-permute-start.9 = (bf16[8,7168]{1,0:T(8,128)(2,1)S(1)}, bf16[8,7168]{1,0:T(8,128)(2,1)S(1)}, u32[]{:S(2)}, u32[]{:S(2)}) collective-permute-start(bf16[8,7168]{1,0:T(8,128)(2,1)S(1)} %stack.9), channel_id=1, source_target_pairs={{0,1},{1,0},{2,3},{3,2},{4,5},{5,4},{6,7},{7,6},{8,9},{9,8},{10,11... | collective-permute-start | bytes 344072 | tf_op jit(solution)/shard_map/ppermute | solution.py:206
  23.0 5.8 %slice-start = ((s8[14680064]{0:T(1024)(128)(4,1)}), s8[4194304]{0:T(1024)(128)(4,1)S(1)}, s32[]{:S(2)}) async-start(s8[14680064]{0:T(1024)(128)(4,1)} %bitcast.3), calls=%async_computation | async-start | bytes 8388608
  23.1 5.7 %slice-start.1 = ((s8[14680064]{0:T(1024)(128)(4,1)}), s8[4194304]{0:T(1024)(128)(4,1)S(1)}, s32[]{:S(2)}) async-start(s8[14680064]{0:T(1024)(128)(4,1)} %bitcast.3), calls=%async_computation.1 | async-start | bytes 8388608
  23.1 5.7 %slice-start.2 = ((s8[14680064]{0:T(1024)(128)(4,1)}), s8[4194304]{0:T(1024)(128)(4,1)S(1)}, s32[]{:S(2)}) async-start(s8[14680064]{0:T(1024)(128)(4,1)} %bitcast.3), calls=%async_computation.2 | async-start | bytes 8388608
  23.1 5.7 %slice-start.3 = ((s8[14680064]{0:T(1024)(128)(4,1)}), s8[2097152]{0:T(1024)(128)(4,1)S(1)}, s32[]{:S(2)}) async-start(s8[14680064]{0:T(1024)(128)(4,1)} %bitcast.3), calls=%async_computation.3 | async-start | bytes 4194304
  28.8 16.6 %copy-start.2 = (s32[8,3]{0,1:T(4,128)S(1)}, s32[8,3]{0,1:T(4,128)}, u32[]{:S(2)}) copy-start(s32[8,3]{0,1:T(4,128)} %param.7) | copy-start | bytes 292
  28.8 16.6 %copy-start.3 = (f32[8,3]{0,1:T(4,128)S(1)}, f32[8,3]{0,1:T(4,128)}, u32[]{:S(2)}) copy-start(f32[8,3]{0,1:T(4,128)} %param.8) | copy-start | bytes 292
  30.9 1.9 %collective-permute-start.11 = (bf16[32,7168]{1,0:T(8,128)(2,1)S(1)}, bf16[32,7168]{1,0:T(8,128)(2,1)S(1)}, u32[]{:S(2)}, u32[]{:S(2)}) collective-permute-start(bf16[32,7168]{1,0:T(8,128)(2,1)S(1)} %get-tuple-element.21), channel_id=1, source_target_pairs={{0,1},{1,0},{2,3},{3,2},{4,5},{5,4},{6,7},{7,6},{8,9},{9,8},{10,11... | collective-permute-start | bytes 1376264 | tf_op jit(solution)/shard_map/ppermute | solution.py:206
  31.2 5.8 %collective-permute-start.10 = (bf16[32,7168]{1,0:T(8,128)(2,1)S(1)}, bf16[32,7168]{1,0:T(8,128)(2,1)S(1)}, u32[]{:S(2)}, u32[]{:S(2)}) collective-permute-start(bf16[32,7168]{1,0:T(8,128)(2,1)S(1)} %get-tuple-element.18), channel_id=1, source_target_pairs={{0,1},{1,0},{2,3},{3,2},{4,5},{5,4},{6,7},{7,6},{8,9},{9,8},{10,11... | collective-permute-start | bytes 1376264 | tf_op jit(solution)/shard_map/ppermute | solution.py:206
  32.9 6.1 %collective-permute-start.17 = (bf16[8,7168]{1,0:T(8,128)(2,1)S(1)}, bf16[8,7168]{1,0:T(8,128)(2,1)S(1)}, u32[]{:S(2)}, u32[]{:S(2)}) collective-permute-start(bf16[8,7168]{1,0:T(8,128)(2,1)S(1)} %get-tuple-element.28), channel_id=1, source_target_pairs={{0,2},{2,0},{4,6},{6,4},{8,10},{10,8},{12,14},{14,12},{1,3},{3,1},... | collective-permute-start | bytes 344072 | tf_op jit(solution)/shard_map/ppermute | solution.py:203
  34.4 7.9 %collective-permute-start.15 = (bf16[8,7168]{1,0:T(8,128)(2,1)S(1)}, bf16[8,7168]{1,0:T(8,128)(2,1)S(1)}, u32[]{:S(2)}, u32[]{:S(2)}) collective-permute-start(bf16[8,7168]{1,0:T(8,128)(2,1)S(1)} %get-tuple-element.26), channel_id=1, source_target_pairs={{0,2},{2,0},{4,6},{6,4},{8,10},{10,8},{12,14},{14,12},{1,3},{3,1},... | collective-permute-start | bytes 344072 | tf_op jit(solution)/shard_map/ppermute | solution.py:203
  35.0 9.5 %collective-permute-start.13 = (bf16[8,7168]{1,0:T(8,128)(2,1)S(1)}, bf16[8,7168]{1,0:T(8,128)(2,1)S(1)}, u32[]{:S(2)}, u32[]{:S(2)}) collective-permute-start(bf16[8,7168]{1,0:T(8,128)(2,1)S(1)} %get-tuple-element.24), channel_id=1, source_target_pairs={{0,2},{2,0},{4,6},{6,4},{8,10},{10,8},{12,14},{14,12},{1,3},{3,1},... | collective-permute-start | bytes 344072 | tf_op jit(solution)/shard_map/ppermute | solution.py:203
  36.5 9.1 %collective-permute-start.12 = (bf16[8,7168]{1,0:T(8,128)(2,1)S(1)}, bf16[8,7168]{1,0:T(8,128)(2,1)S(1)}, u32[]{:S(2)}, u32[]{:S(2)}) collective-permute-start(bf16[8,7168]{1,0:T(8,128)(2,1)S(1)} %get-tuple-element.22), channel_id=1, source_target_pairs={{0,2},{2,0},{4,6},{6,4},{8,10},{10,8},{12,14},{14,12},{1,3},{3,1},... | collective-permute-start | bytes 344072 | tf_op jit(solution)/shard_map/ppermute | solution.py:203
  38.9 10.6 %collective-permute-start.18 = (bf16[8,7168]{1,0:T(8,128)(2,1)S(1)}, bf16[8,7168]{1,0:T(8,128)(2,1)S(1)}, u32[]{:S(2)}, u32[]{:S(2)}) collective-permute-start(bf16[8,7168]{1,0:T(8,128)(2,1)S(1)} %span_sum.5), channel_id=1, source_target_pairs={{0,8},{2,10},{4,12},{6,14},{8,0},{10,2},{12,4},{14,6},{1,9},{3,11}... | collective-permute-start | bytes 344072 | tf_op jit(solution)/shard_map/ppermute | solution.py:200
  42.3 7.8 %collective-permute-start.16 = (bf16[8,7168]{1,0:T(8,128)(2,1)S(1)}, bf16[8,7168]{1,0:T(8,128)(2,1)S(1)}, u32[]{:S(2)}, u32[]{:S(2)}) collective-permute-start(bf16[8,7168]{1,0:T(8,128)(2,1)S(1)} %span_sum.4), channel_id=1, source_target_pairs={{0,12},{2,14},{4,8},{6,10},{8,4},{10,6},{12,0},{14,2},{1,13},{3,15... | collective-permute-start | bytes 344072 | tf_op jit(solution)/shard_map/ppermute | solution.py:200
  44.5 6.8 %collective-permute-start.14 = (bf16[8,7168]{1,0:T(8,128)(2,1)S(1)}, bf16[8,7168]{1,0:T(8,128)(2,1)S(1)}, u32[]{:S(2)}, u32[]{:S(2)}) collective-permute-start(bf16[8,7168]{1,0:T(8,128)(2,1)S(1)} %span_sum.3), channel_id=1, source_target_pairs={{0,4},{2,6},{4,0},{6,2},{8,12},{10,14},{12,8},{14,10},{1,5},{3,7},... | collective-permute-start | bytes 344072 | tf_op jit(solution)/shard_map/ppermute | solution.py:200

commit v10 on v8

--- a/solution.py
+++ b/solution.py
@@ -9,7 +9,8 @@
 
 EXPERTS = 4
 LANES = 128
-RETURN_ORDER = (1, 3, 2)
+RETURN_ORDER = (2, 3, 1)
+SEND_ORDER = (2, 3, 1, 0)
 BLOCK_ORDER = (0, 2, 1, 3)
 N_BLOCK = 256
 LAST_FLOPS = 5_000_000_000
@@ -116,13 +117,16 @@
     blocks = (hidden_ref.shape[0] // rows, rows, tail)
     last = lax.broadcasted_iota(jnp.int32, blocks, 1) == rows - 1
     hidden = hidden_ref[...]
-    ends = jnp.dot(hidden, down_ref[:, width:], preferred_element_type=jnp.float32).reshape(blocks)
-    for i in range(rows - 1):
-        columns = slice(i * tail, (i + 1) * tail)
-        value = jnp.dot(hidden, down_ref[:, columns], preferred_element_type=jnp.float32).reshape(blocks)
-        value = jnp.where(last, jnp.broadcast_to(ends[:, i:i + 1, :], blocks), value).reshape(blocks[0] * rows, tail)
-        for j, ref in enumerate(outs):
-            ref[:, columns] = value[j * count:(j + 1) * count].astype(ref.dtype)
+    ends = None
+    for i in [rows - 2] + list(range(0, rows - 2, 2)):
+        both = jnp.dot(hidden, down_ref[:, i * tail:(i + 2) * tail], preferred_element_type=jnp.float32)
+        pieces = {i: both[:, :tail].reshape(blocks), i + 1: both[:, tail:].reshape(blocks)}
+        if ends is None:
+            ends = pieces.pop(i + 1)
+        for j, value in pieces.items():
+            value = jnp.where(last, jnp.broadcast_to(ends[:, j:j + 1, :], blocks), value).reshape(blocks[0] * rows, tail)
+            for k, ref in enumerate(outs):
+                ref[:, j * tail:(j + 1) * tail] = value[k * count:(k + 1) * count].astype(ref.dtype)
 
 
 def down(hidden, down_weight, span, pair, rows):
@@ -287,25 +291,16 @@
 
     (own_keep, *own_sends), *far = down(hidden, down_weight, span, pair, rows)
     far = [paired(keep, sends) for keep, *sends in far]
-    order = (2, 3, 1, 0)
-    blocks = [{} for _ in far]
-    sums, returned, after = {}, {}, []
-    for wave in (order[:2], order[2:]):
-        places = [BLOCK_ORDER.index(s) for s in wave]
-        for t, arrays in enumerate(far):
-            blocks[t].update(zip(wave, pair_sum(arrays, rows, jnp.bfloat16, places, after)))
-        if not sums:
-            first = [blocks[t][s] for t in range(len(far)) for s in wave][:1]
-            own_sends = [stack([b], first) for b in own_sends]
-            own = pair_sum(paired(own_keep, own_sends), rows, jnp.float32, range(EXPERTS))
-            own = dict(zip(BLOCK_ORDER, own))
-        for s in wave:
-            sums[s] = [own[s]] + [over_span(b[s], -t) for t, b in enumerate(blocks, 1)]
-            if s:
-                total = span_sum(sums[s])
-                returned[s] = over_experts(total, s)
-                after = [total]
-    return combine(sides, sums[0], [returned[s] for s in RETURN_ORDER], width)
+    first, *later = SEND_ORDER
+    blocks = [{first: pair_sum(a, rows, jnp.bfloat16, [BLOCK_ORDER.index(first)])[0]} for a in far]
+    own_sends = [stack([b], [blocks[0][first]]) for b in own_sends]
+    own = dict(zip(BLOCK_ORDER, pair_sum(paired(own_keep, own_sends), rows, jnp.float32, range(EXPERTS))))
+    for block, arrays in zip(blocks, far):
+        places = [BLOCK_ORDER.index(s) for s in later]
+        block.update(zip(later, pair_sum(arrays, rows, jnp.bfloat16, places, [own[first]])))
+    sums = {s: [own[s]] + [over_span(b[s], -t) for t, b in enumerate(blocks, 1)] for s in SEND_ORDER}
+    returned = [over_experts(span_sum(sums[s]), s) for s in RETURN_ORDER]
+    return combine(sides, sums[0], returned, width)
 
 
 def solution(mesh):

time: 50.3 us -> 48.8 us (0.970)
  waiting for transfers between devices: 18.8 us -> 16.3 us
  starting transfers between devices: 21 us -> 22.3 us
    ppermute x8, waiting for transfers between devices: 10.7 us -> 5.53 us  [over_span(): lax.ppermute(value, 'attn', [(i, i // span * span + (i + shift) % span) f...]
    ppermute x6, waiting for transfers between devices: 5.55 us -> 8.19 us  [over_experts(): lax.ppermute(value, 'attn', [(i, (i // span ^ other) * span + i % span) f...]
    ppermute x8, starting transfers between devices: 9.93 us -> 10.8 us  [over_span(): lax.ppermute(value, 'attn', [(i, i // span * span + (i + shift) % span) f...]
where the time goes in v10:
time: 48.8 us; the launch traced here: 48.7 us
  starting transfers between devices  22.3 us (46%)
  waiting for transfers between devices  16.3 us (33%)
  Pallas kernels  9.72 us (20%)
    ppermute x6, starting transfers between devices, over_experts(): lax.ppermute(value, 'attn', [(i, (i // span ^ other) * span + i % span) f...  10.9 us
    ppermute x8, starting transfers between devices, over_span(): lax.ppermute(value, 'attn', [(i, i // span * span + (i + shift) % span) f...  10.8 us
    ppermute x6, waiting for transfers between devices, over_experts(): lax.ppermute(value, 'attn', [(i, (i // span ^ other) * span + i % span) f...  8.19 us
    ppermute x8, waiting for transfers between devices, over_span(): lax.ppermute(value, 'attn', [(i, i // span * span + (i + shift) % span) f...  5.53 us
    pallas_call x1, Pallas kernels, gate_up(): pl.pallas_call(functools.partial(gate_up_kernel, block_of(units, N_BLOCK)...  4.69 us
    ppermute x5, waiting for transfers between devices, over_pair(): lax.ppermute(value, 'ffn', [(i, (i + shift) % pair) for i in range(pair)])  2.6 us
    pallas_call x1, Pallas kernels, down(): pl.pallas_call(functools.partial(down_kernel, rows), in_specs=[pl.BlockSp...  2.22 us
    pallas_call x1, Pallas kernels, pack(): pl.pallas_call(pack_kernel, in_specs=[pl.BlockSpec(memory_space=pltpu.SME...  1.3 us
  transfers between devices with their start and end apart: 19, of which 10 were waited for; matrix products, arithmetic and copies ran while one was open for 0% of the time, Pallas kernels for 1%

profile of v10, /device:TPU:0, one launch (start us, length us, event | category | flops | bytes accessed | tf_op | source)
XLA Modules:
  0.0 48.7 jit_solution(15360325804422466152)
XLA Ops:
  0.0 1.3 %pack.1 = (f32[8,1024]{1,0:T(8,128)S(1)}, bf16[8,6272]{1,0:T(8,128)(2,1)S(1)}, bf16[8,6272]{1,0:T(8,128)(2,1)S(1)}, bf16[8,6272]{1,0:T(8,128)(2,1)S(1)}, bf16[8,6272]{1,0:T(8,128)(2,1)S(1)}) custom-call(s32[1]{0:T(128)} %bitcast.own_expert, bf16[8,7168]{1,0:T(8,128)(2,1)} %tokens_hbm.1, s32[3,8]{1,0:T(4,128)} %bitcast.9, f32[3,8]{1,0:T(4,128)} %bitcast.10), custom_call_target="tpu_custom_call" | custom-call | flops 20000000000 | tf_op jit(solution)/shard_map/pack/pallas_call | solution.py:221
  1.4 4.1 %collective-permute-start = (bf16[8,6272]{1,0:T(8,128)(2,1)S(1)}, bf16[8,6272]{1,0:T(8,128)(2,1)S(1)}, u32[]{:S(2)}, u32[]{:S(2)}) collective-permute-start(bf16[8,6272]{1,0:T(8,128)(2,1)S(1)} %get-tuple-element.23), channel_id=1, source_target_pairs={{0,8},{2,10},{4,12},{6,14},{8,0},{10,2},{12,4},{14,6},{1,9},{3,11}... | collective-permute-start | bytes 301064 | tf_op jit(solution)/shard_map/ppermute | solution.py:269
  5.5 1.6 %collective-permute-start.1 = (bf16[8,6272]{1,0:T(8,128)(2,1)S(1)}, bf16[8,6272]{1,0:T(8,128)(2,1)S(1)}, u32[]{:S(2)}, u32[]{:S(2)}) collective-permute-start(bf16[8,6272]{1,0:T(8,128)(2,1)S(1)} %get-tuple-element.24), channel_id=1, source_target_pairs={{0,4},{2,6},{4,0},{6,2},{8,12},{10,14},{12,8},{14,10},{1,5},{3,7},... | collective-permute-start | bytes 301064 | tf_op jit(solution)/shard_map/ppermute | solution.py:269
  7.0 1.7 %collective-permute-start.3 = (bf16[8,6272]{1,0:T(8,128)(2,1)S(1)}, bf16[8,6272]{1,0:T(8,128)(2,1)S(1)}, u32[]{:S(2)}, u32[]{:S(2)}) collective-permute-start(bf16[8,6272]{1,0:T(8,128)(2,1)S(1)} %get-tuple-element.22.refs_0_), channel_id=1, source_target_pairs={{0,2},{2,0},{4,6},{6,4},{8,10},{10,8},{12,14},{14,12},{1,3},{3,1},... | collective-permute-start | bytes 301064 | tf_op jit(solution)/shard_map/ppermute | solution.py:272
  8.8 2.9 %collective-permute-done.refs_1_ = bf16[8,6272]{1,0:T(8,128)(2,1)S(1)} collective-permute-done((bf16[8,6272]{1,0:T(8,128)(2,1)S(1)}, bf16[8,6272]{1,0:T(8,128)(2,1)S(1)}, u32[]{:S(2)}, u32[]{:S(2)}) %collective-permute-start) | collective-permute-done | bytes 100384 | tf_op jit(solution)/shard_map/ppermute | solution.py:269
  11.7 1.7 %collective-permute-start.4 = (bf16[8,6272]{1,0:T(8,128)(2,1)S(1)}, bf16[8,6272]{1,0:T(8,128)(2,1)S(1)}, u32[]{:S(2)}, u32[]{:S(2)}) collective-permute-start(bf16[8,6272]{1,0:T(8,128)(2,1)S(1)} %collective-permute-done.refs_1_), channel_id=1, source_target_pairs={{0,2},{2,0},{4,6},{6,4},{8,10},{10,8},{12,14},{14,12},{1,3},{3,1},... | collective-permute-start | bytes 301064 | tf_op jit(solution)/shard_map/ppermute | solution.py:272
  13.4 0.3 collective-permute-start.5
  13.8 1.7 %collective-permute-start.6 = (bf16[8,6272]{1,0:T(8,128)(2,1)S(1)}, bf16[8,6272]{1,0:T(8,128)(2,1)S(1)}, u32[]{:S(2)}, u32[]{:S(2)}) collective-permute-start(bf16[8,6272]{1,0:T(8,128)(2,1)S(1)} %collective-permute-done.2.refs_3_), channel_id=1, source_target_pairs={{0,2},{2,0},{4,6},{6,4},{8,10},{10,8},{12,14},{14,12},{1,3},{3,1},... | collective-permute-start | bytes 301064 | tf_op jit(solution)/shard_map/ppermute | solution.py:272
  15.6 1.6 %collective-permute-done.4.refs_5_.refs_1_ = bf16[8,6272]{1,0:T(8,128)(2,1)S(1)} collective-permute-done((bf16[8,6272]{1,0:T(8,128)(2,1)S(1)}, bf16[8,6272]{1,0:T(8,128)(2,1)S(1)}, u32[]{:S(2)}, u32[]{:S(2)}) %collective-permute-start.4) | collective-permute-done | bytes 100384 | tf_op jit(solution)/shard_map/ppermute | solution.py:272
  17.2 1.3 %collective-permute-done.5.refs_6_.refs_2_ = bf16[8,6272]{1,0:T(8,128)(2,1)S(1)} collective-permute-done((bf16[8,6272]{1,0:T(8,128)(2,1)S(1)}, bf16[8,6272]{1,0:T(8,128)(2,1)S(1)}, u32[]{:S(2)}, u32[]{:S(2)}) %collective-permute-start.5) | collective-permute-done | bytes 100384 | tf_op jit(solution)/shard_map/ppermute | solution.py:272
  18.5 0.1 collective-permute-start.8
  18.6 1.0 %collective-permute-done.6.refs_7_.refs_0_ = bf16[8,6272]{1,0:T(8,128)(2,1)S(1)} collective-permute-done((bf16[8,6272]{1,0:T(8,128)(2,1)S(1)}, bf16[8,6272]{1,0:T(8,128)(2,1)S(1)}, u32[]{:S(2)}, u32[]{:S(2)}) %collective-permute-start.6) | collective-permute-done | bytes 100384 | tf_op jit(solution)/shard_map/ppermute | solution.py:272
  19.7 0.2 unpack.1.first_ref
  20.0 1.0 %collective-permute-done.9.refs_2_ = bf16[8,6272]{1,0:T(8,128)(2,1)S(1)} collective-permute-done((bf16[8,6272]{1,0:T(8,128)(2,1)S(1)}, bf16[8,6272]{1,0:T(8,128)(2,1)S(1)}, u32[]{:S(2)}, u32[]{:S(2)}) %collective-permute-start.9) | collective-permute-done | bytes 100384 | tf_op jit(solution)/shard_map/ppermute | solution.py:275
  21.1 4.7 %gate_up.1.hidden_ref = bf16[128,1024]{1,0:T(8,128)(2,1)S(1)} custom-call(bf16[64,7168]{1,0:T(8,128)(2,1)S(1)} %unpack.1.first_ref, bf16[32,6272]{1,0:T(8,128)(2,1)S(1)} %collective-permute-done.7.refs_0_, bf16[24,6272]{1,0:T(8,128)(2,1)S(1)} %collective-permute-done.8.refs_1_, bf16[8,6272]{1,0:T(8,128)(2,1)S(1)} %collective-permute-done.9.refs_2_, ...), custom_call_target="tpu_custom_call" | custom-call | flops 3758096384 | tf_op jit(solution)/shard_map/gate_up/pallas_call | solution.py:103
  25.8 2.2 %down.1 = (f32[32,6272]{1,0:T(8,128)S(1)}, f32[32,6272]{1,0:T(8,128)S(1)}, bf16[32,6272]{1,0:T(8,128)(2,1)S(1)}, bf16[32,6272]{1,0:T(8,128)(2,1)S(1)}) custom-call(bf16[128,1024]{1,0:T(8,128)(2,1)S(1)} %gate_up.1.hidden_ref, bf16[1024,7168]{1,0:T(8,128)(2,1)S(1)} %bitcast.8), custom_call_target="tpu_custom_call" | custom-call | flops 1644167168 | tf_op jit(solution)/shard_map/down/pallas_call | solution.py:136
  28.0 0.2 collective-permute-start.10
  28.3 1.6 %collective-permute-done.10.refs_1_ = bf16[32,6272]{1,0:T(8,128)(2,1)S(1)} collective-permute-done((bf16[32,6272]{1,0:T(8,128)(2,1)S(1)}, bf16[32,6272]{1,0:T(8,128)(2,1)S(1)}, u32[]{:S(2)}, u32[]{:S(2)}) %collective-permute-start.10) | collective-permute-done | bytes 401440 | tf_op jit(solution)/shard_map/ppermute | solution.py:275
  29.9 0.2 collective-permute-start.11
  30.1 1.7 %collective-permute-start.13 = (bf16[8,6272]{1,0:T(8,128)(2,1)S(1)}, bf16[8,6272]{1,0:T(8,128)(2,1)S(1)}, u32[]{:S(2)}, u32[]{:S(2)}) collective-permute-start(bf16[8,6272]{1,0:T(8,128)(2,1)S(1)} %pair_sum.3.refs_1_), channel_id=1, source_target_pairs={{0,2},{2,0},{4,6},{6,4},{8,10},{10,8},{12,14},{14,12},{1,3},{3,1},... | collective-permute-start | bytes 301064 | tf_op jit(solution)/shard_map/ppermute | solution.py:272
  31.8 0.1 pair_sum.4
  31.9 0.1 pair_sum.5
  32.0 1.6 %collective-permute-start.15 = (bf16[8,6272]{1,0:T(8,128)(2,1)S(1)}, bf16[8,6272]{1,0:T(8,128)(2,1)S(1)}, u32[]{:S(2)}, u32[]{:S(2)}) collective-permute-start(bf16[8,6272]{1,0:T(8,128)(2,1)S(1)} %get-tuple-element.34), channel_id=1, source_target_pairs={{0,2},{2,0},{4,6},{6,4},{8,10},{10,8},{12,14},{14,12},{1,3},{3,1},... | collective-permute-start | bytes 301064 | tf_op jit(solution)/shard_map/ppermute | solution.py:272
  33.6 0.4 collective-permute-start.17
  34.1 1.6 %collective-permute-done.13.refs_1_ = bf16[8,6272]{1,0:T(8,128)(2,1)S(1)} collective-permute-done((bf16[8,6272]{1,0:T(8,128)(2,1)S(1)}, bf16[8,6272]{1,0:T(8,128)(2,1)S(1)}, u32[]{:S(2)}, u32[]{:S(2)}) %collective-permute-start.13) | collective-permute-done | bytes 100384 | tf_op jit(solution)/shard_map/ppermute | solution.py:272
  35.8 2.7 %collective-permute-start.14 = (bf16[8,6272]{1,0:T(8,128)(2,1)S(1)}, bf16[8,6272]{1,0:T(8,128)(2,1)S(1)}, u32[]{:S(2)}, u32[]{:S(2)}) collective-permute-start(bf16[8,6272]{1,0:T(8,128)(2,1)S(1)} %span_sum.3), channel_id=1, source_target_pairs={{0,8},{2,10},{4,12},{6,14},{8,0},{10,2},{12,4},{14,6},{1,9},{3,11}... | collective-permute-start | bytes 301064 | tf_op jit(solution)/shard_map/ppermute | solution.py:269
  38.5 1.5 %collective-permute-start.12 = (bf16[8,6272]{1,0:T(8,128)(2,1)S(1)}, bf16[8,6272]{1,0:T(8,128)(2,1)S(1)}, u32[]{:S(2)}, u32[]{:S(2)}) collective-permute-start(bf16[8,6272]{1,0:T(8,128)(2,1)S(1)} %get-tuple-element.32), channel_id=1, source_target_pairs={{0,2},{2,0},{4,6},{6,4},{8,10},{10,8},{12,14},{14,12},{1,3},{3,1},... | collective-permute-start | bytes 301064 | tf_op jit(solution)/shard_map/ppermute | solution.py:272
  40.0 2.4 %collective-permute-start.16 = (bf16[8,6272]{1,0:T(8,128)(2,1)S(1)}, bf16[8,6272]{1,0:T(8,128)(2,1)S(1)}, u32[]{:S(2)}, u32[]{:S(2)}) collective-permute-start(bf16[8,6272]{1,0:T(8,128)(2,1)S(1)} %span_sum.4), channel_id=1, source_target_pairs={{0,12},{2,14},{4,8},{6,10},{8,4},{10,6},{12,0},{14,2},{1,13},{3,15... | collective-permute-start | bytes 301064 | tf_op jit(solution)/shard_map/ppermute | solution.py:269
  42.5 2.2 %collective-permute-done.14.refs_2_ = bf16[8,6272]{1,0:T(8,128)(2,1)S(1)} collective-permute-done((bf16[8,6272]{1,0:T(8,128)(2,1)S(1)}, bf16[8,6272]{1,0:T(8,128)(2,1)S(1)}, u32[]{:S(2)}, u32[]{:S(2)}) %collective-permute-start.14) | collective-permute-done | bytes 100384 | tf_op jit(solution)/shard_map/ppermute | solution.py:269
  44.7 2.0 %collective-permute-done.16.refs_3_ = bf16[8,6272]{1,0:T(8,128)(2,1)S(1)} collective-permute-done((bf16[8,6272]{1,0:T(8,128)(2,1)S(1)}, bf16[8,6272]{1,0:T(8,128)(2,1)S(1)}, u32[]{:S(2)}, u32[]{:S(2)}) %collective-permute-start.16) | collective-permute-done | bytes 100384 | tf_op jit(solution)/shard_map/ppermute | solution.py:269
  46.8 1.0 %collective-permute-done.18.refs_4_ = bf16[8,6272]{1,0:T(8,128)(2,1)S(1)} collective-permute-done((bf16[8,6272]{1,0:T(8,128)(2,1)S(1)}, bf16[8,6272]{1,0:T(8,128)(2,1)S(1)}, u32[]{:S(2)}, u32[]{:S(2)}) %collective-permute-start.18) | collective-permute-done | bytes 100384 | tf_op jit(solution)/shard_map/ppermute | solution.py:269
  47.8 0.9 %combine.1 = bf16[8,7168]{1,0:T(8,128)(2,1)} custom-call(f32[8,1024]{1,0:T(8,128)S(1)} %get-tuple-element.21.sides_ref, f32[8,6272]{1,0:T(8,128)S(1)} %get-tuple-element.30.refs_0_, bf16[8,6272]{1,0:T(8,128)(2,1)S(1)} %collective-permute-done.12.refs_1_, bf16[8,6272]{1,0:T(8,128)(2,1)S(1)} %collective-permute-done.14.refs_2_, ...), custom_call_target="tpu_custom_call" | custom-call | tf_op jit(solution)/shard_map/combine/pallas_call | solution.py:254
  (48 shorter events, 0.5 us)
Async XLA Ops:
  0.0 21.0 %slice-start = ((s8[14680064]{0:T(1024)(128)(4,1)}), s8[4194304]{0:T(1024)(128)(4,1)S(1)}, s32[]{:S(2)}) async-start(s8[14680064]{0:T(1024)(128)(4,1)} %bitcast.3), calls=%async_computation | async-start | bytes 8388608
  0.0 21.0 %slice-start.4 = ((s8[14680064]{0:T(1024)(128)(4,1)}), s8[4194304]{0:T(1024)(128)(4,1)S(1)}, s32[]{:S(2)}) async-start(s8[14680064]{0:T(1024)(128)(4,1)} %bitcast.5), calls=%async_computation.4 | async-start | bytes 8388608
  0.0 21.0 %slice-start.1 = ((s8[14680064]{0:T(1024)(128)(4,1)}), s8[4194304]{0:T(1024)(128)(4,1)S(1)}, s32[]{:S(2)}) async-start(s8[14680064]{0:T(1024)(128)(4,1)} %bitcast.3), calls=%async_computation.1 | async-start | bytes 8388608
  0.0 21.0 %slice-start.2 = ((s8[14680064]{0:T(1024)(128)(4,1)}), s8[4194304]{0:T(1024)(128)(4,1)S(1)}, s32[]{:S(2)}) async-start(s8[14680064]{0:T(1024)(128)(4,1)} %bitcast.3), calls=%async_computation.2 | async-start | bytes 8388608
  0.0 21.0 %slice-start.3 = ((s8[14680064]{0:T(1024)(128)(4,1)}), s8[2097152]{0:T(1024)(128)(4,1)S(1)}, s32[]{:S(2)}) async-start(s8[14680064]{0:T(1024)(128)(4,1)} %bitcast.3), calls=%async_computation.3 | async-start | bytes 4194304
  0.0 21.0 %slice-start.5 = ((s8[14680064]{0:T(1024)(128)(4,1)}), s8[4194304]{0:T(1024)(128)(4,1)S(1)}, s32[]{:S(2)}) async-start(s8[14680064]{0:T(1024)(128)(4,1)} %bitcast.5), calls=%async_computation.5 | async-start | bytes 8388608
  0.0 21.0 %slice-start.6 = ((s8[14680064]{0:T(1024)(128)(4,1)}), s8[4194304]{0:T(1024)(128)(4,1)S(1)}, s32[]{:S(2)}) async-start(s8[14680064]{0:T(1024)(128)(4,1)} %bitcast.5), calls=%async_computation.6 | async-start | bytes 8388608
  0.0 21.0 %slice-start.7 = ((s8[14680064]{0:T(1024)(128)(4,1)}), s8[2097152]{0:T(1024)(128)(4,1)S(1)}, s32[]{:S(2)}) async-start(s8[14680064]{0:T(1024)(128)(4,1)} %bitcast.5), calls=%async_computation.7 | async-start | bytes 4194304
  1.4 10.4 %collective-permute-start = (bf16[8,6272]{1,0:T(8,128)(2,1)S(1)}, bf16[8,6272]{1,0:T(8,128)(2,1)S(1)}, u32[]{:S(2)}, u32[]{:S(2)}) collective-permute-start(bf16[8,6272]{1,0:T(8,128)(2,1)S(1)} %get-tuple-element.23), channel_id=1, source_target_pairs={{0,8},{2,10},{4,12},{6,14},{8,0},{10,2},{12,4},{14,6},{1,9},{3,11}... | collective-permute-start | bytes 301064 | tf_op jit(solution)/shard_map/ppermute | solution.py:269
  5.5 8.0 %collective-permute-start.1 = (bf16[8,6272]{1,0:T(8,128)(2,1)S(1)}, bf16[8,6272]{1,0:T(8,128)(2,1)S(1)}, u32[]{:S(2)}, u32[]{:S(2)}) collective-permute-start(bf16[8,6272]{1,0:T(8,128)(2,1)S(1)} %get-tuple-element.24), channel_id=1, source_target_pairs={{0,4},{2,6},{4,0},{6,2},{8,12},{10,14},{12,8},{14,10},{1,5},{3,7},... | collective-permute-start | bytes 301064 | tf_op jit(solution)/shard_map/ppermute | solution.py:269
  7.0 6.7 %collective-permute-start.2 = (bf16[8,6272]{1,0:T(8,128)(2,1)S(1)}, bf16[8,6272]{1,0:T(8,128)(2,1)S(1)}, u32[]{:S(2)}, u32[]{:S(2)}) collective-permute-start(bf16[8,6272]{1,0:T(8,128)(2,1)S(1)} %get-tuple-element.25), channel_id=1, source_target_pairs={{0,12},{2,14},{4,8},{6,10},{8,4},{10,6},{12,0},{14,2},{1,13},{3,15... | collective-permute-start | bytes 301064 | tf_op jit(solution)/shard_map/ppermute | solution.py:269
  7.0 8.5 %collective-permute-start.3 = (bf16[8,6272]{1,0:T(8,128)(2,1)S(1)}, bf16[8,6272]{1,0:T(8,128)(2,1)S(1)}, u32[]{:S(2)}, u32[]{:S(2)}) collective-permute-start(bf16[8,6272]{1,0:T(8,128)(2,1)S(1)} %get-tuple-element.22.refs_0_), channel_id=1, source_target_pairs={{0,2},{2,0},{4,6},{6,4},{8,10},{10,8},{12,14},{14,12},{1,3},{3,1},... | collective-permute-start | bytes 301064 | tf_op jit(solution)/shard_map/ppermute | solution.py:272
  11.7 5.5 %collective-permute-start.4 = (bf16[8,6272]{1,0:T(8,128)(2,1)S(1)}, bf16[8,6272]{1,0:T(8,128)(2,1)S(1)}, u32[]{:S(2)}, u32[]{:S(2)}) collective-permute-start(bf16[8,6272]{1,0:T(8,128)(2,1)S(1)} %collective-permute-done.refs_1_), channel_id=1, source_target_pairs={{0,2},{2,0},{4,6},{6,4},{8,10},{10,8},{12,14},{14,12},{1,3},{3,1},... | collective-permute-start | bytes 301064 | tf_op jit(solution)/shard_map/ppermute | solution.py:272
  13.4 5.1 %collective-permute-start.5 = (bf16[8,6272]{1,0:T(8,128)(2,1)S(1)}, bf16[8,6272]{1,0:T(8,128)(2,1)S(1)}, u32[]{:S(2)}, u32[]{:S(2)}) collective-permute-start(bf16[8,6272]{1,0:T(8,128)(2,1)S(1)} %collective-permute-done.1.refs_2_), channel_id=1, source_target_pairs={{0,2},{2,0},{4,6},{6,4},{8,10},{10,8},{12,14},{14,12},{1,3},{3,1},... | collective-permute-start | bytes 301064 | tf_op jit(solution)/shard_map/ppermute | solution.py:272
  13.8 5.8 %collective-permute-start.6 = (bf16[8,6272]{1,0:T(8,128)(2,1)S(1)}, bf16[8,6272]{1,0:T(8,128)(2,1)S(1)}, u32[]{:S(2)}, u32[]{:S(2)}) collective-permute-start(bf16[8,6272]{1,0:T(8,128)(2,1)S(1)} %collective-permute-done.2.refs_3_), channel_id=1, source_target_pairs={{0,2},{2,0},{4,6},{6,4},{8,10},{10,8},{12,14},{14,12},{1,3},{3,1},... | collective-permute-start | bytes 301064 | tf_op jit(solution)/shard_map/ppermute | solution.py:272
  15.5 5.5 %collective-permute-start.7 = (bf16[32,6272]{1,0:T(8,128)(2,1)S(1)}, bf16[32,6272]{1,0:T(8,128)(2,1)S(1)}, u32[]{:S(2)}, u32[]{:S(2)}) collective-permute-start(bf16[32,6272]{1,0:T(8,128)(2,1)S(1)} %stack.4), channel_id=1, source_target_pairs={{0,1},{1,0},{2,3},{3,2},{4,5},{5,4},{6,7},{7,6},{8,9},{9,8},{10,11... | collective-permute-start | bytes 1204232 | tf_op jit(solution)/shard_map/ppermute | solution.py:275
  18.5 2.4 %collective-permute-start.8 = (bf16[24,6272]{1,0:T(8,128)(2,1)S(1)}, bf16[24,6272]{1,0:T(8,128)(2,1)S(1)}, u32[]{:S(2)}, u32[]{:S(2)}) collective-permute-start(bf16[24,6272]{1,0:T(8,128)(2,1)S(1)} %stack.5), channel_id=1, source_target_pairs={{0,1},{1,0},{2,3},{3,2},{4,5},{5,4},{6,7},{7,6},{8,9},{9,8},{10,11... | collective-permute-start | bytes 903176 | tf_op jit(solution)/shard_map/ppermute | solution.py:275
  19.6 1.4 %collective-permute-start.9 = (bf16[8,6272]{1,0:T(8,128)(2,1)S(1)}, bf16[8,6272]{1,0:T(8,128)(2,1)S(1)}, u32[]{:S(2)}, u32[]{:S(2)}) collective-permute-start(bf16[8,6272]{1,0:T(8,128)(2,1)S(1)} %stack.6), channel_id=1, source_target_pairs={{0,1},{1,0},{2,3},{3,2},{4,5},{5,4},{6,7},{7,6},{8,9},{9,8},{10,11... | collective-permute-start | bytes 301064 | tf_op jit(solution)/shard_map/ppermute | solution.py:275
  19.7 6.1 %slice-start.8 = ((s8[14680064]{0:T(1024)(128)(4,1)}), s8[4194304]{0:T(1024)(128)(4,1)S(1)}, s32[]{:S(2)}) async-start(s8[14680064]{0:T(1024)(128)(4,1)} %bitcast.7), calls=%async_computation.8 | async-start | bytes 8388608
  19.9 5.9 %slice-start.9 = ((s8[14680064]{0:T(1024)(128)(4,1)}), s8[4194304]{0:T(1024)(128)(4,1)S(1)}, s32[]{:S(2)}) async-start(s8[14680064]{0:T(1024)(128)(4,1)} %bitcast.7), calls=%async_computation.9 | async-start | bytes 8388608
  19.9 5.8 %slice-start.10 = ((s8[14680064]{0:T(1024)(128)(4,1)}), s8[4194304]{0:T(1024)(128)(4,1)S(1)}, s32[]{:S(2)}) async-start(s8[14680064]{0:T(1024)(128)(4,1)} %bitcast.7), calls=%async_computation.10 | async-start | bytes 8388608
  19.9 5.8 %slice-start.11 = ((s8[14680064]{0:T(1024)(128)(4,1)}), s8[2097152]{0:T(1024)(128)(4,1)S(1)}, s32[]{:S(2)}) async-start(s8[14680064]{0:T(1024)(128)(4,1)} %bitcast.7), calls=%async_computation.11 | async-start | bytes 4194304
  28.0 1.8 %collective-permute-start.10 = (bf16[32,6272]{1,0:T(8,128)(2,1)S(1)}, bf16[32,6272]{1,0:T(8,128)(2,1)S(1)}, u32[]{:S(2)}, u32[]{:S(2)}) collective-permute-start(bf16[32,6272]{1,0:T(8,128)(2,1)S(1)} %get-tuple-element.29), channel_id=1, source_target_pairs={{0,1},{1,0},{2,3},{3,2},{4,5},{5,4},{6,7},{7,6},{8,9},{9,8},{10,11... | collective-permute-start | bytes 1204232 | tf_op jit(solution)/shard_map/ppermute | solution.py:275
  29.9 1.9 %collective-permute-start.11 = (bf16[32,6272]{1,0:T(8,128)(2,1)S(1)}, bf16[32,6272]{1,0:T(8,128)(2,1)S(1)}, u32[]{:S(2)}, u32[]{:S(2)}) collective-permute-start(bf16[32,6272]{1,0:T(8,128)(2,1)S(1)} %stack.7), channel_id=1, source_target_pairs={{0,1},{1,0},{2,3},{3,2},{4,5},{5,4},{6,7},{7,6},{8,9},{9,8},{10,11... | collective-permute-start | bytes 1204232 | tf_op jit(solution)/shard_map/ppermute | solution.py:275
  30.1 5.6 %collective-permute-start.13 = (bf16[8,6272]{1,0:T(8,128)(2,1)S(1)}, bf16[8,6272]{1,0:T(8,128)(2,1)S(1)}, u32[]{:S(2)}, u32[]{:S(2)}) collective-permute-start(bf16[8,6272]{1,0:T(8,128)(2,1)S(1)} %pair_sum.3.refs_1_), channel_id=1, source_target_pairs={{0,2},{2,0},{4,6},{6,4},{8,10},{10,8},{12,14},{14,12},{1,3},{3,1},... | collective-permute-start | bytes 301064 | tf_op jit(solution)/shard_map/ppermute | solution.py:272
  32.0 8.0 %collective-permute-start.15 = (bf16[8,6272]{1,0:T(8,128)(2,1)S(1)}, bf16[8,6272]{1,0:T(8,128)(2,1)S(1)}, u32[]{:S(2)}, u32[]{:S(2)}) collective-permute-start(bf16[8,6272]{1,0:T(8,128)(2,1)S(1)} %get-tuple-element.34), channel_id=1, source_target_pairs={{0,2},{2,0},{4,6},{6,4},{8,10},{10,8},{12,14},{14,12},{1,3},{3,1},... | collective-permute-start | bytes 301064 | tf_op jit(solution)/shard_map/ppermute | solution.py:272
  33.6 8.8 %collective-permute-start.17 = (bf16[8,6272]{1,0:T(8,128)(2,1)S(1)}, bf16[8,6272]{1,0:T(8,128)(2,1)S(1)}, u32[]{:S(2)}, u32[]{:S(2)}) collective-permute-start(bf16[8,6272]{1,0:T(8,128)(2,1)S(1)} %get-tuple-element.36), channel_id=1, source_target_pairs={{0,2},{2,0},{4,6},{6,4},{8,10},{10,8},{12,14},{14,12},{1,3},{3,1},... | collective-permute-start | bytes 301064 | tf_op jit(solution)/shard_map/ppermute | solution.py:272
  35.8 8.9 %collective-permute-start.14 = (bf16[8,6272]{1,0:T(8,128)(2,1)S(1)}, bf16[8,6272]{1,0:T(8,128)(2,1)S(1)}, u32[]{:S(2)}, u32[]{:S(2)}) collective-permute-start(bf16[8,6272]{1,0:T(8,128)(2,1)S(1)} %span_sum.3), channel_id=1, source_target_pairs={{0,8},{2,10},{4,12},{6,14},{8,0},{10,2},{12,4},{14,6},{1,9},{3,11}... | collective-permute-start | bytes 301064 | tf_op jit(solution)/shard_map/ppermute | solution.py:269
  38.5 6.2 %collective-permute-start.12 = (bf16[8,6272]{1,0:T(8,128)(2,1)S(1)}, bf16[8,6272]{1,0:T(8,128)(2,1)S(1)}, u32[]{:S(2)}, u32[]{:S(2)}) collective-permute-start(bf16[8,6272]{1,0:T(8,128)(2,1)S(1)} %get-tuple-element.32), channel_id=1, source_target_pairs={{0,2},{2,0},{4,6},{6,4},{8,10},{10,8},{12,14},{14,12},{1,3},{3,1},... | collective-permute-start | bytes 301064 | tf_op jit(solution)/shard_map/ppermute | solution.py:272
  40.0 6.7 %collective-permute-start.16 = (bf16[8,6272]{1,0:T(8,128)(2,1)S(1)}, bf16[8,6272]{1,0:T(8,128)(2,1)S(1)}, u32[]{:S(2)}, u32[]{:S(2)}) collective-permute-start(bf16[8,6272]{1,0:T(8,128)(2,1)S(1)} %span_sum.4), channel_id=1, source_target_pairs={{0,12},{2,14},{4,8},{6,10},{8,4},{10,6},{12,0},{14,2},{1,13},{3,15... | collective-permute-start | bytes 301064 | tf_op jit(solution)/shard_map/ppermute | solution.py:269
  42.4 5.3 %collective-permute-start.18 = (bf16[8,6272]{1,0:T(8,128)(2,1)S(1)}, bf16[8,6272]{1,0:T(8,128)(2,1)S(1)}, u32[]{:S(2)}, u32[]{:S(2)}) collective-permute-start(bf16[8,6272]{1,0:T(8,128)(2,1)S(1)} %span_sum.5), channel_id=1, source_target_pairs={{0,4},{2,6},{4,0},{6,2},{8,12},{10,14},{12,8},{14,10},{1,5},{3,7},... | collective-permute-start | bytes 301064 | tf_op jit(solution)/shard_map/ppermute | solution.py:269

commit v11 on v10

--- a/solution.py
+++ b/solution.py
@@ -10,15 +10,14 @@
 EXPERTS = 4
 LANES = 128
 RETURN_ORDER = (2, 3, 1)
-SEND_ORDER = (2, 3, 1, 0)
 BLOCK_ORDER = (0, 2, 1, 3)
 N_BLOCK = 256
 LAST_FLOPS = 5_000_000_000
 EXCHANGE_FLOPS = 20_000_000_000
 
 
-def params(mib=4):
-    return pltpu.CompilerParams(vmem_limit_bytes=mib * 1024 * 1024)
+def params(rows=0):
+    return pltpu.CompilerParams(vmem_limit_bytes=4 * max(1, -(-rows // 128)) * 1024 * 1024)
 
 
 def cost(flops):
@@ -78,18 +77,29 @@
     return pl.pallas_call(
         functools.partial(unpack_kernel, rows),
         out_shape=jax.ShapeDtypeStruct((total, width), jnp.bfloat16),
-        compiler_params=params(),
+        compiler_params=params(total),
         cost_estimate=cost(1_000_000_000),
         name="unpack",
     )(*values)
 
 
-def gate_up_kernel(n_block, rows, first_ref, *refs):
-    rows_in, (gate_ref, up_ref, hidden_ref, rows_ref) = refs[:-4], refs[-4:]
-    count = first_ref.shape[0]
-    rows_ref[:count, :] = first_ref[...]
-    if rows_in:
-        unpacked(rows_in, rows_ref.at[count:, :], rows)
+def gate_up_kernel(n_block, first_ref, last_ref, gate_ref, up_ref, hidden_ref, rows_ref):
+    rows = last_ref.shape[0]
+    total, width = rows_ref.shape
+    whole = total - 2 * rows
+    rows_ref[:whole, :] = first_ref[:whole, :]
+    tail = width // rows
+    row = lax.broadcasted_iota(jnp.int32, (rows, tail), 0)
+    ends = jnp.zeros((rows, tail), jnp.float32)
+    for i in range(rows):
+        columns = slice(i * tail, (i + 1) * tail)
+        if i < rows - 1:
+            piece = last_ref[:, columns].astype(jnp.float32)
+            ends = jnp.where(row == i, jnp.broadcast_to(piece[rows - 1:, :], (rows, tail)), ends)
+        else:
+            piece = ends
+        both = jnp.concatenate([first_ref[whole:, columns].astype(jnp.float32), piece], axis=0)
+        rows_ref[whole:, columns] = both.astype(jnp.bfloat16)
     for n in range(0, gate_ref.shape[1], n_block):
         columns = slice(n, n + n_block)
         gate = jnp.dot(rows_ref[...], gate_ref[:, columns], preferred_element_type=jnp.float32)
@@ -97,18 +107,18 @@
         hidden_ref[:, columns] = (gate / (1.0 + jnp.exp(-gate)) * up).astype(jnp.bfloat16)
 
 
-def gate_up(first, blocks, gate_weight, up_weight, rows):
-    total = sum(r.shape[0] for r in [first] + blocks)
+def gate_up(first, last, gate_weight, up_weight):
+    total = first.shape[0] + last.shape[0]
     width, units = gate_weight.shape
     return pl.pallas_call(
-        functools.partial(gate_up_kernel, block_of(units, N_BLOCK), rows),
-        in_specs=[pl.BlockSpec(memory_space=pltpu.VMEM)] * (len(blocks) + 3),
+        functools.partial(gate_up_kernel, block_of(units, N_BLOCK)),
+        in_specs=[pl.BlockSpec(memory_space=pltpu.VMEM)] * 4,
         out_shape=jax.ShapeDtypeStruct((total, units), jnp.bfloat16),
         scratch_shapes=[pltpu.VMEM((total, width), jnp.bfloat16)],
-        compiler_params=params(8),
+        compiler_params=params(total),
         cost_estimate=cost(4 * total * width * units),
         name="gate_up",
-    )(first, *blocks, in_vmem(gate_weight), in_vmem(up_weight))
+    )(first, last, in_vmem(gate_weight), in_vmem(up_weight))
 
 
 def down_kernel(rows, hidden_ref, down_ref, *outs):
@@ -137,7 +147,7 @@
         functools.partial(down_kernel, rows),
         in_specs=[pl.BlockSpec(memory_space=pltpu.VMEM)] * 2,
         out_shape=[jax.ShapeDtypeStruct(shape, jnp.bfloat16 if p else jnp.float32) for p in range(pair) for _ in range(span)],
-        compiler_params=params(),
+        compiler_params=params(total),
         cost_estimate=cost(2 * total * width * units),
         name="down",
     )(hidden, in_vmem(down_weight))
@@ -229,34 +239,37 @@
     )(own_expert, *[pltpu.with_memory_space_constraint(a, pltpu.HBM) for a in inputs])
 
 
-def combine_kernel(own_count, sides_ref, *refs):
-    out_ref = refs[-1]
+def combine_kernel(base, places, counts, sides_ref, *refs):
+    *refs, out_ref = refs
     rows, width = out_ref.shape
     tail = width // rows
-    own = refs[0][...]
-    for ref in refs[1:own_count]:
-        own += ref[...].astype(jnp.float32)
     row = lax.broadcasted_iota(jnp.int32, (rows, tail), 0)
-    parts = []
-    others = [ref[...].astype(jnp.float32) for ref in refs[own_count:-1]]
-    for s, packed in zip((0,) + RETURN_ORDER, [own] + others):
+    value = None
+    for ref in refs[:base]:
+        value = ref[...]
+    refs = refs[base:]
+    for s, count in zip(places, counts):
+        packed = sum([ref[...].astype(jnp.float32) for ref in refs[1:count]], refs[0][...].astype(jnp.float32))
+        refs = refs[count:]
         coeff = sides_ref[:, s * LANES:s * LANES + 1]
         shifted = sides_ref[:, (EXPERTS + s) * LANES:(EXPERTS + s) * LANES + 1] > 0.5
         ends = jnp.zeros((rows, tail), jnp.float32)
         for i in range(rows - 1):
             ends = jnp.where(row == i, jnp.broadcast_to(packed[rows - 1:, i * tail:(i + 1) * tail], (rows, tail)), ends)
         whole = jnp.concatenate([packed, ends], axis=1)
-        parts.append(coeff * jnp.where(shifted, pltpu.roll(whole, 1, 0), whole))
-    out_ref[...] = sum(parts[1:], parts[0]).astype(jnp.bfloat16)
-
-
-def combine(sides, own, others, width):
-    return pl.pallas_call(
-        functools.partial(combine_kernel, len(own)),
-        out_shape=jax.ShapeDtypeStruct((own[0].shape[0], width), jnp.bfloat16),
+        term = coeff * jnp.where(shifted, pltpu.roll(whole, 1, 0), whole)
+        value = term if value is None else value + term
+    out_ref[...] = value.astype(out_ref.dtype)
+
+
+def combine(sides, base, places, groups, width, dtype):
+    arrays = [a for group in groups for a in group]
+    return pl.pallas_call(
+        functools.partial(combine_kernel, len(base), tuple(places), tuple(len(g) for g in groups)),
+        out_shape=jax.ShapeDtypeStruct((arrays[0].shape[0], width), dtype),
         compiler_params=params(),
         name="combine",
-    )(sides, *own, *others)
+    )(sides, *base, *arrays)
 
 
 def local(tokens, expert_ids, route_weights, gate_weight, up_weight, down_weight):
@@ -282,25 +295,24 @@
     groups = [stack(column)]
     for part in parts[1:]:
         groups += [stack(part[:-1]), stack(part[-1:], (), LAST_FLOPS)]
-    others = [over_pair(g, p) for p in range(1, pair) for g in groups]
-    plane = unpack([b for part in parts for b in part], rows, width)
-    hidden = gate_up(plane, others, gate_weight, up_weight, rows)
+    *others, last = [over_pair(g, p) for p in range(1, pair) for g in groups]
+    first = unpack([b for part in parts for b in part] + others, rows, width)
+    hidden = gate_up(first, last, gate_weight, up_weight)
 
     def paired(keep, sends):
         return [keep] + [over_pair(b, -p) for p, b in enumerate(sends, 1)]
 
-    (own_keep, *own_sends), *far = down(hidden, down_weight, span, pair, rows)
-    far = [paired(keep, sends) for keep, *sends in far]
-    first, *later = SEND_ORDER
-    blocks = [{first: pair_sum(a, rows, jnp.bfloat16, [BLOCK_ORDER.index(first)])[0]} for a in far]
-    own_sends = [stack([b], [blocks[0][first]]) for b in own_sends]
-    own = dict(zip(BLOCK_ORDER, pair_sum(paired(own_keep, own_sends), rows, jnp.float32, range(EXPERTS))))
-    for block, arrays in zip(blocks, far):
-        places = [BLOCK_ORDER.index(s) for s in later]
-        block.update(zip(later, pair_sum(arrays, rows, jnp.bfloat16, places, [own[first]])))
-    sums = {s: [own[s]] + [over_span(b[s], -t) for t, b in enumerate(blocks, 1)] for s in SEND_ORDER}
-    returned = [over_experts(span_sum(sums[s]), s) for s in RETURN_ORDER]
-    return combine(sides, sums[0], returned, width)
+    sums = [[] for _ in range(EXPERTS)]
+    for t, (keep, *sends) in enumerate(down(hidden, down_weight, span, pair, rows)):
+        arrays = paired(keep, sends)
+        blocks = pair_sum(arrays, rows, jnp.bfloat16 if t else jnp.float32, range(EXPERTS))
+        for s, block in zip(BLOCK_ORDER, blocks):
+            sums[s].append(over_span(block, -t) if t else block)
+
+    returned = {s: over_experts(span_sum(sums[s]), s) for s in RETURN_ORDER}
+    first, *later = RETURN_ORDER
+    early = combine(sides, [], [0, first], [sums[0], [returned[first]]], width, jnp.float32)
+    return combine(sides, [early], later, [[returned[s]] for s in later], width, jnp.bfloat16)
 
 
 def solution(mesh):

time: 48.8 us -> 47.8 us (0.980)
  waiting for transfers between devices: 16.3 us -> 14.9 us
  starting transfers between devices: 22.3 us -> 22.8 us
    ppermute x6, starting transfers between devices: 10.9 us -> 12.4 us  [over_experts(): lax.ppermute(value, 'attn', [(i, (i // span ^ other) * span + i % span) f...]
    ppermute x8, starting transfers between devices: 10.8 us -> 9.59 us  [over_span(): lax.ppermute(value, 'attn', [(i, i // span * span + (i + shift) % span) f...]
    ppermute x6, waiting for transfers between devices: 8.19 us -> 7.46 us  [over_experts(): lax.ppermute(value, 'attn', [(i, (i // span ^ other) * span + i % span) f...]
    ppermute x5, waiting for transfers between devices: 2.6 us -> 2.01 us  [over_pair(): lax.ppermute(value, 'ffn', [(i, (i + shift) % pair) for i in range(pair)])]
  transfers between devices with their start and end apart: 19 -> 19, of which waited for: 10 -> 11; matrix products, arithmetic and copies ran while one was open for 0% -> 0% of each run, Pallas kernels for 1% -> 2%
where the time goes in v11:
time: 47.8 us; the launch traced here: 47.7 us
  starting transfers between devices  22.8 us (48%)
  waiting for transfers between devices  14.9 us (31%)
  Pallas kernels  9.58 us (20%)
    ppermute x6, starting transfers between devices, over_experts(): lax.ppermute(value, 'attn', [(i, (i // span ^ other) * span + i % span) f...  12.4 us
    ppermute x8, starting transfers between devices, over_span(): lax.ppermute(value, 'attn', [(i, i // span * span + (i + shift) % span) f...  9.59 us
    ppermute x6, waiting for transfers between devices, over_experts(): lax.ppermute(value, 'attn', [(i, (i // span ^ other) * span + i % span) f...  7.46 us
    ppermute x8, waiting for transfers between devices, over_span(): lax.ppermute(value, 'attn', [(i, i // span * span + (i + shift) % span) f...  5.39 us
    pallas_call x1, Pallas kernels, gate_up(): pl.pallas_call(functools.partial(gate_up_kernel, block_of(units, N_BLOCK)...  4.36 us
    pallas_call x1, Pallas kernels, down(): pl.pallas_call(functools.partial(down_kernel, rows), in_specs=[pl.BlockSp...  2.21 us
    ppermute x5, waiting for transfers between devices, over_pair(): lax.ppermute(value, 'ffn', [(i, (i + shift) % pair) for i in range(pair)])  2.01 us
    pallas_call x1, Pallas kernels, pack(): pl.pallas_call(pack_kernel, in_specs=[pl.BlockSpec(memory_space=pltpu.SME...  1.3 us
  transfers between devices with their start and end apart: 19, of which 11 were waited for; matrix products, arithmetic and copies ran while one was open for 0% of the time, Pallas kernels for 2%

profile of v11, /device:TPU:0, one launch (start us, length us, event | category | flops | bytes accessed | tf_op | source)
XLA Modules:
  0.0 47.7 jit_solution(17446822716470036131)
XLA Ops:
  0.0 1.3 %pack.1 = (f32[8,1024]{1,0:T(8,128)S(1)}, bf16[8,6272]{1,0:T(8,128)(2,1)S(1)}, bf16[8,6272]{1,0:T(8,128)(2,1)S(1)}, bf16[8,6272]{1,0:T(8,128)(2,1)S(1)}, bf16[8,6272]{1,0:T(8,128)(2,1)S(1)}) custom-call(s32[1]{0:T(128)} %bitcast.own_expert, bf16[8,7168]{1,0:T(8,128)(2,1)} %tokens_hbm.1, s32[3,8]{1,0:T(4,128)} %bitcast.9, f32[3,8]{1,0:T(4,128)} %bitcast.10), custom_call_target="tpu_custom_call" | custom-call | flops 20000000000 | tf_op jit(solution)/shard_map/pack/pallas_call | solution.py:231
  1.4 4.1 %collective-permute-start = (bf16[8,6272]{1,0:T(8,128)(2,1)S(1)}, bf16[8,6272]{1,0:T(8,128)(2,1)S(1)}, u32[]{:S(2)}, u32[]{:S(2)}) collective-permute-start(bf16[8,6272]{1,0:T(8,128)(2,1)S(1)} %get-tuple-element.24), channel_id=1, source_target_pairs={{0,8},{2,10},{4,12},{6,14},{8,0},{10,2},{12,4},{14,6},{1,9},{3,11}... | collective-permute-start | bytes 301064 | tf_op jit(solution)/shard_map/ppermute | solution.py:282
  5.5 1.6 %collective-permute-start.1 = (bf16[8,6272]{1,0:T(8,128)(2,1)S(1)}, bf16[8,6272]{1,0:T(8,128)(2,1)S(1)}, u32[]{:S(2)}, u32[]{:S(2)}) collective-permute-start(bf16[8,6272]{1,0:T(8,128)(2,1)S(1)} %get-tuple-element.25), channel_id=1, source_target_pairs={{0,4},{2,6},{4,0},{6,2},{8,12},{10,14},{12,8},{14,10},{1,5},{3,7},... | collective-permute-start | bytes 301064 | tf_op jit(solution)/shard_map/ppermute | solution.py:282
  7.0 1.7 %collective-permute-start.3 = (bf16[8,6272]{1,0:T(8,128)(2,1)S(1)}, bf16[8,6272]{1,0:T(8,128)(2,1)S(1)}, u32[]{:S(2)}, u32[]{:S(2)}) collective-permute-start(bf16[8,6272]{1,0:T(8,128)(2,1)S(1)} %get-tuple-element.23.refs_0_), channel_id=1, source_target_pairs={{0,2},{2,0},{4,6},{6,4},{8,10},{10,8},{12,14},{14,12},{1,3},{3,1},... | collective-permute-start | bytes 301064 | tf_op jit(solution)/shard_map/ppermute | solution.py:285
  8.8 2.9 %collective-permute-done.refs_1_ = bf16[8,6272]{1,0:T(8,128)(2,1)S(1)} collective-permute-done((bf16[8,6272]{1,0:T(8,128)(2,1)S(1)}, bf16[8,6272]{1,0:T(8,128)(2,1)S(1)}, u32[]{:S(2)}, u32[]{:S(2)}) %collective-permute-start) | collective-permute-done | bytes 100384 | tf_op jit(solution)/shard_map/ppermute | solution.py:282
  11.7 1.7 %collective-permute-start.4 = (bf16[8,6272]{1,0:T(8,128)(2,1)S(1)}, bf16[8,6272]{1,0:T(8,128)(2,1)S(1)}, u32[]{:S(2)}, u32[]{:S(2)}) collective-permute-start(bf16[8,6272]{1,0:T(8,128)(2,1)S(1)} %collective-permute-done.refs_1_), channel_id=1, source_target_pairs={{0,2},{2,0},{4,6},{6,4},{8,10},{10,8},{12,14},{14,12},{1,3},{3,1},... | collective-permute-start | bytes 301064 | tf_op jit(solution)/shard_map/ppermute | solution.py:285
  13.4 0.3 collective-permute-start.5
  13.8 1.7 %collective-permute-start.6 = (bf16[8,6272]{1,0:T(8,128)(2,1)S(1)}, bf16[8,6272]{1,0:T(8,128)(2,1)S(1)}, u32[]{:S(2)}, u32[]{:S(2)}) collective-permute-start(bf16[8,6272]{1,0:T(8,128)(2,1)S(1)} %collective-permute-done.2.refs_3_), channel_id=1, source_target_pairs={{0,2},{2,0},{4,6},{6,4},{8,10},{10,8},{12,14},{14,12},{1,3},{3,1},... | collective-permute-start | bytes 301064 | tf_op jit(solution)/shard_map/ppermute | solution.py:285
  15.6 1.6 %collective-permute-done.4.refs_1_.refs_5_ = bf16[8,6272]{1,0:T(8,128)(2,1)S(1)} collective-permute-done((bf16[8,6272]{1,0:T(8,128)(2,1)S(1)}, bf16[8,6272]{1,0:T(8,128)(2,1)S(1)}, u32[]{:S(2)}, u32[]{:S(2)}) %collective-permute-start.4) | collective-permute-done | bytes 100384 | tf_op jit(solution)/shard_map/ppermute | solution.py:285
  17.2 1.3 %collective-permute-done.5.refs_2_.refs_6_ = bf16[8,6272]{1,0:T(8,128)(2,1)S(1)} collective-permute-done((bf16[8,6272]{1,0:T(8,128)(2,1)S(1)}, bf16[8,6272]{1,0:T(8,128)(2,1)S(1)}, u32[]{:S(2)}, u32[]{:S(2)}) %collective-permute-start.5) | collective-permute-done | bytes 100384 | tf_op jit(solution)/shard_map/ppermute | solution.py:285
  18.6 1.0 %collective-permute-done.6.refs_7_.refs_0_ = bf16[8,6272]{1,0:T(8,128)(2,1)S(1)} collective-permute-done((bf16[8,6272]{1,0:T(8,128)(2,1)S(1)}, bf16[8,6272]{1,0:T(8,128)(2,1)S(1)}, u32[]{:S(2)}, u32[]{:S(2)}) %collective-permute-start.6) | collective-permute-done | bytes 100384 | tf_op jit(solution)/shard_map/ppermute | solution.py:285
  19.7 0.5 %collective-permute-done.8.refs_9_ = bf16[24,6272]{1,0:T(8,128)(2,1)S(1)} collective-permute-done((bf16[24,6272]{1,0:T(8,128)(2,1)S(1)}, bf16[24,6272]{1,0:T(8,128)(2,1)S(1)}, u32[]{:S(2)}, u32[]{:S(2)}) %collective-permute-start.8) | collective-permute-done | bytes 301088 | tf_op jit(solution)/shard_map/ppermute | solution.py:288
  20.2 0.5 unpack.1.first_ref
  20.7 0.3 collective-permute-done.9.last_ref
  21.0 4.4 %gate_up.1.hidden_ref = bf16[128,1024]{1,0:T(8,128)(2,1)S(1)} custom-call(bf16[120,7168]{1,0:T(8,128)(2,1)S(1)} %unpack.1.first_ref, bf16[8,6272]{1,0:T(8,128)(2,1)S(1)} %collective-permute-done.9.last_ref, bf16[7168,1024]{1,0:T(8,128)(2,1)S(1)} %bitcast.6, bf16[7168,1024]{1,0:T(8,128)(2,1)S(1)} %bitcast.8), custom_call_target="tpu_custom_call" | custom-call | flops 3758096384 | tf_op jit(solution)/shard_map/gate_up/pallas_call | solution.py:113
  25.4 0.1 slice-done.3
  25.6 2.2 %down.1 = (f32[32,6272]{1,0:T(8,128)S(1)}, f32[32,6272]{1,0:T(8,128)S(1)}, bf16[32,6272]{1,0:T(8,128)(2,1)S(1)}, bf16[32,6272]{1,0:T(8,128)(2,1)S(1)}) custom-call(bf16[128,1024]{1,0:T(8,128)(2,1)S(1)} %gate_up.1.hidden_ref, bf16[1024,7168]{1,0:T(8,128)(2,1)S(1)} %bitcast.4), custom_call_target="tpu_custom_call" | custom-call | flops 1644167168 | tf_op jit(solution)/shard_map/down/pallas_call | solution.py:146
  27.8 0.2 collective-permute-start.11
  28.0 0.4 collective-permute-start.10
  28.4 1.2 %collective-permute-done.11.refs_1_ = bf16[32,6272]{1,0:T(8,128)(2,1)S(1)} collective-permute-done((bf16[32,6272]{1,0:T(8,128)(2,1)S(1)}, bf16[32,6272]{1,0:T(8,128)(2,1)S(1)}, u32[]{:S(2)}, u32[]{:S(2)}) %collective-permute-start.11) | collective-permute-done | bytes 401440 | tf_op jit(solution)/shard_map/ppermute | solution.py:288
  29.7 1.7 %collective-permute-start.13 = (bf16[8,6272]{1,0:T(8,128)(2,1)S(1)}, bf16[8,6272]{1,0:T(8,128)(2,1)S(1)}, u32[]{:S(2)}, u32[]{:S(2)}) collective-permute-start(bf16[8,6272]{1,0:T(8,128)(2,1)S(1)} %get-tuple-element.34), channel_id=1, source_target_pairs={{0,2},{2,0},{4,6},{6,4},{8,10},{10,8},{12,14},{14,12},{1,3},{3,1},... | collective-permute-start | bytes 301064 | tf_op jit(solution)/shard_map/ppermute | solution.py:285
  31.4 0.3 collective-permute-start.15
  31.8 1.7 %collective-permute-start.17 = (bf16[8,6272]{1,0:T(8,128)(2,1)S(1)}, bf16[8,6272]{1,0:T(8,128)(2,1)S(1)}, u32[]{:S(2)}, u32[]{:S(2)}) collective-permute-start(bf16[8,6272]{1,0:T(8,128)(2,1)S(1)} %get-tuple-element.38), channel_id=1, source_target_pairs={{0,2},{2,0},{4,6},{6,4},{8,10},{10,8},{12,14},{14,12},{1,3},{3,1},... | collective-permute-start | bytes 301064 | tf_op jit(solution)/shard_map/ppermute | solution.py:285
  33.5 0.3 collective-permute-start.12
  33.9 1.5 %collective-permute-done.13.refs_1_ = bf16[8,6272]{1,0:T(8,128)(2,1)S(1)} collective-permute-done((bf16[8,6272]{1,0:T(8,128)(2,1)S(1)}, bf16[8,6272]{1,0:T(8,128)(2,1)S(1)}, u32[]{:S(2)}, u32[]{:S(2)}) %collective-permute-start.13) | collective-permute-done | bytes 100384 | tf_op jit(solution)/shard_map/ppermute | solution.py:285
  35.4 2.6 %collective-permute-start.14 = (bf16[8,6272]{1,0:T(8,128)(2,1)S(1)}, bf16[8,6272]{1,0:T(8,128)(2,1)S(1)}, u32[]{:S(2)}, u32[]{:S(2)}) collective-permute-start(bf16[8,6272]{1,0:T(8,128)(2,1)S(1)} %span_sum.3), channel_id=1, source_target_pairs={{0,8},{2,10},{4,12},{6,14},{8,0},{10,2},{12,4},{14,6},{1,9},{3,11}... | collective-permute-start | bytes 301064 | tf_op jit(solution)/shard_map/ppermute | solution.py:282
  38.0 4.0 %collective-permute-start.16 = (bf16[8,6272]{1,0:T(8,128)(2,1)S(1)}, bf16[8,6272]{1,0:T(8,128)(2,1)S(1)}, u32[]{:S(2)}, u32[]{:S(2)}) collective-permute-start(bf16[8,6272]{1,0:T(8,128)(2,1)S(1)} %span_sum.4), channel_id=1, source_target_pairs={{0,12},{2,14},{4,8},{6,10},{8,4},{10,6},{12,0},{14,2},{1,13},{3,15... | collective-permute-start | bytes 301064 | tf_op jit(solution)/shard_map/ppermute | solution.py:282
  42.2 2.5 %collective-permute-done.14.refs_2_ = bf16[8,6272]{1,0:T(8,128)(2,1)S(1)} collective-permute-done((bf16[8,6272]{1,0:T(8,128)(2,1)S(1)}, bf16[8,6272]{1,0:T(8,128)(2,1)S(1)}, u32[]{:S(2)}, u32[]{:S(2)}) %collective-permute-start.14) | collective-permute-done | bytes 100384 | tf_op jit(solution)/shard_map/ppermute | solution.py:282
  44.7 0.1 combine.2.refs_0_
  44.9 0.9 %collective-permute-done.16.refs_1_ = bf16[8,6272]{1,0:T(8,128)(2,1)S(1)} collective-permute-done((bf16[8,6272]{1,0:T(8,128)(2,1)S(1)}, bf16[8,6272]{1,0:T(8,128)(2,1)S(1)}, u32[]{:S(2)}, u32[]{:S(2)}) %collective-permute-start.16) | collective-permute-done | bytes 100384 | tf_op jit(solution)/shard_map/ppermute | solution.py:282
  45.8 1.1 %collective-permute-done.18.refs_2_ = bf16[8,6272]{1,0:T(8,128)(2,1)S(1)} collective-permute-done((bf16[8,6272]{1,0:T(8,128)(2,1)S(1)}, bf16[8,6272]{1,0:T(8,128)(2,1)S(1)}, u32[]{:S(2)}, u32[]{:S(2)}) %collective-permute-start.18) | collective-permute-done | bytes 100384 | tf_op jit(solution)/shard_map/ppermute | solution.py:282
  46.9 0.8 %combine.3 = bf16[8,7168]{1,0:T(8,128)(2,1)} custom-call(f32[8,1024]{1,0:T(8,128)S(1)} %get-tuple-element.22.sides_ref, f32[8,7168]{1,0:T(8,128)S(1)} %combine.2.refs_0_, bf16[8,6272]{1,0:T(8,128)(2,1)S(1)} %collective-permute-done.16.refs_1_, bf16[8,6272]{1,0:T(8,128)(2,1)S(1)} %collective-permute-done.18.refs_2_), custom_call_target="tpu_custom_call" | custom-call | tf_op jit(solution)/shard_map/combine/pallas_call | solution.py:267
  (47 shorter events, 0.7 us)
Async XLA Ops:
  0.0 21.0 %slice-start.4 = ((s8[14680064]{0:T(1024)(128)(4,1)}), s8[4194304]{0:T(1024)(128)(4,1)S(1)}, s32[]{:S(2)}) async-start(s8[14680064]{0:T(1024)(128)(4,1)} %bitcast.5), calls=%async_computation.4 | async-start | bytes 8388608
  0.0 21.0 %slice-start.8 = ((s8[14680064]{0:T(1024)(128)(4,1)}), s8[4194304]{0:T(1024)(128)(4,1)S(1)}, s32[]{:S(2)}) async-start(s8[14680064]{0:T(1024)(128)(4,1)} %bitcast.7), calls=%async_computation.8 | async-start | bytes 8388608
  0.0 21.0 %slice-start.5 = ((s8[14680064]{0:T(1024)(128)(4,1)}), s8[4194304]{0:T(1024)(128)(4,1)S(1)}, s32[]{:S(2)}) async-start(s8[14680064]{0:T(1024)(128)(4,1)} %bitcast.5), calls=%async_computation.5 | async-start | bytes 8388608
  0.0 21.0 %slice-start.6 = ((s8[14680064]{0:T(1024)(128)(4,1)}), s8[4194304]{0:T(1024)(128)(4,1)S(1)}, s32[]{:S(2)}) async-start(s8[14680064]{0:T(1024)(128)(4,1)} %bitcast.5), calls=%async_computation.6 | async-start | bytes 8388608
  0.0 21.0 %slice-start.7 = ((s8[14680064]{0:T(1024)(128)(4,1)}), s8[2097152]{0:T(1024)(128)(4,1)S(1)}, s32[]{:S(2)}) async-start(s8[14680064]{0:T(1024)(128)(4,1)} %bitcast.5), calls=%async_computation.7 | async-start | bytes 4194304
  0.0 21.0 %slice-start.9 = ((s8[14680064]{0:T(1024)(128)(4,1)}), s8[4194304]{0:T(1024)(128)(4,1)S(1)}, s32[]{:S(2)}) async-start(s8[14680064]{0:T(1024)(128)(4,1)} %bitcast.7), calls=%async_computation.9 | async-start | bytes 8388608
  0.0 21.0 %slice-start.10 = ((s8[14680064]{0:T(1024)(128)(4,1)}), s8[4194304]{0:T(1024)(128)(4,1)S(1)}, s32[]{:S(2)}) async-start(s8[14680064]{0:T(1024)(128)(4,1)} %bitcast.7), calls=%async_computation.10 | async-start | bytes 8388608
  0.0 21.0 %slice-start.11 = ((s8[14680064]{0:T(1024)(128)(4,1)}), s8[2097152]{0:T(1024)(128)(4,1)S(1)}, s32[]{:S(2)}) async-start(s8[14680064]{0:T(1024)(128)(4,1)} %bitcast.7), calls=%async_computation.11 | async-start | bytes 4194304
  1.4 10.4 %collective-permute-start = (bf16[8,6272]{1,0:T(8,128)(2,1)S(1)}, bf16[8,6272]{1,0:T(8,128)(2,1)S(1)}, u32[]{:S(2)}, u32[]{:S(2)}) collective-permute-start(bf16[8,6272]{1,0:T(8,128)(2,1)S(1)} %get-tuple-element.24), channel_id=1, source_target_pairs={{0,8},{2,10},{4,12},{6,14},{8,0},{10,2},{12,4},{14,6},{1,9},{3,11}... | collective-permute-start | bytes 301064 | tf_op jit(solution)/shard_map/ppermute | solution.py:282
  5.5 8.0 %collective-permute-start.1 = (bf16[8,6272]{1,0:T(8,128)(2,1)S(1)}, bf16[8,6272]{1,0:T(8,128)(2,1)S(1)}, u32[]{:S(2)}, u32[]{:S(2)}) collective-permute-start(bf16[8,6272]{1,0:T(8,128)(2,1)S(1)} %get-tuple-element.25), channel_id=1, source_target_pairs={{0,4},{2,6},{4,0},{6,2},{8,12},{10,14},{12,8},{14,10},{1,5},{3,7},... | collective-permute-start | bytes 301064 | tf_op jit(solution)/shard_map/ppermute | solution.py:282
  7.0 6.7 %collective-permute-start.2 = (bf16[8,6272]{1,0:T(8,128)(2,1)S(1)}, bf16[8,6272]{1,0:T(8,128)(2,1)S(1)}, u32[]{:S(2)}, u32[]{:S(2)}) collective-permute-start(bf16[8,6272]{1,0:T(8,128)(2,1)S(1)} %get-tuple-element.26), channel_id=1, source_target_pairs={{0,12},{2,14},{4,8},{6,10},{8,4},{10,6},{12,0},{14,2},{1,13},{3,15... | collective-permute-start | bytes 301064 | tf_op jit(solution)/shard_map/ppermute | solution.py:282
  7.0 8.5 %collective-permute-start.3 = (bf16[8,6272]{1,0:T(8,128)(2,1)S(1)}, bf16[8,6272]{1,0:T(8,128)(2,1)S(1)}, u32[]{:S(2)}, u32[]{:S(2)}) collective-permute-start(bf16[8,6272]{1,0:T(8,128)(2,1)S(1)} %get-tuple-element.23.refs_0_), channel_id=1, source_target_pairs={{0,2},{2,0},{4,6},{6,4},{8,10},{10,8},{12,14},{14,12},{1,3},{3,1},... | collective-permute-start | bytes 301064 | tf_op jit(solution)/shard_map/ppermute | solution.py:285
  11.7 5.5 %collective-permute-start.4 = (bf16[8,6272]{1,0:T(8,128)(2,1)S(1)}, bf16[8,6272]{1,0:T(8,128)(2,1)S(1)}, u32[]{:S(2)}, u32[]{:S(2)}) collective-permute-start(bf16[8,6272]{1,0:T(8,128)(2,1)S(1)} %collective-permute-done.refs_1_), channel_id=1, source_target_pairs={{0,2},{2,0},{4,6},{6,4},{8,10},{10,8},{12,14},{14,12},{1,3},{3,1},... | collective-permute-start | bytes 301064 | tf_op jit(solution)/shard_map/ppermute | solution.py:285
  13.4 5.1 %collective-permute-start.5 = (bf16[8,6272]{1,0:T(8,128)(2,1)S(1)}, bf16[8,6272]{1,0:T(8,128)(2,1)S(1)}, u32[]{:S(2)}, u32[]{:S(2)}) collective-permute-start(bf16[8,6272]{1,0:T(8,128)(2,1)S(1)} %collective-permute-done.1.refs_2_), channel_id=1, source_target_pairs={{0,2},{2,0},{4,6},{6,4},{8,10},{10,8},{12,14},{14,12},{1,3},{3,1},... | collective-permute-start | bytes 301064 | tf_op jit(solution)/shard_map/ppermute | solution.py:285
  13.8 5.8 %collective-permute-start.6 = (bf16[8,6272]{1,0:T(8,128)(2,1)S(1)}, bf16[8,6272]{1,0:T(8,128)(2,1)S(1)}, u32[]{:S(2)}, u32[]{:S(2)}) collective-permute-start(bf16[8,6272]{1,0:T(8,128)(2,1)S(1)} %collective-permute-done.2.refs_3_), channel_id=1, source_target_pairs={{0,2},{2,0},{4,6},{6,4},{8,10},{10,8},{12,14},{14,12},{1,3},{3,1},... | collective-permute-start | bytes 301064 | tf_op jit(solution)/shard_map/ppermute | solution.py:285
  15.5 4.2 %collective-permute-start.7 = (bf16[32,6272]{1,0:T(8,128)(2,1)S(1)}, bf16[32,6272]{1,0:T(8,128)(2,1)S(1)}, u32[]{:S(2)}, u32[]{:S(2)}) collective-permute-start(bf16[32,6272]{1,0:T(8,128)(2,1)S(1)} %stack.3), channel_id=1, source_target_pairs={{0,1},{1,0},{2,3},{3,2},{4,5},{5,4},{6,7},{7,6},{8,9},{9,8},{10,11... | collective-permute-start | bytes 1204232 | tf_op jit(solution)/shard_map/ppermute | solution.py:288
  18.5 1.7 %collective-permute-start.8 = (bf16[24,6272]{1,0:T(8,128)(2,1)S(1)}, bf16[24,6272]{1,0:T(8,128)(2,1)S(1)}, u32[]{:S(2)}, u32[]{:S(2)}) collective-permute-start(bf16[24,6272]{1,0:T(8,128)(2,1)S(1)} %stack.4), channel_id=1, source_target_pairs={{0,1},{1,0},{2,3},{3,2},{4,5},{5,4},{6,7},{7,6},{8,9},{9,8},{10,11... | collective-permute-start | bytes 903176 | tf_op jit(solution)/shard_map/ppermute | solution.py:288
  19.6 1.4 %collective-permute-start.9 = (bf16[8,6272]{1,0:T(8,128)(2,1)S(1)}, bf16[8,6272]{1,0:T(8,128)(2,1)S(1)}, u32[]{:S(2)}, u32[]{:S(2)}) collective-permute-start(bf16[8,6272]{1,0:T(8,128)(2,1)S(1)} %stack.5), channel_id=1, source_target_pairs={{0,1},{1,0},{2,3},{3,2},{4,5},{5,4},{6,7},{7,6},{8,9},{9,8},{10,11... | collective-permute-start | bytes 301064 | tf_op jit(solution)/shard_map/ppermute | solution.py:288
  20.2 5.2 %slice-start = ((s8[14680064]{0:T(1024)(128)(4,1)}), s8[4194304]{0:T(1024)(128)(4,1)S(1)}, s32[]{:S(2)}) async-start(s8[14680064]{0:T(1024)(128)(4,1)} %bitcast.3), calls=%async_computation | async-start | bytes 8388608
  20.7 4.8 %slice-start.1 = ((s8[14680064]{0:T(1024)(128)(4,1)}), s8[4194304]{0:T(1024)(128)(4,1)S(1)}, s32[]{:S(2)}) async-start(s8[14680064]{0:T(1024)(128)(4,1)} %bitcast.3), calls=%async_computation.1 | async-start | bytes 8388608
  20.7 4.8 %slice-start.2 = ((s8[14680064]{0:T(1024)(128)(4,1)}), s8[4194304]{0:T(1024)(128)(4,1)S(1)}, s32[]{:S(2)}) async-start(s8[14680064]{0:T(1024)(128)(4,1)} %bitcast.3), calls=%async_computation.2 | async-start | bytes 8388608
  20.7 4.9 %slice-start.3 = ((s8[14680064]{0:T(1024)(128)(4,1)}), s8[2097152]{0:T(1024)(128)(4,1)S(1)}, s32[]{:S(2)}) async-start(s8[14680064]{0:T(1024)(128)(4,1)} %bitcast.3), calls=%async_computation.3 | async-start | bytes 4194304
  27.8 1.8 %collective-permute-start.11 = (bf16[32,6272]{1,0:T(8,128)(2,1)S(1)}, bf16[32,6272]{1,0:T(8,128)(2,1)S(1)}, u32[]{:S(2)}, u32[]{:S(2)}) collective-permute-start(bf16[32,6272]{1,0:T(8,128)(2,1)S(1)} %get-tuple-element.31), channel_id=1, source_target_pairs={{0,1},{1,0},{2,3},{3,2},{4,5},{5,4},{6,7},{7,6},{8,9},{9,8},{10,11... | collective-permute-start | bytes 1204232 | tf_op jit(solution)/shard_map/ppermute | solution.py:288
  28.0 5.8 %collective-permute-start.10 = (bf16[32,6272]{1,0:T(8,128)(2,1)S(1)}, bf16[32,6272]{1,0:T(8,128)(2,1)S(1)}, u32[]{:S(2)}, u32[]{:S(2)}) collective-permute-start(bf16[32,6272]{1,0:T(8,128)(2,1)S(1)} %get-tuple-element.28), channel_id=1, source_target_pairs={{0,1},{1,0},{2,3},{3,2},{4,5},{5,4},{6,7},{7,6},{8,9},{9,8},{10,11... | collective-permute-start | bytes 1204232 | tf_op jit(solution)/shard_map/ppermute | solution.py:288
  29.7 5.7 %collective-permute-start.13 = (bf16[8,6272]{1,0:T(8,128)(2,1)S(1)}, bf16[8,6272]{1,0:T(8,128)(2,1)S(1)}, u32[]{:S(2)}, u32[]{:S(2)}) collective-permute-start(bf16[8,6272]{1,0:T(8,128)(2,1)S(1)} %get-tuple-element.34), channel_id=1, source_target_pairs={{0,2},{2,0},{4,6},{6,4},{8,10},{10,8},{12,14},{14,12},{1,3},{3,1},... | collective-permute-start | bytes 301064 | tf_op jit(solution)/shard_map/ppermute | solution.py:285
  31.4 6.6 %collective-permute-start.15 = (bf16[8,6272]{1,0:T(8,128)(2,1)S(1)}, bf16[8,6272]{1,0:T(8,128)(2,1)S(1)}, u32[]{:S(2)}, u32[]{:S(2)}) collective-permute-start(bf16[8,6272]{1,0:T(8,128)(2,1)S(1)} %get-tuple-element.36), channel_id=1, source_target_pairs={{0,2},{2,0},{4,6},{6,4},{8,10},{10,8},{12,14},{14,12},{1,3},{3,1},... | collective-permute-start | bytes 301064 | tf_op jit(solution)/shard_map/ppermute | solution.py:285
  31.8 10.3 %collective-permute-start.17 = (bf16[8,6272]{1,0:T(8,128)(2,1)S(1)}, bf16[8,6272]{1,0:T(8,128)(2,1)S(1)}, u32[]{:S(2)}, u32[]{:S(2)}) collective-permute-start(bf16[8,6272]{1,0:T(8,128)(2,1)S(1)} %get-tuple-element.38), channel_id=1, source_target_pairs={{0,2},{2,0},{4,6},{6,4},{8,10},{10,8},{12,14},{14,12},{1,3},{3,1},... | collective-permute-start | bytes 301064 | tf_op jit(solution)/shard_map/ppermute | solution.py:285
  33.5 8.7 %collective-permute-start.12 = (bf16[8,6272]{1,0:T(8,128)(2,1)S(1)}, bf16[8,6272]{1,0:T(8,128)(2,1)S(1)}, u32[]{:S(2)}, u32[]{:S(2)}) collective-permute-start(bf16[8,6272]{1,0:T(8,128)(2,1)S(1)} %get-tuple-element.32), channel_id=1, source_target_pairs={{0,2},{2,0},{4,6},{6,4},{8,10},{10,8},{12,14},{14,12},{1,3},{3,1},... | collective-permute-start | bytes 301064 | tf_op jit(solution)/shard_map/ppermute | solution.py:285
  35.4 9.3 %collective-permute-start.14 = (bf16[8,6272]{1,0:T(8,128)(2,1)S(1)}, bf16[8,6272]{1,0:T(8,128)(2,1)S(1)}, u32[]{:S(2)}, u32[]{:S(2)}) collective-permute-start(bf16[8,6272]{1,0:T(8,128)(2,1)S(1)} %span_sum.3), channel_id=1, source_target_pairs={{0,8},{2,10},{4,12},{6,14},{8,0},{10,2},{12,4},{14,6},{1,9},{3,11}... | collective-permute-start | bytes 301064 | tf_op jit(solution)/shard_map/ppermute | solution.py:282
  38.0 7.8 %collective-permute-start.16 = (bf16[8,6272]{1,0:T(8,128)(2,1)S(1)}, bf16[8,6272]{1,0:T(8,128)(2,1)S(1)}, u32[]{:S(2)}, u32[]{:S(2)}) collective-permute-start(bf16[8,6272]{1,0:T(8,128)(2,1)S(1)} %span_sum.4), channel_id=1, source_target_pairs={{0,12},{2,14},{4,8},{6,10},{8,4},{10,6},{12,0},{14,2},{1,13},{3,15... | collective-permute-start | bytes 301064 | tf_op jit(solution)/shard_map/ppermute | solution.py:282
  42.1 4.7 %collective-permute-start.18 = (bf16[8,6272]{1,0:T(8,128)(2,1)S(1)}, bf16[8,6272]{1,0:T(8,128)(2,1)S(1)}, u32[]{:S(2)}, u32[]{:S(2)}) collective-permute-start(bf16[8,6272]{1,0:T(8,128)(2,1)S(1)} %span_sum.5), channel_id=1, source_target_pairs={{0,4},{2,6},{4,0},{6,2},{8,12},{10,14},{12,8},{14,10},{1,5},{3,7},... | collective-permute-start | bytes 301064 | tf_op jit(solution)/shard_map/ppermute | solution.py:282

commit v12 on v11

--- a/solution.py
+++ b/solution.py
@@ -9,9 +9,9 @@
 
 EXPERTS = 4
 LANES = 128
-RETURN_ORDER = (2, 3, 1)
-BLOCK_ORDER = (0, 2, 1, 3)
-N_BLOCK = 256
+RETURN_ORDER = (3, 2, 1)
+BLOCK_ORDER = (0, 3, 1, 2)
+N_BLOCK = 512
 LAST_FLOPS = 5_000_000_000
 EXCHANGE_FLOPS = 20_000_000_000
 

time: 47.8 us -> 47.1 us (0.985)
  starting transfers between devices: 22.8 us -> 22 us
    ppermute x6, starting transfers between devices: 12.4 us -> 10.7 us  [over_experts(): lax.ppermute(value, 'attn', [(i, (i // span ^ other) * span + i % span) f...]
    ppermute x8, starting transfers between devices: 9.59 us -> 10.5 us  [over_span(): lax.ppermute(value, 'attn', [(i, i // span * span + (i + shift) % span) f...]
  transfers between devices with their start and end apart: 19 -> 19, of which waited for: 11 -> 12; matrix products, arithmetic and copies ran while one was open for 0% -> 0% of each run, Pallas kernels for 2% -> 2%
where the time goes in v12:
time: 47.1 us; the launch traced here: 46.9 us
  starting transfers between devices  22 us (47%)
  waiting for transfers between devices  15.2 us (32%)
  Pallas kernels  9.31 us (20%)
    ppermute x6, starting transfers between devices, over_experts(): lax.ppermute(value, 'attn', [(i, (i // span ^ other) * span + i % span) f...  10.7 us
    ppermute x8, starting transfers between devices, over_span(): lax.ppermute(value, 'attn', [(i, i // span * span + (i + shift) % span) f...  10.5 us
    ppermute x6, waiting for transfers between devices, over_experts(): lax.ppermute(value, 'attn', [(i, (i // span ^ other) * span + i % span) f...  7.93 us
    ppermute x8, waiting for transfers between devices, over_span(): lax.ppermute(value, 'attn', [(i, i // span * span + (i + shift) % span) f...  5.28 us
    pallas_call x1, Pallas kernels, gate_up(): pl.pallas_call(functools.partial(gate_up_kernel, block_of(units, N_BLOCK)...  4.09 us
    pallas_call x1, Pallas kernels, down(): pl.pallas_call(functools.partial(down_kernel, rows), in_specs=[pl.BlockSp...  2.22 us
    ppermute x5, waiting for transfers between devices, over_pair(): lax.ppermute(value, 'ffn', [(i, (i + shift) % pair) for i in range(pair)])  1.99 us
    pallas_call x1, Pallas kernels, pack(): pl.pallas_call(pack_kernel, in_specs=[pl.BlockSpec(memory_space=pltpu.SME...  1.3 us
  transfers between devices with their start and end apart: 19, of which 12 were waited for; matrix products, arithmetic and copies ran while one was open for 0% of the time, Pallas kernels for 2%

profile of v12, /device:TPU:0, one launch (start us, length us, event | category | flops | bytes accessed | tf_op | source)
XLA Modules:
  0.0 46.9 jit_solution(4151368281518284271)
XLA Ops:
  0.0 1.3 %pack.1 = (f32[8,1024]{1,0:T(8,128)S(1)}, bf16[8,6272]{1,0:T(8,128)(2,1)S(1)}, bf16[8,6272]{1,0:T(8,128)(2,1)S(1)}, bf16[8,6272]{1,0:T(8,128)(2,1)S(1)}, bf16[8,6272]{1,0:T(8,128)(2,1)S(1)}) custom-call(s32[1]{0:T(128)} %bitcast.own_expert, bf16[8,7168]{1,0:T(8,128)(2,1)} %tokens_hbm.1, s32[3,8]{1,0:T(4,128)} %bitcast.9, f32[3,8]{1,0:T(4,128)} %bitcast.10), custom_call_target="tpu_custom_call" | custom-call | flops 20000000000 | tf_op jit(solution)/shard_map/pack/pallas_call | solution.py:231
  1.4 5.1 %collective-permute-start = (bf16[8,6272]{1,0:T(8,128)(2,1)S(1)}, bf16[8,6272]{1,0:T(8,128)(2,1)S(1)}, u32[]{:S(2)}, u32[]{:S(2)}) collective-permute-start(bf16[8,6272]{1,0:T(8,128)(2,1)S(1)} %get-tuple-element.24), channel_id=1, source_target_pairs={{0,12},{2,14},{4,8},{6,10},{8,4},{10,6},{12,0},{14,2},{1,13},{3,15... | collective-permute-start | bytes 301064 | tf_op jit(solution)/shard_map/ppermute | solution.py:282
  6.5 0.6 %collective-permute-start.2 = (bf16[8,6272]{1,0:T(8,128)(2,1)S(1)}, bf16[8,6272]{1,0:T(8,128)(2,1)S(1)}, u32[]{:S(2)}, u32[]{:S(2)}) collective-permute-start(bf16[8,6272]{1,0:T(8,128)(2,1)S(1)} %get-tuple-element.26), channel_id=1, source_target_pairs={{0,8},{2,10},{4,12},{6,14},{8,0},{10,2},{12,4},{14,6},{1,9},{3,11}... | collective-permute-start | bytes 301064 | tf_op jit(solution)/shard_map/ppermute | solution.py:282
  7.1 1.7 %collective-permute-start.3 = (bf16[8,6272]{1,0:T(8,128)(2,1)S(1)}, bf16[8,6272]{1,0:T(8,128)(2,1)S(1)}, u32[]{:S(2)}, u32[]{:S(2)}) collective-permute-start(bf16[8,6272]{1,0:T(8,128)(2,1)S(1)} %get-tuple-element.23.refs_0_), channel_id=1, source_target_pairs={{0,2},{2,0},{4,6},{6,4},{8,10},{10,8},{12,14},{14,12},{1,3},{3,1},... | collective-permute-start | bytes 301064 | tf_op jit(solution)/shard_map/ppermute | solution.py:285
  8.8 1.4 %collective-permute-done.refs_1_ = bf16[8,6272]{1,0:T(8,128)(2,1)S(1)} collective-permute-done((bf16[8,6272]{1,0:T(8,128)(2,1)S(1)}, bf16[8,6272]{1,0:T(8,128)(2,1)S(1)}, u32[]{:S(2)}, u32[]{:S(2)}) %collective-permute-start) | collective-permute-done | bytes 100384 | tf_op jit(solution)/shard_map/ppermute | solution.py:282
  10.2 1.7 %collective-permute-start.4 = (bf16[8,6272]{1,0:T(8,128)(2,1)S(1)}, bf16[8,6272]{1,0:T(8,128)(2,1)S(1)}, u32[]{:S(2)}, u32[]{:S(2)}) collective-permute-start(bf16[8,6272]{1,0:T(8,128)(2,1)S(1)} %collective-permute-done.refs_1_), channel_id=1, source_target_pairs={{0,2},{2,0},{4,6},{6,4},{8,10},{10,8},{12,14},{14,12},{1,3},{3,1},... | collective-permute-start | bytes 301064 | tf_op jit(solution)/shard_map/ppermute | solution.py:285
  11.9 0.7 %collective-permute-done.1.refs_2_ = bf16[8,6272]{1,0:T(8,128)(2,1)S(1)} collective-permute-done((bf16[8,6272]{1,0:T(8,128)(2,1)S(1)}, bf16[8,6272]{1,0:T(8,128)(2,1)S(1)}, u32[]{:S(2)}, u32[]{:S(2)}) %collective-permute-start.1) | collective-permute-done | bytes 100384 | tf_op jit(solution)/shard_map/ppermute | solution.py:282
  12.6 1.5 %collective-permute-start.5 = (bf16[8,6272]{1,0:T(8,128)(2,1)S(1)}, bf16[8,6272]{1,0:T(8,128)(2,1)S(1)}, u32[]{:S(2)}, u32[]{:S(2)}) collective-permute-start(bf16[8,6272]{1,0:T(8,128)(2,1)S(1)} %collective-permute-done.1.refs_2_), channel_id=1, source_target_pairs={{0,2},{2,0},{4,6},{6,4},{8,10},{10,8},{12,14},{14,12},{1,3},{3,1},... | collective-permute-start | bytes 301064 | tf_op jit(solution)/shard_map/ppermute | solution.py:285
  14.1 0.8 %collective-permute-done.2.refs_3_ = bf16[8,6272]{1,0:T(8,128)(2,1)S(1)} collective-permute-done((bf16[8,6272]{1,0:T(8,128)(2,1)S(1)}, bf16[8,6272]{1,0:T(8,128)(2,1)S(1)}, u32[]{:S(2)}, u32[]{:S(2)}) %collective-permute-start.2) | collective-permute-done | bytes 100384 | tf_op jit(solution)/shard_map/ppermute | solution.py:282
  14.9 1.5 %collective-permute-start.6 = (bf16[8,6272]{1,0:T(8,128)(2,1)S(1)}, bf16[8,6272]{1,0:T(8,128)(2,1)S(1)}, u32[]{:S(2)}, u32[]{:S(2)}) collective-permute-start(bf16[8,6272]{1,0:T(8,128)(2,1)S(1)} %collective-permute-done.2.refs_3_), channel_id=1, source_target_pairs={{0,2},{2,0},{4,6},{6,4},{8,10},{10,8},{12,14},{14,12},{1,3},{3,1},... | collective-permute-start | bytes 301064 | tf_op jit(solution)/shard_map/ppermute | solution.py:285
  16.6 1.0 %collective-permute-done.5.refs_2_.refs_6_ = bf16[8,6272]{1,0:T(8,128)(2,1)S(1)} collective-permute-done((bf16[8,6272]{1,0:T(8,128)(2,1)S(1)}, bf16[8,6272]{1,0:T(8,128)(2,1)S(1)}, u32[]{:S(2)}, u32[]{:S(2)}) %collective-permute-start.5) | collective-permute-done | bytes 100384 | tf_op jit(solution)/shard_map/ppermute | solution.py:285
  17.7 1.9 %collective-permute-done.6.refs_7_.refs_0_ = bf16[8,6272]{1,0:T(8,128)(2,1)S(1)} collective-permute-done((bf16[8,6272]{1,0:T(8,128)(2,1)S(1)}, bf16[8,6272]{1,0:T(8,128)(2,1)S(1)}, u32[]{:S(2)}, u32[]{:S(2)}) %collective-permute-start.6) | collective-permute-done | bytes 100384 | tf_op jit(solution)/shard_map/ppermute | solution.py:285
  19.7 0.5 unpack.1.first_ref
  20.2 0.8 %collective-permute-done.9.last_ref = bf16[8,6272]{1,0:T(8,128)(2,1)S(1)} collective-permute-done((bf16[8,6272]{1,0:T(8,128)(2,1)S(1)}, bf16[8,6272]{1,0:T(8,128)(2,1)S(1)}, u32[]{:S(2)}, u32[]{:S(2)}) %collective-permute-start.9) | collective-permute-done | bytes 100384 | tf_op jit(solution)/shard_map/ppermute | solution.py:288
  21.0 4.1 %gate_up.1.hidden_ref = bf16[128,1024]{1,0:T(8,128)(2,1)S(1)} custom-call(bf16[120,7168]{1,0:T(8,128)(2,1)S(1)} %unpack.1.first_ref, bf16[8,6272]{1,0:T(8,128)(2,1)S(1)} %collective-permute-done.9.last_ref, bf16[7168,1024]{1,0:T(8,128)(2,1)S(1)} %bitcast.6, bf16[7168,1024]{1,0:T(8,128)(2,1)S(1)} %bitcast.8), custom_call_target="tpu_custom_call" | custom-call | flops 3758096384 | tf_op jit(solution)/shard_map/gate_up/pallas_call | solution.py:113
  25.2 2.2 %down.1 = (f32[32,6272]{1,0:T(8,128)S(1)}, f32[32,6272]{1,0:T(8,128)S(1)}, bf16[32,6272]{1,0:T(8,128)(2,1)S(1)}, bf16[32,6272]{1,0:T(8,128)(2,1)S(1)}) custom-call(bf16[128,1024]{1,0:T(8,128)(2,1)S(1)} %gate_up.1.hidden_ref, bf16[1024,7168]{1,0:T(8,128)(2,1)S(1)} %bitcast.4), custom_call_target="tpu_custom_call" | custom-call | flops 1644167168 | tf_op jit(solution)/shard_map/down/pallas_call | solution.py:146
  27.4 0.4 collective-permute-start.11
  28.0 1.2 %collective-permute-done.11.refs_1_ = bf16[32,6272]{1,0:T(8,128)(2,1)S(1)} collective-permute-done((bf16[32,6272]{1,0:T(8,128)(2,1)S(1)}, bf16[32,6272]{1,0:T(8,128)(2,1)S(1)}, u32[]{:S(2)}, u32[]{:S(2)}) %collective-permute-start.11) | collective-permute-done | bytes 401440 | tf_op jit(solution)/shard_map/ppermute | solution.py:288
  29.3 1.6 %collective-permute-start.13 = (bf16[8,6272]{1,0:T(8,128)(2,1)S(1)}, bf16[8,6272]{1,0:T(8,128)(2,1)S(1)}, u32[]{:S(2)}, u32[]{:S(2)}) collective-permute-start(bf16[8,6272]{1,0:T(8,128)(2,1)S(1)} %get-tuple-element.34), channel_id=1, source_target_pairs={{0,2},{2,0},{4,6},{6,4},{8,10},{10,8},{12,14},{14,12},{1,3},{3,1},... | collective-permute-start | bytes 301064 | tf_op jit(solution)/shard_map/ppermute | solution.py:285
  30.9 0.5 %collective-permute-start.15 = (bf16[8,6272]{1,0:T(8,128)(2,1)S(1)}, bf16[8,6272]{1,0:T(8,128)(2,1)S(1)}, u32[]{:S(2)}, u32[]{:S(2)}) collective-permute-start(bf16[8,6272]{1,0:T(8,128)(2,1)S(1)} %get-tuple-element.36), channel_id=1, source_target_pairs={{0,2},{2,0},{4,6},{6,4},{8,10},{10,8},{12,14},{14,12},{1,3},{3,1},... | collective-permute-start | bytes 301064 | tf_op jit(solution)/shard_map/ppermute | solution.py:285
  31.4 1.5 %collective-permute-start.17 = (bf16[8,6272]{1,0:T(8,128)(2,1)S(1)}, bf16[8,6272]{1,0:T(8,128)(2,1)S(1)}, u32[]{:S(2)}, u32[]{:S(2)}) collective-permute-start(bf16[8,6272]{1,0:T(8,128)(2,1)S(1)} %get-tuple-element.38), channel_id=1, source_target_pairs={{0,2},{2,0},{4,6},{6,4},{8,10},{10,8},{12,14},{14,12},{1,3},{3,1},... | collective-permute-start | bytes 301064 | tf_op jit(solution)/shard_map/ppermute | solution.py:285
  32.9 0.5 %collective-permute-start.12 = (bf16[8,6272]{1,0:T(8,128)(2,1)S(1)}, bf16[8,6272]{1,0:T(8,128)(2,1)S(1)}, u32[]{:S(2)}, u32[]{:S(2)}) collective-permute-start(bf16[8,6272]{1,0:T(8,128)(2,1)S(1)} %get-tuple-element.32), channel_id=1, source_target_pairs={{0,2},{2,0},{4,6},{6,4},{8,10},{10,8},{12,14},{14,12},{1,3},{3,1},... | collective-permute-start | bytes 301064 | tf_op jit(solution)/shard_map/ppermute | solution.py:285
  33.5 1.5 %collective-permute-done.13.refs_1_ = bf16[8,6272]{1,0:T(8,128)(2,1)S(1)} collective-permute-done((bf16[8,6272]{1,0:T(8,128)(2,1)S(1)}, bf16[8,6272]{1,0:T(8,128)(2,1)S(1)}, u32[]{:S(2)}, u32[]{:S(2)}) %collective-permute-start.13) | collective-permute-done | bytes 100384 | tf_op jit(solution)/shard_map/ppermute | solution.py:285
  35.1 2.9 %collective-permute-start.14 = (bf16[8,6272]{1,0:T(8,128)(2,1)S(1)}, bf16[8,6272]{1,0:T(8,128)(2,1)S(1)}, u32[]{:S(2)}, u32[]{:S(2)}) collective-permute-start(bf16[8,6272]{1,0:T(8,128)(2,1)S(1)} %span_sum.3), channel_id=1, source_target_pairs={{0,12},{2,14},{4,8},{6,10},{8,4},{10,6},{12,0},{14,2},{1,13},{3,15... | collective-permute-start | bytes 301064 | tf_op jit(solution)/shard_map/ppermute | solution.py:282
  37.9 0.7 %collective-permute-start.16 = (bf16[8,6272]{1,0:T(8,128)(2,1)S(1)}, bf16[8,6272]{1,0:T(8,128)(2,1)S(1)}, u32[]{:S(2)}, u32[]{:S(2)}) collective-permute-start(bf16[8,6272]{1,0:T(8,128)(2,1)S(1)} %span_sum.4), channel_id=1, source_target_pairs={{0,8},{2,10},{4,12},{6,14},{8,0},{10,2},{12,4},{14,6},{1,9},{3,11}... | collective-permute-start | bytes 301064 | tf_op jit(solution)/shard_map/ppermute | solution.py:282
  38.7 0.7 %collective-permute-done.17.refs_1_ = bf16[8,6272]{1,0:T(8,128)(2,1)S(1)} collective-permute-done((bf16[8,6272]{1,0:T(8,128)(2,1)S(1)}, bf16[8,6272]{1,0:T(8,128)(2,1)S(1)}, u32[]{:S(2)}, u32[]{:S(2)}) %collective-permute-start.17) | collective-permute-done | bytes 100384 | tf_op jit(solution)/shard_map/ppermute | solution.py:285
  39.4 1.4 %collective-permute-start.18 = (bf16[8,6272]{1,0:T(8,128)(2,1)S(1)}, bf16[8,6272]{1,0:T(8,128)(2,1)S(1)}, u32[]{:S(2)}, u32[]{:S(2)}) collective-permute-start(bf16[8,6272]{1,0:T(8,128)(2,1)S(1)} %span_sum.5), channel_id=1, source_target_pairs={{0,4},{2,6},{4,0},{6,2},{8,12},{10,14},{12,8},{14,10},{1,5},{3,7},... | collective-permute-start | bytes 301064 | tf_op jit(solution)/shard_map/ppermute | solution.py:282
  40.7 0.2 collective-permute-done.12.refs_1_
  40.9 1.3 %collective-permute-done.14.refs_2_ = bf16[8,6272]{1,0:T(8,128)(2,1)S(1)} collective-permute-done((bf16[8,6272]{1,0:T(8,128)(2,1)S(1)}, bf16[8,6272]{1,0:T(8,128)(2,1)S(1)}, u32[]{:S(2)}, u32[]{:S(2)}) %collective-permute-start.14) | collective-permute-done | bytes 100384 | tf_op jit(solution)/shard_map/ppermute | solution.py:282
  42.2 0.1 combine.2.refs_0_
  42.4 3.7 %collective-permute-done.16.refs_1_ = bf16[8,6272]{1,0:T(8,128)(2,1)S(1)} collective-permute-done((bf16[8,6272]{1,0:T(8,128)(2,1)S(1)}, bf16[8,6272]{1,0:T(8,128)(2,1)S(1)}, u32[]{:S(2)}, u32[]{:S(2)}) %collective-permute-start.16) | collective-permute-done | bytes 100384 | tf_op jit(solution)/shard_map/ppermute | solution.py:282
  46.1 0.8 %combine.3 = bf16[8,7168]{1,0:T(8,128)(2,1)} custom-call(f32[8,1024]{1,0:T(8,128)S(1)} %get-tuple-element.22.sides_ref, f32[8,7168]{1,0:T(8,128)S(1)} %combine.2.refs_0_, bf16[8,6272]{1,0:T(8,128)(2,1)S(1)} %collective-permute-done.16.refs_1_, bf16[8,6272]{1,0:T(8,128)(2,1)S(1)} %collective-permute-done.18.refs_2_), custom_call_target="tpu_custom_call" | custom-call | tf_op jit(solution)/shard_map/combine/pallas_call | solution.py:267
  (47 shorter events, 0.7 us)
Async XLA Ops:
  0.0 20.9 %slice-start.4 = ((s8[14680064]{0:T(1024)(128)(4,1)}), s8[4194304]{0:T(1024)(128)(4,1)S(1)}, s32[]{:S(2)}) async-start(s8[14680064]{0:T(1024)(128)(4,1)} %bitcast.5), calls=%async_computation.4 | async-start | bytes 8388608
  0.0 20.9 %slice-start.8 = ((s8[14680064]{0:T(1024)(128)(4,1)}), s8[4194304]{0:T(1024)(128)(4,1)S(1)}, s32[]{:S(2)}) async-start(s8[14680064]{0:T(1024)(128)(4,1)} %bitcast.7), calls=%async_computation.8 | async-start | bytes 8388608
  0.0 20.9 %slice-start.5 = ((s8[14680064]{0:T(1024)(128)(4,1)}), s8[4194304]{0:T(1024)(128)(4,1)S(1)}, s32[]{:S(2)}) async-start(s8[14680064]{0:T(1024)(128)(4,1)} %bitcast.5), calls=%async_computation.5 | async-start | bytes 8388608
  0.0 20.9 %slice-start.6 = ((s8[14680064]{0:T(1024)(128)(4,1)}), s8[4194304]{0:T(1024)(128)(4,1)S(1)}, s32[]{:S(2)}) async-start(s8[14680064]{0:T(1024)(128)(4,1)} %bitcast.5), calls=%async_computation.6 | async-start | bytes 8388608
  0.0 21.0 %slice-start.7 = ((s8[14680064]{0:T(1024)(128)(4,1)}), s8[2097152]{0:T(1024)(128)(4,1)S(1)}, s32[]{:S(2)}) async-start(s8[14680064]{0:T(1024)(128)(4,1)} %bitcast.5), calls=%async_computation.7 | async-start | bytes 4194304
  0.0 21.0 %slice-start.9 = ((s8[14680064]{0:T(1024)(128)(4,1)}), s8[4194304]{0:T(1024)(128)(4,1)S(1)}, s32[]{:S(2)}) async-start(s8[14680064]{0:T(1024)(128)(4,1)} %bitcast.7), calls=%async_computation.9 | async-start | bytes 8388608
  0.0 21.0 %slice-start.10 = ((s8[14680064]{0:T(1024)(128)(4,1)}), s8[4194304]{0:T(1024)(128)(4,1)S(1)}, s32[]{:S(2)}) async-start(s8[14680064]{0:T(1024)(128)(4,1)} %bitcast.7), calls=%async_computation.10 | async-start | bytes 8388608
  0.0 21.0 %slice-start.11 = ((s8[14680064]{0:T(1024)(128)(4,1)}), s8[2097152]{0:T(1024)(128)(4,1)S(1)}, s32[]{:S(2)}) async-start(s8[14680064]{0:T(1024)(128)(4,1)} %bitcast.7), calls=%async_computation.11 | async-start | bytes 4194304
  1.4 8.8 %collective-permute-start = (bf16[8,6272]{1,0:T(8,128)(2,1)S(1)}, bf16[8,6272]{1,0:T(8,128)(2,1)S(1)}, u32[]{:S(2)}, u32[]{:S(2)}) collective-permute-start(bf16[8,6272]{1,0:T(8,128)(2,1)S(1)} %get-tuple-element.24), channel_id=1, source_target_pairs={{0,12},{2,14},{4,8},{6,10},{8,4},{10,6},{12,0},{14,2},{1,13},{3,15... | collective-permute-start | bytes 301064 | tf_op jit(solution)/shard_map/ppermute | solution.py:282
  6.5 6.1 %collective-permute-start.1 = (bf16[8,6272]{1,0:T(8,128)(2,1)S(1)}, bf16[8,6272]{1,0:T(8,128)(2,1)S(1)}, u32[]{:S(2)}, u32[]{:S(2)}) collective-permute-start(bf16[8,6272]{1,0:T(8,128)(2,1)S(1)} %get-tuple-element.25), channel_id=1, source_target_pairs={{0,4},{2,6},{4,0},{6,2},{8,12},{10,14},{12,8},{14,10},{1,5},{3,7},... | collective-permute-start | bytes 301064 | tf_op jit(solution)/shard_map/ppermute | solution.py:282
  6.5 8.4 %collective-permute-start.2 = (bf16[8,6272]{1,0:T(8,128)(2,1)S(1)}, bf16[8,6272]{1,0:T(8,128)(2,1)S(1)}, u32[]{:S(2)}, u32[]{:S(2)}) collective-permute-start(bf16[8,6272]{1,0:T(8,128)(2,1)S(1)} %get-tuple-element.26), channel_id=1, source_target_pairs={{0,8},{2,10},{4,12},{6,14},{8,0},{10,2},{12,4},{14,6},{1,9},{3,11}... | collective-permute-start | bytes 301064 | tf_op jit(solution)/shard_map/ppermute | solution.py:282
  7.1 9.4 %collective-permute-start.3 = (bf16[8,6272]{1,0:T(8,128)(2,1)S(1)}, bf16[8,6272]{1,0:T(8,128)(2,1)S(1)}, u32[]{:S(2)}, u32[]{:S(2)}) collective-permute-start(bf16[8,6272]{1,0:T(8,128)(2,1)S(1)} %get-tuple-element.23.refs_0_), channel_id=1, source_target_pairs={{0,2},{2,0},{4,6},{6,4},{8,10},{10,8},{12,14},{14,12},{1,3},{3,1},... | collective-permute-start | bytes 301064 | tf_op jit(solution)/shard_map/ppermute | solution.py:285
  10.2 6.4 %collective-permute-start.4 = (bf16[8,6272]{1,0:T(8,128)(2,1)S(1)}, bf16[8,6272]{1,0:T(8,128)(2,1)S(1)}, u32[]{:S(2)}, u32[]{:S(2)}) collective-permute-start(bf16[8,6272]{1,0:T(8,128)(2,1)S(1)} %collective-permute-done.refs_1_), channel_id=1, source_target_pairs={{0,2},{2,0},{4,6},{6,4},{8,10},{10,8},{12,14},{14,12},{1,3},{3,1},... | collective-permute-start | bytes 301064 | tf_op jit(solution)/shard_map/ppermute | solution.py:285
  12.6 5.0 %collective-permute-start.5 = (bf16[8,6272]{1,0:T(8,128)(2,1)S(1)}, bf16[8,6272]{1,0:T(8,128)(2,1)S(1)}, u32[]{:S(2)}, u32[]{:S(2)}) collective-permute-start(bf16[8,6272]{1,0:T(8,128)(2,1)S(1)} %collective-permute-done.1.refs_2_), channel_id=1, source_target_pairs={{0,2},{2,0},{4,6},{6,4},{8,10},{10,8},{12,14},{14,12},{1,3},{3,1},... | collective-permute-start | bytes 301064 | tf_op jit(solution)/shard_map/ppermute | solution.py:285
  14.9 4.6 %collective-permute-start.6 = (bf16[8,6272]{1,0:T(8,128)(2,1)S(1)}, bf16[8,6272]{1,0:T(8,128)(2,1)S(1)}, u32[]{:S(2)}, u32[]{:S(2)}) collective-permute-start(bf16[8,6272]{1,0:T(8,128)(2,1)S(1)} %collective-permute-done.2.refs_3_), channel_id=1, source_target_pairs={{0,2},{2,0},{4,6},{6,4},{8,10},{10,8},{12,14},{14,12},{1,3},{3,1},... | collective-permute-start | bytes 301064 | tf_op jit(solution)/shard_map/ppermute | solution.py:285
  16.5 3.2 %collective-permute-start.7 = (bf16[32,6272]{1,0:T(8,128)(2,1)S(1)}, bf16[32,6272]{1,0:T(8,128)(2,1)S(1)}, u32[]{:S(2)}, u32[]{:S(2)}) collective-permute-start(bf16[32,6272]{1,0:T(8,128)(2,1)S(1)} %stack.3), channel_id=1, source_target_pairs={{0,1},{1,0},{2,3},{3,2},{4,5},{5,4},{6,7},{7,6},{8,9},{9,8},{10,11... | collective-permute-start | bytes 1204232 | tf_op jit(solution)/shard_map/ppermute | solution.py:288
  17.6 2.1 %collective-permute-start.8 = (bf16[24,6272]{1,0:T(8,128)(2,1)S(1)}, bf16[24,6272]{1,0:T(8,128)(2,1)S(1)}, u32[]{:S(2)}, u32[]{:S(2)}) collective-permute-start(bf16[24,6272]{1,0:T(8,128)(2,1)S(1)} %stack.4), channel_id=1, source_target_pairs={{0,1},{1,0},{2,3},{3,2},{4,5},{5,4},{6,7},{7,6},{8,9},{9,8},{10,11... | collective-permute-start | bytes 903176 | tf_op jit(solution)/shard_map/ppermute | solution.py:288
  19.6 1.4 %collective-permute-start.9 = (bf16[8,6272]{1,0:T(8,128)(2,1)S(1)}, bf16[8,6272]{1,0:T(8,128)(2,1)S(1)}, u32[]{:S(2)}, u32[]{:S(2)}) collective-permute-start(bf16[8,6272]{1,0:T(8,128)(2,1)S(1)} %stack.5), channel_id=1, source_target_pairs={{0,1},{1,0},{2,3},{3,2},{4,5},{5,4},{6,7},{7,6},{8,9},{9,8},{10,11... | collective-permute-start | bytes 301064 | tf_op jit(solution)/shard_map/ppermute | solution.py:288
  19.7 5.4 %slice-start = ((s8[14680064]{0:T(1024)(128)(4,1)}), s8[4194304]{0:T(1024)(128)(4,1)S(1)}, s32[]{:S(2)}) async-start(s8[14680064]{0:T(1024)(128)(4,1)} %bitcast.3), calls=%async_computation | async-start | bytes 8388608
  20.1 5.0 %slice-start.1 = ((s8[14680064]{0:T(1024)(128)(4,1)}), s8[4194304]{0:T(1024)(128)(4,1)S(1)}, s32[]{:S(2)}) async-start(s8[14680064]{0:T(1024)(128)(4,1)} %bitcast.3), calls=%async_computation.1 | async-start | bytes 8388608
  20.2 5.0 %slice-start.2 = ((s8[14680064]{0:T(1024)(128)(4,1)}), s8[4194304]{0:T(1024)(128)(4,1)S(1)}, s32[]{:S(2)}) async-start(s8[14680064]{0:T(1024)(128)(4,1)} %bitcast.3), calls=%async_computation.2 | async-start | bytes 8388608
  20.2 5.0 %slice-start.3 = ((s8[14680064]{0:T(1024)(128)(4,1)}), s8[2097152]{0:T(1024)(128)(4,1)S(1)}, s32[]{:S(2)}) async-start(s8[14680064]{0:T(1024)(128)(4,1)} %bitcast.3), calls=%async_computation.3 | async-start | bytes 4194304
  27.4 1.8 %collective-permute-start.11 = (bf16[32,6272]{1,0:T(8,128)(2,1)S(1)}, bf16[32,6272]{1,0:T(8,128)(2,1)S(1)}, u32[]{:S(2)}, u32[]{:S(2)}) collective-permute-start(bf16[32,6272]{1,0:T(8,128)(2,1)S(1)} %get-tuple-element.31), channel_id=1, source_target_pairs={{0,1},{1,0},{2,3},{3,2},{4,5},{5,4},{6,7},{7,6},{8,9},{9,8},{10,11... | collective-permute-start | bytes 1204232 | tf_op jit(solution)/shard_map/ppermute | solution.py:288
  27.8 5.6 %collective-permute-start.10 = (bf16[32,6272]{1,0:T(8,128)(2,1)S(1)}, bf16[32,6272]{1,0:T(8,128)(2,1)S(1)}, u32[]{:S(2)}, u32[]{:S(2)}) collective-permute-start(bf16[32,6272]{1,0:T(8,128)(2,1)S(1)} %get-tuple-element.28), channel_id=1, source_target_pairs={{0,1},{1,0},{2,3},{3,2},{4,5},{5,4},{6,7},{7,6},{8,9},{9,8},{10,11... | collective-permute-start | bytes 1204232 | tf_op jit(solution)/shard_map/ppermute | solution.py:288
  29.3 5.7 %collective-permute-start.13 = (bf16[8,6272]{1,0:T(8,128)(2,1)S(1)}, bf16[8,6272]{1,0:T(8,128)(2,1)S(1)}, u32[]{:S(2)}, u32[]{:S(2)}) collective-permute-start(bf16[8,6272]{1,0:T(8,128)(2,1)S(1)} %get-tuple-element.34), channel_id=1, source_target_pairs={{0,2},{2,0},{4,6},{6,4},{8,10},{10,8},{12,14},{14,12},{1,3},{3,1},... | collective-permute-start | bytes 301064 | tf_op jit(solution)/shard_map/ppermute | solution.py:285
  30.9 7.0 %collective-permute-start.15 = (bf16[8,6272]{1,0:T(8,128)(2,1)S(1)}, bf16[8,6272]{1,0:T(8,128)(2,1)S(1)}, u32[]{:S(2)}, u32[]{:S(2)}) collective-permute-start(bf16[8,6272]{1,0:T(8,128)(2,1)S(1)} %get-tuple-element.36), channel_id=1, source_target_pairs={{0,2},{2,0},{4,6},{6,4},{8,10},{10,8},{12,14},{14,12},{1,3},{3,1},... | collective-permute-start | bytes 301064 | tf_op jit(solution)/shard_map/ppermute | solution.py:285
  31.4 7.9 %collective-permute-start.17 = (bf16[8,6272]{1,0:T(8,128)(2,1)S(1)}, bf16[8,6272]{1,0:T(8,128)(2,1)S(1)}, u32[]{:S(2)}, u32[]{:S(2)}) collective-permute-start(bf16[8,6272]{1,0:T(8,128)(2,1)S(1)} %get-tuple-element.38), channel_id=1, source_target_pairs={{0,2},{2,0},{4,6},{6,4},{8,10},{10,8},{12,14},{14,12},{1,3},{3,1},... | collective-permute-start | bytes 301064 | tf_op jit(solution)/shard_map/ppermute | solution.py:285
  32.9 8.0 %collective-permute-start.12 = (bf16[8,6272]{1,0:T(8,128)(2,1)S(1)}, bf16[8,6272]{1,0:T(8,128)(2,1)S(1)}, u32[]{:S(2)}, u32[]{:S(2)}) collective-permute-start(bf16[8,6272]{1,0:T(8,128)(2,1)S(1)} %get-tuple-element.32), channel_id=1, source_target_pairs={{0,2},{2,0},{4,6},{6,4},{8,10},{10,8},{12,14},{14,12},{1,3},{3,1},... | collective-permute-start | bytes 301064 | tf_op jit(solution)/shard_map/ppermute | solution.py:285
  35.1 7.2 %collective-permute-start.14 = (bf16[8,6272]{1,0:T(8,128)(2,1)S(1)}, bf16[8,6272]{1,0:T(8,128)(2,1)S(1)}, u32[]{:S(2)}, u32[]{:S(2)}) collective-permute-start(bf16[8,6272]{1,0:T(8,128)(2,1)S(1)} %span_sum.3), channel_id=1, source_target_pairs={{0,12},{2,14},{4,8},{6,10},{8,4},{10,6},{12,0},{14,2},{1,13},{3,15... | collective-permute-start | bytes 301064 | tf_op jit(solution)/shard_map/ppermute | solution.py:282
  37.9 8.2 %collective-permute-start.16 = (bf16[8,6272]{1,0:T(8,128)(2,1)S(1)}, bf16[8,6272]{1,0:T(8,128)(2,1)S(1)}, u32[]{:S(2)}, u32[]{:S(2)}) collective-permute-start(bf16[8,6272]{1,0:T(8,128)(2,1)S(1)} %span_sum.4), channel_id=1, source_target_pairs={{0,8},{2,10},{4,12},{6,14},{8,0},{10,2},{12,4},{14,6},{1,9},{3,11}... | collective-permute-start | bytes 301064 | tf_op jit(solution)/shard_map/ppermute | solution.py:282
  39.4 6.8 %collective-permute-start.18 = (bf16[8,6272]{1,0:T(8,128)(2,1)S(1)}, bf16[8,6272]{1,0:T(8,128)(2,1)S(1)}, u32[]{:S(2)}, u32[]{:S(2)}) collective-permute-start(bf16[8,6272]{1,0:T(8,128)(2,1)S(1)} %span_sum.5), channel_id=1, source_target_pairs={{0,4},{2,6},{4,0},{6,2},{8,12},{10,14},{12,8},{14,10},{1,5},{3,7},... | collective-permute-start | bytes 301064 | tf_op jit(solution)/shard_map/ppermute | solution.py:282

commit v13 on v12

--- a/solution.py
+++ b/solution.py
@@ -11,7 +11,7 @@
 LANES = 128
 RETURN_ORDER = (3, 2, 1)
 BLOCK_ORDER = (0, 3, 1, 2)
-N_BLOCK = 512
+N_BLOCK = 1024
 LAST_FLOPS = 5_000_000_000
 EXCHANGE_FLOPS = 20_000_000_000
 
@@ -128,15 +128,15 @@
     last = lax.broadcasted_iota(jnp.int32, blocks, 1) == rows - 1
     hidden = hidden_ref[...]
     ends = None
-    for i in [rows - 2] + list(range(0, rows - 2, 2)):
-        both = jnp.dot(hidden, down_ref[:, i * tail:(i + 2) * tail], preferred_element_type=jnp.float32)
-        pieces = {i: both[:, :tail].reshape(blocks), i + 1: both[:, tail:].reshape(blocks)}
+    for first in (rows // 2, 0):
+        wide = jnp.dot(hidden, down_ref[:, first * tail:(first + rows // 2) * tail], preferred_element_type=jnp.float32)
         if ends is None:
-            ends = pieces.pop(i + 1)
-        for j, value in pieces.items():
-            value = jnp.where(last, jnp.broadcast_to(ends[:, j:j + 1, :], blocks), value).reshape(blocks[0] * rows, tail)
+            ends = wide[:, -tail:].reshape(blocks)
+        for i in range(first, min(first + rows // 2, rows - 1)):
+            value = wide[:, (i - first) * tail:(i - first + 1) * tail].reshape(blocks)
+            value = jnp.where(last, jnp.broadcast_to(ends[:, i:i + 1, :], blocks), value).reshape(blocks[0] * rows, tail)
             for k, ref in enumerate(outs):
-                ref[:, j * tail:(j + 1) * tail] = value[k * count:(k + 1) * count].astype(ref.dtype)
+                ref[:, i * tail:(i + 1) * tail] = value[k * count:(k + 1) * count].astype(ref.dtype)
 
 
 def down(hidden, down_weight, span, pair, rows):

time: 47.1 us -> 47.1 us (level)
  no operation moved by 1% of the time
where the time goes in v13:
time: 47.1 us; the launch traced here: 47 us
  starting transfers between devices  22 us (47%)
  waiting for transfers between devices  15.2 us (32%)
  Pallas kernels  9.36 us (20%)
    ppermute x6, starting transfers between devices, over_experts(): lax.ppermute(value, 'attn', [(i, (i // span ^ other) * span + i % span) f...  10.7 us
    ppermute x8, starting transfers between devices, over_span(): lax.ppermute(value, 'attn', [(i, i // span * span + (i + shift) % span) f...  10.5 us
    ppermute x6, waiting for transfers between devices, over_experts(): lax.ppermute(value, 'attn', [(i, (i // span ^ other) * span + i % span) f...  7.93 us
    ppermute x8, waiting for transfers between devices, over_span(): lax.ppermute(value, 'attn', [(i, i // span * span + (i + shift) % span) f...  5.3 us
    pallas_call x1, Pallas kernels, gate_up(): pl.pallas_call(functools.partial(gate_up_kernel, block_of(units, N_BLOCK)...  4.06 us
    pallas_call x1, Pallas kernels, down(): pl.pallas_call(functools.partial(down_kernel, rows), in_specs=[pl.BlockSp...  2.29 us
    ppermute x5, waiting for transfers between devices, over_pair(): lax.ppermute(value, 'ffn', [(i, (i + shift) % pair) for i in range(pair)])  2.02 us
    pallas_call x1, Pallas kernels, pack(): pl.pallas_call(pack_kernel, in_specs=[pl.BlockSpec(memory_space=pltpu.SME...  1.3 us
  transfers between devices with their start and end apart: 19, of which 12 were waited for; matrix products, arithmetic and copies ran while one was open for 0% of the time, Pallas kernels for 2%

profile of v13, /device:TPU:0, one launch (start us, length us, event | category | flops | bytes accessed | tf_op | source)
XLA Modules:
  0.0 47.0 jit_solution(16468678996676447561)
XLA Ops:
  0.0 1.3 %pack.1 = (f32[8,1024]{1,0:T(8,128)S(1)}, bf16[8,6272]{1,0:T(8,128)(2,1)S(1)}, bf16[8,6272]{1,0:T(8,128)(2,1)S(1)}, bf16[8,6272]{1,0:T(8,128)(2,1)S(1)}, bf16[8,6272]{1,0:T(8,128)(2,1)S(1)}) custom-call(s32[1]{0:T(128)} %bitcast.own_expert, bf16[8,7168]{1,0:T(8,128)(2,1)} %tokens_hbm.1, s32[3,8]{1,0:T(4,128)} %bitcast.9, f32[3,8]{1,0:T(4,128)} %bitcast.10), custom_call_target="tpu_custom_call" | custom-call | flops 20000000000 | tf_op jit(solution)/shard_map/pack/pallas_call | solution.py:231
  1.4 5.1 %collective-permute-start = (bf16[8,6272]{1,0:T(8,128)(2,1)S(1)}, bf16[8,6272]{1,0:T(8,128)(2,1)S(1)}, u32[]{:S(2)}, u32[]{:S(2)}) collective-permute-start(bf16[8,6272]{1,0:T(8,128)(2,1)S(1)} %get-tuple-element.24), channel_id=1, source_target_pairs={{0,12},{2,14},{4,8},{6,10},{8,4},{10,6},{12,0},{14,2},{1,13},{3,15... | collective-permute-start | bytes 301064 | tf_op jit(solution)/shard_map/ppermute | solution.py:282
  6.5 0.6 %collective-permute-start.2 = (bf16[8,6272]{1,0:T(8,128)(2,1)S(1)}, bf16[8,6272]{1,0:T(8,128)(2,1)S(1)}, u32[]{:S(2)}, u32[]{:S(2)}) collective-permute-start(bf16[8,6272]{1,0:T(8,128)(2,1)S(1)} %get-tuple-element.26), channel_id=1, source_target_pairs={{0,8},{2,10},{4,12},{6,14},{8,0},{10,2},{12,4},{14,6},{1,9},{3,11}... | collective-permute-start | bytes 301064 | tf_op jit(solution)/shard_map/ppermute | solution.py:282
  7.1 1.7 %collective-permute-start.3 = (bf16[8,6272]{1,0:T(8,128)(2,1)S(1)}, bf16[8,6272]{1,0:T(8,128)(2,1)S(1)}, u32[]{:S(2)}, u32[]{:S(2)}) collective-permute-start(bf16[8,6272]{1,0:T(8,128)(2,1)S(1)} %get-tuple-element.23.refs_0_), channel_id=1, source_target_pairs={{0,2},{2,0},{4,6},{6,4},{8,10},{10,8},{12,14},{14,12},{1,3},{3,1},... | collective-permute-start | bytes 301064 | tf_op jit(solution)/shard_map/ppermute | solution.py:285
  8.8 1.4 %collective-permute-done.refs_1_ = bf16[8,6272]{1,0:T(8,128)(2,1)S(1)} collective-permute-done((bf16[8,6272]{1,0:T(8,128)(2,1)S(1)}, bf16[8,6272]{1,0:T(8,128)(2,1)S(1)}, u32[]{:S(2)}, u32[]{:S(2)}) %collective-permute-start) | collective-permute-done | bytes 100384 | tf_op jit(solution)/shard_map/ppermute | solution.py:282
  10.2 1.7 %collective-permute-start.4 = (bf16[8,6272]{1,0:T(8,128)(2,1)S(1)}, bf16[8,6272]{1,0:T(8,128)(2,1)S(1)}, u32[]{:S(2)}, u32[]{:S(2)}) collective-permute-start(bf16[8,6272]{1,0:T(8,128)(2,1)S(1)} %collective-permute-done.refs_1_), channel_id=1, source_target_pairs={{0,2},{2,0},{4,6},{6,4},{8,10},{10,8},{12,14},{14,12},{1,3},{3,1},... | collective-permute-start | bytes 301064 | tf_op jit(solution)/shard_map/ppermute | solution.py:285
  11.9 0.7 %collective-permute-done.1.refs_2_ = bf16[8,6272]{1,0:T(8,128)(2,1)S(1)} collective-permute-done((bf16[8,6272]{1,0:T(8,128)(2,1)S(1)}, bf16[8,6272]{1,0:T(8,128)(2,1)S(1)}, u32[]{:S(2)}, u32[]{:S(2)}) %collective-permute-start.1) | collective-permute-done | bytes 100384 | tf_op jit(solution)/shard_map/ppermute | solution.py:282
  12.6 1.5 %collective-permute-start.5 = (bf16[8,6272]{1,0:T(8,128)(2,1)S(1)}, bf16[8,6272]{1,0:T(8,128)(2,1)S(1)}, u32[]{:S(2)}, u32[]{:S(2)}) collective-permute-start(bf16[8,6272]{1,0:T(8,128)(2,1)S(1)} %collective-permute-done.1.refs_2_), channel_id=1, source_target_pairs={{0,2},{2,0},{4,6},{6,4},{8,10},{10,8},{12,14},{14,12},{1,3},{3,1},... | collective-permute-start | bytes 301064 | tf_op jit(solution)/shard_map/ppermute | solution.py:285
  14.1 0.8 %collective-permute-done.2.refs_3_ = bf16[8,6272]{1,0:T(8,128)(2,1)S(1)} collective-permute-done((bf16[8,6272]{1,0:T(8,128)(2,1)S(1)}, bf16[8,6272]{1,0:T(8,128)(2,1)S(1)}, u32[]{:S(2)}, u32[]{:S(2)}) %collective-permute-start.2) | collective-permute-done | bytes 100384 | tf_op jit(solution)/shard_map/ppermute | solution.py:282
  14.9 1.5 %collective-permute-start.6 = (bf16[8,6272]{1,0:T(8,128)(2,1)S(1)}, bf16[8,6272]{1,0:T(8,128)(2,1)S(1)}, u32[]{:S(2)}, u32[]{:S(2)}) collective-permute-start(bf16[8,6272]{1,0:T(8,128)(2,1)S(1)} %collective-permute-done.2.refs_3_), channel_id=1, source_target_pairs={{0,2},{2,0},{4,6},{6,4},{8,10},{10,8},{12,14},{14,12},{1,3},{3,1},... | collective-permute-start | bytes 301064 | tf_op jit(solution)/shard_map/ppermute | solution.py:285
  16.6 1.0 %collective-permute-done.5.refs_2_.refs_6_ = bf16[8,6272]{1,0:T(8,128)(2,1)S(1)} collective-permute-done((bf16[8,6272]{1,0:T(8,128)(2,1)S(1)}, bf16[8,6272]{1,0:T(8,128)(2,1)S(1)}, u32[]{:S(2)}, u32[]{:S(2)}) %collective-permute-start.5) | collective-permute-done | bytes 100384 | tf_op jit(solution)/shard_map/ppermute | solution.py:285
  17.7 1.9 %collective-permute-done.6.refs_7_.refs_0_ = bf16[8,6272]{1,0:T(8,128)(2,1)S(1)} collective-permute-done((bf16[8,6272]{1,0:T(8,128)(2,1)S(1)}, bf16[8,6272]{1,0:T(8,128)(2,1)S(1)}, u32[]{:S(2)}, u32[]{:S(2)}) %collective-permute-start.6) | collective-permute-done | bytes 100384 | tf_op jit(solution)/shard_map/ppermute | solution.py:285
  19.7 0.5 unpack.1.first_ref
  20.2 0.8 %collective-permute-done.9.last_ref = bf16[8,6272]{1,0:T(8,128)(2,1)S(1)} collective-permute-done((bf16[8,6272]{1,0:T(8,128)(2,1)S(1)}, bf16[8,6272]{1,0:T(8,128)(2,1)S(1)}, u32[]{:S(2)}, u32[]{:S(2)}) %collective-permute-start.9) | collective-permute-done | bytes 100384 | tf_op jit(solution)/shard_map/ppermute | solution.py:288
  21.0 4.1 %gate_up.1.hidden_ref = bf16[128,1024]{1,0:T(8,128)(2,1)S(1)} custom-call(bf16[120,7168]{1,0:T(8,128)(2,1)S(1)} %unpack.1.first_ref, bf16[8,6272]{1,0:T(8,128)(2,1)S(1)} %collective-permute-done.9.last_ref, bf16[7168,1024]{1,0:T(8,128)(2,1)S(1)} %bitcast.6, bf16[7168,1024]{1,0:T(8,128)(2,1)S(1)} %bitcast.8), custom_call_target="tpu_custom_call" | custom-call | flops 3758096384 | tf_op jit(solution)/shard_map/gate_up/pallas_call | solution.py:113
  25.1 2.3 %down.1 = (f32[32,6272]{1,0:T(8,128)S(1)}, f32[32,6272]{1,0:T(8,128)S(1)}, bf16[32,6272]{1,0:T(8,128)(2,1)S(1)}, bf16[32,6272]{1,0:T(8,128)(2,1)S(1)}) custom-call(bf16[128,1024]{1,0:T(8,128)(2,1)S(1)} %gate_up.1.hidden_ref, bf16[1024,7168]{1,0:T(8,128)(2,1)S(1)} %bitcast.4), custom_call_target="tpu_custom_call" | custom-call | flops 1644167168 | tf_op jit(solution)/shard_map/down/pallas_call | solution.py:146
  27.4 0.5 collective-permute-start.11
  28.0 1.2 %collective-permute-done.11.refs_1_ = bf16[32,6272]{1,0:T(8,128)(2,1)S(1)} collective-permute-done((bf16[32,6272]{1,0:T(8,128)(2,1)S(1)}, bf16[32,6272]{1,0:T(8,128)(2,1)S(1)}, u32[]{:S(2)}, u32[]{:S(2)}) %collective-permute-start.11) | collective-permute-done | bytes 401440 | tf_op jit(solution)/shard_map/ppermute | solution.py:288
  29.4 1.6 %collective-permute-start.13 = (bf16[8,6272]{1,0:T(8,128)(2,1)S(1)}, bf16[8,6272]{1,0:T(8,128)(2,1)S(1)}, u32[]{:S(2)}, u32[]{:S(2)}) collective-permute-start(bf16[8,6272]{1,0:T(8,128)(2,1)S(1)} %get-tuple-element.34), channel_id=1, source_target_pairs={{0,2},{2,0},{4,6},{6,4},{8,10},{10,8},{12,14},{14,12},{1,3},{3,1},... | collective-permute-start | bytes 301064 | tf_op jit(solution)/shard_map/ppermute | solution.py:285
  31.0 0.5 %collective-permute-start.15 = (bf16[8,6272]{1,0:T(8,128)(2,1)S(1)}, bf16[8,6272]{1,0:T(8,128)(2,1)S(1)}, u32[]{:S(2)}, u32[]{:S(2)}) collective-permute-start(bf16[8,6272]{1,0:T(8,128)(2,1)S(1)} %get-tuple-element.36), channel_id=1, source_target_pairs={{0,2},{2,0},{4,6},{6,4},{8,10},{10,8},{12,14},{14,12},{1,3},{3,1},... | collective-permute-start | bytes 301064 | tf_op jit(solution)/shard_map/ppermute | solution.py:285
  31.5 1.5 %collective-permute-start.17 = (bf16[8,6272]{1,0:T(8,128)(2,1)S(1)}, bf16[8,6272]{1,0:T(8,128)(2,1)S(1)}, u32[]{:S(2)}, u32[]{:S(2)}) collective-permute-start(bf16[8,6272]{1,0:T(8,128)(2,1)S(1)} %get-tuple-element.38), channel_id=1, source_target_pairs={{0,2},{2,0},{4,6},{6,4},{8,10},{10,8},{12,14},{14,12},{1,3},{3,1},... | collective-permute-start | bytes 301064 | tf_op jit(solution)/shard_map/ppermute | solution.py:285
  33.0 0.5 %collective-permute-start.12 = (bf16[8,6272]{1,0:T(8,128)(2,1)S(1)}, bf16[8,6272]{1,0:T(8,128)(2,1)S(1)}, u32[]{:S(2)}, u32[]{:S(2)}) collective-permute-start(bf16[8,6272]{1,0:T(8,128)(2,1)S(1)} %get-tuple-element.32), channel_id=1, source_target_pairs={{0,2},{2,0},{4,6},{6,4},{8,10},{10,8},{12,14},{14,12},{1,3},{3,1},... | collective-permute-start | bytes 301064 | tf_op jit(solution)/shard_map/ppermute | solution.py:285
  33.6 1.5 %collective-permute-done.13.refs_1_ = bf16[8,6272]{1,0:T(8,128)(2,1)S(1)} collective-permute-done((bf16[8,6272]{1,0:T(8,128)(2,1)S(1)}, bf16[8,6272]{1,0:T(8,128)(2,1)S(1)}, u32[]{:S(2)}, u32[]{:S(2)}) %collective-permute-start.13) | collective-permute-done | bytes 100384 | tf_op jit(solution)/shard_map/ppermute | solution.py:285
  35.1 2.9 %collective-permute-start.14 = (bf16[8,6272]{1,0:T(8,128)(2,1)S(1)}, bf16[8,6272]{1,0:T(8,128)(2,1)S(1)}, u32[]{:S(2)}, u32[]{:S(2)}) collective-permute-start(bf16[8,6272]{1,0:T(8,128)(2,1)S(1)} %span_sum.3), channel_id=1, source_target_pairs={{0,12},{2,14},{4,8},{6,10},{8,4},{10,6},{12,0},{14,2},{1,13},{3,15... | collective-permute-start | bytes 301064 | tf_op jit(solution)/shard_map/ppermute | solution.py:282
  38.0 0.7 %collective-permute-start.16 = (bf16[8,6272]{1,0:T(8,128)(2,1)S(1)}, bf16[8,6272]{1,0:T(8,128)(2,1)S(1)}, u32[]{:S(2)}, u32[]{:S(2)}) collective-permute-start(bf16[8,6272]{1,0:T(8,128)(2,1)S(1)} %span_sum.4), channel_id=1, source_target_pairs={{0,8},{2,10},{4,12},{6,14},{8,0},{10,2},{12,4},{14,6},{1,9},{3,11}... | collective-permute-start | bytes 301064 | tf_op jit(solution)/shard_map/ppermute | solution.py:282
  38.7 0.7 %collective-permute-done.17.refs_1_ = bf16[8,6272]{1,0:T(8,128)(2,1)S(1)} collective-permute-done((bf16[8,6272]{1,0:T(8,128)(2,1)S(1)}, bf16[8,6272]{1,0:T(8,128)(2,1)S(1)}, u32[]{:S(2)}, u32[]{:S(2)}) %collective-permute-start.17) | collective-permute-done | bytes 100384 | tf_op jit(solution)/shard_map/ppermute | solution.py:285
  39.4 1.4 %collective-permute-start.18 = (bf16[8,6272]{1,0:T(8,128)(2,1)S(1)}, bf16[8,6272]{1,0:T(8,128)(2,1)S(1)}, u32[]{:S(2)}, u32[]{:S(2)}) collective-permute-start(bf16[8,6272]{1,0:T(8,128)(2,1)S(1)} %span_sum.5), channel_id=1, source_target_pairs={{0,4},{2,6},{4,0},{6,2},{8,12},{10,14},{12,8},{14,10},{1,5},{3,7},... | collective-permute-start | bytes 301064 | tf_op jit(solution)/shard_map/ppermute | solution.py:282
  40.8 0.2 collective-permute-done.12.refs_1_
  41.0 1.3 %collective-permute-done.14.refs_2_ = bf16[8,6272]{1,0:T(8,128)(2,1)S(1)} collective-permute-done((bf16[8,6272]{1,0:T(8,128)(2,1)S(1)}, bf16[8,6272]{1,0:T(8,128)(2,1)S(1)}, u32[]{:S(2)}, u32[]{:S(2)}) %collective-permute-start.14) | collective-permute-done | bytes 100384 | tf_op jit(solution)/shard_map/ppermute | solution.py:282
  42.3 0.1 combine.2.refs_0_
  42.5 3.7 %collective-permute-done.16.refs_1_ = bf16[8,6272]{1,0:T(8,128)(2,1)S(1)} collective-permute-done((bf16[8,6272]{1,0:T(8,128)(2,1)S(1)}, bf16[8,6272]{1,0:T(8,128)(2,1)S(1)}, u32[]{:S(2)}, u32[]{:S(2)}) %collective-permute-start.16) | collective-permute-done | bytes 100384 | tf_op jit(solution)/shard_map/ppermute | solution.py:282
  46.2 0.8 %combine.3 = bf16[8,7168]{1,0:T(8,128)(2,1)} custom-call(f32[8,1024]{1,0:T(8,128)S(1)} %get-tuple-element.22.sides_ref, f32[8,7168]{1,0:T(8,128)S(1)} %combine.2.refs_0_, bf16[8,6272]{1,0:T(8,128)(2,1)S(1)} %collective-permute-done.16.refs_1_, bf16[8,6272]{1,0:T(8,128)(2,1)S(1)} %collective-permute-done.18.refs_2_), custom_call_target="tpu_custom_call" | custom-call | tf_op jit(solution)/shard_map/combine/pallas_call | solution.py:267
  (47 shorter events, 0.7 us)
Async XLA Ops:
  0.0 20.9 %slice-start.4 = ((s8[14680064]{0:T(1024)(128)(4,1)}), s8[4194304]{0:T(1024)(128)(4,1)S(1)}, s32[]{:S(2)}) async-start(s8[14680064]{0:T(1024)(128)(4,1)} %bitcast.5), calls=%async_computation.4 | async-start | bytes 8388608
  0.0 20.9 %slice-start.8 = ((s8[14680064]{0:T(1024)(128)(4,1)}), s8[4194304]{0:T(1024)(128)(4,1)S(1)}, s32[]{:S(2)}) async-start(s8[14680064]{0:T(1024)(128)(4,1)} %bitcast.7), calls=%async_computation.8 | async-start | bytes 8388608
  0.0 20.9 %slice-start.5 = ((s8[14680064]{0:T(1024)(128)(4,1)}), s8[4194304]{0:T(1024)(128)(4,1)S(1)}, s32[]{:S(2)}) async-start(s8[14680064]{0:T(1024)(128)(4,1)} %bitcast.5), calls=%async_computation.5 | async-start | bytes 8388608
  0.0 20.9 %slice-start.6 = ((s8[14680064]{0:T(1024)(128)(4,1)}), s8[4194304]{0:T(1024)(128)(4,1)S(1)}, s32[]{:S(2)}) async-start(s8[14680064]{0:T(1024)(128)(4,1)} %bitcast.5), calls=%async_computation.6 | async-start | bytes 8388608
  0.0 21.0 %slice-start.7 = ((s8[14680064]{0:T(1024)(128)(4,1)}), s8[2097152]{0:T(1024)(128)(4,1)S(1)}, s32[]{:S(2)}) async-start(s8[14680064]{0:T(1024)(128)(4,1)} %bitcast.5), calls=%async_computation.7 | async-start | bytes 4194304
  0.0 21.0 %slice-start.9 = ((s8[14680064]{0:T(1024)(128)(4,1)}), s8[4194304]{0:T(1024)(128)(4,1)S(1)}, s32[]{:S(2)}) async-start(s8[14680064]{0:T(1024)(128)(4,1)} %bitcast.7), calls=%async_computation.9 | async-start | bytes 8388608
  0.0 21.0 %slice-start.10 = ((s8[14680064]{0:T(1024)(128)(4,1)}), s8[4194304]{0:T(1024)(128)(4,1)S(1)}, s32[]{:S(2)}) async-start(s8[14680064]{0:T(1024)(128)(4,1)} %bitcast.7), calls=%async_computation.10 | async-start | bytes 8388608
  0.0 21.0 %slice-start.11 = ((s8[14680064]{0:T(1024)(128)(4,1)}), s8[2097152]{0:T(1024)(128)(4,1)S(1)}, s32[]{:S(2)}) async-start(s8[14680064]{0:T(1024)(128)(4,1)} %bitcast.7), calls=%async_computation.11 | async-start | bytes 4194304
  1.4 8.8 %collective-permute-start = (bf16[8,6272]{1,0:T(8,128)(2,1)S(1)}, bf16[8,6272]{1,0:T(8,128)(2,1)S(1)}, u32[]{:S(2)}, u32[]{:S(2)}) collective-permute-start(bf16[8,6272]{1,0:T(8,128)(2,1)S(1)} %get-tuple-element.24), channel_id=1, source_target_pairs={{0,12},{2,14},{4,8},{6,10},{8,4},{10,6},{12,0},{14,2},{1,13},{3,15... | collective-permute-start | bytes 301064 | tf_op jit(solution)/shard_map/ppermute | solution.py:282
  6.5 6.1 %collective-permute-start.1 = (bf16[8,6272]{1,0:T(8,128)(2,1)S(1)}, bf16[8,6272]{1,0:T(8,128)(2,1)S(1)}, u32[]{:S(2)}, u32[]{:S(2)}) collective-permute-start(bf16[8,6272]{1,0:T(8,128)(2,1)S(1)} %get-tuple-element.25), channel_id=1, source_target_pairs={{0,4},{2,6},{4,0},{6,2},{8,12},{10,14},{12,8},{14,10},{1,5},{3,7},... | collective-permute-start | bytes 301064 | tf_op jit(solution)/shard_map/ppermute | solution.py:282
  6.5 8.4 %collective-permute-start.2 = (bf16[8,6272]{1,0:T(8,128)(2,1)S(1)}, bf16[8,6272]{1,0:T(8,128)(2,1)S(1)}, u32[]{:S(2)}, u32[]{:S(2)}) collective-permute-start(bf16[8,6272]{1,0:T(8,128)(2,1)S(1)} %get-tuple-element.26), channel_id=1, source_target_pairs={{0,8},{2,10},{4,12},{6,14},{8,0},{10,2},{12,4},{14,6},{1,9},{3,11}... | collective-permute-start | bytes 301064 | tf_op jit(solution)/shard_map/ppermute | solution.py:282
  7.1 9.4 %collective-permute-start.3 = (bf16[8,6272]{1,0:T(8,128)(2,1)S(1)}, bf16[8,6272]{1,0:T(8,128)(2,1)S(1)}, u32[]{:S(2)}, u32[]{:S(2)}) collective-permute-start(bf16[8,6272]{1,0:T(8,128)(2,1)S(1)} %get-tuple-element.23.refs_0_), channel_id=1, source_target_pairs={{0,2},{2,0},{4,6},{6,4},{8,10},{10,8},{12,14},{14,12},{1,3},{3,1},... | collective-permute-start | bytes 301064 | tf_op jit(solution)/shard_map/ppermute | solution.py:285
  10.2 6.4 %collective-permute-start.4 = (bf16[8,6272]{1,0:T(8,128)(2,1)S(1)}, bf16[8,6272]{1,0:T(8,128)(2,1)S(1)}, u32[]{:S(2)}, u32[]{:S(2)}) collective-permute-start(bf16[8,6272]{1,0:T(8,128)(2,1)S(1)} %collective-permute-done.refs_1_), channel_id=1, source_target_pairs={{0,2},{2,0},{4,6},{6,4},{8,10},{10,8},{12,14},{14,12},{1,3},{3,1},... | collective-permute-start | bytes 301064 | tf_op jit(solution)/shard_map/ppermute | solution.py:285
  12.6 5.0 %collective-permute-start.5 = (bf16[8,6272]{1,0:T(8,128)(2,1)S(1)}, bf16[8,6272]{1,0:T(8,128)(2,1)S(1)}, u32[]{:S(2)}, u32[]{:S(2)}) collective-permute-start(bf16[8,6272]{1,0:T(8,128)(2,1)S(1)} %collective-permute-done.1.refs_2_), channel_id=1, source_target_pairs={{0,2},{2,0},{4,6},{6,4},{8,10},{10,8},{12,14},{14,12},{1,3},{3,1},... | collective-permute-start | bytes 301064 | tf_op jit(solution)/shard_map/ppermute | solution.py:285
  14.9 4.6 %collective-permute-start.6 = (bf16[8,6272]{1,0:T(8,128)(2,1)S(1)}, bf16[8,6272]{1,0:T(8,128)(2,1)S(1)}, u32[]{:S(2)}, u32[]{:S(2)}) collective-permute-start(bf16[8,6272]{1,0:T(8,128)(2,1)S(1)} %collective-permute-done.2.refs_3_), channel_id=1, source_target_pairs={{0,2},{2,0},{4,6},{6,4},{8,10},{10,8},{12,14},{14,12},{1,3},{3,1},... | collective-permute-start | bytes 301064 | tf_op jit(solution)/shard_map/ppermute | solution.py:285
  16.5 3.2 %collective-permute-start.7 = (bf16[32,6272]{1,0:T(8,128)(2,1)S(1)}, bf16[32,6272]{1,0:T(8,128)(2,1)S(1)}, u32[]{:S(2)}, u32[]{:S(2)}) collective-permute-start(bf16[32,6272]{1,0:T(8,128)(2,1)S(1)} %stack.3), channel_id=1, source_target_pairs={{0,1},{1,0},{2,3},{3,2},{4,5},{5,4},{6,7},{7,6},{8,9},{9,8},{10,11... | collective-permute-start | bytes 1204232 | tf_op jit(solution)/shard_map/ppermute | solution.py:288
  17.6 2.1 %collective-permute-start.8 = (bf16[24,6272]{1,0:T(8,128)(2,1)S(1)}, bf16[24,6272]{1,0:T(8,128)(2,1)S(1)}, u32[]{:S(2)}, u32[]{:S(2)}) collective-permute-start(bf16[24,6272]{1,0:T(8,128)(2,1)S(1)} %stack.4), channel_id=1, source_target_pairs={{0,1},{1,0},{2,3},{3,2},{4,5},{5,4},{6,7},{7,6},{8,9},{9,8},{10,11... | collective-permute-start | bytes 903176 | tf_op jit(solution)/shard_map/ppermute | solution.py:288
  19.6 1.4 %collective-permute-start.9 = (bf16[8,6272]{1,0:T(8,128)(2,1)S(1)}, bf16[8,6272]{1,0:T(8,128)(2,1)S(1)}, u32[]{:S(2)}, u32[]{:S(2)}) collective-permute-start(bf16[8,6272]{1,0:T(8,128)(2,1)S(1)} %stack.5), channel_id=1, source_target_pairs={{0,1},{1,0},{2,3},{3,2},{4,5},{5,4},{6,7},{7,6},{8,9},{9,8},{10,11... | collective-permute-start | bytes 301064 | tf_op jit(solution)/shard_map/ppermute | solution.py:288
  19.7 5.4 %slice-start = ((s8[14680064]{0:T(1024)(128)(4,1)}), s8[4194304]{0:T(1024)(128)(4,1)S(1)}, s32[]{:S(2)}) async-start(s8[14680064]{0:T(1024)(128)(4,1)} %bitcast.3), calls=%async_computation | async-start | bytes 8388608
  20.1 5.0 %slice-start.1 = ((s8[14680064]{0:T(1024)(128)(4,1)}), s8[4194304]{0:T(1024)(128)(4,1)S(1)}, s32[]{:S(2)}) async-start(s8[14680064]{0:T(1024)(128)(4,1)} %bitcast.3), calls=%async_computation.1 | async-start | bytes 8388608
  20.2 5.0 %slice-start.2 = ((s8[14680064]{0:T(1024)(128)(4,1)}), s8[4194304]{0:T(1024)(128)(4,1)S(1)}, s32[]{:S(2)}) async-start(s8[14680064]{0:T(1024)(128)(4,1)} %bitcast.3), calls=%async_computation.2 | async-start | bytes 8388608
  20.2 5.0 %slice-start.3 = ((s8[14680064]{0:T(1024)(128)(4,1)}), s8[2097152]{0:T(1024)(128)(4,1)S(1)}, s32[]{:S(2)}) async-start(s8[14680064]{0:T(1024)(128)(4,1)} %bitcast.3), calls=%async_computation.3 | async-start | bytes 4194304
  27.4 1.8 %collective-permute-start.11 = (bf16[32,6272]{1,0:T(8,128)(2,1)S(1)}, bf16[32,6272]{1,0:T(8,128)(2,1)S(1)}, u32[]{:S(2)}, u32[]{:S(2)}) collective-permute-start(bf16[32,6272]{1,0:T(8,128)(2,1)S(1)} %get-tuple-element.31), channel_id=1, source_target_pairs={{0,1},{1,0},{2,3},{3,2},{4,5},{5,4},{6,7},{7,6},{8,9},{9,8},{10,11... | collective-permute-start | bytes 1204232 | tf_op jit(solution)/shard_map/ppermute | solution.py:288
  27.9 5.6 %collective-permute-start.10 = (bf16[32,6272]{1,0:T(8,128)(2,1)S(1)}, bf16[32,6272]{1,0:T(8,128)(2,1)S(1)}, u32[]{:S(2)}, u32[]{:S(2)}) collective-permute-start(bf16[32,6272]{1,0:T(8,128)(2,1)S(1)} %get-tuple-element.28), channel_id=1, source_target_pairs={{0,1},{1,0},{2,3},{3,2},{4,5},{5,4},{6,7},{7,6},{8,9},{9,8},{10,11... | collective-permute-start | bytes 1204232 | tf_op jit(solution)/shard_map/ppermute | solution.py:288
  29.4 5.7 %collective-permute-start.13 = (bf16[8,6272]{1,0:T(8,128)(2,1)S(1)}, bf16[8,6272]{1,0:T(8,128)(2,1)S(1)}, u32[]{:S(2)}, u32[]{:S(2)}) collective-permute-start(bf16[8,6272]{1,0:T(8,128)(2,1)S(1)} %get-tuple-element.34), channel_id=1, source_target_pairs={{0,2},{2,0},{4,6},{6,4},{8,10},{10,8},{12,14},{14,12},{1,3},{3,1},... | collective-permute-start | bytes 301064 | tf_op jit(solution)/shard_map/ppermute | solution.py:285
  31.0 7.0 %collective-permute-start.15 = (bf16[8,6272]{1,0:T(8,128)(2,1)S(1)}, bf16[8,6272]{1,0:T(8,128)(2,1)S(1)}, u32[]{:S(2)}, u32[]{:S(2)}) collective-permute-start(bf16[8,6272]{1,0:T(8,128)(2,1)S(1)} %get-tuple-element.36), channel_id=1, source_target_pairs={{0,2},{2,0},{4,6},{6,4},{8,10},{10,8},{12,14},{14,12},{1,3},{3,1},... | collective-permute-start | bytes 301064 | tf_op jit(solution)/shard_map/ppermute | solution.py:285
  31.5 7.9 %collective-permute-start.17 = (bf16[8,6272]{1,0:T(8,128)(2,1)S(1)}, bf16[8,6272]{1,0:T(8,128)(2,1)S(1)}, u32[]{:S(2)}, u32[]{:S(2)}) collective-permute-start(bf16[8,6272]{1,0:T(8,128)(2,1)S(1)} %get-tuple-element.38), channel_id=1, source_target_pairs={{0,2},{2,0},{4,6},{6,4},{8,10},{10,8},{12,14},{14,12},{1,3},{3,1},... | collective-permute-start | bytes 301064 | tf_op jit(solution)/shard_map/ppermute | solution.py:285
  33.0 8.0 %collective-permute-start.12 = (bf16[8,6272]{1,0:T(8,128)(2,1)S(1)}, bf16[8,6272]{1,0:T(8,128)(2,1)S(1)}, u32[]{:S(2)}, u32[]{:S(2)}) collective-permute-start(bf16[8,6272]{1,0:T(8,128)(2,1)S(1)} %get-tuple-element.32), channel_id=1, source_target_pairs={{0,2},{2,0},{4,6},{6,4},{8,10},{10,8},{12,14},{14,12},{1,3},{3,1},... | collective-permute-start | bytes 301064 | tf_op jit(solution)/shard_map/ppermute | solution.py:285
  35.1 7.2 %collective-permute-start.14 = (bf16[8,6272]{1,0:T(8,128)(2,1)S(1)}, bf16[8,6272]{1,0:T(8,128)(2,1)S(1)}, u32[]{:S(2)}, u32[]{:S(2)}) collective-permute-start(bf16[8,6272]{1,0:T(8,128)(2,1)S(1)} %span_sum.3), channel_id=1, source_target_pairs={{0,12},{2,14},{4,8},{6,10},{8,4},{10,6},{12,0},{14,2},{1,13},{3,15... | collective-permute-start | bytes 301064 | tf_op jit(solution)/shard_map/ppermute | solution.py:282
  38.0 8.2 %collective-permute-start.16 = (bf16[8,6272]{1,0:T(8,128)(2,1)S(1)}, bf16[8,6272]{1,0:T(8,128)(2,1)S(1)}, u32[]{:S(2)}, u32[]{:S(2)}) collective-permute-start(bf16[8,6272]{1,0:T(8,128)(2,1)S(1)} %span_sum.4), channel_id=1, source_target_pairs={{0,8},{2,10},{4,12},{6,14},{8,0},{10,2},{12,4},{14,6},{1,9},{3,11}... | collective-permute-start | bytes 301064 | tf_op jit(solution)/shard_map/ppermute | solution.py:282
  39.4 6.8 %collective-permute-start.18 = (bf16[8,6272]{1,0:T(8,128)(2,1)S(1)}, bf16[8,6272]{1,0:T(8,128)(2,1)S(1)}, u32[]{:S(2)}, u32[]{:S(2)}) collective-permute-start(bf16[8,6272]{1,0:T(8,128)(2,1)S(1)} %span_sum.5), channel_id=1, source_target_pairs={{0,4},{2,6},{4,0},{6,2},{8,12},{10,14},{12,8},{14,10},{1,5},{3,7},... | collective-permute-start | bytes 301064 | tf_op jit(solution)/shard_map/ppermute | solution.py:282

commit v14 on v12

--- a/solution.py
+++ b/solution.py
@@ -121,8 +121,8 @@
     )(first, last, in_vmem(gate_weight), in_vmem(up_weight))
 
 
-def down_kernel(rows, hidden_ref, down_ref, *outs):
-    count, width = outs[0].shape
+def down_kernel(rows, sources, hidden_ref, down_ref, *outs):
+    width = outs[0].shape[1]
     tail = down_ref.shape[1] // rows
     blocks = (hidden_ref.shape[0] // rows, rows, tail)
     last = lax.broadcasted_iota(jnp.int32, blocks, 1) == rows - 1
@@ -135,45 +135,53 @@
             ends = pieces.pop(i + 1)
         for j, value in pieces.items():
             value = jnp.where(last, jnp.broadcast_to(ends[:, j:j + 1, :], blocks), value).reshape(blocks[0] * rows, tail)
-            for k, ref in enumerate(outs):
-                ref[:, j * tail:(j + 1) * tail] = value[k * count:(k + 1) * count].astype(ref.dtype)
-
-
-def down(hidden, down_weight, span, pair, rows):
+            for ref, starts in zip(outs, sources):
+                taken = [value[start:start + rows] for start in starts]
+                taken = jnp.concatenate(taken, axis=0) if len(taken) > 1 else taken[0]
+                ref[:, j * tail:(j + 1) * tail] = taken.astype(ref.dtype)
+
+
+def down(hidden, down_weight, span, pair, rows, first):
     total, units = hidden.shape
     width = down_weight.shape[1] // rows * (rows - 1)
-    shape = (total // (span * pair), width)
+    part = total // (span * pair)
+    places = [first] + [i for i in range(part // rows) if i != first]
+
+    def starts(p, t, chosen):
+        return [(p * span + t) * part + i * rows for i in chosen]
+
+    sources = [starts(0, t, range(part // rows)) for t in range(span)]
+    for p in range(1, pair):
+        sources.append([x for t in range(1, span) for x in starts(p, t, places[:1])])
+        sources.append([x for t in range(1, span) for x in starts(p, t, places[1:])] + starts(p, 0, range(part // rows)))
     outs = pl.pallas_call(
-        functools.partial(down_kernel, rows),
+        functools.partial(down_kernel, rows, sources),
         in_specs=[pl.BlockSpec(memory_space=pltpu.VMEM)] * 2,
-        out_shape=[jax.ShapeDtypeStruct(shape, jnp.bfloat16 if p else jnp.float32) for p in range(pair) for _ in range(span)],
+        out_shape=[jax.ShapeDtypeStruct((rows * len(x), width), jnp.float32 if i < span else jnp.bfloat16) for i, x in enumerate(sources)],
         compiler_params=params(total),
         cost_estimate=cost(2 * total * width * units),
         name="down",
     )(hidden, in_vmem(down_weight))
-    return [outs[t::span] for t in range(span)]
-
-
-def pair_sum_kernel(count, places, *refs):
-    outs = refs[-len(places):]
+    return outs[:span], outs[span::2], outs[span + 1::2]
+
+
+def pair_sum_kernel(places, offset, keep_ref, *refs):
+    received, outs = refs[:-len(places)], refs[-len(places):]
     rows = outs[0].shape[0]
-    for place, out_ref in zip(places, outs):
-        part = slice(place * rows, (place + 1) * rows)
-        value = refs[0][part, :]
-        for ref in refs[1:count]:
-            value += ref[part, :].astype(jnp.float32)
+    for i, (place, out_ref) in enumerate(zip(places, outs), offset):
+        value = keep_ref[place * rows:(place + 1) * rows, :]
+        for ref in received:
+            value += ref[i * rows:(i + 1) * rows, :].astype(jnp.float32)
         out_ref[...] = value.astype(out_ref.dtype)
 
 
-def pair_sum(arrays, rows, dtype, places, after=()):
-    width = arrays[0].shape[1]
-    return pl.pallas_call(
-        functools.partial(pair_sum_kernel, len(arrays), places),
-        in_specs=[pl.BlockSpec(memory_space=pltpu.VMEM)] * len(arrays) + [pl.BlockSpec(memory_space=pl.ANY)] * len(after),
-        out_shape=[jax.ShapeDtypeStruct((rows, width), dtype)] * len(places),
+def pair_sum(keep, received, rows, dtype, places, offset):
+    return pl.pallas_call(
+        functools.partial(pair_sum_kernel, places, offset),
+        out_shape=[jax.ShapeDtypeStruct((rows, keep.shape[1]), dtype)] * len(places),
         compiler_params=params(),
         name="pair_sum",
-    )(*arrays, *after)
+    )(keep, *received)
 
 
 def span_sum_kernel(*refs):
@@ -239,34 +247,55 @@
     )(own_expert, *[pltpu.with_memory_space_constraint(a, pltpu.HBM) for a in inputs])
 
 
-def combine_kernel(base, places, counts, sides_ref, *refs):
-    *refs, out_ref = refs
+def combine_kernel(base, places, counts, parts, sides_ref, *refs):
+    if parts:
+        *refs, out_hbm, out_ref, semaphores = refs
+    else:
+        *refs, out_ref = refs
     rows, width = out_ref.shape
     tail = width // rows
     row = lax.broadcasted_iota(jnp.int32, (rows, tail), 0)
-    value = None
-    for ref in refs[:base]:
-        value = ref[...]
-    refs = refs[base:]
+    first, groups = refs[:base], refs[base:]
+    terms = []
     for s, count in zip(places, counts):
-        packed = sum([ref[...].astype(jnp.float32) for ref in refs[1:count]], refs[0][...].astype(jnp.float32))
-        refs = refs[count:]
+        group, groups = groups[:count], groups[count:]
+        packed = sum([ref[...].astype(jnp.float32) for ref in group[1:]], group[0][...].astype(jnp.float32))
         coeff = sides_ref[:, s * LANES:s * LANES + 1]
         shifted = sides_ref[:, (EXPERTS + s) * LANES:(EXPERTS + s) * LANES + 1] > 0.5
-        ends = jnp.zeros((rows, tail), jnp.float32)
-        for i in range(rows - 1):
-            ends = jnp.where(row == i, jnp.broadcast_to(packed[rows - 1:, i * tail:(i + 1) * tail], (rows, tail)), ends)
-        whole = jnp.concatenate([packed, ends], axis=1)
-        term = coeff * jnp.where(shifted, pltpu.roll(whole, 1, 0), whole)
-        value = term if value is None else value + term
-    out_ref[...] = value.astype(out_ref.dtype)
-
-
-def combine(sides, base, places, groups, width, dtype):
+        terms.append((packed, coeff, shifted))
+    copies = []
+    for i in range(rows):
+        columns = slice(i * tail, (i + 1) * tail)
+        value = None
+        for ref in first:
+            value = ref[:, columns]
+        for packed, coeff, shifted in terms:
+            if i < rows - 1:
+                piece = packed[:, columns]
+            else:
+                piece = jnp.zeros((rows, tail), jnp.float32)
+                for j in range(rows - 1):
+                    moved = jnp.broadcast_to(packed[rows - 1:, j * tail:(j + 1) * tail], (rows, tail))
+                    piece = jnp.where(row == j, moved, piece)
+            term = coeff * jnp.where(shifted, pltpu.roll(piece, 1, 0), piece)
+            value = term if value is None else value + term
+        out_ref[:, columns] = value.astype(out_ref.dtype)
+        if parts and (i + 1) % (rows // parts) == 0:
+            done = slice((len(copies) * (rows // parts)) * tail, (i + 1) * tail)
+            copies.append(pltpu.make_async_copy(out_ref.at[:, done], out_hbm.at[:, done], semaphores.at[len(copies)]))
+            copies[-1].start()
+    for copy in copies:
+        copy.wait()
+
+
+def combine(sides, base, places, groups, width, dtype, parts=0):
     arrays = [a for group in groups for a in group]
-    return pl.pallas_call(
-        functools.partial(combine_kernel, len(base), tuple(places), tuple(len(g) for g in groups)),
-        out_shape=jax.ShapeDtypeStruct((arrays[0].shape[0], width), dtype),
+    out_shape = jax.ShapeDtypeStruct((arrays[0].shape[0], width), dtype)
+    return pl.pallas_call(
+        functools.partial(combine_kernel, len(base), tuple(places), tuple(len(g) for g in groups), parts),
+        out_shape=out_shape,
+        out_specs=pl.BlockSpec(memory_space=pl.ANY if parts else pltpu.VMEM),
+        scratch_shapes=[pltpu.VMEM(out_shape.shape, dtype), pltpu.SemaphoreType.DMA((parts,))] if parts else [],
         compiler_params=params(),
         name="combine",
     )(sides, *base, *arrays)
@@ -299,20 +328,28 @@
     first = unpack([b for part in parts for b in part] + others, rows, width)
     hidden = gate_up(first, last, gate_weight, up_weight)
 
-    def paired(keep, sends):
-        return [keep] + [over_pair(b, -p) for p, b in enumerate(sends, 1)]
-
-    sums = [[] for _ in range(EXPERTS)]
-    for t, (keep, *sends) in enumerate(down(hidden, down_weight, span, pair, rows)):
-        arrays = paired(keep, sends)
-        blocks = pair_sum(arrays, rows, jnp.bfloat16 if t else jnp.float32, range(EXPERTS))
-        for s, block in zip(BLOCK_ORDER, blocks):
-            sums[s].append(over_span(block, -t) if t else block)
+    first = BLOCK_ORDER.index(RETURN_ORDER[0])
+    rest = [i for i in range(EXPERTS) if i != first]
+    keeps, firsts, others = down(hidden, down_weight, span, pair, rows, first)
+    received = [over_pair(b, -p) for p, b in enumerate(firsts, 1)]
+    sums = {s: [] for s in range(EXPERTS)}
+    for t in range(1, span):
+        block, = pair_sum(keeps[t], received, rows, jnp.bfloat16, [first], t - 1)
+        sums[RETURN_ORDER[0]].append(over_span(block, -t))
+        after = [block]
+    received = [over_pair(stack([b], after), -p) for p, b in enumerate(others, 1)]
+    for t in range(1, span):
+        blocks = pair_sum(keeps[t], received, rows, jnp.bfloat16, rest, (t - 1) * len(rest))
+        for place, block in zip(rest, blocks):
+            sums[BLOCK_ORDER[place]].append(over_span(block, -t))
+    own = pair_sum(keeps[0], received, rows, jnp.float32, list(range(EXPERTS)), (span - 1) * len(rest))
+    for place, block in enumerate(own):
+        sums[BLOCK_ORDER[place]].insert(0, block)
 
     returned = {s: over_experts(span_sum(sums[s]), s) for s in RETURN_ORDER}
-    first, *later = RETURN_ORDER
-    early = combine(sides, [], [0, first], [sums[0], [returned[first]]], width, jnp.float32)
-    return combine(sides, [early], later, [[returned[s]] for s in later], width, jnp.bfloat16)
+    far, *later = RETURN_ORDER
+    early = combine(sides, [], [0, far], [sums[0], [returned[far]]], width, jnp.float32)
+    return combine(sides, [early], later, [[returned[s]] for s in later], width, jnp.bfloat16, 2)
 
 
 def solution(mesh):

time: 47.1 us -> 47.3 us (level)
  starting transfers between devices: 22 us -> 23.2 us
  waiting for transfers between devices: 15.2 us -> 14.3 us
    ppermute x8, waiting for transfers between devices: 5.28 us -> 3.78 us  [over_span(): lax.ppermute(value, 'attn', [(i, i // span * span + (i + shift) % span) f...]
    ppermute x8, starting transfers between devices: 10.5 us -> 11.6 us  [over_span(): lax.ppermute(value, 'attn', [(i, i // span * span + (i + shift) % span) f...]
    ppermute x6, waiting for transfers between devices: 7.93 us -> 8.51 us  [over_experts(): lax.ppermute(value, 'attn', [(i, (i // span ^ other) * span + i % span) f...]
    pallas_call x3 -> x4, Pallas kernels: 2.38 us -> 2.36 us  [the longest x1 2.21 us: down(): pl.pallas_call(functools.partial(down_kernel, rows, sources), in_specs=[p...]
where the time goes in v14:
time: 47.3 us; the launch traced here: 47.2 us
  starting transfers between devices  23.2 us (49%)
  waiting for transfers between devices  14.3 us (30%)
  Pallas kernels  9.28 us (20%)
    ppermute x8, starting transfers between devices, over_span(): lax.ppermute(value, 'attn', [(i, i // span * span + (i + shift) % span) f...  11.6 us
    ppermute x6, starting transfers between devices, over_experts(): lax.ppermute(value, 'attn', [(i, (i // span ^ other) * span + i % span) f...  10.6 us
    ppermute x6, waiting for transfers between devices, over_experts(): lax.ppermute(value, 'attn', [(i, (i // span ^ other) * span + i % span) f...  8.51 us
    pallas_call x1, Pallas kernels, gate_up(): pl.pallas_call(functools.partial(gate_up_kernel, block_of(units, N_BLOCK)...  4.09 us
    ppermute x8, waiting for transfers between devices, over_span(): lax.ppermute(value, 'attn', [(i, i // span * span + (i + shift) % span) f...  3.78 us
    pallas_call x1, Pallas kernels, down(): pl.pallas_call(functools.partial(down_kernel, rows, sources), in_specs=[p...  2.21 us
    ppermute x5, waiting for transfers between devices, over_pair(): lax.ppermute(value, 'ffn', [(i, (i + shift) % pair) for i in range(pair)])  2 us
    pallas_call x1, Pallas kernels, pack(): pl.pallas_call(pack_kernel, in_specs=[pl.BlockSpec(memory_space=pltpu.SME...  1.3 us
  transfers between devices with their start and end apart: 19, of which 12 were waited for; matrix products, arithmetic and copies ran while one was open for 0% of the time, Pallas kernels for 2%

profile of v14, /device:TPU:0, one launch (start us, length us, event | category | flops | bytes accessed | tf_op | source)
XLA Modules:
  0.0 47.2 jit_solution(17060630949701796498)
XLA Ops:
  0.0 1.3 %pack.1 = (f32[8,1024]{1,0:T(8,128)S(1)}, bf16[8,6272]{1,0:T(8,128)(2,1)S(1)}, bf16[8,6272]{1,0:T(8,128)(2,1)S(1)}, bf16[8,6272]{1,0:T(8,128)(2,1)S(1)}, bf16[8,6272]{1,0:T(8,128)(2,1)S(1)}) custom-call(s32[1]{0:T(128)} %bitcast.own_expert, bf16[8,7168]{1,0:T(8,128)(2,1)} %tokens_hbm.1, s32[3,8]{1,0:T(4,128)} %bitcast.9, f32[3,8]{1,0:T(4,128)} %bitcast.10), custom_call_target="tpu_custom_call" | custom-call | flops 20000000000 | tf_op jit(solution)/shard_map/pack/pallas_call | solution.py:239
  1.4 5.1 %collective-permute-start = (bf16[8,6272]{1,0:T(8,128)(2,1)S(1)}, bf16[8,6272]{1,0:T(8,128)(2,1)S(1)}, u32[]{:S(2)}, u32[]{:S(2)}) collective-permute-start(bf16[8,6272]{1,0:T(8,128)(2,1)S(1)} %get-tuple-element.23), channel_id=1, source_target_pairs={{0,12},{2,14},{4,8},{6,10},{8,4},{10,6},{12,0},{14,2},{1,13},{3,15... | collective-permute-start | bytes 301064 | tf_op jit(solution)/shard_map/ppermute | solution.py:311
  6.5 0.6 %collective-permute-start.2 = (bf16[8,6272]{1,0:T(8,128)(2,1)S(1)}, bf16[8,6272]{1,0:T(8,128)(2,1)S(1)}, u32[]{:S(2)}, u32[]{:S(2)}) collective-permute-start(bf16[8,6272]{1,0:T(8,128)(2,1)S(1)} %get-tuple-element.25), channel_id=1, source_target_pairs={{0,8},{2,10},{4,12},{6,14},{8,0},{10,2},{12,4},{14,6},{1,9},{3,11}... | collective-permute-start | bytes 301064 | tf_op jit(solution)/shard_map/ppermute | solution.py:311
  7.1 1.7 %collective-permute-start.3 = (bf16[8,6272]{1,0:T(8,128)(2,1)S(1)}, bf16[8,6272]{1,0:T(8,128)(2,1)S(1)}, u32[]{:S(2)}, u32[]{:S(2)}) collective-permute-start(bf16[8,6272]{1,0:T(8,128)(2,1)S(1)} %get-tuple-element.22.refs_0_), channel_id=1, source_target_pairs={{0,2},{2,0},{4,6},{6,4},{8,10},{10,8},{12,14},{14,12},{1,3},{3,1},... | collective-permute-start | bytes 301064 | tf_op jit(solution)/shard_map/ppermute | solution.py:314
  8.8 1.4 %collective-permute-done.refs_1_ = bf16[8,6272]{1,0:T(8,128)(2,1)S(1)} collective-permute-done((bf16[8,6272]{1,0:T(8,128)(2,1)S(1)}, bf16[8,6272]{1,0:T(8,128)(2,1)S(1)}, u32[]{:S(2)}, u32[]{:S(2)}) %collective-permute-start) | collective-permute-done | bytes 100384 | tf_op jit(solution)/shard_map/ppermute | solution.py:311
  10.2 1.7 %collective-permute-start.4 = (bf16[8,6272]{1,0:T(8,128)(2,1)S(1)}, bf16[8,6272]{1,0:T(8,128)(2,1)S(1)}, u32[]{:S(2)}, u32[]{:S(2)}) collective-permute-start(bf16[8,6272]{1,0:T(8,128)(2,1)S(1)} %collective-permute-done.refs_1_), channel_id=1, source_target_pairs={{0,2},{2,0},{4,6},{6,4},{8,10},{10,8},{12,14},{14,12},{1,3},{3,1},... | collective-permute-start | bytes 301064 | tf_op jit(solution)/shard_map/ppermute | solution.py:314
  11.9 0.7 %collective-permute-done.1.refs_2_ = bf16[8,6272]{1,0:T(8,128)(2,1)S(1)} collective-permute-done((bf16[8,6272]{1,0:T(8,128)(2,1)S(1)}, bf16[8,6272]{1,0:T(8,128)(2,1)S(1)}, u32[]{:S(2)}, u32[]{:S(2)}) %collective-permute-start.1) | collective-permute-done | bytes 100384 | tf_op jit(solution)/shard_map/ppermute | solution.py:311
  12.6 1.5 %collective-permute-start.5 = (bf16[8,6272]{1,0:T(8,128)(2,1)S(1)}, bf16[8,6272]{1,0:T(8,128)(2,1)S(1)}, u32[]{:S(2)}, u32[]{:S(2)}) collective-permute-start(bf16[8,6272]{1,0:T(8,128)(2,1)S(1)} %collective-permute-done.1.refs_2_), channel_id=1, source_target_pairs={{0,2},{2,0},{4,6},{6,4},{8,10},{10,8},{12,14},{14,12},{1,3},{3,1},... | collective-permute-start | bytes 301064 | tf_op jit(solution)/shard_map/ppermute | solution.py:314
  14.1 0.8 %collective-permute-done.2.refs_3_ = bf16[8,6272]{1,0:T(8,128)(2,1)S(1)} collective-permute-done((bf16[8,6272]{1,0:T(8,128)(2,1)S(1)}, bf16[8,6272]{1,0:T(8,128)(2,1)S(1)}, u32[]{:S(2)}, u32[]{:S(2)}) %collective-permute-start.2) | collective-permute-done | bytes 100384 | tf_op jit(solution)/shard_map/ppermute | solution.py:311
  14.9 1.5 %collective-permute-start.6 = (bf16[8,6272]{1,0:T(8,128)(2,1)S(1)}, bf16[8,6272]{1,0:T(8,128)(2,1)S(1)}, u32[]{:S(2)}, u32[]{:S(2)}) collective-permute-start(bf16[8,6272]{1,0:T(8,128)(2,1)S(1)} %collective-permute-done.2.refs_3_), channel_id=1, source_target_pairs={{0,2},{2,0},{4,6},{6,4},{8,10},{10,8},{12,14},{14,12},{1,3},{3,1},... | collective-permute-start | bytes 301064 | tf_op jit(solution)/shard_map/ppermute | solution.py:314
  16.6 1.0 %collective-permute-done.5.refs_2_.refs_6_ = bf16[8,6272]{1,0:T(8,128)(2,1)S(1)} collective-permute-done((bf16[8,6272]{1,0:T(8,128)(2,1)S(1)}, bf16[8,6272]{1,0:T(8,128)(2,1)S(1)}, u32[]{:S(2)}, u32[]{:S(2)}) %collective-permute-start.5) | collective-permute-done | bytes 100384 | tf_op jit(solution)/shard_map/ppermute | solution.py:314
  17.7 1.9 %collective-permute-done.6.refs_7_.refs_0_ = bf16[8,6272]{1,0:T(8,128)(2,1)S(1)} collective-permute-done((bf16[8,6272]{1,0:T(8,128)(2,1)S(1)}, bf16[8,6272]{1,0:T(8,128)(2,1)S(1)}, u32[]{:S(2)}, u32[]{:S(2)}) %collective-permute-start.6) | collective-permute-done | bytes 100384 | tf_op jit(solution)/shard_map/ppermute | solution.py:314
  19.7 0.5 unpack.1.first_ref
  20.2 0.8 %collective-permute-done.9.last_ref = bf16[8,6272]{1,0:T(8,128)(2,1)S(1)} collective-permute-done((bf16[8,6272]{1,0:T(8,128)(2,1)S(1)}, bf16[8,6272]{1,0:T(8,128)(2,1)S(1)}, u32[]{:S(2)}, u32[]{:S(2)}) %collective-permute-start.9) | collective-permute-done | bytes 100384 | tf_op jit(solution)/shard_map/ppermute | solution.py:317
  21.0 4.1 %gate_up.1.hidden_ref = bf16[128,1024]{1,0:T(8,128)(2,1)S(1)} custom-call(bf16[120,7168]{1,0:T(8,128)(2,1)S(1)} %unpack.1.first_ref, bf16[8,6272]{1,0:T(8,128)(2,1)S(1)} %collective-permute-done.9.last_ref, bf16[7168,1024]{1,0:T(8,128)(2,1)S(1)} %bitcast.6, bf16[7168,1024]{1,0:T(8,128)(2,1)S(1)} %bitcast.8), custom_call_target="tpu_custom_call" | custom-call | flops 3758096384 | tf_op jit(solution)/shard_map/gate_up/pallas_call | solution.py:113
  25.2 2.2 %down.1 = (f32[32,6272]{1,0:T(8,128)S(1)}, f32[32,6272]{1,0:T(8,128)S(1)}, bf16[8,6272]{1,0:T(8,128)(2,1)S(1)}, bf16[56,6272]{1,0:T(8,128)(2,1)S(1)}) custom-call(bf16[128,1024]{1,0:T(8,128)(2,1)S(1)} %gate_up.1.hidden_ref, bf16[1024,7168]{1,0:T(8,128)(2,1)S(1)} %bitcast.4), custom_call_target="tpu_custom_call" | custom-call | flops 1644167168 | tf_op jit(solution)/shard_map/down/pallas_call | solution.py:157
  27.4 0.4 collective-permute-start.10
  27.8 0.9 %collective-permute-done.10.refs_0_ = bf16[8,6272]{1,0:T(8,128)(2,1)S(1)} collective-permute-done((bf16[8,6272]{1,0:T(8,128)(2,1)S(1)}, bf16[8,6272]{1,0:T(8,128)(2,1)S(1)}, u32[]{:S(2)}, u32[]{:S(2)}) %collective-permute-start.10) | collective-permute-done | bytes 100384 | tf_op jit(solution)/shard_map/ppermute | solution.py:317
  28.9 0.4 collective-permute-start.11
  29.3 1.5 %collective-permute-start.13 = (bf16[8,6272]{1,0:T(8,128)(2,1)S(1)}, bf16[8,6272]{1,0:T(8,128)(2,1)S(1)}, u32[]{:S(2)}, u32[]{:S(2)}) collective-permute-start(bf16[8,6272]{1,0:T(8,128)(2,1)S(1)} %pair_sum.3.refs_1_), channel_id=1, source_target_pairs={{0,2},{2,0},{4,6},{6,4},{8,10},{10,8},{12,14},{14,12},{1,3},{3,1},... | collective-permute-start | bytes 301064 | tf_op jit(solution)/shard_map/ppermute | solution.py:314
  30.8 0.3 collective-permute-done.11.refs_0_
  31.1 1.6 %collective-permute-start.15 = (bf16[8,6272]{1,0:T(8,128)(2,1)S(1)}, bf16[8,6272]{1,0:T(8,128)(2,1)S(1)}, u32[]{:S(2)}, u32[]{:S(2)}) collective-permute-start(bf16[8,6272]{1,0:T(8,128)(2,1)S(1)} %get-tuple-element.34), channel_id=1, source_target_pairs={{0,2},{2,0},{4,6},{6,4},{8,10},{10,8},{12,14},{14,12},{1,3},{3,1},... | collective-permute-start | bytes 301064 | tf_op jit(solution)/shard_map/ppermute | solution.py:314
  32.7 0.5 %collective-permute-start.17 = (bf16[8,6272]{1,0:T(8,128)(2,1)S(1)}, bf16[8,6272]{1,0:T(8,128)(2,1)S(1)}, u32[]{:S(2)}, u32[]{:S(2)}) collective-permute-start(bf16[8,6272]{1,0:T(8,128)(2,1)S(1)} %get-tuple-element.36), channel_id=1, source_target_pairs={{0,2},{2,0},{4,6},{6,4},{8,10},{10,8},{12,14},{14,12},{1,3},{3,1},... | collective-permute-start | bytes 301064 | tf_op jit(solution)/shard_map/ppermute | solution.py:314
  33.3 1.5 %collective-permute-start.12 = (bf16[8,6272]{1,0:T(8,128)(2,1)S(1)}, bf16[8,6272]{1,0:T(8,128)(2,1)S(1)}, u32[]{:S(2)}, u32[]{:S(2)}) collective-permute-start(bf16[8,6272]{1,0:T(8,128)(2,1)S(1)} %get-tuple-element.31), channel_id=1, source_target_pairs={{0,2},{2,0},{4,6},{6,4},{8,10},{10,8},{12,14},{14,12},{1,3},{3,1},... | collective-permute-start | bytes 301064 | tf_op jit(solution)/shard_map/ppermute | solution.py:314
  34.9 2.6 %collective-permute-start.14 = (bf16[8,6272]{1,0:T(8,128)(2,1)S(1)}, bf16[8,6272]{1,0:T(8,128)(2,1)S(1)}, u32[]{:S(2)}, u32[]{:S(2)}) collective-permute-start(bf16[8,6272]{1,0:T(8,128)(2,1)S(1)} %span_sum.3), channel_id=1, source_target_pairs={{0,12},{2,14},{4,8},{6,10},{8,4},{10,6},{12,0},{14,2},{1,13},{3,15... | collective-permute-start | bytes 301064 | tf_op jit(solution)/shard_map/ppermute | solution.py:311
  37.5 0.8 %collective-permute-start.16 = (bf16[8,6272]{1,0:T(8,128)(2,1)S(1)}, bf16[8,6272]{1,0:T(8,128)(2,1)S(1)}, u32[]{:S(2)}, u32[]{:S(2)}) collective-permute-start(bf16[8,6272]{1,0:T(8,128)(2,1)S(1)} %span_sum.4), channel_id=1, source_target_pairs={{0,8},{2,10},{4,12},{6,14},{8,0},{10,2},{12,4},{14,6},{1,9},{3,11}... | collective-permute-start | bytes 301064 | tf_op jit(solution)/shard_map/ppermute | solution.py:311
  38.4 0.7 %collective-permute-done.17.refs_1_ = bf16[8,6272]{1,0:T(8,128)(2,1)S(1)} collective-permute-done((bf16[8,6272]{1,0:T(8,128)(2,1)S(1)}, bf16[8,6272]{1,0:T(8,128)(2,1)S(1)}, u32[]{:S(2)}, u32[]{:S(2)}) %collective-permute-start.17) | collective-permute-done | bytes 100384 | tf_op jit(solution)/shard_map/ppermute | solution.py:314
  39.1 1.4 %collective-permute-start.18 = (bf16[8,6272]{1,0:T(8,128)(2,1)S(1)}, bf16[8,6272]{1,0:T(8,128)(2,1)S(1)}, u32[]{:S(2)}, u32[]{:S(2)}) collective-permute-start(bf16[8,6272]{1,0:T(8,128)(2,1)S(1)} %span_sum.5), channel_id=1, source_target_pairs={{0,4},{2,6},{4,0},{6,2},{8,12},{10,14},{12,8},{14,10},{1,5},{3,7},... | collective-permute-start | bytes 301064 | tf_op jit(solution)/shard_map/ppermute | solution.py:311
  40.4 0.2 collective-permute-done.12.refs_1_
  40.6 1.8 %collective-permute-done.14.refs_2_ = bf16[8,6272]{1,0:T(8,128)(2,1)S(1)} collective-permute-done((bf16[8,6272]{1,0:T(8,128)(2,1)S(1)}, bf16[8,6272]{1,0:T(8,128)(2,1)S(1)}, u32[]{:S(2)}, u32[]{:S(2)}) %collective-permute-start.14) | collective-permute-done | bytes 100384 | tf_op jit(solution)/shard_map/ppermute | solution.py:311
  42.6 3.8 %collective-permute-done.16.refs_1_ = bf16[8,6272]{1,0:T(8,128)(2,1)S(1)} collective-permute-done((bf16[8,6272]{1,0:T(8,128)(2,1)S(1)}, bf16[8,6272]{1,0:T(8,128)(2,1)S(1)}, u32[]{:S(2)}, u32[]{:S(2)}) %collective-permute-start.16) | collective-permute-done | bytes 100384 | tf_op jit(solution)/shard_map/ppermute | solution.py:311
  46.4 0.8 %combine.3 = bf16[8,7168]{1,0:T(8,128)(2,1)} custom-call(f32[8,1024]{1,0:T(8,128)S(1)} %get-tuple-element.21.sides_ref, f32[8,7168]{1,0:T(8,128)S(1)} %combine.2.refs_0_, bf16[8,6272]{1,0:T(8,128)(2,1)S(1)} %collective-permute-done.16.refs_1_, bf16[8,6272]{1,0:T(8,128)(2,1)S(1)} %collective-permute-done.18.refs_2_), custom_call_target="tpu_custom_call" | custom-call | tf_op jit(solution)/shard_map/combine/pallas_call | solution.py:294
  (49 shorter events, 0.7 us)
Async XLA Ops:
  0.0 20.9 %slice-start.4 = ((s8[14680064]{0:T(1024)(128)(4,1)}), s8[4194304]{0:T(1024)(128)(4,1)S(1)}, s32[]{:S(2)}) async-start(s8[14680064]{0:T(1024)(128)(4,1)} %bitcast.5), calls=%async_computation.4 | async-start | bytes 8388608
  0.0 20.9 %slice-start.8 = ((s8[14680064]{0:T(1024)(128)(4,1)}), s8[4194304]{0:T(1024)(128)(4,1)S(1)}, s32[]{:S(2)}) async-start(s8[14680064]{0:T(1024)(128)(4,1)} %bitcast.7), calls=%async_computation.8 | async-start | bytes 8388608
  0.0 20.9 %slice-start.5 = ((s8[14680064]{0:T(1024)(128)(4,1)}), s8[4194304]{0:T(1024)(128)(4,1)S(1)}, s32[]{:S(2)}) async-start(s8[14680064]{0:T(1024)(128)(4,1)} %bitcast.5), calls=%async_computation.5 | async-start | bytes 8388608
  0.0 20.9 %slice-start.6 = ((s8[14680064]{0:T(1024)(128)(4,1)}), s8[4194304]{0:T(1024)(128)(4,1)S(1)}, s32[]{:S(2)}) async-start(s8[14680064]{0:T(1024)(128)(4,1)} %bitcast.5), calls=%async_computation.6 | async-start | bytes 8388608
  0.0 21.0 %slice-start.7 = ((s8[14680064]{0:T(1024)(128)(4,1)}), s8[2097152]{0:T(1024)(128)(4,1)S(1)}, s32[]{:S(2)}) async-start(s8[14680064]{0:T(1024)(128)(4,1)} %bitcast.5), calls=%async_computation.7 | async-start | bytes 4194304
  0.0 21.0 %slice-start.9 = ((s8[14680064]{0:T(1024)(128)(4,1)}), s8[4194304]{0:T(1024)(128)(4,1)S(1)}, s32[]{:S(2)}) async-start(s8[14680064]{0:T(1024)(128)(4,1)} %bitcast.7), calls=%async_computation.9 | async-start | bytes 8388608
  0.0 21.0 %slice-start.10 = ((s8[14680064]{0:T(1024)(128)(4,1)}), s8[4194304]{0:T(1024)(128)(4,1)S(1)}, s32[]{:S(2)}) async-start(s8[14680064]{0:T(1024)(128)(4,1)} %bitcast.7), calls=%async_computation.10 | async-start | bytes 8388608
  0.0 21.0 %slice-start.11 = ((s8[14680064]{0:T(1024)(128)(4,1)}), s8[2097152]{0:T(1024)(128)(4,1)S(1)}, s32[]{:S(2)}) async-start(s8[14680064]{0:T(1024)(128)(4,1)} %bitcast.7), calls=%async_computation.11 | async-start | bytes 4194304
  1.4 8.8 %collective-permute-start = (bf16[8,6272]{1,0:T(8,128)(2,1)S(1)}, bf16[8,6272]{1,0:T(8,128)(2,1)S(1)}, u32[]{:S(2)}, u32[]{:S(2)}) collective-permute-start(bf16[8,6272]{1,0:T(8,128)(2,1)S(1)} %get-tuple-element.23), channel_id=1, source_target_pairs={{0,12},{2,14},{4,8},{6,10},{8,4},{10,6},{12,0},{14,2},{1,13},{3,15... | collective-permute-start | bytes 301064 | tf_op jit(solution)/shard_map/ppermute | solution.py:311
  6.5 6.1 %collective-permute-start.1 = (bf16[8,6272]{1,0:T(8,128)(2,1)S(1)}, bf16[8,6272]{1,0:T(8,128)(2,1)S(1)}, u32[]{:S(2)}, u32[]{:S(2)}) collective-permute-start(bf16[8,6272]{1,0:T(8,128)(2,1)S(1)} %get-tuple-element.24), channel_id=1, source_target_pairs={{0,4},{2,6},{4,0},{6,2},{8,12},{10,14},{12,8},{14,10},{1,5},{3,7},... | collective-permute-start | bytes 301064 | tf_op jit(solution)/shard_map/ppermute | solution.py:311
  6.5 8.4 %collective-permute-start.2 = (bf16[8,6272]{1,0:T(8,128)(2,1)S(1)}, bf16[8,6272]{1,0:T(8,128)(2,1)S(1)}, u32[]{:S(2)}, u32[]{:S(2)}) collective-permute-start(bf16[8,6272]{1,0:T(8,128)(2,1)S(1)} %get-tuple-element.25), channel_id=1, source_target_pairs={{0,8},{2,10},{4,12},{6,14},{8,0},{10,2},{12,4},{14,6},{1,9},{3,11}... | collective-permute-start | bytes 301064 | tf_op jit(solution)/shard_map/ppermute | solution.py:311
  7.1 9.4 %collective-permute-start.3 = (bf16[8,6272]{1,0:T(8,128)(2,1)S(1)}, bf16[8,6272]{1,0:T(8,128)(2,1)S(1)}, u32[]{:S(2)}, u32[]{:S(2)}) collective-permute-start(bf16[8,6272]{1,0:T(8,128)(2,1)S(1)} %get-tuple-element.22.refs_0_), channel_id=1, source_target_pairs={{0,2},{2,0},{4,6},{6,4},{8,10},{10,8},{12,14},{14,12},{1,3},{3,1},... | collective-permute-start | bytes 301064 | tf_op jit(solution)/shard_map/ppermute | solution.py:314
  10.2 6.4 %collective-permute-start.4 = (bf16[8,6272]{1,0:T(8,128)(2,1)S(1)}, bf16[8,6272]{1,0:T(8,128)(2,1)S(1)}, u32[]{:S(2)}, u32[]{:S(2)}) collective-permute-start(bf16[8,6272]{1,0:T(8,128)(2,1)S(1)} %collective-permute-done.refs_1_), channel_id=1, source_target_pairs={{0,2},{2,0},{4,6},{6,4},{8,10},{10,8},{12,14},{14,12},{1,3},{3,1},... | collective-permute-start | bytes 301064 | tf_op jit(solution)/shard_map/ppermute | solution.py:314
  12.6 5.0 %collective-permute-start.5 = (bf16[8,6272]{1,0:T(8,128)(2,1)S(1)}, bf16[8,6272]{1,0:T(8,128)(2,1)S(1)}, u32[]{:S(2)}, u32[]{:S(2)}) collective-permute-start(bf16[8,6272]{1,0:T(8,128)(2,1)S(1)} %collective-permute-done.1.refs_2_), channel_id=1, source_target_pairs={{0,2},{2,0},{4,6},{6,4},{8,10},{10,8},{12,14},{14,12},{1,3},{3,1},... | collective-permute-start | bytes 301064 | tf_op jit(solution)/shard_map/ppermute | solution.py:314
  14.9 4.6 %collective-permute-start.6 = (bf16[8,6272]{1,0:T(8,128)(2,1)S(1)}, bf16[8,6272]{1,0:T(8,128)(2,1)S(1)}, u32[]{:S(2)}, u32[]{:S(2)}) collective-permute-start(bf16[8,6272]{1,0:T(8,128)(2,1)S(1)} %collective-permute-done.2.refs_3_), channel_id=1, source_target_pairs={{0,2},{2,0},{4,6},{6,4},{8,10},{10,8},{12,14},{14,12},{1,3},{3,1},... | collective-permute-start | bytes 301064 | tf_op jit(solution)/shard_map/ppermute | solution.py:314
  16.5 3.2 %collective-permute-start.7 = (bf16[32,6272]{1,0:T(8,128)(2,1)S(1)}, bf16[32,6272]{1,0:T(8,128)(2,1)S(1)}, u32[]{:S(2)}, u32[]{:S(2)}) collective-permute-start(bf16[32,6272]{1,0:T(8,128)(2,1)S(1)} %stack.4), channel_id=1, source_target_pairs={{0,1},{1,0},{2,3},{3,2},{4,5},{5,4},{6,7},{7,6},{8,9},{9,8},{10,11... | collective-permute-start | bytes 1204232 | tf_op jit(solution)/shard_map/ppermute | solution.py:317
  17.6 2.1 %collective-permute-start.8 = (bf16[24,6272]{1,0:T(8,128)(2,1)S(1)}, bf16[24,6272]{1,0:T(8,128)(2,1)S(1)}, u32[]{:S(2)}, u32[]{:S(2)}) collective-permute-start(bf16[24,6272]{1,0:T(8,128)(2,1)S(1)} %stack.5), channel_id=1, source_target_pairs={{0,1},{1,0},{2,3},{3,2},{4,5},{5,4},{6,7},{7,6},{8,9},{9,8},{10,11... | collective-permute-start | bytes 903176 | tf_op jit(solution)/shard_map/ppermute | solution.py:317
  19.6 1.4 %collective-permute-start.9 = (bf16[8,6272]{1,0:T(8,128)(2,1)S(1)}, bf16[8,6272]{1,0:T(8,128)(2,1)S(1)}, u32[]{:S(2)}, u32[]{:S(2)}) collective-permute-start(bf16[8,6272]{1,0:T(8,128)(2,1)S(1)} %stack.6), channel_id=1, source_target_pairs={{0,1},{1,0},{2,3},{3,2},{4,5},{5,4},{6,7},{7,6},{8,9},{9,8},{10,11... | collective-permute-start | bytes 301064 | tf_op jit(solution)/shard_map/ppermute | solution.py:317
  19.7 5.4 %slice-start = ((s8[14680064]{0:T(1024)(128)(4,1)}), s8[4194304]{0:T(1024)(128)(4,1)S(1)}, s32[]{:S(2)}) async-start(s8[14680064]{0:T(1024)(128)(4,1)} %bitcast.3), calls=%async_computation | async-start | bytes 8388608
  20.1 5.0 %slice-start.1 = ((s8[14680064]{0:T(1024)(128)(4,1)}), s8[4194304]{0:T(1024)(128)(4,1)S(1)}, s32[]{:S(2)}) async-start(s8[14680064]{0:T(1024)(128)(4,1)} %bitcast.3), calls=%async_computation.1 | async-start | bytes 8388608
  20.2 5.0 %slice-start.2 = ((s8[14680064]{0:T(1024)(128)(4,1)}), s8[4194304]{0:T(1024)(128)(4,1)S(1)}, s32[]{:S(2)}) async-start(s8[14680064]{0:T(1024)(128)(4,1)} %bitcast.3), calls=%async_computation.2 | async-start | bytes 8388608
  20.2 5.0 %slice-start.3 = ((s8[14680064]{0:T(1024)(128)(4,1)}), s8[2097152]{0:T(1024)(128)(4,1)S(1)}, s32[]{:S(2)}) async-start(s8[14680064]{0:T(1024)(128)(4,1)} %bitcast.3), calls=%async_computation.3 | async-start | bytes 4194304
  27.4 1.4 %collective-permute-start.10 = (bf16[8,6272]{1,0:T(8,128)(2,1)S(1)}, bf16[8,6272]{1,0:T(8,128)(2,1)S(1)}, u32[]{:S(2)}, u32[]{:S(2)}) collective-permute-start(bf16[8,6272]{1,0:T(8,128)(2,1)S(1)} %get-tuple-element.29), channel_id=1, source_target_pairs={{0,1},{1,0},{2,3},{3,2},{4,5},{5,4},{6,7},{7,6},{8,9},{9,8},{10,11... | collective-permute-start | bytes 301064 | tf_op jit(solution)/shard_map/ppermute | solution.py:317
  28.9 2.2 %collective-permute-start.11 = (bf16[56,6272]{1,0:T(8,128)(2,1)S(1)}, bf16[56,6272]{1,0:T(8,128)(2,1)S(1)}, u32[]{:S(2)}, u32[]{:S(2)}) collective-permute-start(bf16[56,6272]{1,0:T(8,128)(2,1)S(1)} %stack.7), channel_id=1, source_target_pairs={{0,1},{1,0},{2,3},{3,2},{4,5},{5,4},{6,7},{7,6},{8,9},{9,8},{10,11... | collective-permute-start | bytes 2107400 | tf_op jit(solution)/shard_map/ppermute | solution.py:317
  29.3 5.6 %collective-permute-start.13 = (bf16[8,6272]{1,0:T(8,128)(2,1)S(1)}, bf16[8,6272]{1,0:T(8,128)(2,1)S(1)}, u32[]{:S(2)}, u32[]{:S(2)}) collective-permute-start(bf16[8,6272]{1,0:T(8,128)(2,1)S(1)} %pair_sum.3.refs_1_), channel_id=1, source_target_pairs={{0,2},{2,0},{4,6},{6,4},{8,10},{10,8},{12,14},{14,12},{1,3},{3,1},... | collective-permute-start | bytes 301064 | tf_op jit(solution)/shard_map/ppermute | solution.py:314
  31.1 6.4 %collective-permute-start.15 = (bf16[8,6272]{1,0:T(8,128)(2,1)S(1)}, bf16[8,6272]{1,0:T(8,128)(2,1)S(1)}, u32[]{:S(2)}, u32[]{:S(2)}) collective-permute-start(bf16[8,6272]{1,0:T(8,128)(2,1)S(1)} %get-tuple-element.34), channel_id=1, source_target_pairs={{0,2},{2,0},{4,6},{6,4},{8,10},{10,8},{12,14},{14,12},{1,3},{3,1},... | collective-permute-start | bytes 301064 | tf_op jit(solution)/shard_map/ppermute | solution.py:314
  32.7 6.3 %collective-permute-start.17 = (bf16[8,6272]{1,0:T(8,128)(2,1)S(1)}, bf16[8,6272]{1,0:T(8,128)(2,1)S(1)}, u32[]{:S(2)}, u32[]{:S(2)}) collective-permute-start(bf16[8,6272]{1,0:T(8,128)(2,1)S(1)} %get-tuple-element.36), channel_id=1, source_target_pairs={{0,2},{2,0},{4,6},{6,4},{8,10},{10,8},{12,14},{14,12},{1,3},{3,1},... | collective-permute-start | bytes 301064 | tf_op jit(solution)/shard_map/ppermute | solution.py:314
  33.3 7.4 %collective-permute-start.12 = (bf16[8,6272]{1,0:T(8,128)(2,1)S(1)}, bf16[8,6272]{1,0:T(8,128)(2,1)S(1)}, u32[]{:S(2)}, u32[]{:S(2)}) collective-permute-start(bf16[8,6272]{1,0:T(8,128)(2,1)S(1)} %get-tuple-element.31), channel_id=1, source_target_pairs={{0,2},{2,0},{4,6},{6,4},{8,10},{10,8},{12,14},{14,12},{1,3},{3,1},... | collective-permute-start | bytes 301064 | tf_op jit(solution)/shard_map/ppermute | solution.py:314
  34.9 7.6 %collective-permute-start.14 = (bf16[8,6272]{1,0:T(8,128)(2,1)S(1)}, bf16[8,6272]{1,0:T(8,128)(2,1)S(1)}, u32[]{:S(2)}, u32[]{:S(2)}) collective-permute-start(bf16[8,6272]{1,0:T(8,128)(2,1)S(1)} %span_sum.3), channel_id=1, source_target_pairs={{0,12},{2,14},{4,8},{6,10},{8,4},{10,6},{12,0},{14,2},{1,13},{3,15... | collective-permute-start | bytes 301064 | tf_op jit(solution)/shard_map/ppermute | solution.py:311
  37.5 8.8 %collective-permute-start.16 = (bf16[8,6272]{1,0:T(8,128)(2,1)S(1)}, bf16[8,6272]{1,0:T(8,128)(2,1)S(1)}, u32[]{:S(2)}, u32[]{:S(2)}) collective-permute-start(bf16[8,6272]{1,0:T(8,128)(2,1)S(1)} %span_sum.4), channel_id=1, source_target_pairs={{0,8},{2,10},{4,12},{6,14},{8,0},{10,2},{12,4},{14,6},{1,9},{3,11}... | collective-permute-start | bytes 301064 | tf_op jit(solution)/shard_map/ppermute | solution.py:311
  39.1 7.3 %collective-permute-start.18 = (bf16[8,6272]{1,0:T(8,128)(2,1)S(1)}, bf16[8,6272]{1,0:T(8,128)(2,1)S(1)}, u32[]{:S(2)}, u32[]{:S(2)}) collective-permute-start(bf16[8,6272]{1,0:T(8,128)(2,1)S(1)} %span_sum.5), channel_id=1, source_target_pairs={{0,4},{2,6},{4,0},{6,2},{8,12},{10,14},{12,8},{14,10},{1,5},{3,7},... | collective-permute-start | bytes 301064 | tf_op jit(solution)/shard_map/ppermute | solution.py:311

commit v15 on v14

--- a/solution.py
+++ b/solution.py
@@ -165,23 +165,25 @@
     return outs[:span], outs[span::2], outs[span + 1::2]
 
 
-def pair_sum_kernel(places, offset, keep_ref, *refs):
-    received, outs = refs[:-len(places)], refs[-len(places):]
+def pair_sum_kernel(count, places, indices, keep_ref, *refs):
+    received, outs = refs[:count], refs[-len(places):]
     rows = outs[0].shape[0]
-    for i, (place, out_ref) in enumerate(zip(places, outs), offset):
+    for place, i, out_ref in zip(places, indices, outs):
         value = keep_ref[place * rows:(place + 1) * rows, :]
         for ref in received:
             value += ref[i * rows:(i + 1) * rows, :].astype(jnp.float32)
         out_ref[...] = value.astype(out_ref.dtype)
 
 
-def pair_sum(keep, received, rows, dtype, places, offset):
-    return pl.pallas_call(
-        functools.partial(pair_sum_kernel, places, offset),
+def pair_sum(keep, received, rows, dtype, places, indices, after=()):
+    vmem = [pl.BlockSpec(memory_space=pltpu.VMEM)] * (1 + len(received))
+    return pl.pallas_call(
+        functools.partial(pair_sum_kernel, len(received), places, indices),
+        in_specs=vmem + [pl.BlockSpec(memory_space=pl.ANY)] * len(after),
         out_shape=[jax.ShapeDtypeStruct((rows, keep.shape[1]), dtype)] * len(places),
         compiler_params=params(),
         name="pair_sum",
-    )(keep, *received)
+    )(keep, *received, *after)
 
 
 def span_sum_kernel(*refs):
@@ -332,21 +334,27 @@
     rest = [i for i in range(EXPERTS) if i != first]
     keeps, firsts, others = down(hidden, down_weight, span, pair, rows, first)
     received = [over_pair(b, -p) for p, b in enumerate(firsts, 1)]
-    sums = {s: [] for s in range(EXPERTS)}
+    sums, after = {s: [] for s in range(EXPERTS)}, []
     for t in range(1, span):
-        block, = pair_sum(keeps[t], received, rows, jnp.bfloat16, [first], t - 1)
-        sums[RETURN_ORDER[0]].append(over_span(block, -t))
-        after = [block]
-    received = [over_pair(stack([b], after), -p) for p, b in enumerate(others, 1)]
-    for t in range(1, span):
-        blocks = pair_sum(keeps[t], received, rows, jnp.bfloat16, rest, (t - 1) * len(rest))
-        for place, block in zip(rest, blocks):
-            sums[BLOCK_ORDER[place]].append(over_span(block, -t))
-    own = pair_sum(keeps[0], received, rows, jnp.float32, list(range(EXPERTS)), (span - 1) * len(rest))
+        after += pair_sum(keeps[t], received, rows, jnp.bfloat16, [first], [t - 1])
+        sums[RETURN_ORDER[0]].append(over_span(after[-1], -t))
+    received = [over_pair(stack([b], after[:1]), -p) for p, b in enumerate(others, 1)]
+    own = pair_sum(keeps[0], received, rows, jnp.float32, range(EXPERTS), [(span - 1) * len(rest) + i for i in range(EXPERTS)])
     for place, block in enumerate(own):
         sums[BLOCK_ORDER[place]].insert(0, block)
 
-    returned = {s: over_experts(span_sum(sums[s]), s) for s in RETURN_ORDER}
+    def send_rest(planes, after):
+        for t in range(1, span):
+            places = [BLOCK_ORDER.index(s) for s in planes]
+            indices = [(t - 1) * len(rest) + rest.index(place) for place in places]
+            blocks = pair_sum(keeps[t], received, rows, jnp.bfloat16, places, indices, after)
+            for s, block in zip(planes, blocks):
+                sums[s].append(over_span(block, -t))
+
+    send_rest(RETURN_ORDER[1:], [])
+    totals = {s: span_sum(sums[s]) for s in RETURN_ORDER}
+    send_rest([0], [totals[RETURN_ORDER[1]]])
+    returned = {s: over_experts(totals[s], s) for s in RETURN_ORDER}
     far, *later = RETURN_ORDER
     early = combine(sides, [], [0, far], [sums[0], [returned[far]]], width, jnp.float32)
     return combine(sides, [early], later, [[returned[s]] for s in later], width, jnp.bfloat16, 2)

time: 47.3 us -> 46.6 us (0.985)
  waiting for transfers between devices: 14.3 us -> 12.5 us
  starting transfers between devices: 23.2 us -> 24.3 us
    ppermute x6, waiting for transfers between devices: 8.51 us -> 6.61 us  [over_experts(): lax.ppermute(value, 'attn', [(i, (i // span ^ other) * span + i % span) f...]
    ppermute x6, starting transfers between devices: 10.6 us -> 11.8 us  [over_experts(): lax.ppermute(value, 'attn', [(i, (i // span ^ other) * span + i % span) f...]
  transfers between devices with their start and end apart: 19 -> 19, of which waited for: 12 -> 11; matrix products, arithmetic and copies ran while one was open for 0% -> 0% of each run, Pallas kernels for 2% -> 2%
where the time goes in v15:
time: 46.6 us; the launch traced here: 46.4 us
  starting transfers between devices  24.3 us (52%)
  waiting for transfers between devices  12.5 us (27%)
  Pallas kernels  9.29 us (20%)
    ppermute x6, starting transfers between devices, over_experts(): lax.ppermute(value, 'attn', [(i, (i // span ^ other) * span + i % span) f...  11.8 us
    ppermute x8, starting transfers between devices, over_span(): lax.ppermute(value, 'attn', [(i, i // span * span + (i + shift) % span) f...  11.4 us
    ppermute x6, waiting for transfers between devices, over_experts(): lax.ppermute(value, 'attn', [(i, (i // span ^ other) * span + i % span) f...  6.61 us
    pallas_call x1, Pallas kernels, gate_up(): pl.pallas_call(functools.partial(gate_up_kernel, block_of(units, N_BLOCK)...  4.09 us
    ppermute x8, waiting for transfers between devices, over_span(): lax.ppermute(value, 'attn', [(i, i // span * span + (i + shift) % span) f...  3.87 us
    pallas_call x1, Pallas kernels, down(): pl.pallas_call(functools.partial(down_kernel, rows, sources), in_specs=[p...  2.21 us
    ppermute x5, waiting for transfers between devices, over_pair(): lax.ppermute(value, 'ffn', [(i, (i + shift) % pair) for i in range(pair)])  2 us
    pallas_call x1, Pallas kernels, pack(): pl.pallas_call(pack_kernel, in_specs=[pl.BlockSpec(memory_space=pltpu.SME...  1.3 us
  transfers between devices with their start and end apart: 19, of which 11 were waited for; matrix products, arithmetic and copies ran while one was open for 0% of the time, Pallas kernels for 2%

profile of v15, /device:TPU:0, one launch (start us, length us, event | category | flops | bytes accessed | tf_op | source)
XLA Modules:
  0.0 46.4 jit_solution(1924748668007354338)
XLA Ops:
  0.0 1.3 %pack.1 = (f32[8,1024]{1,0:T(8,128)S(1)}, bf16[8,6272]{1,0:T(8,128)(2,1)S(1)}, bf16[8,6272]{1,0:T(8,128)(2,1)S(1)}, bf16[8,6272]{1,0:T(8,128)(2,1)S(1)}, bf16[8,6272]{1,0:T(8,128)(2,1)S(1)}) custom-call(s32[1]{0:T(128)} %bitcast.own_expert, bf16[8,7168]{1,0:T(8,128)(2,1)} %tokens_hbm.1, s32[3,8]{1,0:T(4,128)} %bitcast.9, f32[3,8]{1,0:T(4,128)} %bitcast.10), custom_call_target="tpu_custom_call" | custom-call | flops 20000000000 | tf_op jit(solution)/shard_map/pack/pallas_call | solution.py:241
  1.4 5.1 %collective-permute-start = (bf16[8,6272]{1,0:T(8,128)(2,1)S(1)}, bf16[8,6272]{1,0:T(8,128)(2,1)S(1)}, u32[]{:S(2)}, u32[]{:S(2)}) collective-permute-start(bf16[8,6272]{1,0:T(8,128)(2,1)S(1)} %get-tuple-element.22), channel_id=1, source_target_pairs={{0,12},{2,14},{4,8},{6,10},{8,4},{10,6},{12,0},{14,2},{1,13},{3,15... | collective-permute-start | bytes 301064 | tf_op jit(solution)/shard_map/ppermute | solution.py:313
  6.5 0.6 %collective-permute-start.2 = (bf16[8,6272]{1,0:T(8,128)(2,1)S(1)}, bf16[8,6272]{1,0:T(8,128)(2,1)S(1)}, u32[]{:S(2)}, u32[]{:S(2)}) collective-permute-start(bf16[8,6272]{1,0:T(8,128)(2,1)S(1)} %get-tuple-element.24), channel_id=1, source_target_pairs={{0,8},{2,10},{4,12},{6,14},{8,0},{10,2},{12,4},{14,6},{1,9},{3,11}... | collective-permute-start | bytes 301064 | tf_op jit(solution)/shard_map/ppermute | solution.py:313
  7.1 1.7 %collective-permute-start.3 = (bf16[8,6272]{1,0:T(8,128)(2,1)S(1)}, bf16[8,6272]{1,0:T(8,128)(2,1)S(1)}, u32[]{:S(2)}, u32[]{:S(2)}) collective-permute-start(bf16[8,6272]{1,0:T(8,128)(2,1)S(1)} %get-tuple-element.21.refs_0_), channel_id=1, source_target_pairs={{0,2},{2,0},{4,6},{6,4},{8,10},{10,8},{12,14},{14,12},{1,3},{3,1},... | collective-permute-start | bytes 301064 | tf_op jit(solution)/shard_map/ppermute | solution.py:316
  8.8 1.4 %collective-permute-done.refs_1_ = bf16[8,6272]{1,0:T(8,128)(2,1)S(1)} collective-permute-done((bf16[8,6272]{1,0:T(8,128)(2,1)S(1)}, bf16[8,6272]{1,0:T(8,128)(2,1)S(1)}, u32[]{:S(2)}, u32[]{:S(2)}) %collective-permute-start) | collective-permute-done | bytes 100384 | tf_op jit(solution)/shard_map/ppermute | solution.py:313
  10.2 1.7 %collective-permute-start.4 = (bf16[8,6272]{1,0:T(8,128)(2,1)S(1)}, bf16[8,6272]{1,0:T(8,128)(2,1)S(1)}, u32[]{:S(2)}, u32[]{:S(2)}) collective-permute-start(bf16[8,6272]{1,0:T(8,128)(2,1)S(1)} %collective-permute-done.refs_1_), channel_id=1, source_target_pairs={{0,2},{2,0},{4,6},{6,4},{8,10},{10,8},{12,14},{14,12},{1,3},{3,1},... | collective-permute-start | bytes 301064 | tf_op jit(solution)/shard_map/ppermute | solution.py:316
  11.9 0.7 %collective-permute-done.1.refs_2_ = bf16[8,6272]{1,0:T(8,128)(2,1)S(1)} collective-permute-done((bf16[8,6272]{1,0:T(8,128)(2,1)S(1)}, bf16[8,6272]{1,0:T(8,128)(2,1)S(1)}, u32[]{:S(2)}, u32[]{:S(2)}) %collective-permute-start.1) | collective-permute-done | bytes 100384 | tf_op jit(solution)/shard_map/ppermute | solution.py:313
  12.6 1.5 %collective-permute-start.5 = (bf16[8,6272]{1,0:T(8,128)(2,1)S(1)}, bf16[8,6272]{1,0:T(8,128)(2,1)S(1)}, u32[]{:S(2)}, u32[]{:S(2)}) collective-permute-start(bf16[8,6272]{1,0:T(8,128)(2,1)S(1)} %collective-permute-done.1.refs_2_), channel_id=1, source_target_pairs={{0,2},{2,0},{4,6},{6,4},{8,10},{10,8},{12,14},{14,12},{1,3},{3,1},... | collective-permute-start | bytes 301064 | tf_op jit(solution)/shard_map/ppermute | solution.py:316
  14.1 0.8 %collective-permute-done.2.refs_3_ = bf16[8,6272]{1,0:T(8,128)(2,1)S(1)} collective-permute-done((bf16[8,6272]{1,0:T(8,128)(2,1)S(1)}, bf16[8,6272]{1,0:T(8,128)(2,1)S(1)}, u32[]{:S(2)}, u32[]{:S(2)}) %collective-permute-start.2) | collective-permute-done | bytes 100384 | tf_op jit(solution)/shard_map/ppermute | solution.py:313
  14.9 1.5 %collective-permute-start.6 = (bf16[8,6272]{1,0:T(8,128)(2,1)S(1)}, bf16[8,6272]{1,0:T(8,128)(2,1)S(1)}, u32[]{:S(2)}, u32[]{:S(2)}) collective-permute-start(bf16[8,6272]{1,0:T(8,128)(2,1)S(1)} %collective-permute-done.2.refs_3_), channel_id=1, source_target_pairs={{0,2},{2,0},{4,6},{6,4},{8,10},{10,8},{12,14},{14,12},{1,3},{3,1},... | collective-permute-start | bytes 301064 | tf_op jit(solution)/shard_map/ppermute | solution.py:316
  16.6 1.0 %collective-permute-done.5.refs_2_.refs_6_ = bf16[8,6272]{1,0:T(8,128)(2,1)S(1)} collective-permute-done((bf16[8,6272]{1,0:T(8,128)(2,1)S(1)}, bf16[8,6272]{1,0:T(8,128)(2,1)S(1)}, u32[]{:S(2)}, u32[]{:S(2)}) %collective-permute-start.5) | collective-permute-done | bytes 100384 | tf_op jit(solution)/shard_map/ppermute | solution.py:316
  17.7 1.9 %collective-permute-done.6.refs_7_.refs_0_ = bf16[8,6272]{1,0:T(8,128)(2,1)S(1)} collective-permute-done((bf16[8,6272]{1,0:T(8,128)(2,1)S(1)}, bf16[8,6272]{1,0:T(8,128)(2,1)S(1)}, u32[]{:S(2)}, u32[]{:S(2)}) %collective-permute-start.6) | collective-permute-done | bytes 100384 | tf_op jit(solution)/shard_map/ppermute | solution.py:316
  19.7 0.5 unpack.1.first_ref
  20.2 0.8 %collective-permute-done.9.last_ref = bf16[8,6272]{1,0:T(8,128)(2,1)S(1)} collective-permute-done((bf16[8,6272]{1,0:T(8,128)(2,1)S(1)}, bf16[8,6272]{1,0:T(8,128)(2,1)S(1)}, u32[]{:S(2)}, u32[]{:S(2)}) %collective-permute-start.9) | collective-permute-done | bytes 100384 | tf_op jit(solution)/shard_map/ppermute | solution.py:319
  21.0 4.1 %gate_up.1.hidden_ref = bf16[128,1024]{1,0:T(8,128)(2,1)S(1)} custom-call(bf16[120,7168]{1,0:T(8,128)(2,1)S(1)} %unpack.1.first_ref, bf16[8,6272]{1,0:T(8,128)(2,1)S(1)} %collective-permute-done.9.last_ref, bf16[7168,1024]{1,0:T(8,128)(2,1)S(1)} %bitcast.6, bf16[7168,1024]{1,0:T(8,128)(2,1)S(1)} %bitcast.8), custom_call_target="tpu_custom_call" | custom-call | flops 3758096384 | tf_op jit(solution)/shard_map/gate_up/pallas_call | solution.py:113
  25.2 2.2 %down.1 = (f32[32,6272]{1,0:T(8,128)S(1)}, f32[32,6272]{1,0:T(8,128)S(1)}, bf16[8,6272]{1,0:T(8,128)(2,1)S(1)}, bf16[56,6272]{1,0:T(8,128)(2,1)S(1)}) custom-call(bf16[128,1024]{1,0:T(8,128)(2,1)S(1)} %gate_up.1.hidden_ref, bf16[1024,7168]{1,0:T(8,128)(2,1)S(1)} %bitcast.4), custom_call_target="tpu_custom_call" | custom-call | flops 1644167168 | tf_op jit(solution)/shard_map/down/pallas_call | solution.py:157
  27.4 0.4 collective-permute-start.10
  27.8 0.9 %collective-permute-done.10.refs_0_ = bf16[8,6272]{1,0:T(8,128)(2,1)S(1)} collective-permute-done((bf16[8,6272]{1,0:T(8,128)(2,1)S(1)}, bf16[8,6272]{1,0:T(8,128)(2,1)S(1)}, u32[]{:S(2)}, u32[]{:S(2)}) %collective-permute-start.10) | collective-permute-done | bytes 100384 | tf_op jit(solution)/shard_map/ppermute | solution.py:319
  28.9 0.4 collective-permute-start.11
  29.3 1.5 %collective-permute-start.14 = (bf16[8,6272]{1,0:T(8,128)(2,1)S(1)}, bf16[8,6272]{1,0:T(8,128)(2,1)S(1)}, u32[]{:S(2)}, u32[]{:S(2)}) collective-permute-start(bf16[8,6272]{1,0:T(8,128)(2,1)S(1)} %pair_sum.4.refs_1_), channel_id=1, source_target_pairs={{0,2},{2,0},{4,6},{6,4},{8,10},{10,8},{12,14},{14,12},{1,3},{3,1},... | collective-permute-start | bytes 301064 | tf_op jit(solution)/shard_map/ppermute | solution.py:316
  30.8 0.3 collective-permute-done.11.refs_0_
  31.1 1.6 %collective-permute-start.12 = (bf16[8,6272]{1,0:T(8,128)(2,1)S(1)}, bf16[8,6272]{1,0:T(8,128)(2,1)S(1)}, u32[]{:S(2)}, u32[]{:S(2)}) collective-permute-start(bf16[8,6272]{1,0:T(8,128)(2,1)S(1)} %get-tuple-element.31), channel_id=1, source_target_pairs={{0,2},{2,0},{4,6},{6,4},{8,10},{10,8},{12,14},{14,12},{1,3},{3,1},... | collective-permute-start | bytes 301064 | tf_op jit(solution)/shard_map/ppermute | solution.py:316
  32.7 0.5 %collective-permute-start.17 = (bf16[8,6272]{1,0:T(8,128)(2,1)S(1)}, bf16[8,6272]{1,0:T(8,128)(2,1)S(1)}, u32[]{:S(2)}, u32[]{:S(2)}) collective-permute-start(bf16[8,6272]{1,0:T(8,128)(2,1)S(1)} %get-tuple-element.34), channel_id=1, source_target_pairs={{0,2},{2,0},{4,6},{6,4},{8,10},{10,8},{12,14},{14,12},{1,3},{3,1},... | collective-permute-start | bytes 301064 | tf_op jit(solution)/shard_map/ppermute | solution.py:316
  33.3 0.9 %collective-permute-done.14.refs_1_ = bf16[8,6272]{1,0:T(8,128)(2,1)S(1)} collective-permute-done((bf16[8,6272]{1,0:T(8,128)(2,1)S(1)}, bf16[8,6272]{1,0:T(8,128)(2,1)S(1)}, u32[]{:S(2)}, u32[]{:S(2)}) %collective-permute-start.14) | collective-permute-done | bytes 100384 | tf_op jit(solution)/shard_map/ppermute | solution.py:316
  34.2 2.9 %collective-permute-start.15 = (bf16[8,6272]{1,0:T(8,128)(2,1)S(1)}, bf16[8,6272]{1,0:T(8,128)(2,1)S(1)}, u32[]{:S(2)}, u32[]{:S(2)}) collective-permute-start(bf16[8,6272]{1,0:T(8,128)(2,1)S(1)} %span_sum.4), channel_id=1, source_target_pairs={{0,12},{2,14},{4,8},{6,10},{8,4},{10,6},{12,0},{14,2},{1,13},{3,15... | collective-permute-start | bytes 301064 | tf_op jit(solution)/shard_map/ppermute | solution.py:313
  37.1 1.4 %collective-permute-start.13 = (bf16[8,6272]{1,0:T(8,128)(2,1)S(1)}, bf16[8,6272]{1,0:T(8,128)(2,1)S(1)}, u32[]{:S(2)}, u32[]{:S(2)}) collective-permute-start(bf16[8,6272]{1,0:T(8,128)(2,1)S(1)} %pair_sum.7), channel_id=1, source_target_pairs={{0,2},{2,0},{4,6},{6,4},{8,10},{10,8},{12,14},{14,12},{1,3},{3,1},... | collective-permute-start | bytes 301064 | tf_op jit(solution)/shard_map/ppermute | solution.py:316
  38.5 1.4 %collective-permute-start.16 = (bf16[8,6272]{1,0:T(8,128)(2,1)S(1)}, bf16[8,6272]{1,0:T(8,128)(2,1)S(1)}, u32[]{:S(2)}, u32[]{:S(2)}) collective-permute-start(bf16[8,6272]{1,0:T(8,128)(2,1)S(1)} %span_sum.3.refs_1_), channel_id=1, source_target_pairs={{0,8},{2,10},{4,12},{6,14},{8,0},{10,2},{12,4},{14,6},{1,9},{3,11}... | collective-permute-start | bytes 301064 | tf_op jit(solution)/shard_map/ppermute | solution.py:313
  39.9 1.8 %collective-permute-start.18 = (bf16[8,6272]{1,0:T(8,128)(2,1)S(1)}, bf16[8,6272]{1,0:T(8,128)(2,1)S(1)}, u32[]{:S(2)}, u32[]{:S(2)}) collective-permute-start(bf16[8,6272]{1,0:T(8,128)(2,1)S(1)} %span_sum.5), channel_id=1, source_target_pairs={{0,4},{2,6},{4,0},{6,2},{8,12},{10,14},{12,8},{14,10},{1,5},{3,7},... | collective-permute-start | bytes 301064 | tf_op jit(solution)/shard_map/ppermute | solution.py:313
  41.7 0.1 collective-permute-done.13.refs_1_
  41.8 0.1 combine.2.refs_0_
  42.0 3.7 %collective-permute-done.16.refs_1_ = bf16[8,6272]{1,0:T(8,128)(2,1)S(1)} collective-permute-done((bf16[8,6272]{1,0:T(8,128)(2,1)S(1)}, bf16[8,6272]{1,0:T(8,128)(2,1)S(1)}, u32[]{:S(2)}, u32[]{:S(2)}) %collective-permute-start.16) | collective-permute-done | bytes 100384 | tf_op jit(solution)/shard_map/ppermute | solution.py:313
  45.7 0.8 %combine.3 = bf16[8,7168]{1,0:T(8,128)(2,1)} custom-call(f32[8,1024]{1,0:T(8,128)S(1)} %get-tuple-element.20.sides_ref, f32[8,7168]{1,0:T(8,128)S(1)} %combine.2.refs_0_, bf16[8,6272]{1,0:T(8,128)(2,1)S(1)} %collective-permute-done.16.refs_1_, bf16[8,6272]{1,0:T(8,128)(2,1)S(1)} %collective-permute-done.18.refs_2_), custom_call_target="tpu_custom_call" | custom-call | tf_op jit(solution)/shard_map/combine/pallas_call | solution.py:296
  (50 shorter events, 0.6 us)
Async XLA Ops:
  0.0 20.9 %slice-start.4 = ((s8[14680064]{0:T(1024)(128)(4,1)}), s8[4194304]{0:T(1024)(128)(4,1)S(1)}, s32[]{:S(2)}) async-start(s8[14680064]{0:T(1024)(128)(4,1)} %bitcast.5), calls=%async_computation.4 | async-start | bytes 8388608
  0.0 20.9 %slice-start.8 = ((s8[14680064]{0:T(1024)(128)(4,1)}), s8[4194304]{0:T(1024)(128)(4,1)S(1)}, s32[]{:S(2)}) async-start(s8[14680064]{0:T(1024)(128)(4,1)} %bitcast.7), calls=%async_computation.8 | async-start | bytes 8388608
  0.0 20.9 %slice-start.5 = ((s8[14680064]{0:T(1024)(128)(4,1)}), s8[4194304]{0:T(1024)(128)(4,1)S(1)}, s32[]{:S(2)}) async-start(s8[14680064]{0:T(1024)(128)(4,1)} %bitcast.5), calls=%async_computation.5 | async-start | bytes 8388608
  0.0 20.9 %slice-start.6 = ((s8[14680064]{0:T(1024)(128)(4,1)}), s8[4194304]{0:T(1024)(128)(4,1)S(1)}, s32[]{:S(2)}) async-start(s8[14680064]{0:T(1024)(128)(4,1)} %bitcast.5), calls=%async_computation.6 | async-start | bytes 8388608
  0.0 21.0 %slice-start.7 = ((s8[14680064]{0:T(1024)(128)(4,1)}), s8[2097152]{0:T(1024)(128)(4,1)S(1)}, s32[]{:S(2)}) async-start(s8[14680064]{0:T(1024)(128)(4,1)} %bitcast.5), calls=%async_computation.7 | async-start | bytes 4194304
  0.0 21.0 %slice-start.9 = ((s8[14680064]{0:T(1024)(128)(4,1)}), s8[4194304]{0:T(1024)(128)(4,1)S(1)}, s32[]{:S(2)}) async-start(s8[14680064]{0:T(1024)(128)(4,1)} %bitcast.7), calls=%async_computation.9 | async-start | bytes 8388608
  0.0 21.0 %slice-start.10 = ((s8[14680064]{0:T(1024)(128)(4,1)}), s8[4194304]{0:T(1024)(128)(4,1)S(1)}, s32[]{:S(2)}) async-start(s8[14680064]{0:T(1024)(128)(4,1)} %bitcast.7), calls=%async_computation.10 | async-start | bytes 8388608
  0.0 21.0 %slice-start.11 = ((s8[14680064]{0:T(1024)(128)(4,1)}), s8[2097152]{0:T(1024)(128)(4,1)S(1)}, s32[]{:S(2)}) async-start(s8[14680064]{0:T(1024)(128)(4,1)} %bitcast.7), calls=%async_computation.11 | async-start | bytes 4194304
  1.4 8.8 %collective-permute-start = (bf16[8,6272]{1,0:T(8,128)(2,1)S(1)}, bf16[8,6272]{1,0:T(8,128)(2,1)S(1)}, u32[]{:S(2)}, u32[]{:S(2)}) collective-permute-start(bf16[8,6272]{1,0:T(8,128)(2,1)S(1)} %get-tuple-element.22), channel_id=1, source_target_pairs={{0,12},{2,14},{4,8},{6,10},{8,4},{10,6},{12,0},{14,2},{1,13},{3,15... | collective-permute-start | bytes 301064 | tf_op jit(solution)/shard_map/ppermute | solution.py:313
  6.5 6.1 %collective-permute-start.1 = (bf16[8,6272]{1,0:T(8,128)(2,1)S(1)}, bf16[8,6272]{1,0:T(8,128)(2,1)S(1)}, u32[]{:S(2)}, u32[]{:S(2)}) collective-permute-start(bf16[8,6272]{1,0:T(8,128)(2,1)S(1)} %get-tuple-element.23), channel_id=1, source_target_pairs={{0,4},{2,6},{4,0},{6,2},{8,12},{10,14},{12,8},{14,10},{1,5},{3,7},... | collective-permute-start | bytes 301064 | tf_op jit(solution)/shard_map/ppermute | solution.py:313
  6.5 8.4 %collective-permute-start.2 = (bf16[8,6272]{1,0:T(8,128)(2,1)S(1)}, bf16[8,6272]{1,0:T(8,128)(2,1)S(1)}, u32[]{:S(2)}, u32[]{:S(2)}) collective-permute-start(bf16[8,6272]{1,0:T(8,128)(2,1)S(1)} %get-tuple-element.24), channel_id=1, source_target_pairs={{0,8},{2,10},{4,12},{6,14},{8,0},{10,2},{12,4},{14,6},{1,9},{3,11}... | collective-permute-start | bytes 301064 | tf_op jit(solution)/shard_map/ppermute | solution.py:313
  7.1 9.4 %collective-permute-start.3 = (bf16[8,6272]{1,0:T(8,128)(2,1)S(1)}, bf16[8,6272]{1,0:T(8,128)(2,1)S(1)}, u32[]{:S(2)}, u32[]{:S(2)}) collective-permute-start(bf16[8,6272]{1,0:T(8,128)(2,1)S(1)} %get-tuple-element.21.refs_0_), channel_id=1, source_target_pairs={{0,2},{2,0},{4,6},{6,4},{8,10},{10,8},{12,14},{14,12},{1,3},{3,1},... | collective-permute-start | bytes 301064 | tf_op jit(solution)/shard_map/ppermute | solution.py:316
  10.2 6.4 %collective-permute-start.4 = (bf16[8,6272]{1,0:T(8,128)(2,1)S(1)}, bf16[8,6272]{1,0:T(8,128)(2,1)S(1)}, u32[]{:S(2)}, u32[]{:S(2)}) collective-permute-start(bf16[8,6272]{1,0:T(8,128)(2,1)S(1)} %collective-permute-done.refs_1_), channel_id=1, source_target_pairs={{0,2},{2,0},{4,6},{6,4},{8,10},{10,8},{12,14},{14,12},{1,3},{3,1},... | collective-permute-start | bytes 301064 | tf_op jit(solution)/shard_map/ppermute | solution.py:316
  12.6 5.0 %collective-permute-start.5 = (bf16[8,6272]{1,0:T(8,128)(2,1)S(1)}, bf16[8,6272]{1,0:T(8,128)(2,1)S(1)}, u32[]{:S(2)}, u32[]{:S(2)}) collective-permute-start(bf16[8,6272]{1,0:T(8,128)(2,1)S(1)} %collective-permute-done.1.refs_2_), channel_id=1, source_target_pairs={{0,2},{2,0},{4,6},{6,4},{8,10},{10,8},{12,14},{14,12},{1,3},{3,1},... | collective-permute-start | bytes 301064 | tf_op jit(solution)/shard_map/ppermute | solution.py:316
  14.9 4.6 %collective-permute-start.6 = (bf16[8,6272]{1,0:T(8,128)(2,1)S(1)}, bf16[8,6272]{1,0:T(8,128)(2,1)S(1)}, u32[]{:S(2)}, u32[]{:S(2)}) collective-permute-start(bf16[8,6272]{1,0:T(8,128)(2,1)S(1)} %collective-permute-done.2.refs_3_), channel_id=1, source_target_pairs={{0,2},{2,0},{4,6},{6,4},{8,10},{10,8},{12,14},{14,12},{1,3},{3,1},... | collective-permute-start | bytes 301064 | tf_op jit(solution)/shard_map/ppermute | solution.py:316
  16.5 3.2 %collective-permute-start.7 = (bf16[32,6272]{1,0:T(8,128)(2,1)S(1)}, bf16[32,6272]{1,0:T(8,128)(2,1)S(1)}, u32[]{:S(2)}, u32[]{:S(2)}) collective-permute-start(bf16[32,6272]{1,0:T(8,128)(2,1)S(1)} %stack.4), channel_id=1, source_target_pairs={{0,1},{1,0},{2,3},{3,2},{4,5},{5,4},{6,7},{7,6},{8,9},{9,8},{10,11... | collective-permute-start | bytes 1204232 | tf_op jit(solution)/shard_map/ppermute | solution.py:319
  17.6 2.1 %collective-permute-start.8 = (bf16[24,6272]{1,0:T(8,128)(2,1)S(1)}, bf16[24,6272]{1,0:T(8,128)(2,1)S(1)}, u32[]{:S(2)}, u32[]{:S(2)}) collective-permute-start(bf16[24,6272]{1,0:T(8,128)(2,1)S(1)} %stack.5), channel_id=1, source_target_pairs={{0,1},{1,0},{2,3},{3,2},{4,5},{5,4},{6,7},{7,6},{8,9},{9,8},{10,11... | collective-permute-start | bytes 903176 | tf_op jit(solution)/shard_map/ppermute | solution.py:319
  19.6 1.4 %collective-permute-start.9 = (bf16[8,6272]{1,0:T(8,128)(2,1)S(1)}, bf16[8,6272]{1,0:T(8,128)(2,1)S(1)}, u32[]{:S(2)}, u32[]{:S(2)}) collective-permute-start(bf16[8,6272]{1,0:T(8,128)(2,1)S(1)} %stack.6), channel_id=1, source_target_pairs={{0,1},{1,0},{2,3},{3,2},{4,5},{5,4},{6,7},{7,6},{8,9},{9,8},{10,11... | collective-permute-start | bytes 301064 | tf_op jit(solution)/shard_map/ppermute | solution.py:319
  19.7 5.4 %slice-start = ((s8[14680064]{0:T(1024)(128)(4,1)}), s8[4194304]{0:T(1024)(128)(4,1)S(1)}, s32[]{:S(2)}) async-start(s8[14680064]{0:T(1024)(128)(4,1)} %bitcast.3), calls=%async_computation | async-start | bytes 8388608
  20.1 5.0 %slice-start.1 = ((s8[14680064]{0:T(1024)(128)(4,1)}), s8[4194304]{0:T(1024)(128)(4,1)S(1)}, s32[]{:S(2)}) async-start(s8[14680064]{0:T(1024)(128)(4,1)} %bitcast.3), calls=%async_computation.1 | async-start | bytes 8388608
  20.2 5.0 %slice-start.2 = ((s8[14680064]{0:T(1024)(128)(4,1)}), s8[4194304]{0:T(1024)(128)(4,1)S(1)}, s32[]{:S(2)}) async-start(s8[14680064]{0:T(1024)(128)(4,1)} %bitcast.3), calls=%async_computation.2 | async-start | bytes 8388608
  20.2 5.0 %slice-start.3 = ((s8[14680064]{0:T(1024)(128)(4,1)}), s8[2097152]{0:T(1024)(128)(4,1)S(1)}, s32[]{:S(2)}) async-start(s8[14680064]{0:T(1024)(128)(4,1)} %bitcast.3), calls=%async_computation.3 | async-start | bytes 4194304
  27.4 1.4 %collective-permute-start.10 = (bf16[8,6272]{1,0:T(8,128)(2,1)S(1)}, bf16[8,6272]{1,0:T(8,128)(2,1)S(1)}, u32[]{:S(2)}, u32[]{:S(2)}) collective-permute-start(bf16[8,6272]{1,0:T(8,128)(2,1)S(1)} %get-tuple-element.28), channel_id=1, source_target_pairs={{0,1},{1,0},{2,3},{3,2},{4,5},{5,4},{6,7},{7,6},{8,9},{9,8},{10,11... | collective-permute-start | bytes 301064 | tf_op jit(solution)/shard_map/ppermute | solution.py:319
  28.9 2.2 %collective-permute-start.11 = (bf16[56,6272]{1,0:T(8,128)(2,1)S(1)}, bf16[56,6272]{1,0:T(8,128)(2,1)S(1)}, u32[]{:S(2)}, u32[]{:S(2)}) collective-permute-start(bf16[56,6272]{1,0:T(8,128)(2,1)S(1)} %stack.7), channel_id=1, source_target_pairs={{0,1},{1,0},{2,3},{3,2},{4,5},{5,4},{6,7},{7,6},{8,9},{9,8},{10,11... | collective-permute-start | bytes 2107400 | tf_op jit(solution)/shard_map/ppermute | solution.py:319
  29.3 4.9 %collective-permute-start.14 = (bf16[8,6272]{1,0:T(8,128)(2,1)S(1)}, bf16[8,6272]{1,0:T(8,128)(2,1)S(1)}, u32[]{:S(2)}, u32[]{:S(2)}) collective-permute-start(bf16[8,6272]{1,0:T(8,128)(2,1)S(1)} %pair_sum.4.refs_1_), channel_id=1, source_target_pairs={{0,2},{2,0},{4,6},{6,4},{8,10},{10,8},{12,14},{14,12},{1,3},{3,1},... | collective-permute-start | bytes 301064 | tf_op jit(solution)/shard_map/ppermute | solution.py:316
  31.1 5.9 %collective-permute-start.12 = (bf16[8,6272]{1,0:T(8,128)(2,1)S(1)}, bf16[8,6272]{1,0:T(8,128)(2,1)S(1)}, u32[]{:S(2)}, u32[]{:S(2)}) collective-permute-start(bf16[8,6272]{1,0:T(8,128)(2,1)S(1)} %get-tuple-element.31), channel_id=1, source_target_pairs={{0,2},{2,0},{4,6},{6,4},{8,10},{10,8},{12,14},{14,12},{1,3},{3,1},... | collective-permute-start | bytes 301064 | tf_op jit(solution)/shard_map/ppermute | solution.py:316
  32.7 7.2 %collective-permute-start.17 = (bf16[8,6272]{1,0:T(8,128)(2,1)S(1)}, bf16[8,6272]{1,0:T(8,128)(2,1)S(1)}, u32[]{:S(2)}, u32[]{:S(2)}) collective-permute-start(bf16[8,6272]{1,0:T(8,128)(2,1)S(1)} %get-tuple-element.34), channel_id=1, source_target_pairs={{0,2},{2,0},{4,6},{6,4},{8,10},{10,8},{12,14},{14,12},{1,3},{3,1},... | collective-permute-start | bytes 301064 | tf_op jit(solution)/shard_map/ppermute | solution.py:316
  34.2 7.5 %collective-permute-start.15 = (bf16[8,6272]{1,0:T(8,128)(2,1)S(1)}, bf16[8,6272]{1,0:T(8,128)(2,1)S(1)}, u32[]{:S(2)}, u32[]{:S(2)}) collective-permute-start(bf16[8,6272]{1,0:T(8,128)(2,1)S(1)} %span_sum.4), channel_id=1, source_target_pairs={{0,12},{2,14},{4,8},{6,10},{8,4},{10,6},{12,0},{14,2},{1,13},{3,15... | collective-permute-start | bytes 301064 | tf_op jit(solution)/shard_map/ppermute | solution.py:313
  37.1 4.7 %collective-permute-start.13 = (bf16[8,6272]{1,0:T(8,128)(2,1)S(1)}, bf16[8,6272]{1,0:T(8,128)(2,1)S(1)}, u32[]{:S(2)}, u32[]{:S(2)}) collective-permute-start(bf16[8,6272]{1,0:T(8,128)(2,1)S(1)} %pair_sum.7), channel_id=1, source_target_pairs={{0,2},{2,0},{4,6},{6,4},{8,10},{10,8},{12,14},{14,12},{1,3},{3,1},... | collective-permute-start | bytes 301064 | tf_op jit(solution)/shard_map/ppermute | solution.py:316
  38.5 7.2 %collective-permute-start.16 = (bf16[8,6272]{1,0:T(8,128)(2,1)S(1)}, bf16[8,6272]{1,0:T(8,128)(2,1)S(1)}, u32[]{:S(2)}, u32[]{:S(2)}) collective-permute-start(bf16[8,6272]{1,0:T(8,128)(2,1)S(1)} %span_sum.3.refs_1_), channel_id=1, source_target_pairs={{0,8},{2,10},{4,12},{6,14},{8,0},{10,2},{12,4},{14,6},{1,9},{3,11}... | collective-permute-start | bytes 301064 | tf_op jit(solution)/shard_map/ppermute | solution.py:313
  39.9 5.7 %collective-permute-start.18 = (bf16[8,6272]{1,0:T(8,128)(2,1)S(1)}, bf16[8,6272]{1,0:T(8,128)(2,1)S(1)}, u32[]{:S(2)}, u32[]{:S(2)}) collective-permute-start(bf16[8,6272]{1,0:T(8,128)(2,1)S(1)} %span_sum.5), channel_id=1, source_target_pairs={{0,4},{2,6},{4,0},{6,2},{8,12},{10,14},{12,8},{14,10},{1,5},{3,7},... | collective-permute-start | bytes 301064 | tf_op jit(solution)/shard_map/ppermute | solution.py:313

commit v16 on v15

--- a/solution.py
+++ b/solution.py
@@ -356,8 +356,8 @@
     send_rest([0], [totals[RETURN_ORDER[1]]])
     returned = {s: over_experts(totals[s], s) for s in RETURN_ORDER}
     far, *later = RETURN_ORDER
-    early = combine(sides, [], [0, far], [sums[0], [returned[far]]], width, jnp.float32)
-    return combine(sides, [early], later, [[returned[s]] for s in later], width, jnp.bfloat16, 2)
+    early = combine(sides, [], [far], [[returned[far]]], width, jnp.float32)
+    return combine(sides, [early], later + [0], [[returned[s]] for s in later] + [sums[0]], width, jnp.bfloat16, 2)
 
 
 def solution(mesh):

time: 46.6 us -> 46.6 us (level)
  no operation moved by 1% of the time
where the time goes in v16:
time: 46.6 us; the launch traced here: 46.5 us
  starting transfers between devices  24.2 us (52%)
  waiting for transfers between devices  12.6 us (27%)
  Pallas kernels  9.33 us (20%)
    ppermute x6, starting transfers between devices, over_experts(): lax.ppermute(value, 'attn', [(i, (i // span ^ other) * span + i % span) f...  11.8 us
    ppermute x8, starting transfers between devices, over_span(): lax.ppermute(value, 'attn', [(i, i // span * span + (i + shift) % span) f...  11.4 us
    ppermute x6, waiting for transfers between devices, over_experts(): lax.ppermute(value, 'attn', [(i, (i // span ^ other) * span + i % span) f...  6.66 us
    pallas_call x1, Pallas kernels, gate_up(): pl.pallas_call(functools.partial(gate_up_kernel, block_of(units, N_BLOCK)...  4.09 us
    ppermute x8, waiting for transfers between devices, over_span(): lax.ppermute(value, 'attn', [(i, i // span * span + (i + shift) % span) f...  3.9 us
    pallas_call x1, Pallas kernels, down(): pl.pallas_call(functools.partial(down_kernel, rows, sources), in_specs=[p...  2.21 us
    ppermute x5, waiting for transfers between devices, over_pair(): lax.ppermute(value, 'ffn', [(i, (i + shift) % pair) for i in range(pair)])  2 us
    pallas_call x1, Pallas kernels, pack(): pl.pallas_call(pack_kernel, in_specs=[pl.BlockSpec(memory_space=pltpu.SME...  1.3 us
  transfers between devices with their start and end apart: 19, of which 11 were waited for; matrix products, arithmetic and copies ran while one was open for 0% of the time, Pallas kernels for 2%

profile of v16, /device:TPU:0, one launch (start us, length us, event | category | flops | bytes accessed | tf_op | source)
XLA Modules:
  0.0 46.5 jit_solution(6540952514968452417)
XLA Ops:
  0.0 1.3 %pack.1 = (f32[8,1024]{1,0:T(8,128)S(1)}, bf16[8,6272]{1,0:T(8,128)(2,1)S(1)}, bf16[8,6272]{1,0:T(8,128)(2,1)S(1)}, bf16[8,6272]{1,0:T(8,128)(2,1)S(1)}, bf16[8,6272]{1,0:T(8,128)(2,1)S(1)}) custom-call(s32[1]{0:T(128)} %bitcast.own_expert, bf16[8,7168]{1,0:T(8,128)(2,1)} %tokens_hbm.1, s32[3,8]{1,0:T(4,128)} %bitcast.9, f32[3,8]{1,0:T(4,128)} %bitcast.10), custom_call_target="tpu_custom_call" | custom-call | flops 20000000000 | tf_op jit(solution)/shard_map/pack/pallas_call | solution.py:241
  1.4 5.1 %collective-permute-start = (bf16[8,6272]{1,0:T(8,128)(2,1)S(1)}, bf16[8,6272]{1,0:T(8,128)(2,1)S(1)}, u32[]{:S(2)}, u32[]{:S(2)}) collective-permute-start(bf16[8,6272]{1,0:T(8,128)(2,1)S(1)} %get-tuple-element.22), channel_id=1, source_target_pairs={{0,12},{2,14},{4,8},{6,10},{8,4},{10,6},{12,0},{14,2},{1,13},{3,15... | collective-permute-start | bytes 301064 | tf_op jit(solution)/shard_map/ppermute | solution.py:313
  6.5 0.6 %collective-permute-start.2 = (bf16[8,6272]{1,0:T(8,128)(2,1)S(1)}, bf16[8,6272]{1,0:T(8,128)(2,1)S(1)}, u32[]{:S(2)}, u32[]{:S(2)}) collective-permute-start(bf16[8,6272]{1,0:T(8,128)(2,1)S(1)} %get-tuple-element.24), channel_id=1, source_target_pairs={{0,8},{2,10},{4,12},{6,14},{8,0},{10,2},{12,4},{14,6},{1,9},{3,11}... | collective-permute-start | bytes 301064 | tf_op jit(solution)/shard_map/ppermute | solution.py:313
  7.1 1.7 %collective-permute-start.3 = (bf16[8,6272]{1,0:T(8,128)(2,1)S(1)}, bf16[8,6272]{1,0:T(8,128)(2,1)S(1)}, u32[]{:S(2)}, u32[]{:S(2)}) collective-permute-start(bf16[8,6272]{1,0:T(8,128)(2,1)S(1)} %get-tuple-element.21.refs_0_), channel_id=1, source_target_pairs={{0,2},{2,0},{4,6},{6,4},{8,10},{10,8},{12,14},{14,12},{1,3},{3,1},... | collective-permute-start | bytes 301064 | tf_op jit(solution)/shard_map/ppermute | solution.py:316
  8.8 1.4 %collective-permute-done.refs_1_ = bf16[8,6272]{1,0:T(8,128)(2,1)S(1)} collective-permute-done((bf16[8,6272]{1,0:T(8,128)(2,1)S(1)}, bf16[8,6272]{1,0:T(8,128)(2,1)S(1)}, u32[]{:S(2)}, u32[]{:S(2)}) %collective-permute-start) | collective-permute-done | bytes 100384 | tf_op jit(solution)/shard_map/ppermute | solution.py:313
  10.2 1.7 %collective-permute-start.4 = (bf16[8,6272]{1,0:T(8,128)(2,1)S(1)}, bf16[8,6272]{1,0:T(8,128)(2,1)S(1)}, u32[]{:S(2)}, u32[]{:S(2)}) collective-permute-start(bf16[8,6272]{1,0:T(8,128)(2,1)S(1)} %collective-permute-done.refs_1_), channel_id=1, source_target_pairs={{0,2},{2,0},{4,6},{6,4},{8,10},{10,8},{12,14},{14,12},{1,3},{3,1},... | collective-permute-start | bytes 301064 | tf_op jit(solution)/shard_map/ppermute | solution.py:316
  11.9 0.7 %collective-permute-done.1.refs_2_ = bf16[8,6272]{1,0:T(8,128)(2,1)S(1)} collective-permute-done((bf16[8,6272]{1,0:T(8,128)(2,1)S(1)}, bf16[8,6272]{1,0:T(8,128)(2,1)S(1)}, u32[]{:S(2)}, u32[]{:S(2)}) %collective-permute-start.1) | collective-permute-done | bytes 100384 | tf_op jit(solution)/shard_map/ppermute | solution.py:313
  12.6 1.5 %collective-permute-start.5 = (bf16[8,6272]{1,0:T(8,128)(2,1)S(1)}, bf16[8,6272]{1,0:T(8,128)(2,1)S(1)}, u32[]{:S(2)}, u32[]{:S(2)}) collective-permute-start(bf16[8,6272]{1,0:T(8,128)(2,1)S(1)} %collective-permute-done.1.refs_2_), channel_id=1, source_target_pairs={{0,2},{2,0},{4,6},{6,4},{8,10},{10,8},{12,14},{14,12},{1,3},{3,1},... | collective-permute-start | bytes 301064 | tf_op jit(solution)/shard_map/ppermute | solution.py:316
  14.1 0.8 %collective-permute-done.2.refs_3_ = bf16[8,6272]{1,0:T(8,128)(2,1)S(1)} collective-permute-done((bf16[8,6272]{1,0:T(8,128)(2,1)S(1)}, bf16[8,6272]{1,0:T(8,128)(2,1)S(1)}, u32[]{:S(2)}, u32[]{:S(2)}) %collective-permute-start.2) | collective-permute-done | bytes 100384 | tf_op jit(solution)/shard_map/ppermute | solution.py:313
  14.9 1.5 %collective-permute-start.6 = (bf16[8,6272]{1,0:T(8,128)(2,1)S(1)}, bf16[8,6272]{1,0:T(8,128)(2,1)S(1)}, u32[]{:S(2)}, u32[]{:S(2)}) collective-permute-start(bf16[8,6272]{1,0:T(8,128)(2,1)S(1)} %collective-permute-done.2.refs_3_), channel_id=1, source_target_pairs={{0,2},{2,0},{4,6},{6,4},{8,10},{10,8},{12,14},{14,12},{1,3},{3,1},... | collective-permute-start | bytes 301064 | tf_op jit(solution)/shard_map/ppermute | solution.py:316
  16.6 1.0 %collective-permute-done.5.refs_2_.refs_6_ = bf16[8,6272]{1,0:T(8,128)(2,1)S(1)} collective-permute-done((bf16[8,6272]{1,0:T(8,128)(2,1)S(1)}, bf16[8,6272]{1,0:T(8,128)(2,1)S(1)}, u32[]{:S(2)}, u32[]{:S(2)}) %collective-permute-start.5) | collective-permute-done | bytes 100384 | tf_op jit(solution)/shard_map/ppermute | solution.py:316
  17.7 1.9 %collective-permute-done.6.refs_7_.refs_0_ = bf16[8,6272]{1,0:T(8,128)(2,1)S(1)} collective-permute-done((bf16[8,6272]{1,0:T(8,128)(2,1)S(1)}, bf16[8,6272]{1,0:T(8,128)(2,1)S(1)}, u32[]{:S(2)}, u32[]{:S(2)}) %collective-permute-start.6) | collective-permute-done | bytes 100384 | tf_op jit(solution)/shard_map/ppermute | solution.py:316
  19.7 0.5 unpack.1.first_ref
  20.2 0.8 %collective-permute-done.9.last_ref = bf16[8,6272]{1,0:T(8,128)(2,1)S(1)} collective-permute-done((bf16[8,6272]{1,0:T(8,128)(2,1)S(1)}, bf16[8,6272]{1,0:T(8,128)(2,1)S(1)}, u32[]{:S(2)}, u32[]{:S(2)}) %collective-permute-start.9) | collective-permute-done | bytes 100384 | tf_op jit(solution)/shard_map/ppermute | solution.py:319
  21.0 4.1 %gate_up.1.hidden_ref = bf16[128,1024]{1,0:T(8,128)(2,1)S(1)} custom-call(bf16[120,7168]{1,0:T(8,128)(2,1)S(1)} %unpack.1.first_ref, bf16[8,6272]{1,0:T(8,128)(2,1)S(1)} %collective-permute-done.9.last_ref, bf16[7168,1024]{1,0:T(8,128)(2,1)S(1)} %bitcast.6, bf16[7168,1024]{1,0:T(8,128)(2,1)S(1)} %bitcast.8), custom_call_target="tpu_custom_call" | custom-call | flops 3758096384 | tf_op jit(solution)/shard_map/gate_up/pallas_call | solution.py:113
  25.2 2.2 %down.1 = (f32[32,6272]{1,0:T(8,128)S(1)}, f32[32,6272]{1,0:T(8,128)S(1)}, bf16[8,6272]{1,0:T(8,128)(2,1)S(1)}, bf16[56,6272]{1,0:T(8,128)(2,1)S(1)}) custom-call(bf16[128,1024]{1,0:T(8,128)(2,1)S(1)} %gate_up.1.hidden_ref, bf16[1024,7168]{1,0:T(8,128)(2,1)S(1)} %bitcast.4), custom_call_target="tpu_custom_call" | custom-call | flops 1644167168 | tf_op jit(solution)/shard_map/down/pallas_call | solution.py:157
  27.4 0.4 collective-permute-start.10
  27.8 0.9 %collective-permute-done.10.refs_0_ = bf16[8,6272]{1,0:T(8,128)(2,1)S(1)} collective-permute-done((bf16[8,6272]{1,0:T(8,128)(2,1)S(1)}, bf16[8,6272]{1,0:T(8,128)(2,1)S(1)}, u32[]{:S(2)}, u32[]{:S(2)}) %collective-permute-start.10) | collective-permute-done | bytes 100384 | tf_op jit(solution)/shard_map/ppermute | solution.py:319
  28.9 0.4 collective-permute-start.11
  29.3 1.5 %collective-permute-start.12 = (bf16[8,6272]{1,0:T(8,128)(2,1)S(1)}, bf16[8,6272]{1,0:T(8,128)(2,1)S(1)}, u32[]{:S(2)}, u32[]{:S(2)}) collective-permute-start(bf16[8,6272]{1,0:T(8,128)(2,1)S(1)} %pair_sum.4.refs_1_), channel_id=1, source_target_pairs={{0,2},{2,0},{4,6},{6,4},{8,10},{10,8},{12,14},{14,12},{1,3},{3,1},... | collective-permute-start | bytes 301064 | tf_op jit(solution)/shard_map/ppermute | solution.py:316
  30.8 0.3 collective-permute-done.11.refs_0_
  31.1 1.6 %collective-permute-start.14 = (bf16[8,6272]{1,0:T(8,128)(2,1)S(1)}, bf16[8,6272]{1,0:T(8,128)(2,1)S(1)}, u32[]{:S(2)}, u32[]{:S(2)}) collective-permute-start(bf16[8,6272]{1,0:T(8,128)(2,1)S(1)} %get-tuple-element.31), channel_id=1, source_target_pairs={{0,2},{2,0},{4,6},{6,4},{8,10},{10,8},{12,14},{14,12},{1,3},{3,1},... | collective-permute-start | bytes 301064 | tf_op jit(solution)/shard_map/ppermute | solution.py:316
  32.7 0.5 %collective-permute-start.16 = (bf16[8,6272]{1,0:T(8,128)(2,1)S(1)}, bf16[8,6272]{1,0:T(8,128)(2,1)S(1)}, u32[]{:S(2)}, u32[]{:S(2)}) collective-permute-start(bf16[8,6272]{1,0:T(8,128)(2,1)S(1)} %get-tuple-element.33), channel_id=1, source_target_pairs={{0,2},{2,0},{4,6},{6,4},{8,10},{10,8},{12,14},{14,12},{1,3},{3,1},... | collective-permute-start | bytes 301064 | tf_op jit(solution)/shard_map/ppermute | solution.py:316
  33.3 0.9 %collective-permute-done.12.refs_1_ = bf16[8,6272]{1,0:T(8,128)(2,1)S(1)} collective-permute-done((bf16[8,6272]{1,0:T(8,128)(2,1)S(1)}, bf16[8,6272]{1,0:T(8,128)(2,1)S(1)}, u32[]{:S(2)}, u32[]{:S(2)}) %collective-permute-start.12) | collective-permute-done | bytes 100384 | tf_op jit(solution)/shard_map/ppermute | solution.py:316
  34.2 2.9 %collective-permute-start.13 = (bf16[8,6272]{1,0:T(8,128)(2,1)S(1)}, bf16[8,6272]{1,0:T(8,128)(2,1)S(1)}, u32[]{:S(2)}, u32[]{:S(2)}) collective-permute-start(bf16[8,6272]{1,0:T(8,128)(2,1)S(1)} %span_sum.3), channel_id=1, source_target_pairs={{0,12},{2,14},{4,8},{6,10},{8,4},{10,6},{12,0},{14,2},{1,13},{3,15... | collective-permute-start | bytes 301064 | tf_op jit(solution)/shard_map/ppermute | solution.py:313
  37.1 1.2 %collective-permute-start.15 = (bf16[8,6272]{1,0:T(8,128)(2,1)S(1)}, bf16[8,6272]{1,0:T(8,128)(2,1)S(1)}, u32[]{:S(2)}, u32[]{:S(2)}) collective-permute-start(bf16[8,6272]{1,0:T(8,128)(2,1)S(1)} %span_sum.4.refs_1_), channel_id=1, source_target_pairs={{0,8},{2,10},{4,12},{6,14},{8,0},{10,2},{12,4},{14,6},{1,9},{3,11}... | collective-permute-start | bytes 301064 | tf_op jit(solution)/shard_map/ppermute | solution.py:313
  38.3 0.1 collective-permute-done.16.refs_1_
  38.5 1.9 %collective-permute-start.17 = (bf16[8,6272]{1,0:T(8,128)(2,1)S(1)}, bf16[8,6272]{1,0:T(8,128)(2,1)S(1)}, u32[]{:S(2)}, u32[]{:S(2)}) collective-permute-start(bf16[8,6272]{1,0:T(8,128)(2,1)S(1)} %span_sum.5), channel_id=1, source_target_pairs={{0,4},{2,6},{4,0},{6,2},{8,12},{10,14},{12,8},{14,10},{1,5},{3,7},... | collective-permute-start | bytes 301064 | tf_op jit(solution)/shard_map/ppermute | solution.py:313
  40.4 1.4 %collective-permute-start.18 = (bf16[8,6272]{1,0:T(8,128)(2,1)S(1)}, bf16[8,6272]{1,0:T(8,128)(2,1)S(1)}, u32[]{:S(2)}, u32[]{:S(2)}) collective-permute-start(bf16[8,6272]{1,0:T(8,128)(2,1)S(1)} %pair_sum.7), channel_id=1, source_target_pairs={{0,2},{2,0},{4,6},{6,4},{8,10},{10,8},{12,14},{14,12},{1,3},{3,1},... | collective-permute-start | bytes 301064 | tf_op jit(solution)/shard_map/ppermute | solution.py:316
  41.8 0.1 combine.2.refs_0_
  41.9 3.8 %collective-permute-done.15.refs_1_ = bf16[8,6272]{1,0:T(8,128)(2,1)S(1)} collective-permute-done((bf16[8,6272]{1,0:T(8,128)(2,1)S(1)}, bf16[8,6272]{1,0:T(8,128)(2,1)S(1)}, u32[]{:S(2)}, u32[]{:S(2)}) %collective-permute-start.15) | collective-permute-done | bytes 100384 | tf_op jit(solution)/shard_map/ppermute | solution.py:313
  45.7 0.8 %combine.3 = bf16[8,7168]{1,0:T(8,128)(2,1)} custom-call(f32[8,1024]{1,0:T(8,128)S(1)} %get-tuple-element.20.sides_ref, f32[8,7168]{1,0:T(8,128)S(1)} %combine.2.refs_0_, bf16[8,6272]{1,0:T(8,128)(2,1)S(1)} %collective-permute-done.15.refs_1_, bf16[8,6272]{1,0:T(8,128)(2,1)S(1)} %collective-permute-done.17.refs_2_, f32[8,6272]{1,0:T(8,128)S(1)} %get-tuple-element.34.refs_3_, ...), custom_call_target="tpu_custom_call" | custom-call | tf_op jit(solution)/shard_map/combine/pallas_call | solution.py:296
  (50 shorter events, 0.6 us)
Async XLA Ops:
  0.0 20.9 %slice-start.4 = ((s8[14680064]{0:T(1024)(128)(4,1)}), s8[4194304]{0:T(1024)(128)(4,1)S(1)}, s32[]{:S(2)}) async-start(s8[14680064]{0:T(1024)(128)(4,1)} %bitcast.5), calls=%async_computation.4 | async-start | bytes 8388608
  0.0 20.9 %slice-start.8 = ((s8[14680064]{0:T(1024)(128)(4,1)}), s8[4194304]{0:T(1024)(128)(4,1)S(1)}, s32[]{:S(2)}) async-start(s8[14680064]{0:T(1024)(128)(4,1)} %bitcast.7), calls=%async_computation.8 | async-start | bytes 8388608
  0.0 20.9 %slice-start.5 = ((s8[14680064]{0:T(1024)(128)(4,1)}), s8[4194304]{0:T(1024)(128)(4,1)S(1)}, s32[]{:S(2)}) async-start(s8[14680064]{0:T(1024)(128)(4,1)} %bitcast.5), calls=%async_computation.5 | async-start | bytes 8388608
  0.0 20.9 %slice-start.6 = ((s8[14680064]{0:T(1024)(128)(4,1)}), s8[4194304]{0:T(1024)(128)(4,1)S(1)}, s32[]{:S(2)}) async-start(s8[14680064]{0:T(1024)(128)(4,1)} %bitcast.5), calls=%async_computation.6 | async-start | bytes 8388608
  0.0 21.0 %slice-start.7 = ((s8[14680064]{0:T(1024)(128)(4,1)}), s8[2097152]{0:T(1024)(128)(4,1)S(1)}, s32[]{:S(2)}) async-start(s8[14680064]{0:T(1024)(128)(4,1)} %bitcast.5), calls=%async_computation.7 | async-start | bytes 4194304
  0.0 21.0 %slice-start.9 = ((s8[14680064]{0:T(1024)(128)(4,1)}), s8[4194304]{0:T(1024)(128)(4,1)S(1)}, s32[]{:S(2)}) async-start(s8[14680064]{0:T(1024)(128)(4,1)} %bitcast.7), calls=%async_computation.9 | async-start | bytes 8388608
  0.0 21.0 %slice-start.10 = ((s8[14680064]{0:T(1024)(128)(4,1)}), s8[4194304]{0:T(1024)(128)(4,1)S(1)}, s32[]{:S(2)}) async-start(s8[14680064]{0:T(1024)(128)(4,1)} %bitcast.7), calls=%async_computation.10 | async-start | bytes 8388608
  0.0 21.0 %slice-start.11 = ((s8[14680064]{0:T(1024)(128)(4,1)}), s8[2097152]{0:T(1024)(128)(4,1)S(1)}, s32[]{:S(2)}) async-start(s8[14680064]{0:T(1024)(128)(4,1)} %bitcast.7), calls=%async_computation.11 | async-start | bytes 4194304
  1.4 8.8 %collective-permute-start = (bf16[8,6272]{1,0:T(8,128)(2,1)S(1)}, bf16[8,6272]{1,0:T(8,128)(2,1)S(1)}, u32[]{:S(2)}, u32[]{:S(2)}) collective-permute-start(bf16[8,6272]{1,0:T(8,128)(2,1)S(1)} %get-tuple-element.22), channel_id=1, source_target_pairs={{0,12},{2,14},{4,8},{6,10},{8,4},{10,6},{12,0},{14,2},{1,13},{3,15... | collective-permute-start | bytes 301064 | tf_op jit(solution)/shard_map/ppermute | solution.py:313
  6.5 6.1 %collective-permute-start.1 = (bf16[8,6272]{1,0:T(8,128)(2,1)S(1)}, bf16[8,6272]{1,0:T(8,128)(2,1)S(1)}, u32[]{:S(2)}, u32[]{:S(2)}) collective-permute-start(bf16[8,6272]{1,0:T(8,128)(2,1)S(1)} %get-tuple-element.23), channel_id=1, source_target_pairs={{0,4},{2,6},{4,0},{6,2},{8,12},{10,14},{12,8},{14,10},{1,5},{3,7},... | collective-permute-start | bytes 301064 | tf_op jit(solution)/shard_map/ppermute | solution.py:313
  6.5 8.4 %collective-permute-start.2 = (bf16[8,6272]{1,0:T(8,128)(2,1)S(1)}, bf16[8,6272]{1,0:T(8,128)(2,1)S(1)}, u32[]{:S(2)}, u32[]{:S(2)}) collective-permute-start(bf16[8,6272]{1,0:T(8,128)(2,1)S(1)} %get-tuple-element.24), channel_id=1, source_target_pairs={{0,8},{2,10},{4,12},{6,14},{8,0},{10,2},{12,4},{14,6},{1,9},{3,11}... | collective-permute-start | bytes 301064 | tf_op jit(solution)/shard_map/ppermute | solution.py:313
  7.1 9.4 %collective-permute-start.3 = (bf16[8,6272]{1,0:T(8,128)(2,1)S(1)}, bf16[8,6272]{1,0:T(8,128)(2,1)S(1)}, u32[]{:S(2)}, u32[]{:S(2)}) collective-permute-start(bf16[8,6272]{1,0:T(8,128)(2,1)S(1)} %get-tuple-element.21.refs_0_), channel_id=1, source_target_pairs={{0,2},{2,0},{4,6},{6,4},{8,10},{10,8},{12,14},{14,12},{1,3},{3,1},... | collective-permute-start | bytes 301064 | tf_op jit(solution)/shard_map/ppermute | solution.py:316
  10.2 6.4 %collective-permute-start.4 = (bf16[8,6272]{1,0:T(8,128)(2,1)S(1)}, bf16[8,6272]{1,0:T(8,128)(2,1)S(1)}, u32[]{:S(2)}, u32[]{:S(2)}) collective-permute-start(bf16[8,6272]{1,0:T(8,128)(2,1)S(1)} %collective-permute-done.refs_1_), channel_id=1, source_target_pairs={{0,2},{2,0},{4,6},{6,4},{8,10},{10,8},{12,14},{14,12},{1,3},{3,1},... | collective-permute-start | bytes 301064 | tf_op jit(solution)/shard_map/ppermute | solution.py:316
  12.6 5.0 %collective-permute-start.5 = (bf16[8,6272]{1,0:T(8,128)(2,1)S(1)}, bf16[8,6272]{1,0:T(8,128)(2,1)S(1)}, u32[]{:S(2)}, u32[]{:S(2)}) collective-permute-start(bf16[8,6272]{1,0:T(8,128)(2,1)S(1)} %collective-permute-done.1.refs_2_), channel_id=1, source_target_pairs={{0,2},{2,0},{4,6},{6,4},{8,10},{10,8},{12,14},{14,12},{1,3},{3,1},... | collective-permute-start | bytes 301064 | tf_op jit(solution)/shard_map/ppermute | solution.py:316
  14.9 4.6 %collective-permute-start.6 = (bf16[8,6272]{1,0:T(8,128)(2,1)S(1)}, bf16[8,6272]{1,0:T(8,128)(2,1)S(1)}, u32[]{:S(2)}, u32[]{:S(2)}) collective-permute-start(bf16[8,6272]{1,0:T(8,128)(2,1)S(1)} %collective-permute-done.2.refs_3_), channel_id=1, source_target_pairs={{0,2},{2,0},{4,6},{6,4},{8,10},{10,8},{12,14},{14,12},{1,3},{3,1},... | collective-permute-start | bytes 301064 | tf_op jit(solution)/shard_map/ppermute | solution.py:316
  16.5 3.2 %collective-permute-start.7 = (bf16[32,6272]{1,0:T(8,128)(2,1)S(1)}, bf16[32,6272]{1,0:T(8,128)(2,1)S(1)}, u32[]{:S(2)}, u32[]{:S(2)}) collective-permute-start(bf16[32,6272]{1,0:T(8,128)(2,1)S(1)} %stack.4), channel_id=1, source_target_pairs={{0,1},{1,0},{2,3},{3,2},{4,5},{5,4},{6,7},{7,6},{8,9},{9,8},{10,11... | collective-permute-start | bytes 1204232 | tf_op jit(solution)/shard_map/ppermute | solution.py:319
  17.6 2.1 %collective-permute-start.8 = (bf16[24,6272]{1,0:T(8,128)(2,1)S(1)}, bf16[24,6272]{1,0:T(8,128)(2,1)S(1)}, u32[]{:S(2)}, u32[]{:S(2)}) collective-permute-start(bf16[24,6272]{1,0:T(8,128)(2,1)S(1)} %stack.5), channel_id=1, source_target_pairs={{0,1},{1,0},{2,3},{3,2},{4,5},{5,4},{6,7},{7,6},{8,9},{9,8},{10,11... | collective-permute-start | bytes 903176 | tf_op jit(solution)/shard_map/ppermute | solution.py:319
  19.6 1.4 %collective-permute-start.9 = (bf16[8,6272]{1,0:T(8,128)(2,1)S(1)}, bf16[8,6272]{1,0:T(8,128)(2,1)S(1)}, u32[]{:S(2)}, u32[]{:S(2)}) collective-permute-start(bf16[8,6272]{1,0:T(8,128)(2,1)S(1)} %stack.6), channel_id=1, source_target_pairs={{0,1},{1,0},{2,3},{3,2},{4,5},{5,4},{6,7},{7,6},{8,9},{9,8},{10,11... | collective-permute-start | bytes 301064 | tf_op jit(solution)/shard_map/ppermute | solution.py:319
  19.7 5.4 %slice-start = ((s8[14680064]{0:T(1024)(128)(4,1)}), s8[4194304]{0:T(1024)(128)(4,1)S(1)}, s32[]{:S(2)}) async-start(s8[14680064]{0:T(1024)(128)(4,1)} %bitcast.3), calls=%async_computation | async-start | bytes 8388608
  20.1 5.0 %slice-start.1 = ((s8[14680064]{0:T(1024)(128)(4,1)}), s8[4194304]{0:T(1024)(128)(4,1)S(1)}, s32[]{:S(2)}) async-start(s8[14680064]{0:T(1024)(128)(4,1)} %bitcast.3), calls=%async_computation.1 | async-start | bytes 8388608
  20.2 5.0 %slice-start.2 = ((s8[14680064]{0:T(1024)(128)(4,1)}), s8[4194304]{0:T(1024)(128)(4,1)S(1)}, s32[]{:S(2)}) async-start(s8[14680064]{0:T(1024)(128)(4,1)} %bitcast.3), calls=%async_computation.2 | async-start | bytes 8388608
  20.2 5.0 %slice-start.3 = ((s8[14680064]{0:T(1024)(128)(4,1)}), s8[2097152]{0:T(1024)(128)(4,1)S(1)}, s32[]{:S(2)}) async-start(s8[14680064]{0:T(1024)(128)(4,1)} %bitcast.3), calls=%async_computation.3 | async-start | bytes 4194304
  27.4 1.4 %collective-permute-start.10 = (bf16[8,6272]{1,0:T(8,128)(2,1)S(1)}, bf16[8,6272]{1,0:T(8,128)(2,1)S(1)}, u32[]{:S(2)}, u32[]{:S(2)}) collective-permute-start(bf16[8,6272]{1,0:T(8,128)(2,1)S(1)} %get-tuple-element.28), channel_id=1, source_target_pairs={{0,1},{1,0},{2,3},{3,2},{4,5},{5,4},{6,7},{7,6},{8,9},{9,8},{10,11... | collective-permute-start | bytes 301064 | tf_op jit(solution)/shard_map/ppermute | solution.py:319
  28.9 2.2 %collective-permute-start.11 = (bf16[56,6272]{1,0:T(8,128)(2,1)S(1)}, bf16[56,6272]{1,0:T(8,128)(2,1)S(1)}, u32[]{:S(2)}, u32[]{:S(2)}) collective-permute-start(bf16[56,6272]{1,0:T(8,128)(2,1)S(1)} %stack.7), channel_id=1, source_target_pairs={{0,1},{1,0},{2,3},{3,2},{4,5},{5,4},{6,7},{7,6},{8,9},{9,8},{10,11... | collective-permute-start | bytes 2107400 | tf_op jit(solution)/shard_map/ppermute | solution.py:319
  29.3 4.9 %collective-permute-start.12 = (bf16[8,6272]{1,0:T(8,128)(2,1)S(1)}, bf16[8,6272]{1,0:T(8,128)(2,1)S(1)}, u32[]{:S(2)}, u32[]{:S(2)}) collective-permute-start(bf16[8,6272]{1,0:T(8,128)(2,1)S(1)} %pair_sum.4.refs_1_), channel_id=1, source_target_pairs={{0,2},{2,0},{4,6},{6,4},{8,10},{10,8},{12,14},{14,12},{1,3},{3,1},... | collective-permute-start | bytes 301064 | tf_op jit(solution)/shard_map/ppermute | solution.py:316
  31.1 5.9 %collective-permute-start.14 = (bf16[8,6272]{1,0:T(8,128)(2,1)S(1)}, bf16[8,6272]{1,0:T(8,128)(2,1)S(1)}, u32[]{:S(2)}, u32[]{:S(2)}) collective-permute-start(bf16[8,6272]{1,0:T(8,128)(2,1)S(1)} %get-tuple-element.31), channel_id=1, source_target_pairs={{0,2},{2,0},{4,6},{6,4},{8,10},{10,8},{12,14},{14,12},{1,3},{3,1},... | collective-permute-start | bytes 301064 | tf_op jit(solution)/shard_map/ppermute | solution.py:316
  32.7 5.8 %collective-permute-start.16 = (bf16[8,6272]{1,0:T(8,128)(2,1)S(1)}, bf16[8,6272]{1,0:T(8,128)(2,1)S(1)}, u32[]{:S(2)}, u32[]{:S(2)}) collective-permute-start(bf16[8,6272]{1,0:T(8,128)(2,1)S(1)} %get-tuple-element.33), channel_id=1, source_target_pairs={{0,2},{2,0},{4,6},{6,4},{8,10},{10,8},{12,14},{14,12},{1,3},{3,1},... | collective-permute-start | bytes 301064 | tf_op jit(solution)/shard_map/ppermute | solution.py:316
  34.2 7.6 %collective-permute-start.13 = (bf16[8,6272]{1,0:T(8,128)(2,1)S(1)}, bf16[8,6272]{1,0:T(8,128)(2,1)S(1)}, u32[]{:S(2)}, u32[]{:S(2)}) collective-permute-start(bf16[8,6272]{1,0:T(8,128)(2,1)S(1)} %span_sum.3), channel_id=1, source_target_pairs={{0,12},{2,14},{4,8},{6,10},{8,4},{10,6},{12,0},{14,2},{1,13},{3,15... | collective-permute-start | bytes 301064 | tf_op jit(solution)/shard_map/ppermute | solution.py:313
  37.1 8.6 %collective-permute-start.15 = (bf16[8,6272]{1,0:T(8,128)(2,1)S(1)}, bf16[8,6272]{1,0:T(8,128)(2,1)S(1)}, u32[]{:S(2)}, u32[]{:S(2)}) collective-permute-start(bf16[8,6272]{1,0:T(8,128)(2,1)S(1)} %span_sum.4.refs_1_), channel_id=1, source_target_pairs={{0,8},{2,10},{4,12},{6,14},{8,0},{10,2},{12,4},{14,6},{1,9},{3,11}... | collective-permute-start | bytes 301064 | tf_op jit(solution)/shard_map/ppermute | solution.py:313
  38.5 7.1 %collective-permute-start.17 = (bf16[8,6272]{1,0:T(8,128)(2,1)S(1)}, bf16[8,6272]{1,0:T(8,128)(2,1)S(1)}, u32[]{:S(2)}, u32[]{:S(2)}) collective-permute-start(bf16[8,6272]{1,0:T(8,128)(2,1)S(1)} %span_sum.5), channel_id=1, source_target_pairs={{0,4},{2,6},{4,0},{6,2},{8,12},{10,14},{12,8},{14,10},{1,5},{3,7},... | collective-permute-start | bytes 301064 | tf_op jit(solution)/shard_map/ppermute | solution.py:313
  40.4 5.2 %collective-permute-start.18 = (bf16[8,6272]{1,0:T(8,128)(2,1)S(1)}, bf16[8,6272]{1,0:T(8,128)(2,1)S(1)}, u32[]{:S(2)}, u32[]{:S(2)}) collective-permute-start(bf16[8,6272]{1,0:T(8,128)(2,1)S(1)} %pair_sum.7), channel_id=1, source_target_pairs={{0,2},{2,0},{4,6},{6,4},{8,10},{10,8},{12,14},{14,12},{1,3},{3,1},... | collective-permute-start | bytes 301064 | tf_op jit(solution)/shard_map/ppermute | solution.py:316

commit v17 on v16

--- a/solution.py
+++ b/solution.py
@@ -202,14 +202,29 @@
     )(*arrays)
 
 
-def pack_kernel(own_expert, tokens_hbm, ids_hbm, weights_hbm, sides_ref, *refs):
-    packed_refs, (tokens_ref, ids_ref, weights_ref, semaphores) = refs[:EXPERTS], refs[EXPERTS:]
-    pairs = [(tokens_hbm, tokens_ref), (ids_hbm, ids_ref), (weights_hbm, weights_ref)]
-    copies = [pltpu.make_async_copy(src, dst, semaphores.at[i]) for i, (src, dst) in enumerate(pairs)]
+def load_kernel(count, *refs):
+    semaphores = refs[-1]
+    copies = [pltpu.make_async_copy(refs[i], refs[count + i], semaphores.at[i]) for i in range(count)]
     for copy in copies:
         copy.start()
     for copy in copies:
         copy.wait()
+
+
+def load(arrays):
+    return pl.pallas_call(
+        functools.partial(load_kernel, len(arrays)),
+        in_specs=[pl.BlockSpec(memory_space=pl.ANY)] * len(arrays),
+        out_specs=[pl.BlockSpec(memory_space=pltpu.VMEM)] * len(arrays),
+        out_shape=[jax.ShapeDtypeStruct(a.shape, a.dtype) for a in arrays],
+        scratch_shapes=[pltpu.SemaphoreType.DMA((len(arrays),))],
+        compiler_params=params(),
+        cost_estimate=cost(0),
+        name="load",
+    )(*[pltpu.with_memory_space_constraint(a, pltpu.HBM) for a in arrays])
+
+
+def pack_kernel(own_expert, tokens_ref, ids_ref, weights_ref, sides_ref, *packed_refs):
     ids, weights = ids_ref[...], weights_ref[...]
     rows, width = tokens_ref.shape
     tail = width // rows
@@ -237,16 +252,14 @@
 def pack(own_expert, tokens, ids, weights):
     rows, width = tokens.shape
     packed = jax.ShapeDtypeStruct((rows, width - width // rows), jnp.bfloat16)
-    inputs = [tokens, ids.T, weights.T]
     return pl.pallas_call(
         pack_kernel,
-        in_specs=[pl.BlockSpec(memory_space=pltpu.SMEM)] + [pl.BlockSpec(memory_space=pl.ANY)] * 3,
+        in_specs=[pl.BlockSpec(memory_space=pltpu.SMEM)] + [pl.BlockSpec(memory_space=pltpu.VMEM)] * 3,
         out_shape=[jax.ShapeDtypeStruct((rows, 2 * EXPERTS * LANES), jnp.float32)] + [packed] * EXPERTS,
-        scratch_shapes=[pltpu.VMEM(a.shape, a.dtype) for a in inputs] + [pltpu.SemaphoreType.DMA((len(inputs),))],
         compiler_params=params(),
         cost_estimate=cost(EXCHANGE_FLOPS),
         name="pack",
-    )(own_expert, *[pltpu.with_memory_space_constraint(a, pltpu.HBM) for a in inputs])
+    )(own_expert, *load([tokens, ids.T, weights.T]))
 
 
 def combine_kernel(base, places, counts, parts, sides_ref, *refs):

time: 46.6 us -> 46.5 us (level)
    pallas_call x1, Pallas kernels: 1.3 us -> 0.22 us  [pack(): pl.pallas_call(pack_kernel, in_specs=[pl.BlockSpec(memory_space=pltpu.SME...]
    pallas_call x0 -> x1, Pallas kernels: none -> 0.93 us  [load(): pl.pallas_call(functools.partial(load_kernel, len(arrays)), in_specs=[pl....]
where the time goes in v17:
time: 46.5 us; the launch traced here: 46.4 us
  starting transfers between devices  24.2 us (52%)
  waiting for transfers between devices  12.6 us (27%)
  Pallas kernels  9.19 us (20%)
    ppermute x6, starting transfers between devices, over_experts(): lax.ppermute(value, 'attn', [(i, (i // span ^ other) * span + i % span) f...  11.8 us
    ppermute x8, starting transfers between devices, over_span(): lax.ppermute(value, 'attn', [(i, i // span * span + (i + shift) % span) f...  11.4 us
    ppermute x6, waiting for transfers between devices, over_experts(): lax.ppermute(value, 'attn', [(i, (i // span ^ other) * span + i % span) f...  6.66 us
    pallas_call x1, Pallas kernels, gate_up(): pl.pallas_call(functools.partial(gate_up_kernel, block_of(units, N_BLOCK)...  4.09 us
    ppermute x8, waiting for transfers between devices, over_span(): lax.ppermute(value, 'attn', [(i, i // span * span + (i + shift) % span) f...  3.89 us
    pallas_call x1, Pallas kernels, down(): pl.pallas_call(functools.partial(down_kernel, rows, sources), in_specs=[p...  2.21 us
    ppermute x5, waiting for transfers between devices, over_pair(): lax.ppermute(value, 'ffn', [(i, (i + shift) % pair) for i in range(pair)])  2 us
    ppermute x5, starting transfers between devices, over_pair(): lax.ppermute(value, 'ffn', [(i, (i + shift) % pair) for i in range(pair)])  1.07 us
  transfers between devices with their start and end apart: 19, of which 11 were waited for; matrix products, arithmetic and copies ran while one was open for 0% of the time, Pallas kernels for 2%

profile of v17, /device:TPU:0, one launch (start us, length us, event | category | flops | bytes accessed | tf_op | source)
XLA Modules:
  0.0 46.4 jit_solution(18324951092023532020)
XLA Ops:
  0.0 0.9 %load.1 = (bf16[8,7168]{1,0:T(8,128)(2,1)S(1)}, s32[3,8]{1,0:T(4,128)S(1)}, f32[3,8]{1,0:T(4,128)S(1)}) custom-call(bf16[8,7168]{1,0:T(8,128)(2,1)} %refs_0_.1, s32[3,8]{1,0:T(4,128)} %bitcast.9, f32[3,8]{1,0:T(4,128)} %bitcast.10), custom_call_target="tpu_custom_call" | custom-call | tf_op jit(solution)/shard_map/load/pallas_call | solution.py:215
  1.0 0.2 pack.1
  1.3 5.1 %collective-permute-start = (bf16[8,6272]{1,0:T(8,128)(2,1)S(1)}, bf16[8,6272]{1,0:T(8,128)(2,1)S(1)}, u32[]{:S(2)}, u32[]{:S(2)}) collective-permute-start(bf16[8,6272]{1,0:T(8,128)(2,1)S(1)} %get-tuple-element.28), channel_id=1, source_target_pairs={{0,12},{2,14},{4,8},{6,10},{8,4},{10,6},{12,0},{14,2},{1,13},{3,15... | collective-permute-start | bytes 301064 | tf_op jit(solution)/shard_map/ppermute | solution.py:326
  6.4 0.6 %collective-permute-start.2 = (bf16[8,6272]{1,0:T(8,128)(2,1)S(1)}, bf16[8,6272]{1,0:T(8,128)(2,1)S(1)}, u32[]{:S(2)}, u32[]{:S(2)}) collective-permute-start(bf16[8,6272]{1,0:T(8,128)(2,1)S(1)} %get-tuple-element.30), channel_id=1, source_target_pairs={{0,8},{2,10},{4,12},{6,14},{8,0},{10,2},{12,4},{14,6},{1,9},{3,11}... | collective-permute-start | bytes 301064 | tf_op jit(solution)/shard_map/ppermute | solution.py:326
  7.0 1.7 %collective-permute-start.3 = (bf16[8,6272]{1,0:T(8,128)(2,1)S(1)}, bf16[8,6272]{1,0:T(8,128)(2,1)S(1)}, u32[]{:S(2)}, u32[]{:S(2)}) collective-permute-start(bf16[8,6272]{1,0:T(8,128)(2,1)S(1)} %get-tuple-element.27.refs_0_), channel_id=1, source_target_pairs={{0,2},{2,0},{4,6},{6,4},{8,10},{10,8},{12,14},{14,12},{1,3},{3,1},... | collective-permute-start | bytes 301064 | tf_op jit(solution)/shard_map/ppermute | solution.py:329
  8.7 1.4 %collective-permute-done.refs_1_ = bf16[8,6272]{1,0:T(8,128)(2,1)S(1)} collective-permute-done((bf16[8,6272]{1,0:T(8,128)(2,1)S(1)}, bf16[8,6272]{1,0:T(8,128)(2,1)S(1)}, u32[]{:S(2)}, u32[]{:S(2)}) %collective-permute-start) | collective-permute-done | bytes 100384 | tf_op jit(solution)/shard_map/ppermute | solution.py:326
  10.1 1.7 %collective-permute-start.4 = (bf16[8,6272]{1,0:T(8,128)(2,1)S(1)}, bf16[8,6272]{1,0:T(8,128)(2,1)S(1)}, u32[]{:S(2)}, u32[]{:S(2)}) collective-permute-start(bf16[8,6272]{1,0:T(8,128)(2,1)S(1)} %collective-permute-done.refs_1_), channel_id=1, source_target_pairs={{0,2},{2,0},{4,6},{6,4},{8,10},{10,8},{12,14},{14,12},{1,3},{3,1},... | collective-permute-start | bytes 301064 | tf_op jit(solution)/shard_map/ppermute | solution.py:329
  11.8 0.7 %collective-permute-done.1.refs_2_ = bf16[8,6272]{1,0:T(8,128)(2,1)S(1)} collective-permute-done((bf16[8,6272]{1,0:T(8,128)(2,1)S(1)}, bf16[8,6272]{1,0:T(8,128)(2,1)S(1)}, u32[]{:S(2)}, u32[]{:S(2)}) %collective-permute-start.1) | collective-permute-done | bytes 100384 | tf_op jit(solution)/shard_map/ppermute | solution.py:326
  12.5 1.5 %collective-permute-start.5 = (bf16[8,6272]{1,0:T(8,128)(2,1)S(1)}, bf16[8,6272]{1,0:T(8,128)(2,1)S(1)}, u32[]{:S(2)}, u32[]{:S(2)}) collective-permute-start(bf16[8,6272]{1,0:T(8,128)(2,1)S(1)} %collective-permute-done.1.refs_2_), channel_id=1, source_target_pairs={{0,2},{2,0},{4,6},{6,4},{8,10},{10,8},{12,14},{14,12},{1,3},{3,1},... | collective-permute-start | bytes 301064 | tf_op jit(solution)/shard_map/ppermute | solution.py:329
  14.0 0.8 %collective-permute-done.2.refs_3_ = bf16[8,6272]{1,0:T(8,128)(2,1)S(1)} collective-permute-done((bf16[8,6272]{1,0:T(8,128)(2,1)S(1)}, bf16[8,6272]{1,0:T(8,128)(2,1)S(1)}, u32[]{:S(2)}, u32[]{:S(2)}) %collective-permute-start.2) | collective-permute-done | bytes 100384 | tf_op jit(solution)/shard_map/ppermute | solution.py:326
  14.8 1.5 %collective-permute-start.6 = (bf16[8,6272]{1,0:T(8,128)(2,1)S(1)}, bf16[8,6272]{1,0:T(8,128)(2,1)S(1)}, u32[]{:S(2)}, u32[]{:S(2)}) collective-permute-start(bf16[8,6272]{1,0:T(8,128)(2,1)S(1)} %collective-permute-done.2.refs_3_), channel_id=1, source_target_pairs={{0,2},{2,0},{4,6},{6,4},{8,10},{10,8},{12,14},{14,12},{1,3},{3,1},... | collective-permute-start | bytes 301064 | tf_op jit(solution)/shard_map/ppermute | solution.py:329
  16.5 1.0 %collective-permute-done.5.refs_2_.refs_6_ = bf16[8,6272]{1,0:T(8,128)(2,1)S(1)} collective-permute-done((bf16[8,6272]{1,0:T(8,128)(2,1)S(1)}, bf16[8,6272]{1,0:T(8,128)(2,1)S(1)}, u32[]{:S(2)}, u32[]{:S(2)}) %collective-permute-start.5) | collective-permute-done | bytes 100384 | tf_op jit(solution)/shard_map/ppermute | solution.py:329
  17.6 1.9 %collective-permute-done.6.refs_7_.refs_0_ = bf16[8,6272]{1,0:T(8,128)(2,1)S(1)} collective-permute-done((bf16[8,6272]{1,0:T(8,128)(2,1)S(1)}, bf16[8,6272]{1,0:T(8,128)(2,1)S(1)}, u32[]{:S(2)}, u32[]{:S(2)}) %collective-permute-start.6) | collective-permute-done | bytes 100384 | tf_op jit(solution)/shard_map/ppermute | solution.py:329
  19.6 0.5 unpack.1.first_ref
  20.1 0.8 %collective-permute-done.9.last_ref = bf16[8,6272]{1,0:T(8,128)(2,1)S(1)} collective-permute-done((bf16[8,6272]{1,0:T(8,128)(2,1)S(1)}, bf16[8,6272]{1,0:T(8,128)(2,1)S(1)}, u32[]{:S(2)}, u32[]{:S(2)}) %collective-permute-start.9) | collective-permute-done | bytes 100384 | tf_op jit(solution)/shard_map/ppermute | solution.py:332
  20.9 4.1 %gate_up.1.hidden_ref = bf16[128,1024]{1,0:T(8,128)(2,1)S(1)} custom-call(bf16[120,7168]{1,0:T(8,128)(2,1)S(1)} %unpack.1.first_ref, bf16[8,6272]{1,0:T(8,128)(2,1)S(1)} %collective-permute-done.9.last_ref, bf16[7168,1024]{1,0:T(8,128)(2,1)S(1)} %bitcast.6, bf16[7168,1024]{1,0:T(8,128)(2,1)S(1)} %bitcast.8), custom_call_target="tpu_custom_call" | custom-call | flops 3758096384 | tf_op jit(solution)/shard_map/gate_up/pallas_call | solution.py:113
  25.1 2.2 %down.1 = (f32[32,6272]{1,0:T(8,128)S(1)}, f32[32,6272]{1,0:T(8,128)S(1)}, bf16[8,6272]{1,0:T(8,128)(2,1)S(1)}, bf16[56,6272]{1,0:T(8,128)(2,1)S(1)}) custom-call(bf16[128,1024]{1,0:T(8,128)(2,1)S(1)} %gate_up.1.hidden_ref, bf16[1024,7168]{1,0:T(8,128)(2,1)S(1)} %bitcast.4), custom_call_target="tpu_custom_call" | custom-call | flops 1644167168 | tf_op jit(solution)/shard_map/down/pallas_call | solution.py:157
  27.3 0.4 collective-permute-start.10
  27.7 0.9 %collective-permute-done.10.refs_0_ = bf16[8,6272]{1,0:T(8,128)(2,1)S(1)} collective-permute-done((bf16[8,6272]{1,0:T(8,128)(2,1)S(1)}, bf16[8,6272]{1,0:T(8,128)(2,1)S(1)}, u32[]{:S(2)}, u32[]{:S(2)}) %collective-permute-start.10) | collective-permute-done | bytes 100384 | tf_op jit(solution)/shard_map/ppermute | solution.py:332
  28.7 0.4 collective-permute-start.11
  29.2 1.5 %collective-permute-start.12 = (bf16[8,6272]{1,0:T(8,128)(2,1)S(1)}, bf16[8,6272]{1,0:T(8,128)(2,1)S(1)}, u32[]{:S(2)}, u32[]{:S(2)}) collective-permute-start(bf16[8,6272]{1,0:T(8,128)(2,1)S(1)} %pair_sum.4.refs_1_), channel_id=1, source_target_pairs={{0,2},{2,0},{4,6},{6,4},{8,10},{10,8},{12,14},{14,12},{1,3},{3,1},... | collective-permute-start | bytes 301064 | tf_op jit(solution)/shard_map/ppermute | solution.py:329
  30.7 0.3 collective-permute-done.11.refs_0_
  31.0 1.6 %collective-permute-start.14 = (bf16[8,6272]{1,0:T(8,128)(2,1)S(1)}, bf16[8,6272]{1,0:T(8,128)(2,1)S(1)}, u32[]{:S(2)}, u32[]{:S(2)}) collective-permute-start(bf16[8,6272]{1,0:T(8,128)(2,1)S(1)} %get-tuple-element.37), channel_id=1, source_target_pairs={{0,2},{2,0},{4,6},{6,4},{8,10},{10,8},{12,14},{14,12},{1,3},{3,1},... | collective-permute-start | bytes 301064 | tf_op jit(solution)/shard_map/ppermute | solution.py:329
  32.6 0.5 %collective-permute-start.16 = (bf16[8,6272]{1,0:T(8,128)(2,1)S(1)}, bf16[8,6272]{1,0:T(8,128)(2,1)S(1)}, u32[]{:S(2)}, u32[]{:S(2)}) collective-permute-start(bf16[8,6272]{1,0:T(8,128)(2,1)S(1)} %get-tuple-element.39), channel_id=1, source_target_pairs={{0,2},{2,0},{4,6},{6,4},{8,10},{10,8},{12,14},{14,12},{1,3},{3,1},... | collective-permute-start | bytes 301064 | tf_op jit(solution)/shard_map/ppermute | solution.py:329
  33.2 0.9 %collective-permute-done.12.refs_1_ = bf16[8,6272]{1,0:T(8,128)(2,1)S(1)} collective-permute-done((bf16[8,6272]{1,0:T(8,128)(2,1)S(1)}, bf16[8,6272]{1,0:T(8,128)(2,1)S(1)}, u32[]{:S(2)}, u32[]{:S(2)}) %collective-permute-start.12) | collective-permute-done | bytes 100384 | tf_op jit(solution)/shard_map/ppermute | solution.py:329
  34.1 2.9 %collective-permute-start.13 = (bf16[8,6272]{1,0:T(8,128)(2,1)S(1)}, bf16[8,6272]{1,0:T(8,128)(2,1)S(1)}, u32[]{:S(2)}, u32[]{:S(2)}) collective-permute-start(bf16[8,6272]{1,0:T(8,128)(2,1)S(1)} %span_sum.3), channel_id=1, source_target_pairs={{0,12},{2,14},{4,8},{6,10},{8,4},{10,6},{12,0},{14,2},{1,13},{3,15... | collective-permute-start | bytes 301064 | tf_op jit(solution)/shard_map/ppermute | solution.py:326
  37.0 1.3 %collective-permute-start.15 = (bf16[8,6272]{1,0:T(8,128)(2,1)S(1)}, bf16[8,6272]{1,0:T(8,128)(2,1)S(1)}, u32[]{:S(2)}, u32[]{:S(2)}) collective-permute-start(bf16[8,6272]{1,0:T(8,128)(2,1)S(1)} %span_sum.4.refs_1_), channel_id=1, source_target_pairs={{0,8},{2,10},{4,12},{6,14},{8,0},{10,2},{12,4},{14,6},{1,9},{3,11}... | collective-permute-start | bytes 301064 | tf_op jit(solution)/shard_map/ppermute | solution.py:326
  38.2 0.1 collective-permute-done.16.refs_1_
  38.4 1.9 %collective-permute-start.17 = (bf16[8,6272]{1,0:T(8,128)(2,1)S(1)}, bf16[8,6272]{1,0:T(8,128)(2,1)S(1)}, u32[]{:S(2)}, u32[]{:S(2)}) collective-permute-start(bf16[8,6272]{1,0:T(8,128)(2,1)S(1)} %span_sum.5), channel_id=1, source_target_pairs={{0,4},{2,6},{4,0},{6,2},{8,12},{10,14},{12,8},{14,10},{1,5},{3,7},... | collective-permute-start | bytes 301064 | tf_op jit(solution)/shard_map/ppermute | solution.py:326
  40.3 1.4 %collective-permute-start.18 = (bf16[8,6272]{1,0:T(8,128)(2,1)S(1)}, bf16[8,6272]{1,0:T(8,128)(2,1)S(1)}, u32[]{:S(2)}, u32[]{:S(2)}) collective-permute-start(bf16[8,6272]{1,0:T(8,128)(2,1)S(1)} %pair_sum.7), channel_id=1, source_target_pairs={{0,2},{2,0},{4,6},{6,4},{8,10},{10,8},{12,14},{14,12},{1,3},{3,1},... | collective-permute-start | bytes 301064 | tf_op jit(solution)/shard_map/ppermute | solution.py:329
  41.8 3.8 %collective-permute-done.15.refs_1_ = bf16[8,6272]{1,0:T(8,128)(2,1)S(1)} collective-permute-done((bf16[8,6272]{1,0:T(8,128)(2,1)S(1)}, bf16[8,6272]{1,0:T(8,128)(2,1)S(1)}, u32[]{:S(2)}, u32[]{:S(2)}) %collective-permute-start.15) | collective-permute-done | bytes 100384 | tf_op jit(solution)/shard_map/ppermute | solution.py:326
  45.5 0.8 %combine.3 = bf16[8,7168]{1,0:T(8,128)(2,1)} custom-call(f32[8,1024]{1,0:T(8,128)S(1)} %get-tuple-element.26.sides_ref, f32[8,7168]{1,0:T(8,128)S(1)} %combine.2.refs_0_, bf16[8,6272]{1,0:T(8,128)(2,1)S(1)} %collective-permute-done.15.refs_1_, bf16[8,6272]{1,0:T(8,128)(2,1)S(1)} %collective-permute-done.17.refs_2_, f32[8,6272]{1,0:T(8,128)S(1)} %get-tuple-element.40.refs_3_, ...), custom_call_target="tpu_custom_call" | custom-call | tf_op jit(solution)/shard_map/combine/pallas_call | solution.py:309
  (51 shorter events, 0.7 us)
Async XLA Ops:
  0.9 19.9 %slice-start.4 = ((s8[14680064]{0:T(1024)(128)(4,1)}), s8[4194304]{0:T(1024)(128)(4,1)S(1)}, s32[]{:S(2)}) async-start(s8[14680064]{0:T(1024)(128)(4,1)} %bitcast.5), calls=%async_computation.4 | async-start | bytes 8388608
  0.9 19.9 %slice-start.8 = ((s8[14680064]{0:T(1024)(128)(4,1)}), s8[4194304]{0:T(1024)(128)(4,1)S(1)}, s32[]{:S(2)}) async-start(s8[14680064]{0:T(1024)(128)(4,1)} %bitcast.7), calls=%async_computation.8 | async-start | bytes 8388608
  1.0 19.9 %slice-start.5 = ((s8[14680064]{0:T(1024)(128)(4,1)}), s8[4194304]{0:T(1024)(128)(4,1)S(1)}, s32[]{:S(2)}) async-start(s8[14680064]{0:T(1024)(128)(4,1)} %bitcast.5), calls=%async_computation.5 | async-start | bytes 8388608
  1.0 19.9 %slice-start.6 = ((s8[14680064]{0:T(1024)(128)(4,1)}), s8[4194304]{0:T(1024)(128)(4,1)S(1)}, s32[]{:S(2)}) async-start(s8[14680064]{0:T(1024)(128)(4,1)} %bitcast.5), calls=%async_computation.6 | async-start | bytes 8388608
  1.0 19.9 %slice-start.7 = ((s8[14680064]{0:T(1024)(128)(4,1)}), s8[2097152]{0:T(1024)(128)(4,1)S(1)}, s32[]{:S(2)}) async-start(s8[14680064]{0:T(1024)(128)(4,1)} %bitcast.5), calls=%async_computation.7 | async-start | bytes 4194304
  1.0 19.9 %slice-start.9 = ((s8[14680064]{0:T(1024)(128)(4,1)}), s8[4194304]{0:T(1024)(128)(4,1)S(1)}, s32[]{:S(2)}) async-start(s8[14680064]{0:T(1024)(128)(4,1)} %bitcast.7), calls=%async_computation.9 | async-start | bytes 8388608
  1.0 19.9 %slice-start.10 = ((s8[14680064]{0:T(1024)(128)(4,1)}), s8[4194304]{0:T(1024)(128)(4,1)S(1)}, s32[]{:S(2)}) async-start(s8[14680064]{0:T(1024)(128)(4,1)} %bitcast.7), calls=%async_computation.10 | async-start | bytes 8388608
  1.0 19.9 %slice-start.11 = ((s8[14680064]{0:T(1024)(128)(4,1)}), s8[2097152]{0:T(1024)(128)(4,1)S(1)}, s32[]{:S(2)}) async-start(s8[14680064]{0:T(1024)(128)(4,1)} %bitcast.7), calls=%async_computation.11 | async-start | bytes 4194304
  1.3 8.8 %collective-permute-start = (bf16[8,6272]{1,0:T(8,128)(2,1)S(1)}, bf16[8,6272]{1,0:T(8,128)(2,1)S(1)}, u32[]{:S(2)}, u32[]{:S(2)}) collective-permute-start(bf16[8,6272]{1,0:T(8,128)(2,1)S(1)} %get-tuple-element.28), channel_id=1, source_target_pairs={{0,12},{2,14},{4,8},{6,10},{8,4},{10,6},{12,0},{14,2},{1,13},{3,15... | collective-permute-start | bytes 301064 | tf_op jit(solution)/shard_map/ppermute | solution.py:326
  6.4 6.1 %collective-permute-start.1 = (bf16[8,6272]{1,0:T(8,128)(2,1)S(1)}, bf16[8,6272]{1,0:T(8,128)(2,1)S(1)}, u32[]{:S(2)}, u32[]{:S(2)}) collective-permute-start(bf16[8,6272]{1,0:T(8,128)(2,1)S(1)} %get-tuple-element.29), channel_id=1, source_target_pairs={{0,4},{2,6},{4,0},{6,2},{8,12},{10,14},{12,8},{14,10},{1,5},{3,7},... | collective-permute-start | bytes 301064 | tf_op jit(solution)/shard_map/ppermute | solution.py:326
  6.4 8.4 %collective-permute-start.2 = (bf16[8,6272]{1,0:T(8,128)(2,1)S(1)}, bf16[8,6272]{1,0:T(8,128)(2,1)S(1)}, u32[]{:S(2)}, u32[]{:S(2)}) collective-permute-start(bf16[8,6272]{1,0:T(8,128)(2,1)S(1)} %get-tuple-element.30), channel_id=1, source_target_pairs={{0,8},{2,10},{4,12},{6,14},{8,0},{10,2},{12,4},{14,6},{1,9},{3,11}... | collective-permute-start | bytes 301064 | tf_op jit(solution)/shard_map/ppermute | solution.py:326
  7.0 9.4 %collective-permute-start.3 = (bf16[8,6272]{1,0:T(8,128)(2,1)S(1)}, bf16[8,6272]{1,0:T(8,128)(2,1)S(1)}, u32[]{:S(2)}, u32[]{:S(2)}) collective-permute-start(bf16[8,6272]{1,0:T(8,128)(2,1)S(1)} %get-tuple-element.27.refs_0_), channel_id=1, source_target_pairs={{0,2},{2,0},{4,6},{6,4},{8,10},{10,8},{12,14},{14,12},{1,3},{3,1},... | collective-permute-start | bytes 301064 | tf_op jit(solution)/shard_map/ppermute | solution.py:329
  10.1 6.4 %collective-permute-start.4 = (bf16[8,6272]{1,0:T(8,128)(2,1)S(1)}, bf16[8,6272]{1,0:T(8,128)(2,1)S(1)}, u32[]{:S(2)}, u32[]{:S(2)}) collective-permute-start(bf16[8,6272]{1,0:T(8,128)(2,1)S(1)} %collective-permute-done.refs_1_), channel_id=1, source_target_pairs={{0,2},{2,0},{4,6},{6,4},{8,10},{10,8},{12,14},{14,12},{1,3},{3,1},... | collective-permute-start | bytes 301064 | tf_op jit(solution)/shard_map/ppermute | solution.py:329
  12.5 5.0 %collective-permute-start.5 = (bf16[8,6272]{1,0:T(8,128)(2,1)S(1)}, bf16[8,6272]{1,0:T(8,128)(2,1)S(1)}, u32[]{:S(2)}, u32[]{:S(2)}) collective-permute-start(bf16[8,6272]{1,0:T(8,128)(2,1)S(1)} %collective-permute-done.1.refs_2_), channel_id=1, source_target_pairs={{0,2},{2,0},{4,6},{6,4},{8,10},{10,8},{12,14},{14,12},{1,3},{3,1},... | collective-permute-start | bytes 301064 | tf_op jit(solution)/shard_map/ppermute | solution.py:329
  14.8 4.6 %collective-permute-start.6 = (bf16[8,6272]{1,0:T(8,128)(2,1)S(1)}, bf16[8,6272]{1,0:T(8,128)(2,1)S(1)}, u32[]{:S(2)}, u32[]{:S(2)}) collective-permute-start(bf16[8,6272]{1,0:T(8,128)(2,1)S(1)} %collective-permute-done.2.refs_3_), channel_id=1, source_target_pairs={{0,2},{2,0},{4,6},{6,4},{8,10},{10,8},{12,14},{14,12},{1,3},{3,1},... | collective-permute-start | bytes 301064 | tf_op jit(solution)/shard_map/ppermute | solution.py:329
  16.4 3.2 %collective-permute-start.7 = (bf16[32,6272]{1,0:T(8,128)(2,1)S(1)}, bf16[32,6272]{1,0:T(8,128)(2,1)S(1)}, u32[]{:S(2)}, u32[]{:S(2)}) collective-permute-start(bf16[32,6272]{1,0:T(8,128)(2,1)S(1)} %stack.4), channel_id=1, source_target_pairs={{0,1},{1,0},{2,3},{3,2},{4,5},{5,4},{6,7},{7,6},{8,9},{9,8},{10,11... | collective-permute-start | bytes 1204232 | tf_op jit(solution)/shard_map/ppermute | solution.py:332
  17.5 2.1 %collective-permute-start.8 = (bf16[24,6272]{1,0:T(8,128)(2,1)S(1)}, bf16[24,6272]{1,0:T(8,128)(2,1)S(1)}, u32[]{:S(2)}, u32[]{:S(2)}) collective-permute-start(bf16[24,6272]{1,0:T(8,128)(2,1)S(1)} %stack.5), channel_id=1, source_target_pairs={{0,1},{1,0},{2,3},{3,2},{4,5},{5,4},{6,7},{7,6},{8,9},{9,8},{10,11... | collective-permute-start | bytes 903176 | tf_op jit(solution)/shard_map/ppermute | solution.py:332
  19.5 1.4 %collective-permute-start.9 = (bf16[8,6272]{1,0:T(8,128)(2,1)S(1)}, bf16[8,6272]{1,0:T(8,128)(2,1)S(1)}, u32[]{:S(2)}, u32[]{:S(2)}) collective-permute-start(bf16[8,6272]{1,0:T(8,128)(2,1)S(1)} %stack.6), channel_id=1, source_target_pairs={{0,1},{1,0},{2,3},{3,2},{4,5},{5,4},{6,7},{7,6},{8,9},{9,8},{10,11... | collective-permute-start | bytes 301064 | tf_op jit(solution)/shard_map/ppermute | solution.py:332
  19.6 5.4 %slice-start = ((s8[14680064]{0:T(1024)(128)(4,1)}), s8[4194304]{0:T(1024)(128)(4,1)S(1)}, s32[]{:S(2)}) async-start(s8[14680064]{0:T(1024)(128)(4,1)} %bitcast.3), calls=%async_computation | async-start | bytes 8388608
  20.0 5.0 %slice-start.1 = ((s8[14680064]{0:T(1024)(128)(4,1)}), s8[4194304]{0:T(1024)(128)(4,1)S(1)}, s32[]{:S(2)}) async-start(s8[14680064]{0:T(1024)(128)(4,1)} %bitcast.3), calls=%async_computation.1 | async-start | bytes 8388608
  20.0 5.0 %slice-start.2 = ((s8[14680064]{0:T(1024)(128)(4,1)}), s8[4194304]{0:T(1024)(128)(4,1)S(1)}, s32[]{:S(2)}) async-start(s8[14680064]{0:T(1024)(128)(4,1)} %bitcast.3), calls=%async_computation.2 | async-start | bytes 8388608
  20.1 5.0 %slice-start.3 = ((s8[14680064]{0:T(1024)(128)(4,1)}), s8[2097152]{0:T(1024)(128)(4,1)S(1)}, s32[]{:S(2)}) async-start(s8[14680064]{0:T(1024)(128)(4,1)} %bitcast.3), calls=%async_computation.3 | async-start | bytes 4194304
  27.3 1.4 %collective-permute-start.10 = (bf16[8,6272]{1,0:T(8,128)(2,1)S(1)}, bf16[8,6272]{1,0:T(8,128)(2,1)S(1)}, u32[]{:S(2)}, u32[]{:S(2)}) collective-permute-start(bf16[8,6272]{1,0:T(8,128)(2,1)S(1)} %get-tuple-element.34), channel_id=1, source_target_pairs={{0,1},{1,0},{2,3},{3,2},{4,5},{5,4},{6,7},{7,6},{8,9},{9,8},{10,11... | collective-permute-start | bytes 301064 | tf_op jit(solution)/shard_map/ppermute | solution.py:332
  28.7 2.2 %collective-permute-start.11 = (bf16[56,6272]{1,0:T(8,128)(2,1)S(1)}, bf16[56,6272]{1,0:T(8,128)(2,1)S(1)}, u32[]{:S(2)}, u32[]{:S(2)}) collective-permute-start(bf16[56,6272]{1,0:T(8,128)(2,1)S(1)} %stack.7), channel_id=1, source_target_pairs={{0,1},{1,0},{2,3},{3,2},{4,5},{5,4},{6,7},{7,6},{8,9},{9,8},{10,11... | collective-permute-start | bytes 2107400 | tf_op jit(solution)/shard_map/ppermute | solution.py:332
  29.2 4.9 %collective-permute-start.12 = (bf16[8,6272]{1,0:T(8,128)(2,1)S(1)}, bf16[8,6272]{1,0:T(8,128)(2,1)S(1)}, u32[]{:S(2)}, u32[]{:S(2)}) collective-permute-start(bf16[8,6272]{1,0:T(8,128)(2,1)S(1)} %pair_sum.4.refs_1_), channel_id=1, source_target_pairs={{0,2},{2,0},{4,6},{6,4},{8,10},{10,8},{12,14},{14,12},{1,3},{3,1},... | collective-permute-start | bytes 301064 | tf_op jit(solution)/shard_map/ppermute | solution.py:329
  31.0 5.9 %collective-permute-start.14 = (bf16[8,6272]{1,0:T(8,128)(2,1)S(1)}, bf16[8,6272]{1,0:T(8,128)(2,1)S(1)}, u32[]{:S(2)}, u32[]{:S(2)}) collective-permute-start(bf16[8,6272]{1,0:T(8,128)(2,1)S(1)} %get-tuple-element.37), channel_id=1, source_target_pairs={{0,2},{2,0},{4,6},{6,4},{8,10},{10,8},{12,14},{14,12},{1,3},{3,1},... | collective-permute-start | bytes 301064 | tf_op jit(solution)/shard_map/ppermute | solution.py:329
  32.6 5.8 %collective-permute-start.16 = (bf16[8,6272]{1,0:T(8,128)(2,1)S(1)}, bf16[8,6272]{1,0:T(8,128)(2,1)S(1)}, u32[]{:S(2)}, u32[]{:S(2)}) collective-permute-start(bf16[8,6272]{1,0:T(8,128)(2,1)S(1)} %get-tuple-element.39), channel_id=1, source_target_pairs={{0,2},{2,0},{4,6},{6,4},{8,10},{10,8},{12,14},{14,12},{1,3},{3,1},... | collective-permute-start | bytes 301064 | tf_op jit(solution)/shard_map/ppermute | solution.py:329
  34.1 7.6 %collective-permute-start.13 = (bf16[8,6272]{1,0:T(8,128)(2,1)S(1)}, bf16[8,6272]{1,0:T(8,128)(2,1)S(1)}, u32[]{:S(2)}, u32[]{:S(2)}) collective-permute-start(bf16[8,6272]{1,0:T(8,128)(2,1)S(1)} %span_sum.3), channel_id=1, source_target_pairs={{0,12},{2,14},{4,8},{6,10},{8,4},{10,6},{12,0},{14,2},{1,13},{3,15... | collective-permute-start | bytes 301064 | tf_op jit(solution)/shard_map/ppermute | solution.py:326
  37.0 8.6 %collective-permute-start.15 = (bf16[8,6272]{1,0:T(8,128)(2,1)S(1)}, bf16[8,6272]{1,0:T(8,128)(2,1)S(1)}, u32[]{:S(2)}, u32[]{:S(2)}) collective-permute-start(bf16[8,6272]{1,0:T(8,128)(2,1)S(1)} %span_sum.4.refs_1_), channel_id=1, source_target_pairs={{0,8},{2,10},{4,12},{6,14},{8,0},{10,2},{12,4},{14,6},{1,9},{3,11}... | collective-permute-start | bytes 301064 | tf_op jit(solution)/shard_map/ppermute | solution.py:326
  38.4 7.2 %collective-permute-start.17 = (bf16[8,6272]{1,0:T(8,128)(2,1)S(1)}, bf16[8,6272]{1,0:T(8,128)(2,1)S(1)}, u32[]{:S(2)}, u32[]{:S(2)}) collective-permute-start(bf16[8,6272]{1,0:T(8,128)(2,1)S(1)} %span_sum.5), channel_id=1, source_target_pairs={{0,4},{2,6},{4,0},{6,2},{8,12},{10,14},{12,8},{14,10},{1,5},{3,7},... | collective-permute-start | bytes 301064 | tf_op jit(solution)/shard_map/ppermute | solution.py:326
  40.3 5.2 %collective-permute-start.18 = (bf16[8,6272]{1,0:T(8,128)(2,1)S(1)}, bf16[8,6272]{1,0:T(8,128)(2,1)S(1)}, u32[]{:S(2)}, u32[]{:S(2)}) collective-permute-start(bf16[8,6272]{1,0:T(8,128)(2,1)S(1)} %pair_sum.7), channel_id=1, source_target_pairs={{0,2},{2,0},{4,6},{6,4},{8,10},{10,8},{12,14},{14,12},{1,3},{3,1},... | collective-permute-start | bytes 301064 | tf_op jit(solution)/shard_map/ppermute | solution.py:329

commit v18 on v17

--- a/solution.py
+++ b/solution.py
@@ -10,7 +10,7 @@
 EXPERTS = 4
 LANES = 128
 RETURN_ORDER = (3, 2, 1)
-BLOCK_ORDER = (0, 3, 1, 2)
+BLOCK_ORDER = (0, 3, 2, 1)
 N_BLOCK = 512
 LAST_FLOPS = 5_000_000_000
 EXCHANGE_FLOPS = 20_000_000_000

time: 46.5 us -> 48.5 us (1.043)
  waiting for transfers between devices: 12.6 us -> 17.1 us
  starting transfers between devices: 24.2 us -> 21.3 us
    ppermute x6, waiting for transfers between devices: 6.66 us -> 8.98 us  [over_experts(): lax.ppermute(value, 'attn', [(i, (i // span ^ other) * span + i % span) f...]
    ppermute x8, waiting for transfers between devices: 3.89 us -> 5.53 us  [over_span(): lax.ppermute(value, 'attn', [(i, i // span * span + (i + shift) % span) f...]
    ppermute x6, starting transfers between devices: 11.8 us -> 10.5 us  [over_experts(): lax.ppermute(value, 'attn', [(i, (i // span ^ other) * span + i % span) f...]
    ppermute x8, starting transfers between devices: 11.4 us -> 10.2 us  [over_span(): lax.ppermute(value, 'attn', [(i, i // span * span + (i + shift) % span) f...]
    ppermute x5, waiting for transfers between devices: 2 us -> 2.6 us  [over_pair(): lax.ppermute(value, 'ffn', [(i, (i + shift) % pair) for i in range(pair)])]
  transfers between devices with their start and end apart: 19 -> 19, of which waited for: 11 -> 13; matrix products, arithmetic and copies ran while one was open for 0% -> 0% of each run, Pallas kernels for 2% -> 2%
where the time goes in v18:
time: 48.5 us; the launch traced here: 48.4 us
  starting transfers between devices  21.3 us (44%)
  waiting for transfers between devices  17.1 us (35%)
  Pallas kernels  9.17 us (19%)
    ppermute x6, starting transfers between devices, over_experts(): lax.ppermute(value, 'attn', [(i, (i // span ^ other) * span + i % span) f...  10.5 us
    ppermute x8, starting transfers between devices, over_span(): lax.ppermute(value, 'attn', [(i, i // span * span + (i + shift) % span) f...  10.2 us
    ppermute x6, waiting for transfers between devices, over_experts(): lax.ppermute(value, 'attn', [(i, (i // span ^ other) * span + i % span) f...  8.98 us
    ppermute x8, waiting for transfers between devices, over_span(): lax.ppermute(value, 'attn', [(i, i // span * span + (i + shift) % span) f...  5.53 us
    pallas_call x1, Pallas kernels, gate_up(): pl.pallas_call(functools.partial(gate_up_kernel, block_of(units, N_BLOCK)...  4.08 us
    ppermute x5, waiting for transfers between devices, over_pair(): lax.ppermute(value, 'ffn', [(i, (i + shift) % pair) for i in range(pair)])  2.6 us
    pallas_call x1, Pallas kernels, down(): pl.pallas_call(functools.partial(down_kernel, rows, sources), in_specs=[p...  2.21 us
  transfers between devices with their start and end apart: 19, of which 13 were waited for; matrix products, arithmetic and copies ran while one was open for 0% of the time, Pallas kernels for 2%

profile of v18, /device:TPU:0, one launch (start us, length us, event | category | flops | bytes accessed | tf_op | source)
XLA Modules:
  0.0 48.4 jit_solution(14889292527361181314)
XLA Ops:
  0.0 0.9 %load.1 = (bf16[8,7168]{1,0:T(8,128)(2,1)S(1)}, s32[3,8]{1,0:T(4,128)S(1)}, f32[3,8]{1,0:T(4,128)S(1)}) custom-call(bf16[8,7168]{1,0:T(8,128)(2,1)} %refs_0_.1, s32[3,8]{1,0:T(4,128)} %bitcast.9, f32[3,8]{1,0:T(4,128)} %bitcast.10), custom_call_target="tpu_custom_call" | custom-call | tf_op jit(solution)/shard_map/load/pallas_call | solution.py:215
  1.3 5.1 %collective-permute-start = (bf16[8,6272]{1,0:T(8,128)(2,1)S(1)}, bf16[8,6272]{1,0:T(8,128)(2,1)S(1)}, u32[]{:S(2)}, u32[]{:S(2)}) collective-permute-start(bf16[8,6272]{1,0:T(8,128)(2,1)S(1)} %get-tuple-element.28), channel_id=1, source_target_pairs={{0,12},{2,14},{4,8},{6,10},{8,4},{10,6},{12,0},{14,2},{1,13},{3,15... | collective-permute-start | bytes 301064 | tf_op jit(solution)/shard_map/ppermute | solution.py:326
  6.4 0.6 %collective-permute-start.2 = (bf16[8,6272]{1,0:T(8,128)(2,1)S(1)}, bf16[8,6272]{1,0:T(8,128)(2,1)S(1)}, u32[]{:S(2)}, u32[]{:S(2)}) collective-permute-start(bf16[8,6272]{1,0:T(8,128)(2,1)S(1)} %get-tuple-element.30), channel_id=1, source_target_pairs={{0,4},{2,6},{4,0},{6,2},{8,12},{10,14},{12,8},{14,10},{1,5},{3,7},... | collective-permute-start | bytes 301064 | tf_op jit(solution)/shard_map/ppermute | solution.py:326
  7.0 1.7 %collective-permute-start.3 = (bf16[8,6272]{1,0:T(8,128)(2,1)S(1)}, bf16[8,6272]{1,0:T(8,128)(2,1)S(1)}, u32[]{:S(2)}, u32[]{:S(2)}) collective-permute-start(bf16[8,6272]{1,0:T(8,128)(2,1)S(1)} %get-tuple-element.27.refs_0_), channel_id=1, source_target_pairs={{0,2},{2,0},{4,6},{6,4},{8,10},{10,8},{12,14},{14,12},{1,3},{3,1},... | collective-permute-start | bytes 301064 | tf_op jit(solution)/shard_map/ppermute | solution.py:329
  8.7 1.5 %collective-permute-done.refs_1_ = bf16[8,6272]{1,0:T(8,128)(2,1)S(1)} collective-permute-done((bf16[8,6272]{1,0:T(8,128)(2,1)S(1)}, bf16[8,6272]{1,0:T(8,128)(2,1)S(1)}, u32[]{:S(2)}, u32[]{:S(2)}) %collective-permute-start) | collective-permute-done | bytes 100384 | tf_op jit(solution)/shard_map/ppermute | solution.py:326
  10.1 1.5 %collective-permute-start.4 = (bf16[8,6272]{1,0:T(8,128)(2,1)S(1)}, bf16[8,6272]{1,0:T(8,128)(2,1)S(1)}, u32[]{:S(2)}, u32[]{:S(2)}) collective-permute-start(bf16[8,6272]{1,0:T(8,128)(2,1)S(1)} %collective-permute-done.refs_1_), channel_id=1, source_target_pairs={{0,2},{2,0},{4,6},{6,4},{8,10},{10,8},{12,14},{14,12},{1,3},{3,1},... | collective-permute-start | bytes 301064 | tf_op jit(solution)/shard_map/ppermute | solution.py:329
  11.7 3.1 %collective-permute-done.1.refs_2_ = bf16[8,6272]{1,0:T(8,128)(2,1)S(1)} collective-permute-done((bf16[8,6272]{1,0:T(8,128)(2,1)S(1)}, bf16[8,6272]{1,0:T(8,128)(2,1)S(1)}, u32[]{:S(2)}, u32[]{:S(2)}) %collective-permute-start.1) | collective-permute-done | bytes 100384 | tf_op jit(solution)/shard_map/ppermute | solution.py:326
  14.8 1.5 %collective-permute-start.5 = (bf16[8,6272]{1,0:T(8,128)(2,1)S(1)}, bf16[8,6272]{1,0:T(8,128)(2,1)S(1)}, u32[]{:S(2)}, u32[]{:S(2)}) collective-permute-start(bf16[8,6272]{1,0:T(8,128)(2,1)S(1)} %collective-permute-done.1.refs_2_), channel_id=1, source_target_pairs={{0,2},{2,0},{4,6},{6,4},{8,10},{10,8},{12,14},{14,12},{1,3},{3,1},... | collective-permute-start | bytes 301064 | tf_op jit(solution)/shard_map/ppermute | solution.py:329
  16.3 0.5 %collective-permute-start.6 = (bf16[8,6272]{1,0:T(8,128)(2,1)S(1)}, bf16[8,6272]{1,0:T(8,128)(2,1)S(1)}, u32[]{:S(2)}, u32[]{:S(2)}) collective-permute-start(bf16[8,6272]{1,0:T(8,128)(2,1)S(1)} %collective-permute-done.2.refs_3_), channel_id=1, source_target_pairs={{0,2},{2,0},{4,6},{6,4},{8,10},{10,8},{12,14},{14,12},{1,3},{3,1},... | collective-permute-start | bytes 301064 | tf_op jit(solution)/shard_map/ppermute | solution.py:329
  17.0 2.9 %collective-permute-done.5.refs_2_.refs_6_ = bf16[8,6272]{1,0:T(8,128)(2,1)S(1)} collective-permute-done((bf16[8,6272]{1,0:T(8,128)(2,1)S(1)}, bf16[8,6272]{1,0:T(8,128)(2,1)S(1)}, u32[]{:S(2)}, u32[]{:S(2)}) %collective-permute-start.5) | collective-permute-done | bytes 100384 | tf_op jit(solution)/shard_map/ppermute | solution.py:329
  20.0 1.0 %collective-permute-done.6.refs_7_.refs_0_ = bf16[8,6272]{1,0:T(8,128)(2,1)S(1)} collective-permute-done((bf16[8,6272]{1,0:T(8,128)(2,1)S(1)}, bf16[8,6272]{1,0:T(8,128)(2,1)S(1)}, u32[]{:S(2)}, u32[]{:S(2)}) %collective-permute-start.6) | collective-permute-done | bytes 100384 | tf_op jit(solution)/shard_map/ppermute | solution.py:329
  21.1 0.5 %collective-permute-done.8.refs_9_ = bf16[24,6272]{1,0:T(8,128)(2,1)S(1)} collective-permute-done((bf16[24,6272]{1,0:T(8,128)(2,1)S(1)}, bf16[24,6272]{1,0:T(8,128)(2,1)S(1)}, u32[]{:S(2)}, u32[]{:S(2)}) %collective-permute-start.8) | collective-permute-done | bytes 301088 | tf_op jit(solution)/shard_map/ppermute | solution.py:332
  21.6 0.5 unpack.1.first_ref
  22.1 0.3 collective-permute-done.9.last_ref
  22.5 4.1 %gate_up.1.hidden_ref = bf16[128,1024]{1,0:T(8,128)(2,1)S(1)} custom-call(bf16[120,7168]{1,0:T(8,128)(2,1)S(1)} %unpack.1.first_ref, bf16[8,6272]{1,0:T(8,128)(2,1)S(1)} %collective-permute-done.9.last_ref, bf16[7168,1024]{1,0:T(8,128)(2,1)S(1)} %bitcast.6, bf16[7168,1024]{1,0:T(8,128)(2,1)S(1)} %bitcast.8), custom_call_target="tpu_custom_call" | custom-call | flops 3758096384 | tf_op jit(solution)/shard_map/gate_up/pallas_call | solution.py:113
  26.6 0.4 slice-done.3
  27.0 2.2 %down.1 = (f32[32,6272]{1,0:T(8,128)S(1)}, f32[32,6272]{1,0:T(8,128)S(1)}, bf16[8,6272]{1,0:T(8,128)(2,1)S(1)}, bf16[56,6272]{1,0:T(8,128)(2,1)S(1)}) custom-call(bf16[128,1024]{1,0:T(8,128)(2,1)S(1)} %gate_up.1.hidden_ref, bf16[1024,7168]{1,0:T(8,128)(2,1)S(1)} %bitcast.4), custom_call_target="tpu_custom_call" | custom-call | flops 1644167168 | tf_op jit(solution)/shard_map/down/pallas_call | solution.py:157
  29.4 1.2 %collective-permute-done.10.refs_0_ = bf16[8,6272]{1,0:T(8,128)(2,1)S(1)} collective-permute-done((bf16[8,6272]{1,0:T(8,128)(2,1)S(1)}, bf16[8,6272]{1,0:T(8,128)(2,1)S(1)}, u32[]{:S(2)}, u32[]{:S(2)}) %collective-permute-start.10) | collective-permute-done | bytes 100384 | tf_op jit(solution)/shard_map/ppermute | solution.py:332
  30.9 1.4 %collective-permute-start.12 = (bf16[8,6272]{1,0:T(8,128)(2,1)S(1)}, bf16[8,6272]{1,0:T(8,128)(2,1)S(1)}, u32[]{:S(2)}, u32[]{:S(2)}) collective-permute-start(bf16[8,6272]{1,0:T(8,128)(2,1)S(1)} %pair_sum.4.refs_1_), channel_id=1, source_target_pairs={{0,2},{2,0},{4,6},{6,4},{8,10},{10,8},{12,14},{14,12},{1,3},{3,1},... | collective-permute-start | bytes 301064 | tf_op jit(solution)/shard_map/ppermute | solution.py:329
  32.3 0.6 %collective-permute-done.11.refs_0_ = bf16[56,6272]{1,0:T(8,128)(2,1)S(1)} collective-permute-done((bf16[56,6272]{1,0:T(8,128)(2,1)S(1)}, bf16[56,6272]{1,0:T(8,128)(2,1)S(1)}, u32[]{:S(2)}, u32[]{:S(2)}) %collective-permute-start.11) | collective-permute-done | bytes 702496 | tf_op jit(solution)/shard_map/ppermute | solution.py:332
  33.0 1.4 %collective-permute-start.14 = (bf16[8,6272]{1,0:T(8,128)(2,1)S(1)}, bf16[8,6272]{1,0:T(8,128)(2,1)S(1)}, u32[]{:S(2)}, u32[]{:S(2)}) collective-permute-start(bf16[8,6272]{1,0:T(8,128)(2,1)S(1)} %get-tuple-element.37), channel_id=1, source_target_pairs={{0,2},{2,0},{4,6},{6,4},{8,10},{10,8},{12,14},{14,12},{1,3},{3,1},... | collective-permute-start | bytes 301064 | tf_op jit(solution)/shard_map/ppermute | solution.py:329
  34.4 0.7 %collective-permute-start.16 = (bf16[8,6272]{1,0:T(8,128)(2,1)S(1)}, bf16[8,6272]{1,0:T(8,128)(2,1)S(1)}, u32[]{:S(2)}, u32[]{:S(2)}) collective-permute-start(bf16[8,6272]{1,0:T(8,128)(2,1)S(1)} %get-tuple-element.39), channel_id=1, source_target_pairs={{0,2},{2,0},{4,6},{6,4},{8,10},{10,8},{12,14},{14,12},{1,3},{3,1},... | collective-permute-start | bytes 301064 | tf_op jit(solution)/shard_map/ppermute | solution.py:329
  35.1 1.1 %collective-permute-done.12.refs_1_ = bf16[8,6272]{1,0:T(8,128)(2,1)S(1)} collective-permute-done((bf16[8,6272]{1,0:T(8,128)(2,1)S(1)}, bf16[8,6272]{1,0:T(8,128)(2,1)S(1)}, u32[]{:S(2)}, u32[]{:S(2)}) %collective-permute-start.12) | collective-permute-done | bytes 100384 | tf_op jit(solution)/shard_map/ppermute | solution.py:329
  36.2 1.9 %collective-permute-start.13 = (bf16[8,6272]{1,0:T(8,128)(2,1)S(1)}, bf16[8,6272]{1,0:T(8,128)(2,1)S(1)}, u32[]{:S(2)}, u32[]{:S(2)}) collective-permute-start(bf16[8,6272]{1,0:T(8,128)(2,1)S(1)} %span_sum.3), channel_id=1, source_target_pairs={{0,12},{2,14},{4,8},{6,10},{8,4},{10,6},{12,0},{14,2},{1,13},{3,15... | collective-permute-start | bytes 301064 | tf_op jit(solution)/shard_map/ppermute | solution.py:326
  38.2 0.5 %collective-permute-done.14.refs_1_ = bf16[8,6272]{1,0:T(8,128)(2,1)S(1)} collective-permute-done((bf16[8,6272]{1,0:T(8,128)(2,1)S(1)}, bf16[8,6272]{1,0:T(8,128)(2,1)S(1)}, u32[]{:S(2)}, u32[]{:S(2)}) %collective-permute-start.14) | collective-permute-done | bytes 100384 | tf_op jit(solution)/shard_map/ppermute | solution.py:329
  38.7 1.6 %collective-permute-start.15 = (bf16[8,6272]{1,0:T(8,128)(2,1)S(1)}, bf16[8,6272]{1,0:T(8,128)(2,1)S(1)}, u32[]{:S(2)}, u32[]{:S(2)}) collective-permute-start(bf16[8,6272]{1,0:T(8,128)(2,1)S(1)} %span_sum.4.refs_1_), channel_id=1, source_target_pairs={{0,8},{2,10},{4,12},{6,14},{8,0},{10,2},{12,4},{14,6},{1,9},{3,11}... | collective-permute-start | bytes 301064 | tf_op jit(solution)/shard_map/ppermute | solution.py:326
  40.4 1.2 %collective-permute-start.17 = (bf16[8,6272]{1,0:T(8,128)(2,1)S(1)}, bf16[8,6272]{1,0:T(8,128)(2,1)S(1)}, u32[]{:S(2)}, u32[]{:S(2)}) collective-permute-start(bf16[8,6272]{1,0:T(8,128)(2,1)S(1)} %span_sum.5), channel_id=1, source_target_pairs={{0,4},{2,6},{4,0},{6,2},{8,12},{10,14},{12,8},{14,10},{1,5},{3,7},... | collective-permute-start | bytes 301064 | tf_op jit(solution)/shard_map/ppermute | solution.py:326
  41.5 1.5 %collective-permute-start.18 = (bf16[8,6272]{1,0:T(8,128)(2,1)S(1)}, bf16[8,6272]{1,0:T(8,128)(2,1)S(1)}, u32[]{:S(2)}, u32[]{:S(2)}) collective-permute-start(bf16[8,6272]{1,0:T(8,128)(2,1)S(1)} %pair_sum.7), channel_id=1, source_target_pairs={{0,2},{2,0},{4,6},{6,4},{8,10},{10,8},{12,14},{14,12},{1,3},{3,1},... | collective-permute-start | bytes 301064 | tf_op jit(solution)/shard_map/ppermute | solution.py:329
  43.1 0.4 collective-permute-done.13.refs_0_
  43.6 3.7 %collective-permute-done.15.refs_1_ = bf16[8,6272]{1,0:T(8,128)(2,1)S(1)} collective-permute-done((bf16[8,6272]{1,0:T(8,128)(2,1)S(1)}, bf16[8,6272]{1,0:T(8,128)(2,1)S(1)}, u32[]{:S(2)}, u32[]{:S(2)}) %collective-permute-start.15) | collective-permute-done | bytes 100384 | tf_op jit(solution)/shard_map/ppermute | solution.py:326
  47.3 0.3 collective-permute-done.17.refs_2_
  47.5 0.8 %combine.3 = bf16[8,7168]{1,0:T(8,128)(2,1)} custom-call(f32[8,1024]{1,0:T(8,128)S(1)} %get-tuple-element.26.sides_ref, f32[8,7168]{1,0:T(8,128)S(1)} %combine.2.refs_0_, bf16[8,6272]{1,0:T(8,128)(2,1)S(1)} %collective-permute-done.15.refs_1_, bf16[8,6272]{1,0:T(8,128)(2,1)S(1)} %collective-permute-done.17.refs_2_, f32[8,6272]{1,0:T(8,128)S(1)} %get-tuple-element.40.refs_3_, ...), custom_call_target="tpu_custom_call" | custom-call | tf_op jit(solution)/shard_map/combine/pallas_call | solution.py:309
  (51 shorter events, 1.4 us)
Async XLA Ops:
  0.9 21.5 %slice-start.4 = ((s8[14680064]{0:T(1024)(128)(4,1)}), s8[4194304]{0:T(1024)(128)(4,1)S(1)}, s32[]{:S(2)}) async-start(s8[14680064]{0:T(1024)(128)(4,1)} %bitcast.5), calls=%async_computation.4 | async-start | bytes 8388608
  0.9 21.5 %slice-start.8 = ((s8[14680064]{0:T(1024)(128)(4,1)}), s8[4194304]{0:T(1024)(128)(4,1)S(1)}, s32[]{:S(2)}) async-start(s8[14680064]{0:T(1024)(128)(4,1)} %bitcast.7), calls=%async_computation.8 | async-start | bytes 8388608
  1.0 21.4 %slice-start.5 = ((s8[14680064]{0:T(1024)(128)(4,1)}), s8[4194304]{0:T(1024)(128)(4,1)S(1)}, s32[]{:S(2)}) async-start(s8[14680064]{0:T(1024)(128)(4,1)} %bitcast.5), calls=%async_computation.5 | async-start | bytes 8388608
  1.0 21.4 %slice-start.6 = ((s8[14680064]{0:T(1024)(128)(4,1)}), s8[4194304]{0:T(1024)(128)(4,1)S(1)}, s32[]{:S(2)}) async-start(s8[14680064]{0:T(1024)(128)(4,1)} %bitcast.5), calls=%async_computation.6 | async-start | bytes 8388608
  1.0 21.4 %slice-start.7 = ((s8[14680064]{0:T(1024)(128)(4,1)}), s8[2097152]{0:T(1024)(128)(4,1)S(1)}, s32[]{:S(2)}) async-start(s8[14680064]{0:T(1024)(128)(4,1)} %bitcast.5), calls=%async_computation.7 | async-start | bytes 4194304
  1.0 21.4 %slice-start.9 = ((s8[14680064]{0:T(1024)(128)(4,1)}), s8[4194304]{0:T(1024)(128)(4,1)S(1)}, s32[]{:S(2)}) async-start(s8[14680064]{0:T(1024)(128)(4,1)} %bitcast.7), calls=%async_computation.9 | async-start | bytes 8388608
  1.0 21.4 %slice-start.10 = ((s8[14680064]{0:T(1024)(128)(4,1)}), s8[4194304]{0:T(1024)(128)(4,1)S(1)}, s32[]{:S(2)}) async-start(s8[14680064]{0:T(1024)(128)(4,1)} %bitcast.7), calls=%async_computation.10 | async-start | bytes 8388608
  1.0 21.4 %slice-start.11 = ((s8[14680064]{0:T(1024)(128)(4,1)}), s8[2097152]{0:T(1024)(128)(4,1)S(1)}, s32[]{:S(2)}) async-start(s8[14680064]{0:T(1024)(128)(4,1)} %bitcast.7), calls=%async_computation.11 | async-start | bytes 4194304
  1.3 8.9 %collective-permute-start = (bf16[8,6272]{1,0:T(8,128)(2,1)S(1)}, bf16[8,6272]{1,0:T(8,128)(2,1)S(1)}, u32[]{:S(2)}, u32[]{:S(2)}) collective-permute-start(bf16[8,6272]{1,0:T(8,128)(2,1)S(1)} %get-tuple-element.28), channel_id=1, source_target_pairs={{0,12},{2,14},{4,8},{6,10},{8,4},{10,6},{12,0},{14,2},{1,13},{3,15... | collective-permute-start | bytes 301064 | tf_op jit(solution)/shard_map/ppermute | solution.py:326
  6.4 8.4 %collective-permute-start.1 = (bf16[8,6272]{1,0:T(8,128)(2,1)S(1)}, bf16[8,6272]{1,0:T(8,128)(2,1)S(1)}, u32[]{:S(2)}, u32[]{:S(2)}) collective-permute-start(bf16[8,6272]{1,0:T(8,128)(2,1)S(1)} %get-tuple-element.29), channel_id=1, source_target_pairs={{0,8},{2,10},{4,12},{6,14},{8,0},{10,2},{12,4},{14,6},{1,9},{3,11}... | collective-permute-start | bytes 301064 | tf_op jit(solution)/shard_map/ppermute | solution.py:326
  6.4 10.0 %collective-permute-start.2 = (bf16[8,6272]{1,0:T(8,128)(2,1)S(1)}, bf16[8,6272]{1,0:T(8,128)(2,1)S(1)}, u32[]{:S(2)}, u32[]{:S(2)}) collective-permute-start(bf16[8,6272]{1,0:T(8,128)(2,1)S(1)} %get-tuple-element.30), channel_id=1, source_target_pairs={{0,4},{2,6},{4,0},{6,2},{8,12},{10,14},{12,8},{14,10},{1,5},{3,7},... | collective-permute-start | bytes 301064 | tf_op jit(solution)/shard_map/ppermute | solution.py:326
  7.0 10.0 %collective-permute-start.3 = (bf16[8,6272]{1,0:T(8,128)(2,1)S(1)}, bf16[8,6272]{1,0:T(8,128)(2,1)S(1)}, u32[]{:S(2)}, u32[]{:S(2)}) collective-permute-start(bf16[8,6272]{1,0:T(8,128)(2,1)S(1)} %get-tuple-element.27.refs_0_), channel_id=1, source_target_pairs={{0,2},{2,0},{4,6},{6,4},{8,10},{10,8},{12,14},{14,12},{1,3},{3,1},... | collective-permute-start | bytes 301064 | tf_op jit(solution)/shard_map/ppermute | solution.py:329
  10.1 6.9 %collective-permute-start.4 = (bf16[8,6272]{1,0:T(8,128)(2,1)S(1)}, bf16[8,6272]{1,0:T(8,128)(2,1)S(1)}, u32[]{:S(2)}, u32[]{:S(2)}) collective-permute-start(bf16[8,6272]{1,0:T(8,128)(2,1)S(1)} %collective-permute-done.refs_1_), channel_id=1, source_target_pairs={{0,2},{2,0},{4,6},{6,4},{8,10},{10,8},{12,14},{14,12},{1,3},{3,1},... | collective-permute-start | bytes 301064 | tf_op jit(solution)/shard_map/ppermute | solution.py:329
  14.8 5.1 %collective-permute-start.5 = (bf16[8,6272]{1,0:T(8,128)(2,1)S(1)}, bf16[8,6272]{1,0:T(8,128)(2,1)S(1)}, u32[]{:S(2)}, u32[]{:S(2)}) collective-permute-start(bf16[8,6272]{1,0:T(8,128)(2,1)S(1)} %collective-permute-done.1.refs_2_), channel_id=1, source_target_pairs={{0,2},{2,0},{4,6},{6,4},{8,10},{10,8},{12,14},{14,12},{1,3},{3,1},... | collective-permute-start | bytes 301064 | tf_op jit(solution)/shard_map/ppermute | solution.py:329
  16.3 4.7 %collective-permute-start.6 = (bf16[8,6272]{1,0:T(8,128)(2,1)S(1)}, bf16[8,6272]{1,0:T(8,128)(2,1)S(1)}, u32[]{:S(2)}, u32[]{:S(2)}) collective-permute-start(bf16[8,6272]{1,0:T(8,128)(2,1)S(1)} %collective-permute-done.2.refs_3_), channel_id=1, source_target_pairs={{0,2},{2,0},{4,6},{6,4},{8,10},{10,8},{12,14},{14,12},{1,3},{3,1},... | collective-permute-start | bytes 301064 | tf_op jit(solution)/shard_map/ppermute | solution.py:329
  16.9 4.2 %collective-permute-start.7 = (bf16[32,6272]{1,0:T(8,128)(2,1)S(1)}, bf16[32,6272]{1,0:T(8,128)(2,1)S(1)}, u32[]{:S(2)}, u32[]{:S(2)}) collective-permute-start(bf16[32,6272]{1,0:T(8,128)(2,1)S(1)} %stack.4), channel_id=1, source_target_pairs={{0,1},{1,0},{2,3},{3,2},{4,5},{5,4},{6,7},{7,6},{8,9},{9,8},{10,11... | collective-permute-start | bytes 1204232 | tf_op jit(solution)/shard_map/ppermute | solution.py:332
  20.0 1.7 %collective-permute-start.8 = (bf16[24,6272]{1,0:T(8,128)(2,1)S(1)}, bf16[24,6272]{1,0:T(8,128)(2,1)S(1)}, u32[]{:S(2)}, u32[]{:S(2)}) collective-permute-start(bf16[24,6272]{1,0:T(8,128)(2,1)S(1)} %stack.5), channel_id=1, source_target_pairs={{0,1},{1,0},{2,3},{3,2},{4,5},{5,4},{6,7},{7,6},{8,9},{9,8},{10,11... | collective-permute-start | bytes 903176 | tf_op jit(solution)/shard_map/ppermute | solution.py:332
  21.0 1.4 %collective-permute-start.9 = (bf16[8,6272]{1,0:T(8,128)(2,1)S(1)}, bf16[8,6272]{1,0:T(8,128)(2,1)S(1)}, u32[]{:S(2)}, u32[]{:S(2)}) collective-permute-start(bf16[8,6272]{1,0:T(8,128)(2,1)S(1)} %stack.6), channel_id=1, source_target_pairs={{0,1},{1,0},{2,3},{3,2},{4,5},{5,4},{6,7},{7,6},{8,9},{9,8},{10,11... | collective-permute-start | bytes 301064 | tf_op jit(solution)/shard_map/ppermute | solution.py:332
  21.6 4.9 %slice-start = ((s8[14680064]{0:T(1024)(128)(4,1)}), s8[4194304]{0:T(1024)(128)(4,1)S(1)}, s32[]{:S(2)}) async-start(s8[14680064]{0:T(1024)(128)(4,1)} %bitcast.3), calls=%async_computation | async-start | bytes 8388608
  22.1 4.5 %slice-start.1 = ((s8[14680064]{0:T(1024)(128)(4,1)}), s8[4194304]{0:T(1024)(128)(4,1)S(1)}, s32[]{:S(2)}) async-start(s8[14680064]{0:T(1024)(128)(4,1)} %bitcast.3), calls=%async_computation.1 | async-start | bytes 8388608
  22.1 4.5 %slice-start.2 = ((s8[14680064]{0:T(1024)(128)(4,1)}), s8[4194304]{0:T(1024)(128)(4,1)S(1)}, s32[]{:S(2)}) async-start(s8[14680064]{0:T(1024)(128)(4,1)} %bitcast.3), calls=%async_computation.2 | async-start | bytes 8388608
  22.1 4.9 %slice-start.3 = ((s8[14680064]{0:T(1024)(128)(4,1)}), s8[2097152]{0:T(1024)(128)(4,1)S(1)}, s32[]{:S(2)}) async-start(s8[14680064]{0:T(1024)(128)(4,1)} %bitcast.3), calls=%async_computation.3 | async-start | bytes 4194304
  29.2 1.4 %collective-permute-start.10 = (bf16[8,6272]{1,0:T(8,128)(2,1)S(1)}, bf16[8,6272]{1,0:T(8,128)(2,1)S(1)}, u32[]{:S(2)}, u32[]{:S(2)}) collective-permute-start(bf16[8,6272]{1,0:T(8,128)(2,1)S(1)} %get-tuple-element.34), channel_id=1, source_target_pairs={{0,1},{1,0},{2,3},{3,2},{4,5},{5,4},{6,7},{7,6},{8,9},{9,8},{10,11... | collective-permute-start | bytes 301064 | tf_op jit(solution)/shard_map/ppermute | solution.py:332
  30.7 2.2 %collective-permute-start.11 = (bf16[56,6272]{1,0:T(8,128)(2,1)S(1)}, bf16[56,6272]{1,0:T(8,128)(2,1)S(1)}, u32[]{:S(2)}, u32[]{:S(2)}) collective-permute-start(bf16[56,6272]{1,0:T(8,128)(2,1)S(1)} %stack.7), channel_id=1, source_target_pairs={{0,1},{1,0},{2,3},{3,2},{4,5},{5,4},{6,7},{7,6},{8,9},{9,8},{10,11... | collective-permute-start | bytes 2107400 | tf_op jit(solution)/shard_map/ppermute | solution.py:332
  30.9 5.3 %collective-permute-start.12 = (bf16[8,6272]{1,0:T(8,128)(2,1)S(1)}, bf16[8,6272]{1,0:T(8,128)(2,1)S(1)}, u32[]{:S(2)}, u32[]{:S(2)}) collective-permute-start(bf16[8,6272]{1,0:T(8,128)(2,1)S(1)} %pair_sum.4.refs_1_), channel_id=1, source_target_pairs={{0,2},{2,0},{4,6},{6,4},{8,10},{10,8},{12,14},{14,12},{1,3},{3,1},... | collective-permute-start | bytes 301064 | tf_op jit(solution)/shard_map/ppermute | solution.py:329
  33.0 5.7 %collective-permute-start.14 = (bf16[8,6272]{1,0:T(8,128)(2,1)S(1)}, bf16[8,6272]{1,0:T(8,128)(2,1)S(1)}, u32[]{:S(2)}, u32[]{:S(2)}) collective-permute-start(bf16[8,6272]{1,0:T(8,128)(2,1)S(1)} %get-tuple-element.37), channel_id=1, source_target_pairs={{0,2},{2,0},{4,6},{6,4},{8,10},{10,8},{12,14},{14,12},{1,3},{3,1},... | collective-permute-start | bytes 301064 | tf_op jit(solution)/shard_map/ppermute | solution.py:329
  34.4 6.0 %collective-permute-start.16 = (bf16[8,6272]{1,0:T(8,128)(2,1)S(1)}, bf16[8,6272]{1,0:T(8,128)(2,1)S(1)}, u32[]{:S(2)}, u32[]{:S(2)}) collective-permute-start(bf16[8,6272]{1,0:T(8,128)(2,1)S(1)} %get-tuple-element.39), channel_id=1, source_target_pairs={{0,2},{2,0},{4,6},{6,4},{8,10},{10,8},{12,14},{14,12},{1,3},{3,1},... | collective-permute-start | bytes 301064 | tf_op jit(solution)/shard_map/ppermute | solution.py:329
  36.2 7.2 %collective-permute-start.13 = (bf16[8,6272]{1,0:T(8,128)(2,1)S(1)}, bf16[8,6272]{1,0:T(8,128)(2,1)S(1)}, u32[]{:S(2)}, u32[]{:S(2)}) collective-permute-start(bf16[8,6272]{1,0:T(8,128)(2,1)S(1)} %span_sum.3), channel_id=1, source_target_pairs={{0,12},{2,14},{4,8},{6,10},{8,4},{10,6},{12,0},{14,2},{1,13},{3,15... | collective-permute-start | bytes 301064 | tf_op jit(solution)/shard_map/ppermute | solution.py:326
  38.7 8.5 %collective-permute-start.15 = (bf16[8,6272]{1,0:T(8,128)(2,1)S(1)}, bf16[8,6272]{1,0:T(8,128)(2,1)S(1)}, u32[]{:S(2)}, u32[]{:S(2)}) collective-permute-start(bf16[8,6272]{1,0:T(8,128)(2,1)S(1)} %span_sum.4.refs_1_), channel_id=1, source_target_pairs={{0,8},{2,10},{4,12},{6,14},{8,0},{10,2},{12,4},{14,6},{1,9},{3,11}... | collective-permute-start | bytes 301064 | tf_op jit(solution)/shard_map/ppermute | solution.py:326
  40.4 7.2 %collective-permute-start.17 = (bf16[8,6272]{1,0:T(8,128)(2,1)S(1)}, bf16[8,6272]{1,0:T(8,128)(2,1)S(1)}, u32[]{:S(2)}, u32[]{:S(2)}) collective-permute-start(bf16[8,6272]{1,0:T(8,128)(2,1)S(1)} %span_sum.5), channel_id=1, source_target_pairs={{0,4},{2,6},{4,0},{6,2},{8,12},{10,14},{12,8},{14,10},{1,5},{3,7},... | collective-permute-start | bytes 301064 | tf_op jit(solution)/shard_map/ppermute | solution.py:326
  41.5 6.0 %collective-permute-start.18 = (bf16[8,6272]{1,0:T(8,128)(2,1)S(1)}, bf16[8,6272]{1,0:T(8,128)(2,1)S(1)}, u32[]{:S(2)}, u32[]{:S(2)}) collective-permute-start(bf16[8,6272]{1,0:T(8,128)(2,1)S(1)} %pair_sum.7), channel_id=1, source_target_pairs={{0,2},{2,0},{4,6},{6,4},{8,10},{10,8},{12,14},{14,12},{1,3},{3,1},... | collective-permute-start | bytes 301064 | tf_op jit(solution)/shard_map/ppermute | solution.py:329

commit v19 on v17

--- a/solution.py
+++ b/solution.py
@@ -370,7 +370,7 @@
     returned = {s: over_experts(totals[s], s) for s in RETURN_ORDER}
     far, *later = RETURN_ORDER
     early = combine(sides, [], [far], [[returned[far]]], width, jnp.float32)
-    return combine(sides, [early], later + [0], [[returned[s]] for s in later] + [sums[0]], width, jnp.bfloat16, 2)
+    return combine(sides, [early], later + [0], [[returned[s]] for s in later] + [sums[0]], width, jnp.bfloat16, 4)
 
 
 def solution(mesh):

time: 46.5 us -> 46.5 us (level)
  no operation moved by 1% of the time
where the time goes in v19:
time: 46.5 us; the launch traced here: 46.4 us
  starting transfers between devices  24.2 us (52%)
  waiting for transfers between devices  12.6 us (27%)
  Pallas kernels  9.19 us (20%)
    ppermute x6, starting transfers between devices, over_experts(): lax.ppermute(value, 'attn', [(i, (i // span ^ other) * span + i % span) f...  11.8 us
    ppermute x8, starting transfers between devices, over_span(): lax.ppermute(value, 'attn', [(i, i // span * span + (i + shift) % span) f...  11.4 us
    ppermute x6, waiting for transfers between devices, over_experts(): lax.ppermute(value, 'attn', [(i, (i // span ^ other) * span + i % span) f...  6.66 us
    pallas_call x1, Pallas kernels, gate_up(): pl.pallas_call(functools.partial(gate_up_kernel, block_of(units, N_BLOCK)...  4.09 us
    ppermute x8, waiting for transfers between devices, over_span(): lax.ppermute(value, 'attn', [(i, i // span * span + (i + shift) % span) f...  3.89 us
    pallas_call x1, Pallas kernels, down(): pl.pallas_call(functools.partial(down_kernel, rows, sources), in_specs=[p...  2.21 us
    ppermute x5, waiting for transfers between devices, over_pair(): lax.ppermute(value, 'ffn', [(i, (i + shift) % pair) for i in range(pair)])  2 us
    ppermute x5, starting transfers between devices, over_pair(): lax.ppermute(value, 'ffn', [(i, (i + shift) % pair) for i in range(pair)])  1.07 us
  transfers between devices with their start and end apart: 19, of which 11 were waited for; matrix products, arithmetic and copies ran while one was open for 0% of the time, Pallas kernels for 2%

profile of v19, /device:TPU:0, one launch (start us, length us, event | category | flops | bytes accessed | tf_op | source)
XLA Modules:
  0.0 46.4 jit_solution(511553334810501475)
XLA Ops:
  0.0 0.9 %load.1 = (bf16[8,7168]{1,0:T(8,128)(2,1)S(1)}, s32[3,8]{1,0:T(4,128)S(1)}, f32[3,8]{1,0:T(4,128)S(1)}) custom-call(bf16[8,7168]{1,0:T(8,128)(2,1)} %refs_0_.1, s32[3,8]{1,0:T(4,128)} %bitcast.9, f32[3,8]{1,0:T(4,128)} %bitcast.10), custom_call_target="tpu_custom_call" | custom-call | tf_op jit(solution)/shard_map/load/pallas_call | solution.py:215
  1.0 0.2 pack.1
  1.3 5.1 %collective-permute-start = (bf16[8,6272]{1,0:T(8,128)(2,1)S(1)}, bf16[8,6272]{1,0:T(8,128)(2,1)S(1)}, u32[]{:S(2)}, u32[]{:S(2)}) collective-permute-start(bf16[8,6272]{1,0:T(8,128)(2,1)S(1)} %get-tuple-element.28), channel_id=1, source_target_pairs={{0,12},{2,14},{4,8},{6,10},{8,4},{10,6},{12,0},{14,2},{1,13},{3,15... | collective-permute-start | bytes 301064 | tf_op jit(solution)/shard_map/ppermute | solution.py:326
  6.4 0.6 %collective-permute-start.2 = (bf16[8,6272]{1,0:T(8,128)(2,1)S(1)}, bf16[8,6272]{1,0:T(8,128)(2,1)S(1)}, u32[]{:S(2)}, u32[]{:S(2)}) collective-permute-start(bf16[8,6272]{1,0:T(8,128)(2,1)S(1)} %get-tuple-element.30), channel_id=1, source_target_pairs={{0,8},{2,10},{4,12},{6,14},{8,0},{10,2},{12,4},{14,6},{1,9},{3,11}... | collective-permute-start | bytes 301064 | tf_op jit(solution)/shard_map/ppermute | solution.py:326
  7.0 1.7 %collective-permute-start.3 = (bf16[8,6272]{1,0:T(8,128)(2,1)S(1)}, bf16[8,6272]{1,0:T(8,128)(2,1)S(1)}, u32[]{:S(2)}, u32[]{:S(2)}) collective-permute-start(bf16[8,6272]{1,0:T(8,128)(2,1)S(1)} %get-tuple-element.27.refs_0_), channel_id=1, source_target_pairs={{0,2},{2,0},{4,6},{6,4},{8,10},{10,8},{12,14},{14,12},{1,3},{3,1},... | collective-permute-start | bytes 301064 | tf_op jit(solution)/shard_map/ppermute | solution.py:329
  8.7 1.4 %collective-permute-done.refs_1_ = bf16[8,6272]{1,0:T(8,128)(2,1)S(1)} collective-permute-done((bf16[8,6272]{1,0:T(8,128)(2,1)S(1)}, bf16[8,6272]{1,0:T(8,128)(2,1)S(1)}, u32[]{:S(2)}, u32[]{:S(2)}) %collective-permute-start) | collective-permute-done | bytes 100384 | tf_op jit(solution)/shard_map/ppermute | solution.py:326
  10.1 1.7 %collective-permute-start.4 = (bf16[8,6272]{1,0:T(8,128)(2,1)S(1)}, bf16[8,6272]{1,0:T(8,128)(2,1)S(1)}, u32[]{:S(2)}, u32[]{:S(2)}) collective-permute-start(bf16[8,6272]{1,0:T(8,128)(2,1)S(1)} %collective-permute-done.refs_1_), channel_id=1, source_target_pairs={{0,2},{2,0},{4,6},{6,4},{8,10},{10,8},{12,14},{14,12},{1,3},{3,1},... | collective-permute-start | bytes 301064 | tf_op jit(solution)/shard_map/ppermute | solution.py:329
  11.8 0.7 %collective-permute-done.1.refs_2_ = bf16[8,6272]{1,0:T(8,128)(2,1)S(1)} collective-permute-done((bf16[8,6272]{1,0:T(8,128)(2,1)S(1)}, bf16[8,6272]{1,0:T(8,128)(2,1)S(1)}, u32[]{:S(2)}, u32[]{:S(2)}) %collective-permute-start.1) | collective-permute-done | bytes 100384 | tf_op jit(solution)/shard_map/ppermute | solution.py:326
  12.5 1.5 %collective-permute-start.5 = (bf16[8,6272]{1,0:T(8,128)(2,1)S(1)}, bf16[8,6272]{1,0:T(8,128)(2,1)S(1)}, u32[]{:S(2)}, u32[]{:S(2)}) collective-permute-start(bf16[8,6272]{1,0:T(8,128)(2,1)S(1)} %collective-permute-done.1.refs_2_), channel_id=1, source_target_pairs={{0,2},{2,0},{4,6},{6,4},{8,10},{10,8},{12,14},{14,12},{1,3},{3,1},... | collective-permute-start | bytes 301064 | tf_op jit(solution)/shard_map/ppermute | solution.py:329
  14.0 0.8 %collective-permute-done.2.refs_3_ = bf16[8,6272]{1,0:T(8,128)(2,1)S(1)} collective-permute-done((bf16[8,6272]{1,0:T(8,128)(2,1)S(1)}, bf16[8,6272]{1,0:T(8,128)(2,1)S(1)}, u32[]{:S(2)}, u32[]{:S(2)}) %collective-permute-start.2) | collective-permute-done | bytes 100384 | tf_op jit(solution)/shard_map/ppermute | solution.py:326
  14.8 1.5 %collective-permute-start.6 = (bf16[8,6272]{1,0:T(8,128)(2,1)S(1)}, bf16[8,6272]{1,0:T(8,128)(2,1)S(1)}, u32[]{:S(2)}, u32[]{:S(2)}) collective-permute-start(bf16[8,6272]{1,0:T(8,128)(2,1)S(1)} %collective-permute-done.2.refs_3_), channel_id=1, source_target_pairs={{0,2},{2,0},{4,6},{6,4},{8,10},{10,8},{12,14},{14,12},{1,3},{3,1},... | collective-permute-start | bytes 301064 | tf_op jit(solution)/shard_map/ppermute | solution.py:329
  16.5 1.0 %collective-permute-done.5.refs_2_.refs_6_ = bf16[8,6272]{1,0:T(8,128)(2,1)S(1)} collective-permute-done((bf16[8,6272]{1,0:T(8,128)(2,1)S(1)}, bf16[8,6272]{1,0:T(8,128)(2,1)S(1)}, u32[]{:S(2)}, u32[]{:S(2)}) %collective-permute-start.5) | collective-permute-done | bytes 100384 | tf_op jit(solution)/shard_map/ppermute | solution.py:329
  17.6 1.9 %collective-permute-done.6.refs_7_.refs_0_ = bf16[8,6272]{1,0:T(8,128)(2,1)S(1)} collective-permute-done((bf16[8,6272]{1,0:T(8,128)(2,1)S(1)}, bf16[8,6272]{1,0:T(8,128)(2,1)S(1)}, u32[]{:S(2)}, u32[]{:S(2)}) %collective-permute-start.6) | collective-permute-done | bytes 100384 | tf_op jit(solution)/shard_map/ppermute | solution.py:329
  19.6 0.5 unpack.1.first_ref
  20.1 0.8 %collective-permute-done.9.last_ref = bf16[8,6272]{1,0:T(8,128)(2,1)S(1)} collective-permute-done((bf16[8,6272]{1,0:T(8,128)(2,1)S(1)}, bf16[8,6272]{1,0:T(8,128)(2,1)S(1)}, u32[]{:S(2)}, u32[]{:S(2)}) %collective-permute-start.9) | collective-permute-done | bytes 100384 | tf_op jit(solution)/shard_map/ppermute | solution.py:332
  20.9 4.1 %gate_up.1.hidden_ref = bf16[128,1024]{1,0:T(8,128)(2,1)S(1)} custom-call(bf16[120,7168]{1,0:T(8,128)(2,1)S(1)} %unpack.1.first_ref, bf16[8,6272]{1,0:T(8,128)(2,1)S(1)} %collective-permute-done.9.last_ref, bf16[7168,1024]{1,0:T(8,128)(2,1)S(1)} %bitcast.6, bf16[7168,1024]{1,0:T(8,128)(2,1)S(1)} %bitcast.8), custom_call_target="tpu_custom_call" | custom-call | flops 3758096384 | tf_op jit(solution)/shard_map/gate_up/pallas_call | solution.py:113
  25.1 2.2 %down.1 = (f32[32,6272]{1,0:T(8,128)S(1)}, f32[32,6272]{1,0:T(8,128)S(1)}, bf16[8,6272]{1,0:T(8,128)(2,1)S(1)}, bf16[56,6272]{1,0:T(8,128)(2,1)S(1)}) custom-call(bf16[128,1024]{1,0:T(8,128)(2,1)S(1)} %gate_up.1.hidden_ref, bf16[1024,7168]{1,0:T(8,128)(2,1)S(1)} %bitcast.4), custom_call_target="tpu_custom_call" | custom-call | flops 1644167168 | tf_op jit(solution)/shard_map/down/pallas_call | solution.py:157
  27.3 0.4 collective-permute-start.10
  27.7 0.9 %collective-permute-done.10.refs_0_ = bf16[8,6272]{1,0:T(8,128)(2,1)S(1)} collective-permute-done((bf16[8,6272]{1,0:T(8,128)(2,1)S(1)}, bf16[8,6272]{1,0:T(8,128)(2,1)S(1)}, u32[]{:S(2)}, u32[]{:S(2)}) %collective-permute-start.10) | collective-permute-done | bytes 100384 | tf_op jit(solution)/shard_map/ppermute | solution.py:332
  28.7 0.4 collective-permute-start.11
  29.2 1.5 %collective-permute-start.12 = (bf16[8,6272]{1,0:T(8,128)(2,1)S(1)}, bf16[8,6272]{1,0:T(8,128)(2,1)S(1)}, u32[]{:S(2)}, u32[]{:S(2)}) collective-permute-start(bf16[8,6272]{1,0:T(8,128)(2,1)S(1)} %pair_sum.4.refs_1_), channel_id=1, source_target_pairs={{0,2},{2,0},{4,6},{6,4},{8,10},{10,8},{12,14},{14,12},{1,3},{3,1},... | collective-permute-start | bytes 301064 | tf_op jit(solution)/shard_map/ppermute | solution.py:329
  30.7 0.3 collective-permute-done.11.refs_0_
  31.0 1.6 %collective-permute-start.14 = (bf16[8,6272]{1,0:T(8,128)(2,1)S(1)}, bf16[8,6272]{1,0:T(8,128)(2,1)S(1)}, u32[]{:S(2)}, u32[]{:S(2)}) collective-permute-start(bf16[8,6272]{1,0:T(8,128)(2,1)S(1)} %get-tuple-element.37), channel_id=1, source_target_pairs={{0,2},{2,0},{4,6},{6,4},{8,10},{10,8},{12,14},{14,12},{1,3},{3,1},... | collective-permute-start | bytes 301064 | tf_op jit(solution)/shard_map/ppermute | solution.py:329
  32.6 0.5 %collective-permute-start.16 = (bf16[8,6272]{1,0:T(8,128)(2,1)S(1)}, bf16[8,6272]{1,0:T(8,128)(2,1)S(1)}, u32[]{:S(2)}, u32[]{:S(2)}) collective-permute-start(bf16[8,6272]{1,0:T(8,128)(2,1)S(1)} %get-tuple-element.39), channel_id=1, source_target_pairs={{0,2},{2,0},{4,6},{6,4},{8,10},{10,8},{12,14},{14,12},{1,3},{3,1},... | collective-permute-start | bytes 301064 | tf_op jit(solution)/shard_map/ppermute | solution.py:329
  33.2 0.9 %collective-permute-done.12.refs_1_ = bf16[8,6272]{1,0:T(8,128)(2,1)S(1)} collective-permute-done((bf16[8,6272]{1,0:T(8,128)(2,1)S(1)}, bf16[8,6272]{1,0:T(8,128)(2,1)S(1)}, u32[]{:S(2)}, u32[]{:S(2)}) %collective-permute-start.12) | collective-permute-done | bytes 100384 | tf_op jit(solution)/shard_map/ppermute | solution.py:329
  34.1 2.9 %collective-permute-start.13 = (bf16[8,6272]{1,0:T(8,128)(2,1)S(1)}, bf16[8,6272]{1,0:T(8,128)(2,1)S(1)}, u32[]{:S(2)}, u32[]{:S(2)}) collective-permute-start(bf16[8,6272]{1,0:T(8,128)(2,1)S(1)} %span_sum.3), channel_id=1, source_target_pairs={{0,12},{2,14},{4,8},{6,10},{8,4},{10,6},{12,0},{14,2},{1,13},{3,15... | collective-permute-start | bytes 301064 | tf_op jit(solution)/shard_map/ppermute | solution.py:326
  37.0 1.3 %collective-permute-start.15 = (bf16[8,6272]{1,0:T(8,128)(2,1)S(1)}, bf16[8,6272]{1,0:T(8,128)(2,1)S(1)}, u32[]{:S(2)}, u32[]{:S(2)}) collective-permute-start(bf16[8,6272]{1,0:T(8,128)(2,1)S(1)} %span_sum.4.refs_1_), channel_id=1, source_target_pairs={{0,8},{2,10},{4,12},{6,14},{8,0},{10,2},{12,4},{14,6},{1,9},{3,11}... | collective-permute-start | bytes 301064 | tf_op jit(solution)/shard_map/ppermute | solution.py:326
  38.2 0.1 collective-permute-done.16.refs_1_
  38.4 1.9 %collective-permute-start.17 = (bf16[8,6272]{1,0:T(8,128)(2,1)S(1)}, bf16[8,6272]{1,0:T(8,128)(2,1)S(1)}, u32[]{:S(2)}, u32[]{:S(2)}) collective-permute-start(bf16[8,6272]{1,0:T(8,128)(2,1)S(1)} %span_sum.5), channel_id=1, source_target_pairs={{0,4},{2,6},{4,0},{6,2},{8,12},{10,14},{12,8},{14,10},{1,5},{3,7},... | collective-permute-start | bytes 301064 | tf_op jit(solution)/shard_map/ppermute | solution.py:326
  40.3 1.4 %collective-permute-start.18 = (bf16[8,6272]{1,0:T(8,128)(2,1)S(1)}, bf16[8,6272]{1,0:T(8,128)(2,1)S(1)}, u32[]{:S(2)}, u32[]{:S(2)}) collective-permute-start(bf16[8,6272]{1,0:T(8,128)(2,1)S(1)} %pair_sum.7), channel_id=1, source_target_pairs={{0,2},{2,0},{4,6},{6,4},{8,10},{10,8},{12,14},{14,12},{1,3},{3,1},... | collective-permute-start | bytes 301064 | tf_op jit(solution)/shard_map/ppermute | solution.py:329
  41.8 3.8 %collective-permute-done.15.refs_1_ = bf16[8,6272]{1,0:T(8,128)(2,1)S(1)} collective-permute-done((bf16[8,6272]{1,0:T(8,128)(2,1)S(1)}, bf16[8,6272]{1,0:T(8,128)(2,1)S(1)}, u32[]{:S(2)}, u32[]{:S(2)}) %collective-permute-start.15) | collective-permute-done | bytes 100384 | tf_op jit(solution)/shard_map/ppermute | solution.py:326
  45.5 0.8 %combine.3 = bf16[8,7168]{1,0:T(8,128)(2,1)} custom-call(f32[8,1024]{1,0:T(8,128)S(1)} %get-tuple-element.26.sides_ref, f32[8,7168]{1,0:T(8,128)S(1)} %combine.2.refs_0_, bf16[8,6272]{1,0:T(8,128)(2,1)S(1)} %collective-permute-done.15.refs_1_, bf16[8,6272]{1,0:T(8,128)(2,1)S(1)} %collective-permute-done.17.refs_2_, f32[8,6272]{1,0:T(8,128)S(1)} %get-tuple-element.40.refs_3_, ...), custom_call_target="tpu_custom_call" | custom-call | tf_op jit(solution)/shard_map/combine/pallas_call | solution.py:309
  (51 shorter events, 0.7 us)
Async XLA Ops:
  0.9 19.9 %slice-start.4 = ((s8[14680064]{0:T(1024)(128)(4,1)}), s8[4194304]{0:T(1024)(128)(4,1)S(1)}, s32[]{:S(2)}) async-start(s8[14680064]{0:T(1024)(128)(4,1)} %bitcast.5), calls=%async_computation.4 | async-start | bytes 8388608
  0.9 19.9 %slice-start.8 = ((s8[14680064]{0:T(1024)(128)(4,1)}), s8[4194304]{0:T(1024)(128)(4,1)S(1)}, s32[]{:S(2)}) async-start(s8[14680064]{0:T(1024)(128)(4,1)} %bitcast.7), calls=%async_computation.8 | async-start | bytes 8388608
  1.0 19.9 %slice-start.5 = ((s8[14680064]{0:T(1024)(128)(4,1)}), s8[4194304]{0:T(1024)(128)(4,1)S(1)}, s32[]{:S(2)}) async-start(s8[14680064]{0:T(1024)(128)(4,1)} %bitcast.5), calls=%async_computation.5 | async-start | bytes 8388608
  1.0 19.9 %slice-start.6 = ((s8[14680064]{0:T(1024)(128)(4,1)}), s8[4194304]{0:T(1024)(128)(4,1)S(1)}, s32[]{:S(2)}) async-start(s8[14680064]{0:T(1024)(128)(4,1)} %bitcast.5), calls=%async_computation.6 | async-start | bytes 8388608
  1.0 19.9 %slice-start.7 = ((s8[14680064]{0:T(1024)(128)(4,1)}), s8[2097152]{0:T(1024)(128)(4,1)S(1)}, s32[]{:S(2)}) async-start(s8[14680064]{0:T(1024)(128)(4,1)} %bitcast.5), calls=%async_computation.7 | async-start | bytes 4194304
  1.0 19.9 %slice-start.9 = ((s8[14680064]{0:T(1024)(128)(4,1)}), s8[4194304]{0:T(1024)(128)(4,1)S(1)}, s32[]{:S(2)}) async-start(s8[14680064]{0:T(1024)(128)(4,1)} %bitcast.7), calls=%async_computation.9 | async-start | bytes 8388608
  1.0 19.9 %slice-start.10 = ((s8[14680064]{0:T(1024)(128)(4,1)}), s8[4194304]{0:T(1024)(128)(4,1)S(1)}, s32[]{:S(2)}) async-start(s8[14680064]{0:T(1024)(128)(4,1)} %bitcast.7), calls=%async_computation.10 | async-start | bytes 8388608
  1.0 19.9 %slice-start.11 = ((s8[14680064]{0:T(1024)(128)(4,1)}), s8[2097152]{0:T(1024)(128)(4,1)S(1)}, s32[]{:S(2)}) async-start(s8[14680064]{0:T(1024)(128)(4,1)} %bitcast.7), calls=%async_computation.11 | async-start | bytes 4194304
  1.3 8.8 %collective-permute-start = (bf16[8,6272]{1,0:T(8,128)(2,1)S(1)}, bf16[8,6272]{1,0:T(8,128)(2,1)S(1)}, u32[]{:S(2)}, u32[]{:S(2)}) collective-permute-start(bf16[8,6272]{1,0:T(8,128)(2,1)S(1)} %get-tuple-element.28), channel_id=1, source_target_pairs={{0,12},{2,14},{4,8},{6,10},{8,4},{10,6},{12,0},{14,2},{1,13},{3,15... | collective-permute-start | bytes 301064 | tf_op jit(solution)/shard_map/ppermute | solution.py:326
  6.4 6.1 %collective-permute-start.1 = (bf16[8,6272]{1,0:T(8,128)(2,1)S(1)}, bf16[8,6272]{1,0:T(8,128)(2,1)S(1)}, u32[]{:S(2)}, u32[]{:S(2)}) collective-permute-start(bf16[8,6272]{1,0:T(8,128)(2,1)S(1)} %get-tuple-element.29), channel_id=1, source_target_pairs={{0,4},{2,6},{4,0},{6,2},{8,12},{10,14},{12,8},{14,10},{1,5},{3,7},... | collective-permute-start | bytes 301064 | tf_op jit(solution)/shard_map/ppermute | solution.py:326
  6.4 8.4 %collective-permute-start.2 = (bf16[8,6272]{1,0:T(8,128)(2,1)S(1)}, bf16[8,6272]{1,0:T(8,128)(2,1)S(1)}, u32[]{:S(2)}, u32[]{:S(2)}) collective-permute-start(bf16[8,6272]{1,0:T(8,128)(2,1)S(1)} %get-tuple-element.30), channel_id=1, source_target_pairs={{0,8},{2,10},{4,12},{6,14},{8,0},{10,2},{12,4},{14,6},{1,9},{3,11}... | collective-permute-start | bytes 301064 | tf_op jit(solution)/shard_map/ppermute | solution.py:326
  7.0 9.4 %collective-permute-start.3 = (bf16[8,6272]{1,0:T(8,128)(2,1)S(1)}, bf16[8,6272]{1,0:T(8,128)(2,1)S(1)}, u32[]{:S(2)}, u32[]{:S(2)}) collective-permute-start(bf16[8,6272]{1,0:T(8,128)(2,1)S(1)} %get-tuple-element.27.refs_0_), channel_id=1, source_target_pairs={{0,2},{2,0},{4,6},{6,4},{8,10},{10,8},{12,14},{14,12},{1,3},{3,1},... | collective-permute-start | bytes 301064 | tf_op jit(solution)/shard_map/ppermute | solution.py:329
  10.1 6.4 %collective-permute-start.4 = (bf16[8,6272]{1,0:T(8,128)(2,1)S(1)}, bf16[8,6272]{1,0:T(8,128)(2,1)S(1)}, u32[]{:S(2)}, u32[]{:S(2)}) collective-permute-start(bf16[8,6272]{1,0:T(8,128)(2,1)S(1)} %collective-permute-done.refs_1_), channel_id=1, source_target_pairs={{0,2},{2,0},{4,6},{6,4},{8,10},{10,8},{12,14},{14,12},{1,3},{3,1},... | collective-permute-start | bytes 301064 | tf_op jit(solution)/shard_map/ppermute | solution.py:329
  12.5 5.0 %collective-permute-start.5 = (bf16[8,6272]{1,0:T(8,128)(2,1)S(1)}, bf16[8,6272]{1,0:T(8,128)(2,1)S(1)}, u32[]{:S(2)}, u32[]{:S(2)}) collective-permute-start(bf16[8,6272]{1,0:T(8,128)(2,1)S(1)} %collective-permute-done.1.refs_2_), channel_id=1, source_target_pairs={{0,2},{2,0},{4,6},{6,4},{8,10},{10,8},{12,14},{14,12},{1,3},{3,1},... | collective-permute-start | bytes 301064 | tf_op jit(solution)/shard_map/ppermute | solution.py:329
  14.8 4.6 %collective-permute-start.6 = (bf16[8,6272]{1,0:T(8,128)(2,1)S(1)}, bf16[8,6272]{1,0:T(8,128)(2,1)S(1)}, u32[]{:S(2)}, u32[]{:S(2)}) collective-permute-start(bf16[8,6272]{1,0:T(8,128)(2,1)S(1)} %collective-permute-done.2.refs_3_), channel_id=1, source_target_pairs={{0,2},{2,0},{4,6},{6,4},{8,10},{10,8},{12,14},{14,12},{1,3},{3,1},... | collective-permute-start | bytes 301064 | tf_op jit(solution)/shard_map/ppermute | solution.py:329
  16.4 3.2 %collective-permute-start.7 = (bf16[32,6272]{1,0:T(8,128)(2,1)S(1)}, bf16[32,6272]{1,0:T(8,128)(2,1)S(1)}, u32[]{:S(2)}, u32[]{:S(2)}) collective-permute-start(bf16[32,6272]{1,0:T(8,128)(2,1)S(1)} %stack.4), channel_id=1, source_target_pairs={{0,1},{1,0},{2,3},{3,2},{4,5},{5,4},{6,7},{7,6},{8,9},{9,8},{10,11... | collective-permute-start | bytes 1204232 | tf_op jit(solution)/shard_map/ppermute | solution.py:332
  17.5 2.1 %collective-permute-start.8 = (bf16[24,6272]{1,0:T(8,128)(2,1)S(1)}, bf16[24,6272]{1,0:T(8,128)(2,1)S(1)}, u32[]{:S(2)}, u32[]{:S(2)}) collective-permute-start(bf16[24,6272]{1,0:T(8,128)(2,1)S(1)} %stack.5), channel_id=1, source_target_pairs={{0,1},{1,0},{2,3},{3,2},{4,5},{5,4},{6,7},{7,6},{8,9},{9,8},{10,11... | collective-permute-start | bytes 903176 | tf_op jit(solution)/shard_map/ppermute | solution.py:332
  19.5 1.4 %collective-permute-start.9 = (bf16[8,6272]{1,0:T(8,128)(2,1)S(1)}, bf16[8,6272]{1,0:T(8,128)(2,1)S(1)}, u32[]{:S(2)}, u32[]{:S(2)}) collective-permute-start(bf16[8,6272]{1,0:T(8,128)(2,1)S(1)} %stack.6), channel_id=1, source_target_pairs={{0,1},{1,0},{2,3},{3,2},{4,5},{5,4},{6,7},{7,6},{8,9},{9,8},{10,11... | collective-permute-start | bytes 301064 | tf_op jit(solution)/shard_map/ppermute | solution.py:332
  19.6 5.4 %slice-start = ((s8[14680064]{0:T(1024)(128)(4,1)}), s8[4194304]{0:T(1024)(128)(4,1)S(1)}, s32[]{:S(2)}) async-start(s8[14680064]{0:T(1024)(128)(4,1)} %bitcast.3), calls=%async_computation | async-start | bytes 8388608
  20.0 5.0 %slice-start.1 = ((s8[14680064]{0:T(1024)(128)(4,1)}), s8[4194304]{0:T(1024)(128)(4,1)S(1)}, s32[]{:S(2)}) async-start(s8[14680064]{0:T(1024)(128)(4,1)} %bitcast.3), calls=%async_computation.1 | async-start | bytes 8388608
  20.0 5.0 %slice-start.2 = ((s8[14680064]{0:T(1024)(128)(4,1)}), s8[4194304]{0:T(1024)(128)(4,1)S(1)}, s32[]{:S(2)}) async-start(s8[14680064]{0:T(1024)(128)(4,1)} %bitcast.3), calls=%async_computation.2 | async-start | bytes 8388608
  20.1 5.0 %slice-start.3 = ((s8[14680064]{0:T(1024)(128)(4,1)}), s8[2097152]{0:T(1024)(128)(4,1)S(1)}, s32[]{:S(2)}) async-start(s8[14680064]{0:T(1024)(128)(4,1)} %bitcast.3), calls=%async_computation.3 | async-start | bytes 4194304
  27.3 1.4 %collective-permute-start.10 = (bf16[8,6272]{1,0:T(8,128)(2,1)S(1)}, bf16[8,6272]{1,0:T(8,128)(2,1)S(1)}, u32[]{:S(2)}, u32[]{:S(2)}) collective-permute-start(bf16[8,6272]{1,0:T(8,128)(2,1)S(1)} %get-tuple-element.34), channel_id=1, source_target_pairs={{0,1},{1,0},{2,3},{3,2},{4,5},{5,4},{6,7},{7,6},{8,9},{9,8},{10,11... | collective-permute-start | bytes 301064 | tf_op jit(solution)/shard_map/ppermute | solution.py:332
  28.7 2.2 %collective-permute-start.11 = (bf16[56,6272]{1,0:T(8,128)(2,1)S(1)}, bf16[56,6272]{1,0:T(8,128)(2,1)S(1)}, u32[]{:S(2)}, u32[]{:S(2)}) collective-permute-start(bf16[56,6272]{1,0:T(8,128)(2,1)S(1)} %stack.7), channel_id=1, source_target_pairs={{0,1},{1,0},{2,3},{3,2},{4,5},{5,4},{6,7},{7,6},{8,9},{9,8},{10,11... | collective-permute-start | bytes 2107400 | tf_op jit(solution)/shard_map/ppermute | solution.py:332
  29.2 4.9 %collective-permute-start.12 = (bf16[8,6272]{1,0:T(8,128)(2,1)S(1)}, bf16[8,6272]{1,0:T(8,128)(2,1)S(1)}, u32[]{:S(2)}, u32[]{:S(2)}) collective-permute-start(bf16[8,6272]{1,0:T(8,128)(2,1)S(1)} %pair_sum.4.refs_1_), channel_id=1, source_target_pairs={{0,2},{2,0},{4,6},{6,4},{8,10},{10,8},{12,14},{14,12},{1,3},{3,1},... | collective-permute-start | bytes 301064 | tf_op jit(solution)/shard_map/ppermute | solution.py:329
  31.0 5.9 %collective-permute-start.14 = (bf16[8,6272]{1,0:T(8,128)(2,1)S(1)}, bf16[8,6272]{1,0:T(8,128)(2,1)S(1)}, u32[]{:S(2)}, u32[]{:S(2)}) collective-permute-start(bf16[8,6272]{1,0:T(8,128)(2,1)S(1)} %get-tuple-element.37), channel_id=1, source_target_pairs={{0,2},{2,0},{4,6},{6,4},{8,10},{10,8},{12,14},{14,12},{1,3},{3,1},... | collective-permute-start | bytes 301064 | tf_op jit(solution)/shard_map/ppermute | solution.py:329
  32.6 5.8 %collective-permute-start.16 = (bf16[8,6272]{1,0:T(8,128)(2,1)S(1)}, bf16[8,6272]{1,0:T(8,128)(2,1)S(1)}, u32[]{:S(2)}, u32[]{:S(2)}) collective-permute-start(bf16[8,6272]{1,0:T(8,128)(2,1)S(1)} %get-tuple-element.39), channel_id=1, source_target_pairs={{0,2},{2,0},{4,6},{6,4},{8,10},{10,8},{12,14},{14,12},{1,3},{3,1},... | collective-permute-start | bytes 301064 | tf_op jit(solution)/shard_map/ppermute | solution.py:329
  34.1 7.6 %collective-permute-start.13 = (bf16[8,6272]{1,0:T(8,128)(2,1)S(1)}, bf16[8,6272]{1,0:T(8,128)(2,1)S(1)}, u32[]{:S(2)}, u32[]{:S(2)}) collective-permute-start(bf16[8,6272]{1,0:T(8,128)(2,1)S(1)} %span_sum.3), channel_id=1, source_target_pairs={{0,12},{2,14},{4,8},{6,10},{8,4},{10,6},{12,0},{14,2},{1,13},{3,15... | collective-permute-start | bytes 301064 | tf_op jit(solution)/shard_map/ppermute | solution.py:326
  37.0 8.6 %collective-permute-start.15 = (bf16[8,6272]{1,0:T(8,128)(2,1)S(1)}, bf16[8,6272]{1,0:T(8,128)(2,1)S(1)}, u32[]{:S(2)}, u32[]{:S(2)}) collective-permute-start(bf16[8,6272]{1,0:T(8,128)(2,1)S(1)} %span_sum.4.refs_1_), channel_id=1, source_target_pairs={{0,8},{2,10},{4,12},{6,14},{8,0},{10,2},{12,4},{14,6},{1,9},{3,11}... | collective-permute-start | bytes 301064 | tf_op jit(solution)/shard_map/ppermute | solution.py:326
  38.4 7.2 %collective-permute-start.17 = (bf16[8,6272]{1,0:T(8,128)(2,1)S(1)}, bf16[8,6272]{1,0:T(8,128)(2,1)S(1)}, u32[]{:S(2)}, u32[]{:S(2)}) collective-permute-start(bf16[8,6272]{1,0:T(8,128)(2,1)S(1)} %span_sum.5), channel_id=1, source_target_pairs={{0,4},{2,6},{4,0},{6,2},{8,12},{10,14},{12,8},{14,10},{1,5},{3,7},... | collective-permute-start | bytes 301064 | tf_op jit(solution)/shard_map/ppermute | solution.py:326
  40.3 5.2 %collective-permute-start.18 = (bf16[8,6272]{1,0:T(8,128)(2,1)S(1)}, bf16[8,6272]{1,0:T(8,128)(2,1)S(1)}, u32[]{:S(2)}, u32[]{:S(2)}) collective-permute-start(bf16[8,6272]{1,0:T(8,128)(2,1)S(1)} %pair_sum.7), channel_id=1, source_target_pairs={{0,2},{2,0},{4,6},{6,4},{8,10},{10,8},{12,14},{14,12},{1,3},{3,1},... | collective-permute-start | bytes 301064 | tf_op jit(solution)/shard_map/ppermute | solution.py:329
